TPU v7x, 32 devices: a whole 2x2x4 slice. The times are simulated.
32 devices in a mesh: ctx: 8 (over y, x, core), fsdp: 4 (over z).
Axes of the slice: x: 2, y: 2, z: 4, core: 2. Of those that a mesh axis runs over, the one named last changes fastest.
Arguments:
- tokens: bfloat16 [4, 2048, 768], P('fsdp', 'ctx'), may hold values from -6 to 6
- prev_logits: float32 [4, 2048, 12], P('fsdp', 'ctx'), may hold values from -6 to 6
- routes: int32 [4, 2048, 2], P('fsdp', 'ctx'), may hold values from 0 to 11, all different within a row; in each aligned block of 256 rows (0 to 255, 256 to 511, ..., all dimensions but the last counted through in order) at most 64 rows name the same one
- lengths: int32 [4], P('fsdp'), may hold values from 512 to 2048, as said below
- cotangent: bfloat16 [4, 2048, 768], P('fsdp', 'ctx'), may hold values from -6 to 6
- w_qkv: bfloat16 [768, 2304], P('fsdp'), may hold values from -0.21875 to 0.21875
- w_out: bfloat16 [768, 768], P('fsdp'), may hold values from -4 to 4
- gain_attn: bfloat16 [768], replicated, may hold values from 0.25 to 1.75
- gain_moe: bfloat16 [768], replicated, may hold values from 0.25 to 1.75
- w_router: float32 [768, 12], replicated, may hold values from -0.15625 to 0.15625
- w_residual: float32 [12, 12], replicated, may hold values from -0.875 to 0.875
- const_vec: bfloat16 [2, 768], replicated, may hold values from -6 to 6
- w_expert: bfloat16 [8, 2048, 3, 768], P(None, 'fsdp'), may hold values from -0.21875 to 0.21875
Outputs:
- output: bfloat16 [4, 2048, 768], P('fsdp', 'ctx')
- grad_tokens: float32 [4, 2048, 768], P('fsdp', 'ctx')
- grad_prev_logits: float32 [4, 2048, 12], P('fsdp', 'ctx')
- grad_w_qkv: float32 [768, 2304], P('fsdp')
- grad_w_out: float32 [768, 768], P('fsdp')
- grad_gain_attn: float32 [768], replicated
- grad_gain_moe: float32 [768], replicated
- grad_w_router: float32 [768, 12], replicated
- grad_w_residual: float32 [12, 12], replicated
- grad_const_vec: float32 [2, 768], replicated
- grad_w_expert: float32 [8, 2048, 3, 768], P(None, 'fsdp')
Inputs may be any that keep to these rules, and one draw needn't show every extreme that they name: `routes`: each row names two different ids. Ids 0 to 7 are feed-forward experts, 8 the zero expert, 9 the copy expert, 10 and 11 the constant experts. In the 256 positions of one slot on one device no id is named by more than 64 rows. `lengths`: one slot drawn from the seed has length 2048.
All inputs are finite; a program needn't handle non-finite values.
Results may differ from a plain program's by a relative error of at most 0.02.
Values may be sent and summed in bfloat16 or wider, within the bound.
A program may use at most 256 MiB of HBM per device.

v0:
```python
import math

import jax
import jax.numpy as jnp
from jax import lax
from jax.sharding import PartitionSpec as P

HEAD_DIM = 64


EPSILON = 1e-05
MASKED = -1e30
HIGHEST = lax.Precision.HIGHEST


def normalize_rows(values, gain_row):
    scaling = lax.rsqrt(jnp.mean(values * values, axis=-1, keepdims=True) + EPSILON)
    return (values * scaling * gain_row, scaling)


def normalize_back(values, scaling, gain_row, grad_out):
    grad_hat = grad_out * gain_row
    grad_gain = jnp.sum(grad_out * values * scaling, axis=(0, 1))
    grad_values = scaling * grad_hat - values * scaling**3 * jnp.mean(
        grad_hat * values, axis=-1, keepdims=True
    )
    return (grad_values, grad_gain)


def rope_tables(positions, head_size):
    half_dim = head_size // 2
    frequency = jnp.exp(
        jnp.arange(half_dim, dtype=jnp.float32) * (-2.0 * math.log(10000.0) / head_size)
    )
    angles = positions.astype(jnp.float32)[:, None] * frequency[None, :]
    return (jnp.cos(angles)[:, None, :], jnp.sin(angles)[:, None, :])


def rotate(values, cosine_table, sine_table):
    half_dim = values.shape[-1] // 2
    first_half = values[..., :half_dim]
    second_half = values[..., half_dim:]
    return jnp.concatenate(
        [
            first_half * cosine_table - second_half * sine_table,
            second_half * cosine_table + first_half * sine_table,
        ],
        axis=-1,
    )


def masked_scores(queries, key_rows, allowed):
    scaling = queries.shape[-1] ** (-0.5)
    scores = (
        jnp.einsum("qhd,khd->hqk", queries, key_rows, preferred_element_type=jnp.float32) * scaling
    )
    return jnp.where(allowed[None], scores, MASKED)


def attend_forward(queries, key_rows, values, allowed):
    scores = masked_scores(queries, key_rows, allowed)
    row_max = jnp.max(scores, axis=-1, keepdims=True)
    weights = jnp.exp(scores - row_max)
    row_total = jnp.sum(weights, axis=-1, keepdims=True)
    probabilities = (weights / row_total).astype(jnp.bfloat16)
    attended = jnp.einsum("hqk,khd->qhd", probabilities, values, preferred_element_type=jnp.float32)
    return (attended, row_max, row_total)


def attend_backward(queries, key_rows, values, allowed, row_max, row_total, grad_out):
    scaling = queries.shape[-1] ** (-0.5)
    scores = masked_scores(queries, key_rows, allowed)
    probabilities = jnp.exp(scores - row_max) / row_total
    probs_low = probabilities.astype(jnp.bfloat16)
    grad_probs = jnp.einsum("qhd,khd->hqk", grad_out, values, preferred_element_type=jnp.float32)
    inner_sum = jnp.sum(probabilities * grad_probs, axis=-1, keepdims=True)
    grad_scores = (probabilities * (grad_probs - inner_sum)).astype(jnp.bfloat16)
    grad_queries = (
        jnp.einsum("hqk,khd->qhd", grad_scores, key_rows, preferred_element_type=jnp.float32)
        * scaling
    )
    grad_keys = (
        jnp.einsum("hqk,qhd->khd", grad_scores, queries, preferred_element_type=jnp.float32)
        * scaling
    )
    grad_values = jnp.einsum(
        "hqk,qhd->khd", probs_low, grad_out, preferred_element_type=jnp.float32
    )
    return (grad_queries, grad_keys, grad_values)


def per_device(
    tokens,
    prev_logits,
    routes,
    lengths,
    cotangent,
    w_qkv,
    w_out,
    gain_attn,
    gain_moe,
    w_router,
    w_residual,
    const_vec,
    w_expert,
):
    groups, piece_len, model_width = tokens.shape
    head_count = model_width // HEAD_DIM
    part_heads = 2
    part_count = head_count // part_heads
    slot_len = piece_len * lax.axis_size("ctx")
    positions = lax.axis_index("ctx") * piece_len + jnp.arange(piece_len, dtype=jnp.int32)
    key_positions = jnp.arange(slot_len, dtype=jnp.int32)
    live_rows = (positions[None, :] < lengths[:, None]).astype(jnp.float32)[..., None]
    experts = w_expert.shape[0]
    capacity = piece_len // 4
    slot_count = experts * capacity
    split_shape = (groups, piece_len, head_count, HEAD_DIM)
    full_qkv, full_out = (
        lax.all_gather(w_qkv, "fsdp", axis=0, tiled=True),
        lax.all_gather(w_out, "fsdp", axis=0, tiled=True),
    )
    inputs = tokens.astype(jnp.float32)
    gain_one = gain_attn.astype(jnp.float32)
    gain_two = gain_moe.astype(jnp.float32)
    normed_one, scale_one = normalize_rows(inputs, gain_one)
    normed_one_low = normed_one.astype(jnp.bfloat16)
    projected = jnp.einsum(
        "gpd,de->gpe", normed_one_low, full_qkv, preferred_element_type=jnp.float32
    )
    cosine_table, sine_table = rope_tables(positions, HEAD_DIM)
    queries = rotate(
        projected[..., :model_width].reshape(split_shape), cosine_table, sine_table
    ).astype(jnp.bfloat16)
    key_local = (
        rotate(
            projected[..., model_width : 2 * model_width].reshape(split_shape),
            cosine_table,
            sine_table,
        )
        .astype(jnp.bfloat16)
        .reshape(groups, piece_len, model_width)
    )
    value_local = projected[..., 2 * model_width :].astype(jnp.bfloat16)
    key_all, value_all = (
        lax.all_gather(key_local, "ctx", axis=1, tiled=True),
        lax.all_gather(value_local, "ctx", axis=1, tiled=True),
    )
    key_all = key_all.reshape(groups, slot_len, head_count, HEAD_DIM)
    value_all = value_all.reshape(groups, slot_len, head_count, HEAD_DIM)
    maxima_list = []
    totals_list = []
    group_index = 0
    allowed = (key_positions[None, :] <= positions[:, None]) & (
        key_positions[None, :] < lengths[group_index]
    )
    mask_list = [allowed]
    head_parts = []
    for part_index in range(part_count):
        first_head = part_index * part_heads
        last_head = first_head + part_heads
        attended, row_max, row_total = attend_forward(
            queries[group_index, :, first_head:last_head],
            key_all[group_index, :, first_head:last_head],
            value_all[group_index, :, first_head:last_head],
            allowed,
        )
        head_parts.append(attended)
        maxima_list.append(row_max)
        totals_list.append(row_total)
    attended_list = [jnp.concatenate(head_parts, axis=1)]
    mixed_low = (
        jnp.stack(attended_list).reshape(groups, piece_len, model_width).astype(jnp.bfloat16)
    )
    attention = jnp.einsum("gpd,de->gpe", mixed_low, full_out, preferred_element_type=jnp.float32)
    residual_sum = inputs + attention
    normed_two, scale_two = normalize_rows(residual_sum, gain_two)
    routed_low = normed_two.astype(jnp.bfloat16)
    routed = routed_low.astype(jnp.float32)
    logits = jnp.einsum("gpd,de->gpe", routed, w_router, precision=HIGHEST) + jnp.einsum(
        "gpi,ie->gpe", prev_logits, w_residual, precision=HIGHEST
    )
    id_range = jnp.arange(experts + 4, dtype=jnp.int32)
    route_hot = (routes[..., None] == id_range).astype(jnp.float32)
    chosen = jnp.sum(route_hot * logits[:, :, None, :], axis=-1)
    chosen_exp = jnp.exp(chosen - jnp.max(chosen, axis=-1, keepdims=True))
    gate_weights = chosen_exp / jnp.sum(chosen_exp, axis=-1, keepdims=True)
    assign_hot = route_hot[..., :experts].reshape(groups, 2 * piece_len, experts)
    earlier = jnp.cumsum(assign_hot, axis=1) - assign_hot
    order_in = jnp.sum(earlier * assign_hot, axis=-1)
    expert_of = jnp.sum(assign_hot * jnp.arange(experts, dtype=jnp.float32), axis=-1)
    is_ffn = jnp.sum(assign_hot, axis=-1)
    slot_of = jnp.where(is_ffn > 0.5, expert_of * capacity + order_in, -1.0)
    slot_hot = (slot_of[..., None] == jnp.arange(slot_count, dtype=jnp.float32)).astype(jnp.float32)
    dispatch = jnp.sum(slot_hot.reshape(groups, piece_len, 2, slot_count), axis=2)
    buffers = jnp.einsum(
        "gps,gpd->gsd",
        dispatch.astype(jnp.bfloat16),
        routed_low,
        preferred_element_type=jnp.float32,
    ).astype(jnp.bfloat16)
    buffers = buffers.reshape(groups, experts, capacity, model_width)

    def expert_forward(expert, outputs):
        local_rows = lax.dynamic_index_in_dim(w_expert, expert, 0, keepdims=False)
        full_rows = lax.all_gather(local_rows, "fsdp", axis=0, tiled=True)
        expert_in = lax.dynamic_index_in_dim(buffers, expert, 1, keepdims=False)
        gate_proj = jnp.einsum(
            "gcd,fd->gcf", expert_in, full_rows[:, 0], preferred_element_type=jnp.float32
        )
        up_proj = jnp.einsum(
            "gcd,fd->gcf", expert_in, full_rows[:, 1], preferred_element_type=jnp.float32
        )
        hidden = (jax.nn.silu(gate_proj) * up_proj).astype(jnp.bfloat16)
        result = jnp.einsum(
            "gcf,fd->gcd", hidden, full_rows[:, 2], preferred_element_type=jnp.float32
        )
        return lax.dynamic_update_index_in_dim(outputs, result, expert, 1)

    expert_out = lax.fori_loop(
        0, experts, expert_forward, jnp.zeros((groups, experts, capacity, model_width), jnp.float32)
    )
    y_assign = jnp.einsum(
        "gas,gsd->gad",
        slot_hot,
        expert_out.reshape(groups, slot_count, model_width),
        precision=HIGHEST,
    ).reshape(groups, piece_len, 2, model_width)
    copy_hot = route_hot[..., experts + 1]
    const_hot = route_hot[..., experts + 2 :]
    constants = const_vec.astype(jnp.float32)
    assign_out = (
        y_assign
        + copy_hot[..., None] * routed[:, :, None, :]
        + jnp.einsum("gpkj,jd->gpkd", const_hot, constants, precision=HIGHEST)
    )
    moe_sum = jnp.sum(gate_weights[..., None] * assign_out, axis=2)
    output = (live_rows * (residual_sum + moe_sum)).astype(jnp.bfloat16)
    grad_block = live_rows * cotangent.astype(jnp.float32)
    grad_assign = gate_weights[..., None] * grad_block[:, :, None, :]
    grad_gate = jnp.sum(grad_block[:, :, None, :] * assign_out, axis=-1)
    grad_chosen = gate_weights * (
        grad_gate - jnp.sum(gate_weights * grad_gate, axis=-1, keepdims=True)
    )
    grad_logits = jnp.sum(grad_chosen[..., None] * route_hot, axis=2)
    grad_router = jnp.einsum("gpd,gpe->de", routed, grad_logits, precision=HIGHEST)
    grad_mixing = jnp.einsum("gpi,gpe->ie", prev_logits, grad_logits, precision=HIGHEST)
    grad_previous = jnp.einsum("gpe,ie->gpi", grad_logits, w_residual, precision=HIGHEST)
    grad_const = jnp.einsum("gpkd,gpkj->jd", grad_assign, const_hot, precision=HIGHEST)
    grad_routed = jnp.einsum("gpe,de->gpd", grad_logits, w_router, precision=HIGHEST) + jnp.sum(
        copy_hot[..., None] * grad_assign, axis=2
    )
    grad_slots = jnp.einsum(
        "gas,gad->gsd",
        slot_hot,
        grad_assign.reshape(groups, 2 * piece_len, model_width),
        precision=HIGHEST,
    ).astype(jnp.bfloat16)
    grad_slots = grad_slots.reshape(groups, experts, capacity, model_width)

    def expert_backward(expert, carry):
        grad_buffers, grad_weights = carry
        local_rows = lax.dynamic_index_in_dim(w_expert, expert, 0, keepdims=False)
        full_rows = lax.all_gather(local_rows, "fsdp", axis=0, tiled=True)
        expert_in = lax.dynamic_index_in_dim(buffers, expert, 1, keepdims=False)
        grad_out_e = lax.dynamic_index_in_dim(grad_slots, expert, 1, keepdims=False)
        gate_proj = jnp.einsum(
            "gcd,fd->gcf", expert_in, full_rows[:, 0], preferred_element_type=jnp.float32
        )
        up_proj = jnp.einsum(
            "gcd,fd->gcf", expert_in, full_rows[:, 1], preferred_element_type=jnp.float32
        )
        sigmoid_gate = jax.nn.sigmoid(gate_proj)
        silu_gate = gate_proj * sigmoid_gate
        hidden = (silu_gate * up_proj).astype(jnp.bfloat16)
        grad_hidden = jnp.einsum(
            "gcd,fd->gcf", grad_out_e, full_rows[:, 2], preferred_element_type=jnp.float32
        )
        grad_gate_proj = (
            grad_hidden * up_proj * sigmoid_gate * (1.0 + gate_proj * (1.0 - sigmoid_gate))
        ).astype(jnp.bfloat16)
        grad_up_proj = (grad_hidden * silu_gate).astype(jnp.bfloat16)
        grad_in = jnp.einsum(
            "gcf,fd->gcd", grad_gate_proj, full_rows[:, 0], preferred_element_type=jnp.float32
        ) + jnp.einsum(
            "gcf,fd->gcd", grad_up_proj, full_rows[:, 1], preferred_element_type=jnp.float32
        )
        term = jnp.stack(
            [
                jnp.einsum(
                    "gcf,gcd->fd", grad_gate_proj, expert_in, preferred_element_type=jnp.float32
                ),
                jnp.einsum(
                    "gcf,gcd->fd", grad_up_proj, expert_in, preferred_element_type=jnp.float32
                ),
                jnp.einsum("gcf,gcd->fd", hidden, grad_out_e, preferred_element_type=jnp.float32),
            ],
            axis=1,
        )
        shard = lax.psum_scatter(
            term.astype(jnp.bfloat16), "fsdp", scatter_dimension=0, tiled=True
        ).astype(jnp.float32)
        return (
            lax.dynamic_update_index_in_dim(grad_buffers, grad_in, expert, 1),
            lax.dynamic_update_index_in_dim(grad_weights, shard, expert, 0),
        )

    grad_buffers, grad_weights = lax.fori_loop(
        0,
        experts,
        expert_backward,
        (
            jnp.zeros((groups, experts, capacity, model_width), jnp.float32),
            jnp.zeros(w_expert.shape, jnp.float32),
        ),
    )
    grad_routed = grad_routed + jnp.einsum(
        "gps,gsd->gpd",
        dispatch,
        grad_buffers.reshape(groups, slot_count, model_width),
        precision=HIGHEST,
    )
    grad_norm_two, grad_gain_two = normalize_back(residual_sum, scale_two, gain_two, grad_routed)
    grad_residual = grad_block + grad_norm_two
    grad_attention = grad_residual.astype(jnp.bfloat16)
    grad_wout = jnp.einsum(
        "gpd,gpe->de", mixed_low, grad_attention, preferred_element_type=jnp.float32
    )
    grad_mixed = (
        jnp.einsum("gpe,de->gpd", grad_attention, full_out, preferred_element_type=jnp.float32)
        .astype(jnp.bfloat16)
        .reshape(split_shape)
    )
    group_index = 0
    query_parts = []
    key_parts = []
    value_parts = []
    for part_index in range(part_count):
        first_head = part_index * part_heads
        last_head = first_head + part_heads
        grad_query, grad_key, grad_value = attend_backward(
            queries[group_index, :, first_head:last_head],
            key_all[group_index, :, first_head:last_head],
            value_all[group_index, :, first_head:last_head],
            mask_list[group_index],
            maxima_list[part_count * group_index + part_index],
            totals_list[part_count * group_index + part_index],
            grad_mixed[group_index, :, first_head:last_head],
        )
        query_parts.append(grad_query)
        key_parts.append(grad_key)
        value_parts.append(grad_value)
    query_grads = [jnp.concatenate(query_parts, axis=1)]
    key_grads_list = [jnp.concatenate(key_parts, axis=1)]
    value_grads_list = [jnp.concatenate(value_parts, axis=1)]
    key_grad_all = jnp.stack(key_grads_list).reshape(groups, slot_len, model_width)
    value_grad_all = jnp.stack(value_grads_list).reshape(groups, slot_len, model_width)
    key_grad, value_grad = (
        lax.psum_scatter(
            key_grad_all.astype(jnp.bfloat16), "ctx", scatter_dimension=1, tiled=True
        ).astype(jnp.float32),
        lax.psum_scatter(
            value_grad_all.astype(jnp.bfloat16), "ctx", scatter_dimension=1, tiled=True
        ).astype(jnp.float32),
    )
    query_back = rotate(jnp.stack(query_grads), cosine_table, -sine_table).reshape(
        groups, piece_len, model_width
    )
    key_back = rotate(key_grad.reshape(split_shape), cosine_table, -sine_table).reshape(
        groups, piece_len, model_width
    )
    grad_projected = jnp.concatenate([query_back, key_back, value_grad], axis=-1).astype(
        jnp.bfloat16
    )
    grad_wqkv = jnp.einsum(
        "gpd,gpe->de", normed_one_low, grad_projected, preferred_element_type=jnp.float32
    )
    grad_normed_one = jnp.einsum(
        "gpe,de->gpd", grad_projected, full_qkv, preferred_element_type=jnp.float32
    )
    grad_norm_one, grad_gain_one = normalize_back(inputs, scale_one, gain_one, grad_normed_one)
    grad_inputs = grad_residual + grad_norm_one
    wqkv_part, wout_part = (
        lax.psum_scatter(
            grad_wqkv.astype(jnp.bfloat16), "fsdp", scatter_dimension=0, tiled=True
        ).astype(jnp.float32),
        lax.psum_scatter(
            grad_wout.astype(jnp.bfloat16), "fsdp", scatter_dimension=0, tiled=True
        ).astype(jnp.float32),
    )
    wqkv_sum, wout_sum, expert_sum = (
        lax.psum(wqkv_part.astype(jnp.bfloat16), "ctx").astype(jnp.float32),
        lax.psum(wout_part.astype(jnp.bfloat16), "ctx").astype(jnp.float32),
        lax.psum(grad_weights.astype(jnp.bfloat16), "ctx").astype(jnp.float32),
    )
    gain_one_sum, gain_two_sum, router_sum, mixing_sum, const_sum = lax.psum(
        (grad_gain_one, grad_gain_two, grad_router, grad_mixing, grad_const), ("ctx", "fsdp")
    )
    return (
        output,
        grad_inputs,
        grad_previous,
        wqkv_sum,
        wout_sum,
        gain_one_sum,
        gain_two_sum,
        router_sum,
        mixing_sum,
        const_sum,
        expert_sum,
    )


def solution(mesh):
    return jax.shard_map(
        per_device,
        mesh=mesh,
        in_specs=(
            P("fsdp", "ctx", None),
            P("fsdp", "ctx", None),
            P("fsdp", "ctx", None),
            P("fsdp"),
            P("fsdp", "ctx", None),
            P("fsdp", None),
            P("fsdp", None),
            P(),
            P(),
            P(),
            P(),
            P(),
            P(None, "fsdp", None, None),
        ),
        out_specs=(
            P("fsdp", "ctx", None),
            P("fsdp", "ctx", None),
            P("fsdp", "ctx", None),
            P("fsdp", None),
            P("fsdp", None),
            P(),
            P(),
            P(),
            P(),
            P(),
            P(None, "fsdp", None, None),
        ),
        check_vma=False,
    )
```

profile of v0, /device:TPU:0, one launch (start us, length us, event | category | flops | bytes accessed | tf_op | source)
XLA Modules:
  0.0 4976.6 jit_solution(3344185641361876115)
XLA Ops:
  11.3 71.1 %all-gather.13.cloned.1.call-done = bf16[768,2304]{1,0:T(8,128)(2,1)} async-done(((bf16[192,2304]{1,0:T(8,128)(2,1)}), bf16[768,2304]{1,0:T(8,128)(2,1)}) %all-gather.13.cloned.1.call-update) | async-done | bytes 3538960 | tf_op jit(solution)/shard_map/all_gather | solution.py:120
  102.2 23.3 all-gather.17.cloned.1.call-done
  125.5 4.6 fusion.305
  130.0 4.7 fusion.302
  134.7 4.7 fusion.299
  139.4 20.9 all-gather.15.cloned.1.call-done
  160.3 4.9 copy.74
  174.3 4.6 fusion.308
  181.9 4.6 fusion.311
  189.6 4.8 fusion.314
  203.1 1413.6 %while.28 = (s32[]{:T(128)}, f32[1,8,64,768]{3,2,1,0:T(8,128)}, bf16[1,8,64,768]{3,2,1,0:T(8,128)(2,1)S(1)}, bf16[8,512,3,768]{3,1,2,0:T(8,128)(2,1)}, s32[]{:T(128)}) while((s32[]{:T(128)}, f32[1,8,64,768]{3,2,1,0:T(8,128)}, bf16[1,8,64,768]{3,2,1,0:T(8,128)(2,1)S(1)}, bf16[8,512,3,768]{3,1,2,0:T(8,128)(2,1)}, s32[]{:T(128)}) %tuple.135), condition=%wide.region_24.25_spmd, body=%wide.region_23.24_spmd.sunk | while | flops 604766208 | bytes 50988148 | solution.py:220
  206.3 166.9 %all-gather.21.cloned.1.call-done = bf16[1,2048,3,768]{3,1,2,0:T(8,128)(2,1)} async-done(((bf16[1,512,3,768]{3,1,2,0:T(8,128)(2,1)}), bf16[1,2048,3,768]{3,1,2,0:T(8,128)(2,1)}) %all-gather.21.cloned.1.call-update) | async-done | bytes 9437200 | tf_op jit(solution)/shard_map/while/body/eval_jaxpr/all_gather | solution.py:206
  376.2 5.2 fusion.382
  384.6 165.1 %all-gather.21.cloned.1.call-done = bf16[1,2048,3,768]{3,1,2,0:T(8,128)(2,1)} async-done(((bf16[1,512,3,768]{3,1,2,0:T(8,128)(2,1)}), bf16[1,2048,3,768]{3,1,2,0:T(8,128)(2,1)}) %all-gather.21.cloned.1.call-update) | async-done | bytes 9437200 | tf_op jit(solution)/shard_map/while/body/eval_jaxpr/all_gather | solution.py:206
  552.7 5.2 fusion.382
  561.1 165.1 %all-gather.21.cloned.1.call-done = bf16[1,2048,3,768]{3,1,2,0:T(8,128)(2,1)} async-done(((bf16[1,512,3,768]{3,1,2,0:T(8,128)(2,1)}), bf16[1,2048,3,768]{3,1,2,0:T(8,128)(2,1)}) %all-gather.21.cloned.1.call-update) | async-done | bytes 9437200 | tf_op jit(solution)/shard_map/while/body/eval_jaxpr/all_gather | solution.py:206
  729.2 5.2 fusion.382
  737.6 165.1 %all-gather.21.cloned.1.call-done = bf16[1,2048,3,768]{3,1,2,0:T(8,128)(2,1)} async-done(((bf16[1,512,3,768]{3,1,2,0:T(8,128)(2,1)}), bf16[1,2048,3,768]{3,1,2,0:T(8,128)(2,1)}) %all-gather.21.cloned.1.call-update) | async-done | bytes 9437200 | tf_op jit(solution)/shard_map/while/body/eval_jaxpr/all_gather | solution.py:206
  905.6 5.2 fusion.382
  914.0 165.1 %all-gather.21.cloned.1.call-done = bf16[1,2048,3,768]{3,1,2,0:T(8,128)(2,1)} async-done(((bf16[1,512,3,768]{3,1,2,0:T(8,128)(2,1)}), bf16[1,2048,3,768]{3,1,2,0:T(8,128)(2,1)}) %all-gather.21.cloned.1.call-update) | async-done | bytes 9437200 | tf_op jit(solution)/shard_map/while/body/eval_jaxpr/all_gather | solution.py:206
  1082.1 5.2 fusion.382
  1090.5 165.1 %all-gather.21.cloned.1.call-done = bf16[1,2048,3,768]{3,1,2,0:T(8,128)(2,1)} async-done(((bf16[1,512,3,768]{3,1,2,0:T(8,128)(2,1)}), bf16[1,2048,3,768]{3,1,2,0:T(8,128)(2,1)}) %all-gather.21.cloned.1.call-update) | async-done | bytes 9437200 | tf_op jit(solution)/shard_map/while/body/eval_jaxpr/all_gather | solution.py:206
  1258.6 5.2 fusion.382
  1267.0 165.1 %all-gather.21.cloned.1.call-done = bf16[1,2048,3,768]{3,1,2,0:T(8,128)(2,1)} async-done(((bf16[1,512,3,768]{3,1,2,0:T(8,128)(2,1)}), bf16[1,2048,3,768]{3,1,2,0:T(8,128)(2,1)}) %all-gather.21.cloned.1.call-update) | async-done | bytes 9437200 | tf_op jit(solution)/shard_map/while/body/eval_jaxpr/all_gather | solution.py:206
  1435.1 5.2 fusion.382
  1443.5 165.1 %all-gather.21.cloned.1.call-done = bf16[1,2048,3,768]{3,1,2,0:T(8,128)(2,1)} async-done(((bf16[1,512,3,768]{3,1,2,0:T(8,128)(2,1)}), bf16[1,2048,3,768]{3,1,2,0:T(8,128)(2,1)}) %all-gather.21.cloned.1.call-update) | async-done | bytes 9437200 | tf_op jit(solution)/shard_map/while/body/eval_jaxpr/all_gather | solution.py:206
  1611.6 5.2 fusion.382
  1633.5 2800.9 %while.29 = (s32[]{:T(128)}, f32[1,8,64,768]{3,2,1,0:T(8,128)}, bf16[8,512,3,768]{3,1,2,0:T(8,128)(2,1)}, bf16[1,8,64,768]{3,2,1,0:T(8,128)(2,1)S(1)}, bf16[8,51...) while((s32[]{:T(128)}, f32[1,8,64,768]{3,2,1,0:T(8,128)}, ...), condition=%wide.region_32.33_spmd, body=%wide.region_30.32_spmd.sunk | while | flops 1628487680 | bytes 133038272 | solution.py:308
  1636.8 165.1 %all-gather.23.cloned.1.call-done = bf16[1,2048,3,768]{3,1,2,0:T(8,128)(2,1)} async-done(((bf16[1,512,3,768]{3,1,2,0:T(8,128)(2,1)}), bf16[1,2048,3,768]{3,1,2,0:T(8,128)(2,1)}) %all-gather.23.cloned.1.call-update) | async-done | bytes 9437200 | tf_op jit(solution)/shard_map/while/body/eval_jaxpr/all_gather | solution.py:264
  1813.9 4.5 pad_maximum_fusion.9
  1824.4 153.7 %reduce-scatter.14.cloned.1.call-done = bf16[512,3,768]{2,0,1:T(8,128)(2,1)} async-done(((bf16[2048,3,768]{2,0,1:T(8,128)(2,1)}), bf16[512,3,768]{2,0,1:T(8,128)(2,1)}) %reduce-scatter.14.cloned.1.call-update) | async-done | bytes 2359312 | tf_op jit(solution)/shard_map/while/body/eval_jaxpr/reduce_scatter | solution.py:300
  1984.6 167.7 %all-gather.23.cloned.1.call-done = bf16[1,2048,3,768]{3,1,2,0:T(8,128)(2,1)} async-done(((bf16[1,512,3,768]{3,1,2,0:T(8,128)(2,1)}), bf16[1,2048,3,768]{3,1,2,0:T(8,128)(2,1)}) %all-gather.23.cloned.1.call-update) | async-done | bytes 9437200 | tf_op jit(solution)/shard_map/while/body/eval_jaxpr/all_gather | solution.py:264
  2164.4 4.5 pad_maximum_fusion.9
  2174.8 153.7 %reduce-scatter.14.cloned.1.call-done = bf16[512,3,768]{2,0,1:T(8,128)(2,1)} async-done(((bf16[2048,3,768]{2,0,1:T(8,128)(2,1)}), bf16[512,3,768]{2,0,1:T(8,128)(2,1)}) %reduce-scatter.14.cloned.1.call-update) | async-done | bytes 2359312 | tf_op jit(solution)/shard_map/while/body/eval_jaxpr/reduce_scatter | solution.py:300
  2335.1 167.7 %all-gather.23.cloned.1.call-done = bf16[1,2048,3,768]{3,1,2,0:T(8,128)(2,1)} async-done(((bf16[1,512,3,768]{3,1,2,0:T(8,128)(2,1)}), bf16[1,2048,3,768]{3,1,2,0:T(8,128)(2,1)}) %all-gather.23.cloned.1.call-update) | async-done | bytes 9437200 | tf_op jit(solution)/shard_map/while/body/eval_jaxpr/all_gather | solution.py:264
  2514.8 4.5 pad_maximum_fusion.9
  2525.3 153.7 %reduce-scatter.14.cloned.1.call-done = bf16[512,3,768]{2,0,1:T(8,128)(2,1)} async-done(((bf16[2048,3,768]{2,0,1:T(8,128)(2,1)}), bf16[512,3,768]{2,0,1:T(8,128)(2,1)}) %reduce-scatter.14.cloned.1.call-update) | async-done | bytes 2359312 | tf_op jit(solution)/shard_map/while/body/eval_jaxpr/reduce_scatter | solution.py:300
  2685.5 167.7 %all-gather.23.cloned.1.call-done = bf16[1,2048,3,768]{3,1,2,0:T(8,128)(2,1)} async-done(((bf16[1,512,3,768]{3,1,2,0:T(8,128)(2,1)}), bf16[1,2048,3,768]{3,1,2,0:T(8,128)(2,1)}) %all-gather.23.cloned.1.call-update) | async-done | bytes 9437200 | tf_op jit(solution)/shard_map/while/body/eval_jaxpr/all_gather | solution.py:264
  2865.3 4.5 pad_maximum_fusion.9
  2875.7 153.7 %reduce-scatter.14.cloned.1.call-done = bf16[512,3,768]{2,0,1:T(8,128)(2,1)} async-done(((bf16[2048,3,768]{2,0,1:T(8,128)(2,1)}), bf16[512,3,768]{2,0,1:T(8,128)(2,1)}) %reduce-scatter.14.cloned.1.call-update) | async-done | bytes 2359312 | tf_op jit(solution)/shard_map/while/body/eval_jaxpr/reduce_scatter | solution.py:300
  3035.9 167.7 %all-gather.23.cloned.1.call-done = bf16[1,2048,3,768]{3,1,2,0:T(8,128)(2,1)} async-done(((bf16[1,512,3,768]{3,1,2,0:T(8,128)(2,1)}), bf16[1,2048,3,768]{3,1,2,0:T(8,128)(2,1)}) %all-gather.23.cloned.1.call-update) | async-done | bytes 9437200 | tf_op jit(solution)/shard_map/while/body/eval_jaxpr/all_gather | solution.py:264
  3215.7 4.5 pad_maximum_fusion.9
  3226.2 153.7 %reduce-scatter.14.cloned.1.call-done = bf16[512,3,768]{2,0,1:T(8,128)(2,1)} async-done(((bf16[2048,3,768]{2,0,1:T(8,128)(2,1)}), bf16[512,3,768]{2,0,1:T(8,128)(2,1)}) %reduce-scatter.14.cloned.1.call-update) | async-done | bytes 2359312 | tf_op jit(solution)/shard_map/while/body/eval_jaxpr/reduce_scatter | solution.py:300
  3386.4 167.7 %all-gather.23.cloned.1.call-done = bf16[1,2048,3,768]{3,1,2,0:T(8,128)(2,1)} async-done(((bf16[1,512,3,768]{3,1,2,0:T(8,128)(2,1)}), bf16[1,2048,3,768]{3,1,2,0:T(8,128)(2,1)}) %all-gather.23.cloned.1.call-update) | async-done | bytes 9437200 | tf_op jit(solution)/shard_map/while/body/eval_jaxpr/all_gather | solution.py:264
  3566.2 4.5 pad_maximum_fusion.9
  3576.6 153.7 %reduce-scatter.14.cloned.1.call-done = bf16[512,3,768]{2,0,1:T(8,128)(2,1)} async-done(((bf16[2048,3,768]{2,0,1:T(8,128)(2,1)}), bf16[512,3,768]{2,0,1:T(8,128)(2,1)}) %reduce-scatter.14.cloned.1.call-update) | async-done | bytes 2359312 | tf_op jit(solution)/shard_map/while/body/eval_jaxpr/reduce_scatter | solution.py:300
  3736.8 167.7 %all-gather.23.cloned.1.call-done = bf16[1,2048,3,768]{3,1,2,0:T(8,128)(2,1)} async-done(((bf16[1,512,3,768]{3,1,2,0:T(8,128)(2,1)}), bf16[1,2048,3,768]{3,1,2,0:T(8,128)(2,1)}) %all-gather.23.cloned.1.call-update) | async-done | bytes 9437200 | tf_op jit(solution)/shard_map/while/body/eval_jaxpr/all_gather | solution.py:264
  3916.6 4.5 pad_maximum_fusion.9
  3927.1 153.7 %reduce-scatter.14.cloned.1.call-done = bf16[512,3,768]{2,0,1:T(8,128)(2,1)} async-done(((bf16[2048,3,768]{2,0,1:T(8,128)(2,1)}), bf16[512,3,768]{2,0,1:T(8,128)(2,1)}) %reduce-scatter.14.cloned.1.call-update) | async-done | bytes 2359312 | tf_op jit(solution)/shard_map/while/body/eval_jaxpr/reduce_scatter | solution.py:300
  4087.3 167.7 %all-gather.23.cloned.1.call-done = bf16[1,2048,3,768]{3,1,2,0:T(8,128)(2,1)} async-done(((bf16[1,512,3,768]{3,1,2,0:T(8,128)(2,1)}), bf16[1,2048,3,768]{3,1,2,0:T(8,128)(2,1)}) %all-gather.23.cloned.1.call-update) | async-done | bytes 9437200 | tf_op jit(solution)/shard_map/while/body/eval_jaxpr/all_gather | solution.py:264
  4267.1 4.5 pad_maximum_fusion.9
  4277.5 153.7 %reduce-scatter.14.cloned.1.call-done = bf16[512,3,768]{2,0,1:T(8,128)(2,1)} async-done(((bf16[2048,3,768]{2,0,1:T(8,128)(2,1)}), bf16[512,3,768]{2,0,1:T(8,128)(2,1)}) %reduce-scatter.14.cloned.1.call-update) | async-done | bytes 2359312 | tf_op jit(solution)/shard_map/while/body/eval_jaxpr/reduce_scatter | solution.py:300
  4440.7 5.2 multiply_reduce_fusion
  4466.6 4.1 multiply_convert_fusion.4
  4495.6 4.0 fusion.78
  4499.6 4.0 fusion.80
  4526.3 8.7 reduce-scatter.6.cloned.1.call-done
  4537.5 47.4 reduce-scatter.8.cloned.1.call-done
  4584.9 4.0 convolution_convert_fusion.3
  4589.0 28.0 reduce-scatter.12.cloned.1.call-done
  4617.0 67.4 %reduce-scatter.10.cloned.1.call-done = bf16[192,2304]{1,0:T(8,128)(2,1)} async-done(((bf16[768,2304]{1,0:T(8,128)(2,1)}), bf16[192,2304]{1,0:T(8,128)(2,1)}) %reduce-scatter.10.cloned.1.call-update) | async-done | bytes 884752 | tf_op jit(solution)/shard_map/reduce_scatter | solution.py:384
  4690.5 42.8 all-reduce
  4735.1 209.0 %all-reduce.4.cloned.1.call-done = (bf16[192,2304]{1,0:T(8,128)(2,1)}, bf16[192,768]{1,0:T(8,128)(2,1)}, bf16[8,512,3,768]{3,1,2,0:T(8,128)(2,1)}) async-done(((bf16[192,2304]{1,0:T(8,128)(2,1)}, bf16[192,768]{1,0:T(8,128)(2,1)}, bf16[8,512,3,768]{3,1,2,0:T(8,128)(2,1)}), (bf16[192,2304]{1,0:T(8,128)(2,1)}, bf16[192,768]{1,0:T(8,128)(2,1)}, bf16[8,512,3,768]{3,1,2,0:T(8,128)(2,1)})) %all-reduce.4.cloned.1.call-update) | async-done | bytes 20054032 | tf_op jit(solution)/shard_map/psum | solution.py:392
  4948.5 20.8 convert_element_type.303
  (424 shorter events, 397.4 us)
Async XLA Ops:
  7.2 193.4 %copy-start = (f32[768,12]{0,1:T(8,128)S(1)}, f32[768,12]{0,1:T(8,128)}, u32[]{:S(2)}) copy-start(f32[768,12]{0,1:T(8,128)} %param.26) | copy-start | bytes 110596
  7.2 75.1 %all-gather.13.cloned.1.call-start = ((), (), s32[]{:S(2)}) async-start(), calls=%async_computation.5 | async-start | bytes 4423680 | tf_op jit(solution)/shard_map/all_gather | solution.py:120
  7.9 117.5 %all-gather.17.cloned.1.call-start = ((), (), s32[]{:S(2)}) async-start(), calls=%async_computation.7 | async-start | bytes 3538944 | tf_op jit(solution)/shard_map/all_gather | solution.py:146
  8.7 76.9 %copy-start.43 = (f32[768]{0:T(1024)}, f32[768]{0:T(1024)S(1)}, u32[]{:S(2)}) copy-start(f32[768]{0:T(1024)S(1)} %convert_element_type.267) | copy-start | bytes 9220
  10.4 75.2 %copy-start.52 = (f32[256]{0:T(256)}, f32[256]{0:T(256)S(1)}, u32[]{:S(2)}) copy-start(f32[256]{0:T(256)S(1)} %get-tuple-element.315) | copy-start | bytes 3076
  11.2 80.2 %copy-start.38 = (f32[256,32]{0,1:T(8,128)}, f32[256,32]{0,1:T(8,128)S(1)}, u32[]{:S(2)}) copy-start(f32[256,32]{0,1:T(8,128)S(1)} %get-tuple-element.313) | copy-start | bytes 98308
  89.1 6.2 copy-start.51
  89.1 7.0 copy-start.70
  93.0 93.5 %copy-start.11 = (bf16[1,256,12,32]{1,3,2,0:T(8,128)(2,1)}, bf16[1,256,12,32]{1,3,2,0:T(8,128)(2,1)S(1)}, u32[]{:S(2)}) copy-start(bf16[1,256,12,32]{1,3,2,0:T(8,128)(2,1)S(1)} %get-tuple-element.296) | copy-start | bytes 589828
  93.1 93.5 %copy-start.13 = (bf16[1,256,12,32]{1,3,2,0:T(8,128)(2,1)}, bf16[1,256,12,32]{1,3,2,0:T(8,128)(2,1)S(1)}, u32[]{:S(2)}) copy-start(bf16[1,256,12,32]{1,3,2,0:T(8,128)(2,1)S(1)} %get-tuple-element.297) | copy-start | bytes 589828
  93.9 66.4 %all-gather.15.cloned.1.call-start = ((), (), s32[]{:S(2)}) async-start(), calls=%async_computation.6 | async-start | bytes 3538944 | tf_op jit(solution)/shard_map/all_gather | solution.py:147
  94.8 102.8 %all-gather.19.cloned.1.call-start = ((), (), s32[]{:S(2)}) async-start(), calls=%async_computation.8 | async-start | bytes 1474560 | tf_op jit(solution)/shard_map/all_gather | solution.py:121
  95.4 1525.7 %copy-start.47 = (pred[1,256,2,12]{1,3,2,0:T(8,128)(4,1)}, pred[1,256,2,12]{1,3,2,0:T(8,128)(4,1)S(1)}, u32[]{:S(2)}) copy-start(pred[1,256,2,12]{1,3,2,0:T(8,128)(4,1)S(1)} %get-tuple-element.308) | copy-start | bytes 18436
  96.1 6.1 copy-start.54
  100.8 93.6 %copy-start.36 = (pred[256,2048]{1,0:T(8,128)(4,1)}, pred[256,2048]{1,0:T(8,128)(4,1)S(1)}, u32[]{:S(2)}) copy-start(pred[256,2048]{1,0:T(8,128)(4,1)S(1)} %fusion.109) | copy-start | bytes 1572868
  102.2 1518.9 %copy-start.9 = (f32[256,768]{1,0:T(8,128)}, f32[256,768]{1,0:T(8,128)S(1)}, u32[]{:S(2)}) copy-start(f32[256,768]{1,0:T(8,128)S(1)} %fusion.165) | copy-start | bytes 2359300
  102.2 92.2 %copy-start.40 = (bf16[256,2,64]{0,2,1:T(8,128)(2,1)}, bf16[256,2,64]{0,2,1:T(8,128)(2,1)S(1)}, u32[]{:S(2)}) copy-start(bf16[256,2,64]{0,2,1:T(8,128)(2,1)S(1)} %fusion.211) | copy-start | bytes 196612
  130.0 41.2 copy-start.60
  134.7 33.5 copy-start.62
  139.4 25.8 copy-start.64
  201.4 1419.7 %copy-start.45 = (f32[256,2]{0,1:T(2,128)}, f32[256,2]{0,1:T(2,128)S(1)}, u32[]{:S(2)}) copy-start(f32[256,2]{0,1:T(2,128)S(1)} %fusion.219) | copy-start | bytes 6148
  203.1 170.1 %all-gather.21.cloned.1.call-start = ((), (), s32[]{:S(2)}) async-start(), calls=%async_computation.14 | async-start | bytes 11796480 | tf_op jit(solution)/shard_map/while/body/eval_jaxpr/all_gather | solution.py:206
  381.4 168.4 %all-gather.21.cloned.1.call-start = ((), (), s32[]{:S(2)}) async-start(), calls=%async_computation.14 | async-start | bytes 11796480 | tf_op jit(solution)/shard_map/while/body/eval_jaxpr/all_gather | solution.py:206
  557.8 168.4 %all-gather.21.cloned.1.call-start = ((), (), s32[]{:S(2)}) async-start(), calls=%async_computation.14 | async-start | bytes 11796480 | tf_op jit(solution)/shard_map/while/body/eval_jaxpr/all_gather | solution.py:206
  734.3 168.4 %all-gather.21.cloned.1.call-start = ((), (), s32[]{:S(2)}) async-start(), calls=%async_computation.14 | async-start | bytes 11796480 | tf_op jit(solution)/shard_map/while/body/eval_jaxpr/all_gather | solution.py:206
  910.8 168.4 %all-gather.21.cloned.1.call-start = ((), (), s32[]{:S(2)}) async-start(), calls=%async_computation.14 | async-start | bytes 11796480 | tf_op jit(solution)/shard_map/while/body/eval_jaxpr/all_gather | solution.py:206
  1087.3 168.4 %all-gather.21.cloned.1.call-start = ((), (), s32[]{:S(2)}) async-start(), calls=%async_computation.14 | async-start | bytes 11796480 | tf_op jit(solution)/shard_map/while/body/eval_jaxpr/all_gather | solution.py:206
  1263.8 168.4 %all-gather.21.cloned.1.call-start = ((), (), s32[]{:S(2)}) async-start(), calls=%async_computation.14 | async-start | bytes 11796480 | tf_op jit(solution)/shard_map/while/body/eval_jaxpr/all_gather | solution.py:206
  1440.2 168.4 %all-gather.21.cloned.1.call-start = ((), (), s32[]{:S(2)}) async-start(), calls=%async_computation.14 | async-start | bytes 11796480 | tf_op jit(solution)/shard_map/while/body/eval_jaxpr/all_gather | solution.py:206
  1633.5 168.4 %all-gather.23.cloned.1.call-start = ((), (), s32[]{:S(2)}) async-start(), calls=%async_computation.15 | async-start | bytes 11796480 | tf_op jit(solution)/shard_map/while/body/eval_jaxpr/all_gather | solution.py:264
  1636.8 341.3 %reduce-scatter.14.cloned.1.call-start = ((), (), s32[]{:S(2)}) async-start(), calls=%async_computation.16 | async-start | bytes 11796480 | tf_op jit(solution)/shard_map/while/body/eval_jaxpr/reduce_scatter | solution.py:300
  1981.3 171.0 %all-gather.23.cloned.1.call-start = ((), (), s32[]{:S(2)}) async-start(), calls=%async_computation.15 | async-start | bytes 11796480 | tf_op jit(solution)/shard_map/while/body/eval_jaxpr/all_gather | solution.py:264
  1984.6 344.0 %reduce-scatter.14.cloned.1.call-start = ((), (), s32[]{:S(2)}) async-start(), calls=%async_computation.16 | async-start | bytes 11796480 | tf_op jit(solution)/shard_map/while/body/eval_jaxpr/reduce_scatter | solution.py:300
  2331.8 171.0 %all-gather.23.cloned.1.call-start = ((), (), s32[]{:S(2)}) async-start(), calls=%async_computation.15 | async-start | bytes 11796480 | tf_op jit(solution)/shard_map/while/body/eval_jaxpr/all_gather | solution.py:264
  2335.0 344.0 %reduce-scatter.14.cloned.1.call-start = ((), (), s32[]{:S(2)}) async-start(), calls=%async_computation.16 | async-start | bytes 11796480 | tf_op jit(solution)/shard_map/while/body/eval_jaxpr/reduce_scatter | solution.py:300
  2682.2 171.0 %all-gather.23.cloned.1.call-start = ((), (), s32[]{:S(2)}) async-start(), calls=%async_computation.15 | async-start | bytes 11796480 | tf_op jit(solution)/shard_map/while/body/eval_jaxpr/all_gather | solution.py:264
  2685.4 344.0 %reduce-scatter.14.cloned.1.call-start = ((), (), s32[]{:S(2)}) async-start(), calls=%async_computation.16 | async-start | bytes 11796480 | tf_op jit(solution)/shard_map/while/body/eval_jaxpr/reduce_scatter | solution.py:300
  3032.6 171.0 %all-gather.23.cloned.1.call-start = ((), (), s32[]{:S(2)}) async-start(), calls=%async_computation.15 | async-start | bytes 11796480 | tf_op jit(solution)/shard_map/while/body/eval_jaxpr/all_gather | solution.py:264
  3035.9 344.0 %reduce-scatter.14.cloned.1.call-start = ((), (), s32[]{:S(2)}) async-start(), calls=%async_computation.16 | async-start | bytes 11796480 | tf_op jit(solution)/shard_map/while/body/eval_jaxpr/reduce_scatter | solution.py:300
  3383.1 171.0 %all-gather.23.cloned.1.call-start = ((), (), s32[]{:S(2)}) async-start(), calls=%async_computation.15 | async-start | bytes 11796480 | tf_op jit(solution)/shard_map/while/body/eval_jaxpr/all_gather | solution.py:264
  3386.3 344.0 %reduce-scatter.14.cloned.1.call-start = ((), (), s32[]{:S(2)}) async-start(), calls=%async_computation.16 | async-start | bytes 11796480 | tf_op jit(solution)/shard_map/while/body/eval_jaxpr/reduce_scatter | solution.py:300
  3733.5 171.0 %all-gather.23.cloned.1.call-start = ((), (), s32[]{:S(2)}) async-start(), calls=%async_computation.15 | async-start | bytes 11796480 | tf_op jit(solution)/shard_map/while/body/eval_jaxpr/all_gather | solution.py:264
  3736.8 344.0 %reduce-scatter.14.cloned.1.call-start = ((), (), s32[]{:S(2)}) async-start(), calls=%async_computation.16 | async-start | bytes 11796480 | tf_op jit(solution)/shard_map/while/body/eval_jaxpr/reduce_scatter | solution.py:300
  4084.0 171.0 %all-gather.23.cloned.1.call-start = ((), (), s32[]{:S(2)}) async-start(), calls=%async_computation.15 | async-start | bytes 11796480 | tf_op jit(solution)/shard_map/while/body/eval_jaxpr/all_gather | solution.py:264
  4087.2 344.0 %reduce-scatter.14.cloned.1.call-start = ((), (), s32[]{:S(2)}) async-start(), calls=%async_computation.16 | async-start | bytes 11796480 | tf_op jit(solution)/shard_map/while/body/eval_jaxpr/reduce_scatter | solution.py:300
  4434.4 100.6 %reduce-scatter.6.cloned.1.call-start = ((), (), s32[]{:S(2)}) async-start(), calls=%async_computation.9 | async-start | bytes 3538944 | tf_op jit(solution)/shard_map/reduce_scatter | solution.py:359
  4440.6 18.3 copy-start.37
  4440.7 5.7 copy-start.28
  4440.7 5.7 copy-start.69
  4465.1 5.6 copy-start.1
  4473.8 11.4 copy-start.2
  4474.8 9.0 copy-start.4
  4487.8 97.1 %reduce-scatter.8.cloned.1.call-start = ((), (), s32[]{:S(2)}) async-start(), calls=%async_computation.10 | async-start | bytes 3538944 | tf_op jit(solution)/shard_map/reduce_scatter | solution.py:362
  4511.4 105.6 %reduce-scatter.12.cloned.1.call-start = ((), (), s32[]{:S(2)}) async-start(), calls=%async_computation.12 | async-start | bytes 1474560 | tf_op jit(solution)/shard_map/reduce_scatter | solution.py:387
  4513.9 170.6 %reduce-scatter.10.cloned.1.call-start = ((), (), s32[]{:S(2)}) async-start(), calls=%async_computation.11 | async-start | bytes 4423680 | tf_op jit(solution)/shard_map/reduce_scatter | solution.py:384
  4513.9 6.7 copy-start.7
  4513.9 6.7 copy-start.31
  4523.5 12.6 copy-start.39
  4523.5 12.6 copy-start.42
  4526.3 58.6 %copy-start.16 = (bf16[1,256,768]{2,1,0:T(8,128)(2,1)S(1)}, bf16[1,256,768]{2,1,0:T(8,128)(2,1)}, u32[]{:S(2)}) copy-start(bf16[1,256,768]{2,1,0:T(8,128)(2,1)} %param.17) | copy-start | bytes 1179652
  4526.3 58.6 %copy-start.44 = (f32[768]{0:T(1024)S(1)}, f32[768]{0:T(1024)}, u32[]{:S(2)}) copy-start(f32[768]{0:T(1024)} %copy-done.43) | copy-start | bytes 9220
  4526.3 58.6 %copy-start.53 = (f32[256]{0:T(256)S(1)}, f32[256]{0:T(256)}, u32[]{:S(2)}) copy-start(f32[256]{0:T(256)} %copy-done.52) | copy-start | bytes 3076
  4589.0 355.2 %all-reduce.4.cloned.1.call-start = ((), (), s32[]{:S(2)}) async-start(), calls=%async_computation.13 | async-start | bytes 40108032 | tf_op jit(solution)/shard_map/psum | solution.py:392
  4687.1 46.9 copy-start.58
  (40 other events, 126.3 us)
Sparse Core Ops, SparseCore 0:
  9.6 72.6 all-gather.12
  94.0 31.3 all-gather.16
  127.9 32.3 all-gather.14
  161.7 30.4 all-gather.18
  206.5 166.7 all-gather.20
  384.7 164.9 all-gather.20
  561.2 164.9 all-gather.20
  737.7 164.9 all-gather.20
  914.2 164.9 all-gather.20
  1090.6 164.9 all-gather.20
  1267.1 164.9 all-gather.20
  1443.6 164.9 all-gather.20
  1636.9 164.9 all-gather.22
  1818.6 159.4 reduce-scatter.13
  1984.7 167.5 all-gather.22
  2169.0 159.4 reduce-scatter.13
  2335.1 167.6 all-gather.22
  2519.5 159.4 reduce-scatter.13
  2685.6 167.6 all-gather.22
  2869.9 159.4 reduce-scatter.13
  3036.0 167.6 all-gather.22
  3220.4 159.4 reduce-scatter.13
  3386.4 167.6 all-gather.22
  3570.8 159.4 reduce-scatter.13
  3736.9 167.6 all-gather.22
  3921.3 159.4 reduce-scatter.13
  4087.3 167.6 all-gather.22
  4271.7 159.4 reduce-scatter.13
  4487.9 47.0 reduce-scatter.5
  4538.6 46.2 reduce-scatter.7
  4587.8 29.1 reduce-scatter.11
  4619.3 65.0 reduce-scatter.9
  4689.1 255.0 all-reduce.3
where the time goes:
time: 4990 us; the launch traced here: 4980 us
  waiting for transfers between devices  4370 us (88%)
  matrix products  347 us (7%)
  other arithmetic  115 us (2%)
  local copies, waits for them, and re-layouts  84.5 us (2%)
    all_gather x8, waiting for transfers between devices, expert_backward(): full_rows = lax.all_gather(local_rows, 'fsdp', axis=0, tiled=True)  1340 us
    all_gather x8, waiting for transfers between devices, expert_forward(): full_rows = lax.all_gather(local_rows, 'fsdp', axis=0, tiled=True)  1320 us
    reduce_scatter x8, waiting for transfers between devices, expert_backward(): lax.psum_scatter(term.astype(jnp.bfloat16), 'fsdp', scatter_dimension=0,...  1230 us
    psum x1, waiting for transfers between devices, per_device(): lax.psum(wqkv_part.astype(jnp.bfloat16), 'ctx').astype(jnp.float32)  209 us
  transfers between devices with their start and end apart: 33, of which 32 were waited for; matrix products, arithmetic and copies ran while one was open for 3% of the time, Pallas kernels for 0%

commit v1 on v0

--- a/solution.py
+++ b/solution.py
@@ -190,55 +190,97 @@
     order_in = jnp.sum(earlier * assign_hot, axis=-1)
     expert_of = jnp.sum(assign_hot * jnp.arange(experts, dtype=jnp.float32), axis=-1)
     is_ffn = jnp.sum(assign_hot, axis=-1)
-    slot_of = jnp.where(is_ffn > 0.5, expert_of * capacity + order_in, -1.0)
-    slot_hot = (slot_of[..., None] == jnp.arange(slot_count, dtype=jnp.float32)).astype(jnp.float32)
-    dispatch = jnp.sum(slot_hot.reshape(groups, piece_len, 2, slot_count), axis=2)
+    slot_of = jnp.where(is_ffn > 0.5, expert_of * capacity + order_in, -1.0).reshape(
+        groups, piece_len, 2
+    )
+    slot_hot = slot_of[..., None] == jnp.arange(slot_count, dtype=jnp.float32)
+    slot_gate = jnp.sum(jnp.where(slot_hot, gate_weights[..., None], 0.0), axis=(1, 2))
+    cotangent_low = live_rows.astype(jnp.bfloat16) * cotangent
+    row_pairs = lax.all_gather(
+        jnp.concatenate([routed_low, cotangent_low], axis=-1), "fsdp", axis=0, tiled=True
+    )
+    all_slot_of = lax.all_gather(slot_of, "fsdp", axis=0, tiled=True)
+    all_gate = lax.all_gather(slot_gate, "fsdp", axis=0, tiled=True)
+    peers = row_pairs.shape[0]
+    all_hot = (
+        jnp.sum(
+            (all_slot_of[..., None] == jnp.arange(slot_count, dtype=jnp.float32)).astype(
+                jnp.float32
+            ),
+            axis=2,
+        )
+        .astype(jnp.bfloat16)
+        .reshape(peers, piece_len, experts, capacity)
+    )
+    gate_rows = all_gate.reshape(peers, experts, capacity).swapaxes(0, 1)[..., None]
     buffers = jnp.einsum(
-        "gps,gpd->gsd",
-        dispatch.astype(jnp.bfloat16),
-        routed_low,
-        preferred_element_type=jnp.float32,
+        "gpec,gpd->egcd", all_hot, row_pairs, preferred_element_type=jnp.float32
     ).astype(jnp.bfloat16)
-    buffers = buffers.reshape(groups, experts, capacity, model_width)
-
-    def expert_forward(expert, outputs):
-        local_rows = lax.dynamic_index_in_dim(w_expert, expert, 0, keepdims=False)
-        full_rows = lax.all_gather(local_rows, "fsdp", axis=0, tiled=True)
-        expert_in = lax.dynamic_index_in_dim(buffers, expert, 1, keepdims=False)
-        gate_proj = jnp.einsum(
-            "gcd,fd->gcf", expert_in, full_rows[:, 0], preferred_element_type=jnp.float32
-        )
-        up_proj = jnp.einsum(
-            "gcd,fd->gcf", expert_in, full_rows[:, 1], preferred_element_type=jnp.float32
-        )
-        hidden = (jax.nn.silu(gate_proj) * up_proj).astype(jnp.bfloat16)
-        result = jnp.einsum(
-            "gcf,fd->gcd", hidden, full_rows[:, 2], preferred_element_type=jnp.float32
-        )
-        return lax.dynamic_update_index_in_dim(outputs, result, expert, 1)
-
-    expert_out = lax.fori_loop(
-        0, experts, expert_forward, jnp.zeros((groups, experts, capacity, model_width), jnp.float32)
-    )
-    y_assign = jnp.einsum(
-        "gas,gsd->gad",
-        slot_hot,
-        expert_out.reshape(groups, slot_count, model_width),
-        precision=HIGHEST,
-    ).reshape(groups, piece_len, 2, model_width)
+    expert_in = buffers[..., :model_width].reshape(experts, peers * capacity, model_width)
+    block_rows = buffers[..., model_width:].astype(jnp.float32)
+    grad_out = (
+        (gate_rows * block_rows)
+        .astype(jnp.bfloat16)
+        .reshape(experts, peers * capacity, model_width)
+    )
+    w_gate, w_up, w_down = w_expert[:, :, 0], w_expert[:, :, 1], w_expert[:, :, 2]
+
+    def apply(spec, left, right):
+        return jnp.einsum(spec, left, right, preferred_element_type=jnp.float32)
+
+    gate_proj = apply("ecd,efd->ecf", expert_in, w_gate)
+    up_proj = apply("ecd,efd->ecf", expert_in, w_up)
+    sigmoid_gate = jax.nn.sigmoid(gate_proj)
+    silu_gate = gate_proj * sigmoid_gate
+    hidden = (silu_gate * up_proj).astype(jnp.bfloat16)
+    expert_out = apply("ecf,efd->ecd", hidden, w_down).reshape(buffers.shape[:3] + (model_width,))
+    grad_hidden = apply("ecd,efd->ecf", grad_out, w_down)
+    grad_gate_proj = (
+        grad_hidden * up_proj * sigmoid_gate * (1.0 + gate_proj * (1.0 - sigmoid_gate))
+    ).astype(jnp.bfloat16)
+    grad_up_proj = (grad_hidden * silu_gate).astype(jnp.bfloat16)
+    grad_in = (
+        apply("ecf,efd->ecd", grad_gate_proj, w_gate) + apply("ecf,efd->ecd", grad_up_proj, w_up)
+    ).reshape(expert_out.shape)
+    grad_weights = jnp.stack(
+        [
+            apply("ecf,ecd->efd", grad_gate_proj, expert_in).astype(jnp.bfloat16),
+            apply("ecf,ecd->efd", grad_up_proj, expert_in).astype(jnp.bfloat16),
+            apply("ecf,ecd->efd", hidden, grad_out).astype(jnp.bfloat16),
+        ],
+        axis=2,
+    )
+    returned = jnp.concatenate([gate_rows * expert_out, grad_in], axis=-1).astype(jnp.bfloat16)
+    token_parts = apply("gpec,egcd->gpd", all_hot, returned).astype(jnp.bfloat16)
+    token_sums = lax.psum_scatter(token_parts, "fsdp", scatter_dimension=0, tiled=True).astype(
+        jnp.float32
+    )
+    ffn_sum, ffn_grad = token_sums[..., :model_width], token_sums[..., model_width:]
+    slot_dot = lax.psum_scatter(
+        jnp.sum(block_rows * expert_out, axis=-1).swapaxes(0, 1).reshape(peers, slot_count),
+        "fsdp",
+        scatter_dimension=0,
+        tiled=True,
+    )
     copy_hot = route_hot[..., experts + 1]
     const_hot = route_hot[..., experts + 2 :]
     constants = const_vec.astype(jnp.float32)
-    assign_out = (
-        y_assign
-        + copy_hot[..., None] * routed[:, :, None, :]
-        + jnp.einsum("gpkj,jd->gpkd", const_hot, constants, precision=HIGHEST)
-    )
-    moe_sum = jnp.sum(gate_weights[..., None] * assign_out, axis=2)
+    gate_const = jnp.sum(gate_weights[..., None] * const_hot, axis=2)
+    copy_gate = jnp.sum(gate_weights * copy_hot, axis=2, keepdims=True)
+    moe_sum = (
+        ffn_sum
+        + copy_gate * routed
+        + jnp.einsum("gpj,jd->gpd", gate_const, constants, precision=HIGHEST)
+    )
     output = (live_rows * (residual_sum + moe_sum)).astype(jnp.bfloat16)
     grad_block = live_rows * cotangent.astype(jnp.float32)
-    grad_assign = gate_weights[..., None] * grad_block[:, :, None, :]
-    grad_gate = jnp.sum(grad_block[:, :, None, :] * assign_out, axis=-1)
+    copy_dot = jnp.sum(grad_block * routed, axis=-1)[..., None]
+    const_dot = jnp.einsum("gpd,jd->gpj", grad_block, constants, precision=HIGHEST)
+    grad_gate = (
+        jnp.sum(jnp.where(slot_hot, slot_dot[:, None, None, :], 0.0), axis=-1)
+        + copy_hot * copy_dot
+        + jnp.sum(const_hot * const_dot[:, :, None, :], axis=-1)
+    )
     grad_chosen = gate_weights * (
         grad_gate - jnp.sum(gate_weights * grad_gate, axis=-1, keepdims=True)
     )
@@ -246,79 +288,11 @@
     grad_router = jnp.einsum("gpd,gpe->de", routed, grad_logits, precision=HIGHEST)
     grad_mixing = jnp.einsum("gpi,gpe->ie", prev_logits, grad_logits, precision=HIGHEST)
     grad_previous = jnp.einsum("gpe,ie->gpi", grad_logits, w_residual, precision=HIGHEST)
-    grad_const = jnp.einsum("gpkd,gpkj->jd", grad_assign, const_hot, precision=HIGHEST)
-    grad_routed = jnp.einsum("gpe,de->gpd", grad_logits, w_router, precision=HIGHEST) + jnp.sum(
-        copy_hot[..., None] * grad_assign, axis=2
-    )
-    grad_slots = jnp.einsum(
-        "gas,gad->gsd",
-        slot_hot,
-        grad_assign.reshape(groups, 2 * piece_len, model_width),
-        precision=HIGHEST,
-    ).astype(jnp.bfloat16)
-    grad_slots = grad_slots.reshape(groups, experts, capacity, model_width)
-
-    def expert_backward(expert, carry):
-        grad_buffers, grad_weights = carry
-        local_rows = lax.dynamic_index_in_dim(w_expert, expert, 0, keepdims=False)
-        full_rows = lax.all_gather(local_rows, "fsdp", axis=0, tiled=True)
-        expert_in = lax.dynamic_index_in_dim(buffers, expert, 1, keepdims=False)
-        grad_out_e = lax.dynamic_index_in_dim(grad_slots, expert, 1, keepdims=False)
-        gate_proj = jnp.einsum(
-            "gcd,fd->gcf", expert_in, full_rows[:, 0], preferred_element_type=jnp.float32
-        )
-        up_proj = jnp.einsum(
-            "gcd,fd->gcf", expert_in, full_rows[:, 1], preferred_element_type=jnp.float32
-        )
-        sigmoid_gate = jax.nn.sigmoid(gate_proj)
-        silu_gate = gate_proj * sigmoid_gate
-        hidden = (silu_gate * up_proj).astype(jnp.bfloat16)
-        grad_hidden = jnp.einsum(
-            "gcd,fd->gcf", grad_out_e, full_rows[:, 2], preferred_element_type=jnp.float32
-        )
-        grad_gate_proj = (
-            grad_hidden * up_proj * sigmoid_gate * (1.0 + gate_proj * (1.0 - sigmoid_gate))
-        ).astype(jnp.bfloat16)
-        grad_up_proj = (grad_hidden * silu_gate).astype(jnp.bfloat16)
-        grad_in = jnp.einsum(
-            "gcf,fd->gcd", grad_gate_proj, full_rows[:, 0], preferred_element_type=jnp.float32
-        ) + jnp.einsum(
-            "gcf,fd->gcd", grad_up_proj, full_rows[:, 1], preferred_element_type=jnp.float32
-        )
-        term = jnp.stack(
-            [
-                jnp.einsum(
-                    "gcf,gcd->fd", grad_gate_proj, expert_in, preferred_element_type=jnp.float32
-                ),
-                jnp.einsum(
-                    "gcf,gcd->fd", grad_up_proj, expert_in, preferred_element_type=jnp.float32
-                ),
-                jnp.einsum("gcf,gcd->fd", hidden, grad_out_e, preferred_element_type=jnp.float32),
-            ],
-            axis=1,
-        )
-        shard = lax.psum_scatter(
-            term.astype(jnp.bfloat16), "fsdp", scatter_dimension=0, tiled=True
-        ).astype(jnp.float32)
-        return (
-            lax.dynamic_update_index_in_dim(grad_buffers, grad_in, expert, 1),
-            lax.dynamic_update_index_in_dim(grad_weights, shard, expert, 0),
-        )
-
-    grad_buffers, grad_weights = lax.fori_loop(
-        0,
-        experts,
-        expert_backward,
-        (
-            jnp.zeros((groups, experts, capacity, model_width), jnp.float32),
-            jnp.zeros(w_expert.shape, jnp.float32),
-        ),
-    )
-    grad_routed = grad_routed + jnp.einsum(
-        "gps,gsd->gpd",
-        dispatch,
-        grad_buffers.reshape(groups, slot_count, model_width),
-        precision=HIGHEST,
+    grad_const = jnp.einsum("gpd,gpj->jd", grad_block, gate_const, precision=HIGHEST)
+    grad_routed = (
+        jnp.einsum("gpe,de->gpd", grad_logits, w_router, precision=HIGHEST)
+        + copy_gate * grad_block
+        + ffn_grad
     )
     grad_norm_two, grad_gain_two = normalize_back(residual_sum, scale_two, gain_two, grad_routed)
     grad_residual = grad_block + grad_norm_two
@@ -391,7 +365,7 @@
     wqkv_sum, wout_sum, expert_sum = (
         lax.psum(wqkv_part.astype(jnp.bfloat16), "ctx").astype(jnp.float32),
         lax.psum(wout_part.astype(jnp.bfloat16), "ctx").astype(jnp.float32),
-        lax.psum(grad_weights.astype(jnp.bfloat16), "ctx").astype(jnp.float32),
+        lax.psum(grad_weights, "ctx").astype(jnp.float32),
     )
     gain_one_sum, gain_two_sum, router_sum, mixing_sum, const_sum = lax.psum(
         (grad_gain_one, grad_gain_two, grad_router, grad_mixing, grad_const), ("ctx", "fsdp")

time: 4990 us -> 960 us (0.19)
  waiting for transfers between devices: 4370 us -> 573 us
  matrix products: 347 us -> 183 us
  other arithmetic: 115 us -> 54.1 us
    all_gather x16 -> x1, waiting for transfers between devices: 2660 us -> 46 us  [per_device(): lax.all_gather(jnp.concatenate([routed_low, cotangent_low], axis=-1), 'fs...]
    reduce_scatter x8 -> x1, waiting for transfers between devices: 1230 us -> 58.2 us  [per_device(): lax.psum_scatter(token_parts, 'fsdp', scatter_dimension=0, tiled=True)]
    dot_general x86 -> x13, matrix products: 221 us -> 55.5 us  [the longest x10 51.8 us: apply(): return jnp.einsum(spec, left, right, preferred_element_type=jnp.float32)]
    dynamic_slice x16 -> x0, local copies, waits for them, and re-layouts: 51.4 us -> none  [the longest x8 25.7 us: expert_forward(): local_rows = lax.dynamic_index_in_dim(w_expert, expert, 0, keepdims=False)]
  transfers between devices with their start and end apart: 33 -> 11, of which waited for: 32 -> 10; matrix products, arithmetic and copies ran while one was open for 3% -> 13% of each run, Pallas kernels for 0% -> 0%
where the time goes in v1:
time: 960 us; the launch traced here: 952 us
  waiting for transfers between devices  573 us (60%)
  matrix products  183 us (19%)
  blocking collectives  76 us (8%)
  other arithmetic  54.1 us (6%)
  local copies, waits for them, and re-layouts  48.7 us (5%)
  between operations  16.1 us (2%)
    psum x1, waiting for transfers between devices, per_device(): lax.psum(grad_weights, 'ctx').astype(jnp.float32)  207 us
    all_gather x1, waiting for transfers between devices, per_device(): lax.all_gather(w_qkv, 'fsdp', axis=0, tiled=True)  71.1 us
    reduce_scatter x1, waiting for transfers between devices, per_device(): lax.psum_scatter(grad_wqkv.astype(jnp.bfloat16), 'fsdp', scatter_dimensio...  67.2 us
    reduce_scatter x1, waiting for transfers between devices, per_device(): lax.psum_scatter(token_parts, 'fsdp', scatter_dimension=0, tiled=True)  58.2 us
    dot_general x10, matrix products, apply(): return jnp.einsum(spec, left, right, preferred_element_type=jnp.float32)  51.8 us
    reduce_scatter x1, waiting for transfers between devices, per_device(): lax.psum_scatter(value_grad_all.astype(jnp.bfloat16), 'ctx', scatter_dime...  49.2 us
    all_gather x1, waiting for transfers between devices, per_device(): lax.all_gather(jnp.concatenate([routed_low, cotangent_low], axis=-1), 'fs...  46 us
    psum x1, blocking collectives, per_device(): lax.psum((grad_gain_one, grad_gain_two, grad_router, grad_mixing, grad_co...  42.9 us
  transfers between devices with their start and end apart: 11, of which 10 were waited for; matrix products, arithmetic and copies ran while one was open for 13% of the time, Pallas kernels for 0%

profile of v1, /device:TPU:0, one launch (start us, length us, event | category | flops | bytes accessed | tf_op | source)
XLA Modules:
  0.0 952.0 jit_solution(10698296496381457507)
XLA Ops:
  11.3 71.1 %all-gather.8.cloned.1.call-done = bf16[768,2304]{1,0:T(8,128)(2,1)} async-done(((bf16[192,2304]{1,0:T(8,128)(2,1)}), bf16[768,2304]{1,0:T(8,128)(2,1)}) %all-gather.8.cloned.1.call-update) | async-done | bytes 3538960 | tf_op jit(solution)/shard_map/all_gather | solution.py:120
  82.3 3.3 convolution_bitcast_fusion
  86.8 2.3 copy.148
  89.2 2.3 copy.149
  96.7 28.8 %all-gather.12.cloned.1.call-done = bf16[1,2048,768]{1,2,0:T(8,128)(2,1)} async-done(((bf16[1,256,768]{1,2,0:T(8,128)(2,1)}), bf16[1,2048,768]{1,2,0:T(8,128)(2,1)}) %all-gather.12.cloned.1.call-update) | async-done | bytes 3145744 | tf_op jit(solution)/shard_map/all_gather | solution.py:146
  125.5 4.7 fusion.285
  130.1 4.6 fusion.288
  134.7 4.7 fusion.291
  139.3 20.9 %all-gather.10.cloned.1.call-done = bf16[1,2048,768]{2,1,0:T(8,128)(2,1)} async-done(((bf16[1,256,768]{2,1,0:T(8,128)(2,1)}), bf16[1,2048,768]{2,1,0:T(8,128)(2,1)}) %all-gather.10.cloned.1.call-update) | async-done | bytes 3145744 | tf_op jit(solution)/shard_map/all_gather | solution.py:147
  160.3 4.9 copy.147
  165.1 3.0 fusion.113
  168.2 3.1 fusion.112
  171.3 3.0 fusion.111
  174.3 4.6 fusion.294
  178.9 3.0 fusion.110
  181.9 4.6 fusion.297
  186.6 3.0 fusion.109
  189.6 4.9 fusion.300
  194.5 3.1 fusion.108
  204.3 12.0 %all_gather.25 = f32[4,256,2]{1,2,0:T(2,128)S(1)} all-gather(f32[1,256,2]{1,2,0:T(2,128)S(1)} %bitcast_select_fusion), channel_id=1, replica_groups=mesh['ctx'=8,'fsdp'=4] {'fsdp'}, dimensions={0}, use_global_device_ids=true | all-gather | bytes 10240 | tf_op jit(solution)/shard_map/all_gather | solution.py:202
  219.5 46.0 %all-gather.16.cloned.1.call-done = bf16[4,256,1536]{2,1,0:T(8,128)(2,1)} async-done(((bf16[1,256,1536]{2,1,0:T(8,128)(2,1)}), bf16[4,256,1536]{2,1,0:T(8,128)(2,1)}) %all-gather.16.cloned.1.call-update) | async-done | bytes 3145744 | tf_op jit(solution)/shard_map/all_gather | solution.py:199
  265.5 8.5 fusion.301
  274.0 5.5 convert_bitcast_fusion.3
  280.0 2.2 copy-done.3
  283.8 6.8 fusion.22
  290.6 9.6 %multiply_convert_fusion.9 = (bf16[8,256,512]{2,1,0:T(8,128)(2,1)}, f32[8,256,512]{2,1,0:T(8,128)}) fusion(f32[8,256,512]{2,1,0:T(8,128)} %fusion.22, bf16[8,256,768]{2,1,0:T(8,128)(2,1)} %bitcast.609, bf16[8,512,3,768]{3,1,2,0:T(8,128)(2,1)} %param.25), kind=kOutput, calls=%fused_computation.55 | convolution fusion | flops 1616904192 | bytes 19922944 | tf_op jit(solution)/shard_map/ecd,efd->ecf/dot_general | solution.py:229
  300.2 3.4 fusion.14
  303.6 4.9 fusion.7
  308.6 9.3 all-reduce
  318.9 11.9 %all-gather.1 = f32[4,1,512]{2,1,0:T(1,128)S(1)} all-gather(f32[1,1,512]{2,1,0:T(1,128)S(1)} %bitcast.687), channel_id=2, replica_groups=mesh['ctx'=8,'fsdp'=4] {'fsdp'}, dimensions={0}, use_global_device_ids=true | all-gather | bytes 10240 | tf_op jit(solution)/shard_map/all_gather | solution.py:203
  330.9 4.7 multiply_convert_fusion
  335.8 9.8 %multiply_convert_fusion.8 = (bf16[8,256,512]{2,1,0:T(8,128)(2,1)S(1)}, bf16[8,256,512]{2,1,0:T(8,128)(2,1)S(1)}) fusion(f32[8,256,512]{2,1,0:T(8,128)} %fusion.22, f32[8,256,512]{2,1,0:T(8,128)} %get-tuple-element.140, bf16[8,256,768]{2,1,0:T(8,128)(2,1)S(1)} %bitcast.612, bf16[8,512,3,768]{3,1,2,0:T(8,128)(2,1)} %param.25), kind=kOutput, calls=%fused_computation.54 | convolution fusion | flops 1624244224 | bytes 22020096 | tf_op jit(solution)/shard_map/ecd,efd->ecf/dot_general | solution.py:229
  345.6 6.1 fusion.16
  351.8 4.8 add_convert_fusion
  356.6 3.2 bitcast_convert_fusion
  360.8 58.2 %reduce-scatter.6.cloned.1.call-done = bf16[1,256,1536]{2,1,0:T(8,128)(2,1)} async-done(((bf16[4,256,1536]{2,1,0:T(8,128)(2,1)}), bf16[1,256,1536]{2,1,0:T(8,128)(2,1)}) %reduce-scatter.6.cloned.1.call-update) | async-done | bytes 786448 | tf_op jit(solution)/shard_map/reduce_scatter | solution.py:255
  425.0 3.4 multiply_reduce_fusion.5
  431.1 4.0 multiply_reduce_fusion.4
  435.2 2.9 multiply_reduce_fusion.3
  438.4 2.7 multiply_reduce_fusion.2
  441.7 2.8 multiply_reduce_fusion.1
  444.9 2.9 multiply_reduce_fusion
  447.8 2.9 multiply_convert_fusion.5
  451.2 3.1 multiply_convert_fusion.4
  454.9 3.1 multiply_convert_fusion.3
  458.5 3.1 multiply_convert_fusion.2
  466.4 3.9 fusion.46
  470.2 3.9 fusion.48
  474.1 4.0 fusion.50
  478.1 4.0 fusion.52
  482.0 3.9 fusion.54
  485.9 3.9 fusion.56
  493.6 2.9 fusion.105
  500.9 11.8 %reduce-scatter.8.cloned.1.call-done = bf16[1,256,768]{1,2,0:T(8,128)(2,1)} async-done(((bf16[1,2048,768]{1,2,0:T(8,128)(2,1)}), bf16[1,256,768]{1,2,0:T(8,128)(2,1)}) %reduce-scatter.8.cloned.1.call-update) | async-done | bytes 393232 | tf_op jit(solution)/shard_map/reduce_scatter | solution.py:333
  514.1 49.2 %reduce-scatter.10.cloned.1.call-done = bf16[1,256,768]{1,2,0:T(8,128)(2,1)} async-done(((bf16[1,2048,768]{1,2,0:T(8,128)(2,1)}), bf16[1,256,768]{1,2,0:T(8,128)(2,1)}) %reduce-scatter.10.cloned.1.call-update) | async-done | bytes 393232 | tf_op jit(solution)/shard_map/reduce_scatter | solution.py:336
  563.3 4.0 convolution_convert_fusion
  567.4 4.5 convert_bitcast_fusion
  575.7 7.9 pad_maximum_fusion
  583.6 11.3 %reduce-scatter.14.cloned.1.call-done = bf16[192,768]{1,0:T(8,128)(2,1)} async-done(((bf16[768,768]{1,0:T(8,128)(2,1)}), bf16[192,768]{1,0:T(8,128)(2,1)}) %reduce-scatter.14.cloned.1.call-update) | async-done | bytes 294928 | tf_op jit(solution)/shard_map/reduce_scatter | solution.py:361
  594.9 67.2 %reduce-scatter.12.cloned.1.call-done = bf16[192,2304]{1,0:T(8,128)(2,1)} async-done(((bf16[768,2304]{1,0:T(8,128)(2,1)}), bf16[192,2304]{1,0:T(8,128)(2,1)}) %reduce-scatter.12.cloned.1.call-update) | async-done | bytes 884752 | tf_op jit(solution)/shard_map/reduce_scatter | solution.py:358
  666.5 3.7 fusion.136
  670.2 42.9 %all-reduce.1 = (f32[768]{0:T(1024)}, f32[768]{0:T(1024)}, f32[768,12]{0,1:T(8,128)}, f32[12,12]{0,1:T(8,128)S(1)}, f32[2,768]{1,0:T(2,128)}) all-reduce(f32[768]{0:T(1024)S(1)} %get-tuple-element.79, f32[768]{0:T(1024)S(1)} %get-tuple-element.77, f32[768,12]{0,1:T(8,128)S(1)} %fusion.169, ...), channel_id=1, replica_groups=mesh['ctx'=8,'fsdp'=4] {'ctx','fsdp'}, use_global_device_ids=true, to_apply=%region_49.50 | all-reduce | flops 12432 | bytes 99456 | tf_op jit(solution)/shard_map/psum | solution.py:370
  714.9 207.3 %all-reduce.5.cloned.1.call-done = (bf16[8,512,3,768]{3,1,0,2:T(8,128)(2,1)}, bf16[192,2304]{1,0:T(8,128)(2,1)}, bf16[192,768]{1,0:T(8,128)(2,1)}) async-done(((bf16[8,512,3,768]{3,1,0,2:T(8,128)(2,1)}, bf16[192,2304]{1,0:T(8,128)(2,1)}, bf16[192,768]{1,0:T(8,128)(2,1)}), (bf16[8,512,3,768]{3,1,0,2:T(8,128)(2,1)}, bf16[192,2304]{1,0:T(8,128)(2,1)}, bf16[192,768]{1,0:T(8,128)(2,1)})) %all-reduce.5.cloned.1.call-update) | async-done | bytes 20054032 | tf_op jit(solution)/shard_map/psum | solution.py:368
  922.1 20.9 %copy.170 = f32[8,512,3,768]{3,1,2,0:T(8,128)} copy(bf16[8,512,3,768]{3,1,0,2:T(8,128)(2,1)} %get-tuple-element.94) | data formatting | bytes 56623104
  (276 shorter events, 61.3 us)
Async XLA Ops:
  7.2 211.5 %copy-start = (f32[768,12]{0,1:T(8,128)S(1)}, f32[768,12]{0,1:T(8,128)}, u32[]{:S(2)}) copy-start(f32[768,12]{0,1:T(8,128)} %param.22) | copy-start | bytes 110596
  7.2 75.1 %all-gather.8.cloned.1.call-start = ((), (), s32[]{:S(2)}) async-start(), calls=%async_computation.5 | async-start | bytes 4423680 | tf_op jit(solution)/shard_map/all_gather | solution.py:120
  7.9 117.5 %all-gather.12.cloned.1.call-start = ((), (), s32[]{:S(2)}) async-start(), calls=%async_computation.7 | async-start | bytes 3538944 | tf_op jit(solution)/shard_map/all_gather | solution.py:146
  8.7 78.2 %copy-start.60 = (f32[768]{0:T(1024)}, f32[768]{0:T(1024)S(1)}, u32[]{:S(2)}) copy-start(f32[768]{0:T(1024)S(1)} %convert_element_type.252) | copy-start | bytes 9220
  10.4 76.4 %copy-start.65 = (f32[256]{0:T(256)}, f32[256]{0:T(256)S(1)}, u32[]{:S(2)}) copy-start(f32[256]{0:T(256)S(1)} %get-tuple-element.122) | copy-start | bytes 3076
  11.2 80.2 %copy-start.56 = (f32[256,32]{0,1:T(8,128)}, f32[256,32]{0,1:T(8,128)S(1)}, u32[]{:S(2)}) copy-start(f32[256,32]{0,1:T(8,128)S(1)} %get-tuple-element.120) | copy-start | bytes 98308
  86.8 9.2 copy-start.71
  86.8 9.7 %copy-start.34 = (bf16[1,256,768]{2,1,0:T(8,128)(2,1)S(1)}, bf16[1,256,768]{2,1,0:T(8,128)(2,1)}, u32[]{:S(2)}) copy-start(bf16[1,256,768]{2,1,0:T(8,128)(2,1)} %param.17) | copy-start | bytes 1179652
  93.1 93.5 %copy-start.25 = (bf16[1,256,12,32]{1,3,2,0:T(8,128)(2,1)}, bf16[1,256,12,32]{1,3,2,0:T(8,128)(2,1)S(1)}, u32[]{:S(2)}) copy-start(bf16[1,256,12,32]{1,3,2,0:T(8,128)(2,1)S(1)} %get-tuple-element.108) | copy-start | bytes 589828
  93.9 66.4 %all-gather.10.cloned.1.call-start = ((), (), s32[]{:S(2)}) async-start(), calls=%async_computation.6 | async-start | bytes 3538944 | tf_op jit(solution)/shard_map/all_gather | solution.py:147
  94.8 102.9 %all-gather.14.cloned.1.call-start = ((), (), s32[]{:S(2)}) async-start(), calls=%async_computation.8 | async-start | bytes 1474560 | tf_op jit(solution)/shard_map/all_gather | solution.py:121
  95.3 170.2 %all-gather.16.cloned.1.call-start = ((), (), s32[]{:S(2)}) async-start(), calls=%async_computation.9 | async-start | bytes 3932160 | tf_op jit(solution)/shard_map/all_gather | solution.py:199
  96.5 98.0 %copy-start.51 = (pred[256,2048]{1,0:T(8,128)(4,1)}, pred[256,2048]{1,0:T(8,128)(4,1)S(1)}, u32[]{:S(2)}) copy-start(pred[256,2048]{1,0:T(8,128)(4,1)S(1)} %fusion.83) | copy-start | bytes 1572868
  197.6 4.3 copy-start.47
  197.6 4.3 copy-start.64
  200.8 18.3 %copy-start.23 = (bf16[1,256,768]{2,1,0:T(8,128)(2,1)}, bf16[1,256,768]{2,1,0:T(8,128)(2,1)S(1)}, u32[]{:S(2)}) copy-start(bf16[1,256,768]{2,1,0:T(8,128)(2,1)S(1)} %get-tuple-element.98) | copy-start | bytes 1179652
  200.8 17.3 %copy-start.72 = (u32[32]{0:T(128)S(1)}, u32[32]{0:T(128)}, u32[]{:S(2)}) copy-start(u32[32]{0:T(128)} %constant.48) | copy-start | bytes 388
  200.8 18.3 %copy-start.62 = (f32[1,256,12]{1,0,2:T(1,128)S(1)}, f32[1,256,12]{1,0,2:T(1,128)}, u32[]{:S(2)}) copy-start(f32[1,256,12]{1,0,2:T(1,128)} %param.14) | copy-start | bytes 36868
  200.9 18.3 %copy-start.67 = (f32[12,12]{1,0:T(8,128)S(1)}, f32[12,12]{1,0:T(8,128)}, u32[]{:S(2)}) copy-start(f32[12,12]{1,0:T(8,128)} %param.23) | copy-start | bytes 1732
  201.8 217.2 %reduce-scatter.6.cloned.1.call-start = ((), (), s32[]{:S(2)}) async-start(), calls=%async_computation.10 | async-start | bytes 3932160 | tf_op jit(solution)/shard_map/reduce_scatter | solution.py:255
  283.8 16.4 %slice-start = ((s8[18874368]{0:T(1024)(128)(4,1)}), s8[4194304]{0:T(1024)(128)(4,1)S(1)}, s32[]{:S(2)}) async-start(s8[18874368]{0:T(1024)(128)(4,1)} %bitcast.606), calls=%async_computation.16 | async-start | bytes 8388608
  283.8 16.4 %slice-start.1 = ((s8[18874368]{0:T(1024)(128)(4,1)}), s8[4194304]{0:T(1024)(128)(4,1)S(1)}, s32[]{:S(2)}) async-start(s8[18874368]{0:T(1024)(128)(4,1)} %bitcast.606), calls=%async_computation.17 | async-start | bytes 8388608
  290.6 9.6 %slice-start.2 = ((s8[18874368]{0:T(1024)(128)(4,1)}), s8[4194304]{0:T(1024)(128)(4,1)S(1)}, s32[]{:S(2)}) async-start(s8[18874368]{0:T(1024)(128)(4,1)} %bitcast.606), calls=%async_computation.18 | async-start | bytes 8388608
  290.6 9.6 %slice-start.3 = ((s8[18874368]{0:T(1024)(128)(4,1)}), s8[4194304]{0:T(1024)(128)(4,1)S(1)}, s32[]{:S(2)}) async-start(s8[18874368]{0:T(1024)(128)(4,1)} %bitcast.606), calls=%async_computation.19 | async-start | bytes 8388608
  290.6 9.6 %slice-start.4 = ((s8[18874368]{0:T(1024)(128)(4,1)}), s8[2097152]{0:T(1024)(128)(4,1)S(1)}, s32[]{:S(2)}) async-start(s8[18874368]{0:T(1024)(128)(4,1)} %bitcast.606), calls=%async_computation.20 | async-start | bytes 4194304
  303.6 4.9 copy-start.2
  335.8 9.8 %copy-start.20 = (bf16[8,4,64,768]{3,2,1,0:T(8,128)(2,1)}, bf16[8,4,64,768]{3,2,1,0:T(8,128)(2,1)S(1)}, u32[]{:S(2)}) copy-start(bf16[8,4,64,768]{3,2,1,0:T(8,128)(2,1)S(1)} %copy.161) | copy-start | bytes 9437188
  345.6 6.1 copy-start.18
  345.6 6.1 copy-start.27
  351.8 4.8 copy-start.49
  359.9 60.5 %copy-start.7 = (f32[1,256,768]{2,1,0:T(8,128)S(1)}, f32[1,256,768]{2,1,0:T(8,128)}, u32[]{:S(2)}) copy-start(f32[1,256,768]{2,1,0:T(8,128)} %copy-done.6) | copy-start | bytes 2359300
  359.9 152.8 %reduce-scatter.8.cloned.1.call-start = ((), (), s32[]{:S(2)}) async-start(), calls=%async_computation.11 | async-start | bytes 3538944 | tf_op jit(solution)/shard_map/reduce_scatter | solution.py:333
  422.8 67.1 %copy-start.21 = (f32[1,256,768]{2,1,0:T(8,128)}, f32[1,256,768]{2,1,0:T(8,128)S(1)}, u32[]{:S(2)}) copy-start(f32[1,256,768]{2,1,0:T(8,128)S(1)} %subtract_add_fusion) | copy-start | bytes 2359300
  425.0 3.7 copy-start.43
  431.1 4.0 copy-start.37
  431.1 4.0 copy-start.45
  450.7 3.7 copy-start.9
  451.2 3.7 copy-start.42
  458.0 3.7 copy-start.12
  458.5 3.7 copy-start.44
  466.3 97.0 %reduce-scatter.10.cloned.1.call-start = ((), (), s32[]{:S(2)}) async-start(), calls=%async_computation.12 | async-start | bytes 3538944 | tf_op jit(solution)/shard_map/reduce_scatter | solution.py:336
  485.9 4.0 copy-start.48
  489.9 105.0 %reduce-scatter.14.cloned.1.call-start = ((), (), s32[]{:S(2)}) async-start(), calls=%async_computation.14 | async-start | bytes 1474560 | tf_op jit(solution)/shard_map/reduce_scatter | solution.py:361
  491.4 170.7 %reduce-scatter.12.cloned.1.call-start = ((), (), s32[]{:S(2)}) async-start(), calls=%async_computation.13 | async-start | bytes 4423680 | tf_op jit(solution)/shard_map/reduce_scatter | solution.py:358
  491.7 4.9 copy-start.11
  491.7 6.9 copy-start.13
  491.7 6.9 copy-start.46
  493.6 5.7 copy-start.15
  498.5 15.2 %copy-start.57 = (f32[256,32]{0,1:T(8,128)S(1)}, f32[256,32]{0,1:T(8,128)}, u32[]{:S(2)}) copy-start(f32[256,32]{0,1:T(8,128)} %copy-done.56) | copy-start | bytes 98308
  498.6 15.2 %copy-start.59 = (f32[256,32]{0,1:T(8,128)S(1)}, f32[256,32]{0,1:T(8,128)}, u32[]{:S(2)}) copy-start(f32[256,32]{0,1:T(8,128)} %get-tuple-element.118) | copy-start | bytes 98308
  500.1 63.2 %copy-start.32 = (bf16[1,256,768]{2,1,0:T(8,128)(2,1)S(1)}, bf16[1,256,768]{2,1,0:T(8,128)(2,1)}, u32[]{:S(2)}) copy-start(bf16[1,256,768]{2,1,0:T(8,128)(2,1)} %param.13) | copy-start | bytes 1179652
  500.1 63.2 %copy-start.61 = (f32[768]{0:T(1024)S(1)}, f32[768]{0:T(1024)}, u32[]{:S(2)}) copy-start(f32[768]{0:T(1024)} %copy-done.60) | copy-start | bytes 9220
  500.1 63.2 %copy-start.66 = (f32[256]{0:T(256)S(1)}, f32[256]{0:T(256)}, u32[]{:S(2)}) copy-start(f32[256]{0:T(256)} %copy-done.65) | copy-start | bytes 3076
  514.1 53.2 %copy-start.54 = (bf16[1,256,12,64]{1,3,2,0:T(8,128)(2,1)}, bf16[1,256,12,64]{1,3,2,0:T(8,128)(2,1)S(1)}, u32[]{:S(2)}) copy-start(bf16[1,256,12,64]{1,3,2,0:T(8,128)(2,1)S(1)} %get-tuple-element.155) | copy-start | bytes 1179652
  514.1 53.2 %copy-start.55 = (bf16[1,256,12,64]{1,3,2,0:T(8,128)(2,1)}, bf16[1,256,12,64]{1,3,2,0:T(8,128)(2,1)S(1)}, u32[]{:S(2)}) copy-start(bf16[1,256,12,64]{1,3,2,0:T(8,128)(2,1)S(1)} %get-tuple-element.156) | copy-start | bytes 1179652
  567.4 4.6 copy-start.5
  567.4 354.7 %all-reduce.5.cloned.1.call-start = ((), (), s32[]{:S(2)}) async-start(), calls=%async_computation.15 | async-start | bytes 40108032 | tf_op jit(solution)/shard_map/psum | solution.py:368
  567.4 4.5 copy-start.19
  662.1 4.4 copy-start.33
  666.5 47.3 %copy-start.22 = (f32[1,256,768]{2,1,0:T(8,128)S(1)}, f32[1,256,768]{2,1,0:T(8,128)}, u32[]{:S(2)}) copy-start(f32[1,256,768]{2,1,0:T(8,128)} %copy-done.21) | copy-start | bytes 2359300
  666.5 47.3 %copy-start.69 = (f32[256]{0:T(256)S(1)}, f32[256]{0:T(256)}, u32[]{:S(2)}) copy-start(f32[256]{0:T(256)} %get-tuple-element.121) | copy-start | bytes 3076
  922.1 20.9 %copy-start.50 = (bf16[192,2304]{1,0:T(8,128)(2,1)S(1)}, bf16[192,2304]{1,0:T(8,128)(2,1)}, u32[]{:S(2)}) copy-start(bf16[192,2304]{1,0:T(8,128)(2,1)} %get-tuple-element.95) | copy-start | bytes 2654212
  922.1 22.3 %copy-start.58 = (bf16[192,768]{1,0:T(8,128)(2,1)S(1)}, bf16[192,768]{1,0:T(8,128)(2,1)}, u32[]{:S(2)}) copy-start(bf16[192,768]{1,0:T(8,128)(2,1)} %get-tuple-element.96) | copy-start | bytes 884740
  922.1 23.1 %copy-start.1 = (f32[768,12]{0,1:T(8,128)S(1)}, f32[768,12]{0,1:T(8,128)}, u32[]{:S(2)}) copy-start(f32[768,12]{0,1:T(8,128)} %param.22) | copy-start | bytes 110596
  (25 other events, 61.9 us)
Sparse Core Ops, SparseCore 0:
  9.6 72.6 all-gather.7
  94.0 31.3 all-gather.11
  127.9 32.3 all-gather.9
  161.7 30.4 all-gather.13
  201.9 63.4 all-gather.15
  360.0 58.9 reduce-scatter.5
  466.4 46.2 reduce-scatter.7
  517.0 46.2 reduce-scatter.9
  565.6 29.1 reduce-scatter.13
  597.0 65.0 reduce-scatter.11
  666.9 255.1 all-reduce.4

commit v2 on v1

--- a/solution.py
+++ b/solution.py
@@ -1,8 +1,12 @@
+import itertools
 import math
 
 import jax
 import jax.numpy as jnp
 from jax import lax
+from jax.experimental import pallas as pl
+from jax.experimental.pallas import tpu as pltpu
+
 from jax.sharding import PartitionSpec as P
 
 HEAD_DIM = 64
@@ -11,6 +15,672 @@
 EPSILON = 1e-05
 MASKED = -1e30
 HIGHEST = lax.Precision.HIGHEST
+
+
+LOGICAL = pl.DeviceIdType.MESH
+VMEM_LIMIT = 56 * 1024 * 1024
+
+
+class Copies:
+    def __init__(self, send, recv):
+        self.send, self.recv, self.used = send, recv, 0
+
+    def make(self, source, target, peer):
+        index = self.used
+        self.used += 1
+        return pltpu.make_async_remote_copy(
+            source, target, self.send.at[index], self.recv.at[index],
+            device_id=peer, device_id_type=LOGICAL,
+        )
+
+
+def meet(peers):
+    barrier = pltpu.get_barrier_semaphore()
+    for allowed, peer in peers:
+        @pl.when(allowed)
+        def _():
+            pl.semaphore_signal(barrier, 1, device_id=peer, device_id_type=LOGICAL)
+    awaited = sum(jnp.where(allowed, 1, 0) for allowed, _ in peers)
+    pl.semaphore_wait(barrier, awaited)
+
+
+def together(*streams):
+    for _ in itertools.zip_longest(*streams):
+        pass
+
+
+def within(value, count):
+    return (value >= 0) & (value < count)
+
+
+def bounded(value, count):
+    return jnp.minimum(jnp.maximum(value, 0), count - 1)
+
+
+def line_peers(count):
+    rank = lax.axis_index("fsdp")
+    return [
+        (within(rank + way, count), {"fsdp": bounded(rank + way, count)}) for way in (1, -1)
+    ]
+
+
+def ring_peers(axis, count, stride=1):
+    rank = lax.axis_index(axis)
+    return [
+        (rank >= 0, {axis: lax.rem(rank + stride * step, count)})
+        for step in range(1, count // stride)
+    ]
+
+
+def own_place(count):
+    rank = lax.axis_index("ctx")
+    core = lax.rem(rank, 2)
+    return rank, core, rank // 2, count // 2, rank + 1 - 2 * core
+
+
+def plane_peers(count):
+    rank, core, chip, chips, sibling = own_place(count)
+    peers = [(rank >= 0, {"ctx": sibling})]
+    if chips == 4:
+        across, along, _ = square(chip)
+        return peers + [(rank >= 0, {"ctx": 2 * c + core}) for c in (across, along)]
+    return peers + ring_peers("ctx", count, 2)
+
+
+def square(chip):
+    side, row = lax.rem(chip, 2), chip // 2
+    across = chip + 1 - 2 * side
+    along = chip + 2 - 4 * row
+    return across, along, across + 2 - 4 * row
+
+
+def line_gather(copies, own, slot, count, arrived=None):
+    rank = lax.axis_index("fsdp")
+    sent, latest = [], {}
+    for hop in range(1, count + 1):
+        for way in (1, -1):
+            origin = rank - way * (hop - 1)
+            held = slot(bounded(origin, count))
+            if hop > 1:
+                earlier = latest[way]
+
+                @pl.when(within(origin, count))
+                def _():
+                    earlier.wait_recv()
+
+                if arrived is not None:
+                    arrived(within(origin, count), bounded(origin, count), held)
+            if hop < count:
+                copy = copies.make(
+                    own if hop == 1 else held, held, {"fsdp": bounded(rank + way, count)}
+                )
+                allowed = within(origin, count) & within(rank + way, count)
+
+                @pl.when(allowed)
+                def _():
+                    copy.start()
+
+                sent.append((allowed, copy))
+                latest[way] = copy
+        yield
+    for allowed, copy in sent:
+
+        @pl.when(allowed)
+        def _():
+            copy.wait_send()
+
+
+def line_reduce(copies, part, passing, landing, count, total):
+    rank = lax.axis_index("fsdp")
+    sent, arriving = [], {}
+    for step in range(count - 1, 0, -1):
+        for side, way in enumerate((1, -1)):
+            goal = rank + way * step
+            allowed = within(goal, count)
+            copy = copies.make(
+                passing.at[side, step - 1],
+                landing.at[side, step - 1],
+                {"fsdp": bounded(rank + way, count)},
+            )
+            arriving[side, step - 1] = copy
+            own = part(bounded(goal, count))
+            has_earlier = allowed & within(rank - way, count)
+            if step < count - 1:
+                earlier = arriving[side, step]
+
+                @pl.when(has_earlier)
+                def _():
+                    earlier.wait_recv()
+                    passing[side, step - 1] = (
+                        own[...].astype(jnp.float32) + landing[side, step].astype(jnp.float32)
+                    ).astype(passing.dtype)
+
+                @pl.when(allowed & jnp.logical_not(within(rank - way, count)))
+                def _():
+                    passing[side, step - 1] = own[...]
+            else:
+
+                @pl.when(allowed)
+                def _():
+                    passing[side, step - 1] = own[...]
+
+            @pl.when(allowed)
+            def _():
+                copy.start()
+
+            sent.append((allowed, copy))
+        yield
+    total[...] = part(rank)[...].astype(jnp.float32)
+    for side, way in enumerate((1, -1)):
+        last = arriving[side, 0]
+
+        @pl.when(within(rank - way, count))
+        def _():
+            last.wait_recv()
+            total[...] += landing[side, 0].astype(jnp.float32)
+    for allowed, copy in sent:
+
+        @pl.when(allowed)
+        def _():
+            copy.wait_send()
+
+
+def push_gather(copies, own, slot, axis, count, stride=1):
+    rank = lax.axis_index(axis)
+    sent = []
+    for step in range(1, count // stride):
+        copy = copies.make(own, slot(step), {axis: lax.rem(rank + stride * step, count)})
+        copy.start()
+        sent.append(copy)
+    yield
+    for copy in sent:
+        copy.wait()
+
+
+def plane_gather(copies, own, slot, count):
+    rank, core, chip, chips, sibling = own_place(count)
+    sent, forwarded = [], []
+
+    def send(source, target, peer):
+        copy = copies.make(source, target, {"ctx": peer})
+        copy.start()
+        sent.append(copy)
+        return copy
+
+    def forward(index, part):
+        copy = copies.make(slot(index, part), slot(index, part), {"ctx": sibling})
+        copy.start()
+        forwarded.append(copy)
+
+    if chips == 4:
+        across, along, _ = square(chip)
+        side_x, side_y = 2 * across + core, 2 * along + core
+        corner = 2 * square(chip)[2] + core
+        first_x = send(own(1), slot(rank, 1), side_x)
+        second_y = send(own(2), slot(rank, 2), side_y)
+        second_x = send(own(2), slot(rank, 2), side_x)
+        first_y = send(own(1), slot(rank, 1), side_y)
+        copy = copies.make(own(0), slot(rank, 0), {"ctx": sibling})
+        copy.start()
+        forwarded.append(copy)
+        yield
+        first_x.wait_recv()
+        corner_first = send(slot(side_x, 1), slot(side_x, 1), side_y)
+        forward(side_x, 1)
+        second_y.wait_recv()
+        corner_second = send(slot(side_y, 2), slot(side_y, 2), side_x)
+        forward(side_y, 2)
+        yield
+        second_x.wait_recv()
+        forward(side_x, 2)
+        first_y.wait_recv()
+        forward(side_y, 1)
+        yield
+        corner_first.wait_recv()
+        forward(corner, 1)
+        corner_second.wait_recv()
+        forward(corner, 2)
+        yield
+    else:
+        pending = []
+        for step in range(1, chips):
+            peer = lax.rem(rank + 2 * step, count)
+            pending.append((lax.rem(rank + count - 2 * step, count), send(own(0), slot(rank, 0), peer)))
+        copy = copies.make(own(0), slot(rank, 0), {"ctx": sibling})
+        copy.start()
+        forwarded.append(copy)
+        yield
+        for origin, copy in pending:
+            copy.wait_recv()
+            forward(origin, 0)
+        yield
+    for copy in sent:
+        copy.wait_send()
+    for copy in forwarded:
+        copy.wait()
+
+
+def plane_reduce(copies, paired, passing, landing, count, finish):
+    rank, core, chip, chips, sibling = own_place(count)
+    sent = []
+
+    def send(source, target, peer_chip):
+        copy = copies.make(source, target, {"ctx": 2 * peer_chip + core})
+        copy.start()
+        sent.append(copy)
+        return copy
+
+    if chips == 4:
+        across, along, corner = square(chip)
+        via_x = send(paired(corner, 1), landing.at[0], across)
+        via_y = send(paired(corner, 2), landing.at[1], along)
+        own_x = send(paired(across, 1), landing.at[2], across)
+        own_y = send(paired(along, 2), landing.at[3], along)
+        yield
+        via_x.wait_recv()
+        passing[0] = (
+            paired(along, 1)[...].astype(jnp.float32) + landing[0].astype(jnp.float32)
+        ).astype(passing.dtype)
+        last_first = send(passing.at[0], landing.at[4], along)
+        via_y.wait_recv()
+        passing[1] = (
+            paired(across, 2)[...].astype(jnp.float32) + landing[1].astype(jnp.float32)
+        ).astype(passing.dtype)
+        last_second = send(passing.at[1], landing.at[5], across)
+        yield
+        own_x.wait_recv()
+        own_y.wait_recv()
+        last_first.wait_recv()
+        last_second.wait_recv()
+        for half in (1, 2):
+            total = paired(chip, half)[...].astype(jnp.float32)
+            total = total + landing[1 + half].astype(jnp.float32)
+            total = total + landing[3 + half].astype(jnp.float32)
+            finish(half, total)
+    else:
+        for step in range(1, chips):
+            send(paired(lax.rem(chip + step, chips), 0), landing.at[step - 1], lax.rem(chip + step, chips))
+        yield
+        total = paired(chip, 0)[...].astype(jnp.float32)
+        for step, copy in enumerate(sent):
+            copy.wait_recv()
+            total = total + landing[step].astype(jnp.float32)
+        finish(0, total)
+    for copy in sent:
+        copy.wait_send()
+
+
+def remote_call(kernel, name, results, operands, in_spaces, out_spaces, scratch, copies, cost):
+    ids = ("weights", "keys", "rows", "row_sums", "key_sums", "totals")
+    return pl.pallas_call(
+        kernel,
+        out_shape=results,
+        in_specs=[pl.BlockSpec(memory_space=space) for space in in_spaces],
+        out_specs=[pl.BlockSpec(memory_space=space) for space in out_spaces],
+        scratch_shapes=list(scratch)
+        + [pltpu.SemaphoreType.DMA((copies,)), pltpu.SemaphoreType.DMA((copies,))],
+        compiler_params=pltpu.CompilerParams(
+            collective_id=ids.index(name), has_side_effects=True, vmem_limit_bytes=VMEM_LIMIT
+        ),
+        cost_estimate=pl.CostEstimate(flops=0, bytes_accessed=cost, transcendentals=0),
+        name=name,
+    )(*operands)
+
+
+def struct(shape, dtype):
+    return jax.ShapeDtypeStruct(shape, dtype)
+
+
+class SharedBlock:
+    def __init__(self, copies, source, target, count, ctx_count):
+        _, core, _, _, self.sibling = own_place(ctx_count)
+        half = source.shape[0] // 2
+        rows = pl.ds(pl.multiple_of(core * half, math.gcd(half, 256)), half)
+        self.copies, self.forwarded = copies, []
+        self.stream = line_gather(
+            copies, source.at[rows], lambda i: target.at[i, rows], count, self.arrived
+        )
+
+    def arrived(self, allowed, _, held):
+        copy = self.copies.make(held, held, {"ctx": self.sibling})
+
+        @pl.when(allowed)
+        def _():
+            copy.start()
+
+        self.forwarded.append((allowed, copy))
+
+    def wait(self):
+        for allowed, copy in self.forwarded:
+
+            @pl.when(allowed)
+            def _():
+                copy.wait()
+
+
+def gather_weights(weight, count, ctx_count):
+    rows, width = weight.shape
+
+    def kernel(source, target, local, send, recv):
+        copies = Copies(send, recv)
+        rank = lax.axis_index("fsdp")
+        meet(line_peers(count) + plane_peers(ctx_count)[:1])
+        keep = pltpu.make_async_copy(source, target.at[rank], local)
+        keep.start()
+        block = SharedBlock(copies, source, target, count, ctx_count)
+        together(block.stream)
+        block.wait()
+        keep.wait()
+
+    (full,) = remote_call(
+        kernel, "weights", [struct((count, rows, width), weight.dtype)], [weight],
+        [pl.ANY], [pl.ANY], [pltpu.SemaphoreType.DMA], 4 * count, count * rows * width * 4,
+    )
+    return full.reshape(count * rows, width)
+
+
+def gather_keys(block, weights, count, ctx_count):
+    rows, width = block.shape
+    half = rows // 2
+
+    def kernel(*refs):
+        own, *sources = refs[: 1 + len(weights)]
+        gathered, *targets = refs[1 + len(weights) : 2 + 2 * len(weights)]
+        local, send, recv = refs[2 + 2 * len(weights) :]
+        copies = Copies(send, recv)
+        rank, place = lax.axis_index("fsdp"), lax.axis_index("ctx")
+        spans = (pl.ds(0, rows), pl.ds(0, half), pl.ds(half, half))
+        meet(line_peers(count) + plane_peers(ctx_count))
+        kept = [pltpu.make_async_copy(own, gathered.at[place], local.at[0])]
+        kept += [
+            pltpu.make_async_copy(source, target.at[rank], local.at[1 + i])
+            for i, (source, target) in enumerate(zip(sources, targets))
+        ]
+        for copy in kept:
+            copy.start()
+        blocks = [SharedBlock(copies, s, t, count, ctx_count) for s, t in zip(sources, targets)]
+        together(
+            plane_gather(
+                copies,
+                lambda part: own.at[spans[part]],
+                lambda i, part: gathered.at[i, spans[part]],
+                ctx_count,
+            ),
+            *[b.stream for b in blocks],
+        )
+        for b in blocks:
+            b.wait()
+        for copy in kept:
+            copy.wait()
+
+    results = [struct((ctx_count, rows, width), block.dtype)]
+    results += [struct((count,) + w.shape, w.dtype) for w in weights]
+    gathered, *full = remote_call(
+        kernel, "keys", results, [block, *weights],
+        [pl.ANY] * (1 + len(weights)), [pl.ANY] * (1 + len(weights)),
+        [pltpu.SemaphoreType.DMA((1 + len(weights),))],
+        16 + 2 * ctx_count + 4 * count * len(weights),
+        ctx_count * rows * width * 4,
+    )
+    return gathered.reshape(ctx_count * rows, width), [
+        f.reshape(count * f.shape[1], f.shape[2]) for f in full
+    ]
+
+
+def gather_rows(block, notes, count):
+    def kernel(own, own_notes, gathered, all_notes, local, send, recv):
+        copies = Copies(send, recv)
+        rank = lax.axis_index("fsdp")
+        meet(ring_peers("fsdp", count))
+        kept = [
+            pltpu.make_async_copy(own, gathered.at[rank], local.at[0]),
+            pltpu.make_async_copy(own_notes, all_notes.at[rank], local.at[1]),
+        ]
+        for copy in kept:
+            copy.start()
+        together(
+            push_gather(copies, own_notes, lambda step: all_notes.at[rank], "fsdp", count),
+            line_gather(copies, own, lambda i: gathered.at[i], count),
+        )
+        for copy in kept:
+            copy.wait()
+
+    return remote_call(
+        kernel, "rows",
+        [struct((count,) + block.shape, block.dtype), struct((count,) + notes.shape, notes.dtype)],
+        [block, notes], [pl.ANY] * 2, [pl.ANY] * 2, [pltpu.SemaphoreType.DMA((2,))],
+        4 * count, count * block.size * 4,
+    )
+
+
+def reduce_rows(parts, notes, count):
+    _, rows, width = parts.shape
+
+    def kernel(given, given_notes, total, notes_total, passing, landing, noted, send, recv):
+        copies = Copies(send, recv)
+        rank = lax.axis_index("fsdp")
+        meet(ring_peers("fsdp", count))
+        pushes = []
+        for step in range(1, count):
+            peer = lax.rem(rank + step, count)
+            copy = copies.make(given_notes.at[peer], noted.at[step - 1], {"fsdp": peer})
+            copy.start()
+            pushes.append(copy)
+        together(
+            line_reduce(copies, lambda d: given.at[d], passing, landing, count, total)
+        )
+        sums = given_notes[rank]
+        for step, copy in enumerate(pushes):
+            copy.wait()
+            sums = sums + noted[step]
+        notes_total[...] = sums
+
+    return remote_call(
+        kernel, "row_sums",
+        [struct((rows, width), jnp.float32), struct(notes.shape[1:], notes.dtype)],
+        [parts, notes], [pltpu.VMEM] * 2, [pltpu.VMEM] * 2,
+        [
+            pltpu.VMEM((2, count - 1, rows, width), parts.dtype),
+            pltpu.VMEM((2, count - 1, rows, width), parts.dtype),
+            pltpu.VMEM((count - 1,) + notes.shape[1:], notes.dtype),
+        ],
+        4 * count, count * rows * width * 4,
+    )
+
+
+def reduce_keys(parts, row_parts, count, ctx_count):
+    _, rows, width = parts.shape
+    chips = ctx_count // 2
+    half = rows // 2
+    lands = (6, half, width) if chips == 4 else (chips - 1, rows, width)
+
+    def kernel(given, given_rows, total, rows_total, met, paired, passing, landing,
+               row_passing, row_landing, send, recv):
+        copies = Copies(send, recv)
+        _, core, _, _, sibling = own_place(ctx_count)
+        spans = (pl.ds(0, rows), pl.ds(0, half), pl.ds(half, half))
+        meet(ring_peers("fsdp", count) + plane_peers(ctx_count))
+        exchanged = []
+        for q in range(chips):
+            copy = copies.make(given.at[2 * q + 1 - core], met.at[q], {"ctx": sibling})
+            copy.start()
+            exchanged.append(copy)
+
+        def finish(part, value):
+            total[spans[part], :] = value
+
+        def planes():
+            yield
+            for q, copy in enumerate(exchanged):
+                copy.wait_recv()
+                paired[q] = (
+                    given[2 * q + core].astype(jnp.float32) + met[q].astype(jnp.float32)
+                ).astype(paired.dtype)
+            yield from plane_reduce(
+                copies, lambda q, part: paired.at[q, spans[part]],
+                passing, landing, ctx_count, finish,
+            )
+
+        together(
+            planes(),
+            line_reduce(
+                copies, lambda d: given_rows.at[d], row_passing, row_landing, count, rows_total
+            ),
+        )
+        for copy in exchanged:
+            copy.wait_send()
+
+    _, row_count, row_width = row_parts.shape
+    return remote_call(
+        kernel, "key_sums",
+        [struct((rows, width), jnp.float32), struct((row_count, row_width), jnp.float32)],
+        [parts, row_parts], [pltpu.VMEM] * 2, [pltpu.VMEM] * 2,
+        [
+            pltpu.VMEM((chips, rows, width), parts.dtype),
+            pltpu.VMEM((chips, rows, width), parts.dtype),
+            pltpu.VMEM((2, half, width), parts.dtype),
+            pltpu.VMEM(lands, parts.dtype),
+            pltpu.VMEM((2, count - 1, row_count, row_width), parts.dtype),
+            pltpu.VMEM((2, count - 1, row_count, row_width), parts.dtype),
+        ],
+        2 * chips + 8 + 2 * count, ctx_count * rows * width * 4,
+    )
+
+
+def reduce_weights(parts, small, count, ctx_count):
+    _, rows, width = parts.shape
+    chips = ctx_count // 2
+    half, share = rows // 2, width // chips
+    row_unit = math.gcd(half, 256)
+    first = max(count // 2, 1)
+    lands = (6, first, half, share) if chips == 4 else (chips - 1, count, half, share)
+
+    def kernel(given, given_small, total, small_total, met, paired, passing, landing, merged,
+               line_passing, line_landing, line_total, own_total, small_met, small_sum,
+               small_plane, small_plane_sum, small_line, send, recv):
+        copies = Copies(send, recv)
+        rank = lax.axis_index("fsdp")
+        place, core, chip, _, sibling = own_place(ctx_count)
+        spans = (pl.ds(0, count), pl.ds(0, first), pl.ds(first, count - first))
+        mine = pl.ds(pl.multiple_of(core * half, row_unit), half)
+        theirs = pl.ds(pl.multiple_of((1 - core) * half, row_unit), half)
+
+        def columns(q):
+            return pl.ds(pl.multiple_of(q * share, 128), share)
+
+        meet(
+            ring_peers("fsdp", count)
+            + ring_peers("ctx", ctx_count, 2)
+            + plane_peers(ctx_count)[:1]
+        )
+        small_pair = copies.make(given_small, small_met, {"ctx": sibling})
+        small_pair.start()
+        exchanged = []
+        for d in range(count):
+            copy = copies.make(given.at[d, theirs], met.at[d], {"ctx": sibling})
+            copy.start()
+            exchanged.append(copy)
+
+        def small_stream():
+            small_pair.wait()
+            small_sum[...] = given_small[...] + small_met[...]
+            pushes = []
+            for step in range(1, chips):
+                copy = copies.make(
+                    small_sum, small_plane.at[step - 1],
+                    {"ctx": lax.rem(place + 2 * step, ctx_count)},
+                )
+                copy.start()
+                pushes.append(copy)
+            yield
+            for copy in pushes:
+                copy.wait()
+            small_plane_sum[...] = small_sum[...] + jnp.sum(small_plane[...], axis=0)
+            pushes = []
+            for step in range(1, count):
+                copy = copies.make(
+                    small_plane_sum, small_line.at[step - 1],
+                    {"fsdp": lax.rem(rank + step, count)},
+                )
+                copy.start()
+                pushes.append(copy)
+            yield
+            yield
+            for copy in pushes:
+                copy.wait()
+            small_total[...] = small_plane_sum[...] + jnp.sum(small_line[...], axis=0)
+
+        def finish(part, value):
+            merged[spans[part]] = value.astype(merged.dtype)
+
+        def large_stream():
+            for d, copy in enumerate(exchanged):
+                copy.wait_recv()
+                for q in range(chips):
+                    paired[q, d] = (
+                        given[d, mine, q * share : (q + 1) * share].astype(jnp.float32)
+                        + met[d, :, q * share : (q + 1) * share].astype(jnp.float32)
+                    ).astype(paired.dtype)
+            yield from plane_reduce(
+                copies, lambda q, part: paired.at[q, spans[part]],
+                passing, landing, ctx_count, finish,
+            )
+            yield from line_reduce(
+                copies, lambda d: merged.at[d], line_passing, line_landing, count, line_total
+            )
+            own_total[...] = line_total[...].astype(own_total.dtype)
+            sent = []
+            forwarded = []
+            copy = copies.make(own_total, total.at[mine, columns(chip)], {"ctx": sibling})
+            copy.start()
+            forwarded.append(copy)
+            for step in range(1, chips):
+                copy = copies.make(
+                    own_total, total.at[mine, columns(chip)],
+                    {"ctx": lax.rem(place + 2 * step, ctx_count)},
+                )
+                copy.start()
+                sent.append(copy)
+            total[mine, columns(chip)] = own_total[...]
+            for step, copy in enumerate(sent, 1):
+                copy.wait_recv()
+                held = total.at[mine, columns(lax.rem(chip + chips - step, chips))]
+                copy = copies.make(held, held, {"ctx": sibling})
+                copy.start()
+                forwarded.append(copy)
+            for copy in sent:
+                copy.wait_send()
+            for copy in forwarded:
+                copy.wait()
+
+        together(small_stream(), large_stream())
+        for copy in exchanged:
+            copy.wait_send()
+
+    kind = parts.dtype
+    f32 = jnp.float32
+    return remote_call(
+        kernel, "totals",
+        [struct((rows, width), kind), struct(small.shape, f32)],
+        [parts, small], [pltpu.VMEM] * 2, [pltpu.VMEM] * 2,
+        [
+            pltpu.VMEM((count, half, width), kind),
+            pltpu.VMEM((chips, count, half, share), kind),
+            pltpu.VMEM((2, first, half, share), kind),
+            pltpu.VMEM(lands, kind),
+            pltpu.VMEM((count, half, share), kind),
+            pltpu.VMEM((2, count - 1, half, share), kind),
+            pltpu.VMEM((2, count - 1, half, share), kind),
+            pltpu.VMEM((half, share), f32),
+            pltpu.VMEM((half, share), kind),
+            pltpu.VMEM(small.shape, f32),
+            pltpu.VMEM(small.shape, f32),
+            pltpu.VMEM((chips - 1,) + small.shape, f32),
+            pltpu.VMEM(small.shape, f32),
+            pltpu.VMEM((count - 1,) + small.shape, f32),
+        ],
+        count + 8 + 3 * count + 4 * chips, parts.size * 8,
+    )
 
 
 def normalize_rows(values, gain_row):
@@ -116,38 +786,39 @@
     capacity = piece_len // 4
     slot_count = experts * capacity
     split_shape = (groups, piece_len, head_count, HEAD_DIM)
-    full_qkv, full_out = (
-        lax.all_gather(w_qkv, "fsdp", axis=0, tiled=True),
-        lax.all_gather(w_out, "fsdp", axis=0, tiled=True),
-    )
+    fsdp_count, ctx_count = lax.axis_size("fsdp"), lax.axis_size("ctx")
+    full_kv = gather_weights(w_qkv[:, model_width:], fsdp_count, ctx_count)
     inputs = tokens.astype(jnp.float32)
     gain_one = gain_attn.astype(jnp.float32)
     gain_two = gain_moe.astype(jnp.float32)
     normed_one, scale_one = normalize_rows(inputs, gain_one)
     normed_one_low = normed_one.astype(jnp.bfloat16)
-    projected = jnp.einsum(
-        "gpd,de->gpe", normed_one_low, full_qkv, preferred_element_type=jnp.float32
-    )
+    projected = jnp.einsum("gpd,de->gpe", normed_one_low, full_kv, preferred_element_type=jnp.float32)
     cosine_table, sine_table = rope_tables(positions, HEAD_DIM)
+    key_local = (
+        rotate(projected[..., :model_width].reshape(split_shape), cosine_table, sine_table)
+        .astype(jnp.bfloat16)
+        .reshape(piece_len, model_width)
+    )
+    value_local = projected[0, :, model_width:].astype(jnp.bfloat16)
+    all_pairs, (full_query, full_out) = gather_keys(
+        jnp.concatenate([key_local, value_local], axis=-1),
+        [w_qkv[:, :model_width], w_out],
+        fsdp_count,
+        ctx_count,
+    )
+    cotangent_low = live_rows.astype(jnp.bfloat16) * cotangent
+    cotangent_own, all_pairs = lax.optimization_barrier((cotangent_low, all_pairs))
+    cotangent_rows = lax.all_gather(cotangent_own, "fsdp", axis=0, tiled=True)
     queries = rotate(
-        projected[..., :model_width].reshape(split_shape), cosine_table, sine_table
+        jnp.einsum(
+            "gpd,de->gpe", normed_one_low, full_query, preferred_element_type=jnp.float32
+        ).reshape(split_shape),
+        cosine_table,
+        sine_table,
     ).astype(jnp.bfloat16)
-    key_local = (
-        rotate(
-            projected[..., model_width : 2 * model_width].reshape(split_shape),
-            cosine_table,
-            sine_table,
-        )
-        .astype(jnp.bfloat16)
-        .reshape(groups, piece_len, model_width)
-    )
-    value_local = projected[..., 2 * model_width :].astype(jnp.bfloat16)
-    key_all, value_all = (
-        lax.all_gather(key_local, "ctx", axis=1, tiled=True),
-        lax.all_gather(value_local, "ctx", axis=1, tiled=True),
-    )
-    key_all = key_all.reshape(groups, slot_len, head_count, HEAD_DIM)
-    value_all = value_all.reshape(groups, slot_len, head_count, HEAD_DIM)
+    key_all = all_pairs[:, :model_width].reshape(groups, slot_len, head_count, HEAD_DIM)
+    value_all = all_pairs[:, model_width:].reshape(groups, slot_len, head_count, HEAD_DIM)
     maxima_list = []
     totals_list = []
     group_index = 0
@@ -193,26 +864,21 @@
     slot_of = jnp.where(is_ffn > 0.5, expert_of * capacity + order_in, -1.0).reshape(
         groups, piece_len, 2
     )
-    slot_hot = slot_of[..., None] == jnp.arange(slot_count, dtype=jnp.float32)
-    slot_gate = jnp.sum(jnp.where(slot_hot, gate_weights[..., None], 0.0), axis=(1, 2))
-    cotangent_low = live_rows.astype(jnp.bfloat16) * cotangent
-    row_pairs = lax.all_gather(
-        jnp.concatenate([routed_low, cotangent_low], axis=-1), "fsdp", axis=0, tiled=True
-    )
-    all_slot_of = lax.all_gather(slot_of, "fsdp", axis=0, tiled=True)
-    all_gate = lax.all_gather(slot_gate, "fsdp", axis=0, tiled=True)
-    peers = row_pairs.shape[0]
+    notes = jnp.concatenate([slot_of[0].T, gate_weights[0].T, jnp.zeros((4, piece_len))], axis=0)
+    routed_rows, all_notes = gather_rows(routed_low[0], notes, fsdp_count)
+    peers = fsdp_count
+    all_slot_of = all_notes[:, :2].swapaxes(1, 2)
+    slot_hot = all_slot_of[..., None] == jnp.arange(slot_count, dtype=jnp.float32)
+    all_gate = jnp.sum(
+        jnp.where(slot_hot, all_notes[:, 2:4].swapaxes(1, 2)[..., None], 0.0), axis=(1, 2)
+    )
     all_hot = (
-        jnp.sum(
-            (all_slot_of[..., None] == jnp.arange(slot_count, dtype=jnp.float32)).astype(
-                jnp.float32
-            ),
-            axis=2,
-        )
+        jnp.sum(slot_hot.astype(jnp.float32), axis=2)
         .astype(jnp.bfloat16)
         .reshape(peers, piece_len, experts, capacity)
     )
     gate_rows = all_gate.reshape(peers, experts, capacity).swapaxes(0, 1)[..., None]
+    row_pairs = jnp.concatenate([routed_rows, cotangent_rows], axis=-1)
     buffers = jnp.einsum(
         "gpec,gpd->egcd", all_hot, row_pairs, preferred_element_type=jnp.float32
     ).astype(jnp.bfloat16)
@@ -242,6 +908,15 @@
     grad_in = (
         apply("ecf,efd->ecd", grad_gate_proj, w_gate) + apply("ecf,efd->ecd", grad_up_proj, w_up)
     ).reshape(expert_out.shape)
+    slot_dot = jnp.sum(block_rows * expert_out, axis=-1).swapaxes(0, 1).reshape(peers, slot_count)
+    route_dot = jnp.sum(jnp.where(slot_hot, slot_dot[:, None, None, :], 0.0), axis=-1)
+    dot_notes = jnp.concatenate(
+        [route_dot.swapaxes(1, 2), jnp.zeros((peers, 6, piece_len), jnp.float32)], axis=1
+    )
+    grad_parts = apply("gpec,egcd->gpd", all_hot, grad_in.astype(jnp.bfloat16)).astype(jnp.bfloat16)
+    out_parts = apply(
+        "gpec,egcd->gpd", all_hot, (gate_rows * expert_out).astype(jnp.bfloat16)
+    ).astype(jnp.bfloat16)
     grad_weights = jnp.stack(
         [
             apply("ecf,ecd->efd", grad_gate_proj, expert_in).astype(jnp.bfloat16),
@@ -250,34 +925,23 @@
         ],
         axis=2,
     )
-    returned = jnp.concatenate([gate_rows * expert_out, grad_in], axis=-1).astype(jnp.bfloat16)
-    token_parts = apply("gpec,egcd->gpd", all_hot, returned).astype(jnp.bfloat16)
-    token_sums = lax.psum_scatter(token_parts, "fsdp", scatter_dimension=0, tiled=True).astype(
-        jnp.float32
-    )
-    ffn_sum, ffn_grad = token_sums[..., :model_width], token_sums[..., model_width:]
-    slot_dot = lax.psum_scatter(
-        jnp.sum(block_rows * expert_out, axis=-1).swapaxes(0, 1).reshape(peers, slot_count),
-        "fsdp",
-        scatter_dimension=0,
-        tiled=True,
-    )
+    grad_weights, grad_parts = lax.optimization_barrier((grad_weights, grad_parts))
+    expert_sum = lax.psum(grad_weights, "ctx").astype(jnp.float32)
+    ffn_grad, dot_sums = reduce_rows(grad_parts, dot_notes, fsdp_count)
+    ffn_grad = ffn_grad[None]
     copy_hot = route_hot[..., experts + 1]
     const_hot = route_hot[..., experts + 2 :]
     constants = const_vec.astype(jnp.float32)
     gate_const = jnp.sum(gate_weights[..., None] * const_hot, axis=2)
     copy_gate = jnp.sum(gate_weights * copy_hot, axis=2, keepdims=True)
-    moe_sum = (
-        ffn_sum
-        + copy_gate * routed
-        + jnp.einsum("gpj,jd->gpd", gate_const, constants, precision=HIGHEST)
-    )
-    output = (live_rows * (residual_sum + moe_sum)).astype(jnp.bfloat16)
+    special_sum = copy_gate * routed + jnp.einsum(
+        "gpj,jd->gpd", gate_const, constants, precision=HIGHEST
+    )
     grad_block = live_rows * cotangent.astype(jnp.float32)
     copy_dot = jnp.sum(grad_block * routed, axis=-1)[..., None]
     const_dot = jnp.einsum("gpd,jd->gpj", grad_block, constants, precision=HIGHEST)
     grad_gate = (
-        jnp.sum(jnp.where(slot_hot, slot_dot[:, None, None, :], 0.0), axis=-1)
+        dot_sums[:2].T[None]
         + copy_hot * copy_dot
         + jnp.sum(const_hot * const_dot[:, :, None, :], axis=-1)
     )
@@ -327,16 +991,17 @@
     query_grads = [jnp.concatenate(query_parts, axis=1)]
     key_grads_list = [jnp.concatenate(key_parts, axis=1)]
     value_grads_list = [jnp.concatenate(value_parts, axis=1)]
-    key_grad_all = jnp.stack(key_grads_list).reshape(groups, slot_len, model_width)
-    value_grad_all = jnp.stack(value_grads_list).reshape(groups, slot_len, model_width)
-    key_grad, value_grad = (
-        lax.psum_scatter(
-            key_grad_all.astype(jnp.bfloat16), "ctx", scatter_dimension=1, tiled=True
-        ).astype(jnp.float32),
-        lax.psum_scatter(
-            value_grad_all.astype(jnp.bfloat16), "ctx", scatter_dimension=1, tiled=True
-        ).astype(jnp.float32),
-    )
+    pair_grads = jnp.concatenate(
+        [
+            key_grads_list[0].reshape(ctx_count, piece_len, model_width),
+            value_grads_list[0].reshape(ctx_count, piece_len, model_width),
+        ],
+        axis=-1,
+    ).astype(jnp.bfloat16)
+    pair_grad, ffn_sum = reduce_keys(pair_grads, out_parts, fsdp_count, ctx_count)
+    output = (live_rows * (residual_sum + special_sum + ffn_sum[None])).astype(jnp.bfloat16)
+    key_grad = pair_grad[None, :, :model_width]
+    value_grad = pair_grad[None, :, model_width:]
     query_back = rotate(jnp.stack(query_grads), cosine_table, -sine_table).reshape(
         groups, piece_len, model_width
     )
@@ -350,26 +1015,35 @@
         "gpd,gpe->de", normed_one_low, grad_projected, preferred_element_type=jnp.float32
     )
     grad_normed_one = jnp.einsum(
-        "gpe,de->gpd", grad_projected, full_qkv, preferred_element_type=jnp.float32
+        "gpe,de->gpd",
+        grad_projected[..., :model_width],
+        full_query,
+        preferred_element_type=jnp.float32,
+    ) + jnp.einsum(
+        "gpe,de->gpd",
+        grad_projected[..., model_width:],
+        full_kv,
+        preferred_element_type=jnp.float32,
     )
     grad_norm_one, grad_gain_one = normalize_back(inputs, scale_one, gain_one, grad_normed_one)
     grad_inputs = grad_residual + grad_norm_one
-    wqkv_part, wout_part = (
-        lax.psum_scatter(
-            grad_wqkv.astype(jnp.bfloat16), "fsdp", scatter_dimension=0, tiled=True
-        ).astype(jnp.float32),
-        lax.psum_scatter(
-            grad_wout.astype(jnp.bfloat16), "fsdp", scatter_dimension=0, tiled=True
-        ).astype(jnp.float32),
-    )
-    wqkv_sum, wout_sum, expert_sum = (
-        lax.psum(wqkv_part.astype(jnp.bfloat16), "ctx").astype(jnp.float32),
-        lax.psum(wout_part.astype(jnp.bfloat16), "ctx").astype(jnp.float32),
-        lax.psum(grad_weights, "ctx").astype(jnp.float32),
-    )
-    gain_one_sum, gain_two_sum, router_sum, mixing_sum, const_sum = lax.psum(
-        (grad_gain_one, grad_gain_two, grad_router, grad_mixing, grad_const), ("ctx", "fsdp")
-    )
+    weight_parts = (
+        jnp.concatenate([grad_wqkv, grad_wout], axis=-1)
+        .astype(jnp.bfloat16)
+        .reshape(fsdp_count, -1, 4 * model_width)
+    )
+    few = experts + 4
+    mixing_row = jnp.pad(grad_mixing.reshape(1, -1), ((0, 0), (0, model_width - few * few)))
+    small = jnp.concatenate(
+        [grad_router.T, grad_const, grad_gain_one[None], grad_gain_two[None], mixing_row], axis=0
+    )
+    small = jnp.pad(small, ((0, -small.shape[0] % 8), (0, 0)))
+    weight_sum, small_sum = reduce_weights(weight_parts, small, fsdp_count, ctx_count)
+    weight_sum = weight_sum.astype(jnp.float32)
+    wqkv_sum, wout_sum = weight_sum[:, : 3 * model_width], weight_sum[:, 3 * model_width :]
+    router_sum, const_sum = small_sum[:few].T, small_sum[few : few + 2]
+    gain_one_sum, gain_two_sum = small_sum[few + 2], small_sum[few + 3]
+    mixing_sum = small_sum[few + 4, : few * few].reshape(few, few)
     return (
         output,
         grad_inputs,

time: 960 us -> 657 us (0.68)
  waiting for transfers between devices: 573 us -> 0.04 us
  Pallas kernels: 0 us -> 271 us
  blocking collectives: 76 us -> 0 us
  local copies, waits for them, and re-layouts: 48.7 us -> 103 us
  other arithmetic: 54.1 us -> 68.2 us
  matrix products: 183 us -> 193 us
    pallas_call x0 -> x6, Pallas kernels: none -> 271 us  [remote_call(): pl.pallas_call(kernel, out_shape=results, in_specs=[pl.BlockSpec(memory_s...]
    psum x1, waiting for transfers between devices: 207 us -> 0.01 us  [per_device(): expert_sum = lax.psum(grad_weights, 'ctx').astype(jnp.float32)]
    reduce_scatter x5 -> x0, waiting for transfers between devices: 198 us -> none  [the longest x1 67.2 us: per_device(): lax.psum_scatter(grad_wqkv.astype(jnp.bfloat16), 'fsdp', scatter_dimensio...]
    all_gather x5 -> x1, waiting for transfers between devices: 167 us -> 0.01 us  [per_device(): cotangent_rows = lax.all_gather(cotangent_own, 'fsdp', axis=0, tiled=True)]
    psum x1 -> x0, blocking collectives: 42.9 us -> none  [per_device(): lax.psum((grad_gain_one, grad_gain_two, grad_router, grad_mixing, grad_co...]
    slice x3 -> x14, local copies, waits for them, and re-layouts: 3.22 us -> 28.7 us  [the longest x2 9.67 us: per_device(): all_pairs[:, :model_width].reshape(groups, slot_len, head_count, HEAD_DIM)]
    all_gather x2 -> x0, blocking collectives: 23.9 us -> none  [the longest x1 12 us: per_device(): all_slot_of = lax.all_gather(slot_of, 'fsdp', axis=0, tiled=True)]
    reshape x1 -> x3, local copies, waits for them, and re-layouts: 0.08 us -> 10.4 us  [the longest x1 5.32 us: per_device(): key_grads_list[0].reshape(ctx_count, piece_len, model_width)]
  transfers between devices with their start and end apart: 11 -> 2, of which waited for: 10 -> 0; matrix products, arithmetic and copies ran while one was open for 13% -> 36% of each run, Pallas kernels for 0% -> 30%
where the time goes in v2:
time: 657 us; the launch traced here: 652 us
  Pallas kernels  271 us (41%)
  matrix products  193 us (29%)
  local copies, waits for them, and re-layouts  103 us (16%)
  other arithmetic  68.2 us (10%)
  between operations  16.4 us (2%)
    pallas_call x6, Pallas kernels, remote_call(): pl.pallas_call(kernel, out_shape=results, in_specs=[pl.BlockSpec(memory_s...  271 us
    dot_general x11, matrix products, apply(): return jnp.einsum(spec, left, right, preferred_element_type=jnp.float32)  55.4 us
    unnamed x218, local copies, waits for them, and re-layouts  43 us
    sub x6, matrix products, attend_forward(): weights = jnp.exp(scores - row_max)  31.3 us
    dot_general x6, matrix products, attend_backward(): jnp.einsum('hqk,qhd->khd', probs_low, grad_out, preferred_element_type=jn...  23.9 us
    dot_general x6, matrix products, attend_forward(): jnp.einsum('hqk,khd->qhd', probabilities, values, preferred_element_type=...  22 us
    dot_general x6, matrix products, attend_backward(): jnp.einsum('qhd,khd->hqk', grad_out, values, preferred_element_type=jnp.f...  18.7 us
    convert_element_type x6, other arithmetic, attend_backward(): (probabilities * (grad_probs - inner_sum)).astype(jnp.bfloat16)  15 us
  transfers between devices with their start and end apart: 2, of which 0 were waited for; matrix products, arithmetic and copies ran while one was open for 36% of the time, Pallas kernels for 30%

profile of v2, /device:TPU:0, one launch (start us, length us, event | category | flops | bytes accessed | tf_op | source)
XLA Modules:
  0.0 652.1 jit_solution(11374529608900318442)
XLA Ops:
  13.3 29.5 %weights.1 = bf16[4,192,1536]{2,1,0:T(8,128)(2,1)} custom-call(bf16[192,1536]{1,0:T(8,128)(2,1)} %slice.202.source), custom_call_target="tpu_custom_call" | custom-call | bytes 4718592 | tf_op jit(solution)/shard_map/weights/pallas_call | solution.py:315
  42.8 2.5 convolution_bitcast_fusion
  49.4 45.5 %keys.1 = (bf16[8,256,1536]{2,1,0:T(8,128)(2,1)}, bf16[4,192,768]{2,1,0:T(8,128)(2,1)}, bf16[4,192,768]{2,1,0:T(8,128)(2,1)}) custom-call(bf16[256,1536]{1,0:T(8,128)(2,1)} %pad_maximum_fusion.3.refs_0_, bf16[192,768]{1,0:T(8,128)(2,1)} %slice.207.refs_1_, bf16[192,768]{1,0:T(8,128)(2,1)} %refs_2_.1), custom_call_target="tpu_custom_call" | custom-call | bytes 12582912 | tf_op jit(solution)/shard_map/keys/pallas_call | solution.py:315
  95.1 4.9 fusion.294
  100.0 4.8 copy.160
  104.8 2.4 copy.159
  111.1 5.2 fusion.307
  116.4 5.4 fusion.295
  121.8 5.3 fusion.298
  127.0 5.3 fusion.301
  132.3 5.3 fusion.304
  145.5 3.2 copy.158
  148.8 4.9 fusion.310
  153.7 3.7 fusion.122
  157.4 3.7 fusion.121
  161.0 3.7 fusion.120
  164.7 3.7 fusion.119
  168.4 3.7 fusion.118
  172.1 3.7 fusion.117
  175.8 2.6 multiply_reduce_fusion.8
  182.7 32.3 %rows.1 = (bf16[4,256,768]{2,1,0:T(8,128)(2,1)}, f32[4,8,256]{2,1,0:T(8,128)}) custom-call(bf16[256,768]{1,0:T(8,128)(2,1)} %bitcast.666, f32[8,256]{1,0:T(8,128)} %maximum_maximum_fusion.own_notes), custom_call_target="tpu_custom_call" | custom-call | bytes 3145728 | tf_op jit(solution)/shard_map/rows/pallas_call | solution.py:315
  220.7 8.0 %fusion.34 = f32[4,1536,512]{1,2,0} fusion(bf16[4,256,512]{2,1,0:T(8,128)(2,1)S(1)} %convert_reduce_fusion, bf16[4,256,768]{2,1,0:T(8,128)(2,1)} %all-gather.2.cloned.1.call-done, bf16[4,256,768]{2,1,0:T(8,128)(2,1)S(1)} %copy-done.49), kind=kOutput, calls=%fused_computation.78 | convolution fusion | flops 1616904192 | bytes 16777216
  228.8 5.5 convert_bitcast_fusion.3
  238.6 6.7 %fusion.10 = f32[8,256,512]{2,1,0:T(8,128)} fusion(bf16[8,256,768]{2,1,0:T(8,128)(2,1)S(1)} %bitcast.630, bf16[8,512,3,768]{3,1,2,0:T(8,128)(2,1)} %param.25), kind=kOutput, calls=%fused_computation.14 | convolution fusion | flops 1610612736 | bytes 13631488 | tf_op jit(solution)/shard_map/ecd,efd->ecf/dot_general | solution.py:895
  245.3 9.5 %multiply_convert_fusion.7 = (bf16[8,256,512]{2,1,0:T(8,128)(2,1)}, f32[8,256,512]{2,1,0:T(8,128)}) fusion(f32[8,256,512]{2,1,0:T(8,128)} %fusion.10, bf16[8,256,768]{2,1,0:T(8,128)(2,1)} %bitcast.631, bf16[8,512,3,768]{3,1,2,0:T(8,128)(2,1)} %param.25), kind=kOutput, calls=%fused_computation.51 | convolution fusion | flops 1616904192 | bytes 19922944 | tf_op jit(solution)/shard_map/ecd,efd->ecf/dot_general | solution.py:895
  254.9 3.4 fusion.16
  258.3 4.9 fusion.7
  264.7 2.5 fusion.6
  270.6 9.6 %multiply_convert_fusion.9 = (bf16[8,256,512]{2,1,0:T(8,128)(2,1)S(1)}, bf16[8,256,512]{2,1,0:T(8,128)(2,1)}) fusion(f32[8,256,512]{2,1,0:T(8,128)} %fusion.10, f32[8,256,512]{2,1,0:T(8,128)} %get-tuple-element.152, bf16[8,256,768]{2,1,0:T(8,128)(2,1)S(1)} %bitcast.641, bf16[8,512,3,768]{3,1,2,0:T(8,128)(2,1)} %param.25), kind=kOutput, calls=%fused_computation.53 | convolution fusion | flops 1624244224 | bytes 22020096 | tf_op jit(solution)/shard_map/ecd,efd->ecf/dot_general | solution.py:895
  281.5 4.7 fusion.8
  286.3 3.5 convert_bitcast_fusion.2
  290.3 6.2 convert_bitcast_fusion.1
  296.5 5.4 add_convert_fusion
  305.4 7.9 %pad_maximum_fusion = bf16[8,512,3,768]{3,1,0,2:T(8,128)(2,1)} fusion(bf16[8,512,1,768]{3,1,0,2:T(8,128)(2,1)S(1)} %convert_bitcast_fusion, bf16[8,512,1,768]{3,1,0,2:T(8,128)(2,1)S(1)} %bitcast.635, bf16[8,512,1,768]{3,1,0,2:T(8,128)(2,1)S(1)} %convert_bitcast_fusion.2), kind=kLoop, calls=%fused_computation.6 | loop fusion | flops 18874368 | bytes 37748736 | tf_op jit(solution)/shard_map/stack | solution.py:920
  313.3 32.7 %row_sums.1 = (f32[256,768]{1,0:T(8,128)}, f32[8,256]{1,0:T(8,128)}) custom-call(bf16[4,256,768]{2,1,0:T(8,128)(2,1)} %bitcast_convert_fusion.1.given, f32[4,8,256]{2,1,0:T(8,128)} %concatenate.91.given_notes), custom_call_target="tpu_custom_call" | custom-call | bytes 3145728 | tf_op jit(solution)/shard_map/row_sums/pallas_call | solution.py:315
  351.1 3.9 fusion.48
  355.0 3.9 fusion.50
  358.8 3.9 fusion.52
  362.7 3.8 fusion.54
  366.6 4.1 fusion.56
  370.7 4.4 fusion.58
  375.0 4.7 copy.198
  379.7 5.0 copy.178
  384.8 5.4 multiply_reduce_fusion.1
  390.2 2.8 multiply_reduce_fusion.2
  393.5 2.9 multiply_reduce_fusion.3
  397.2 2.8 multiply_reduce_fusion.4
  400.5 2.9 multiply_reduce_fusion.5
  403.3 3.0 multiply_convert_fusion.6
  407.7 3.2 multiply_convert_fusion.2
  410.9 3.8 multiply_convert_fusion.3
  414.7 3.7 multiply_convert_fusion.4
  426.0 2.9 copy.197
  428.9 5.3 copy.177
  434.2 6.5 pad_maximum_fusion.1.given
  440.7 2.3 bitcast_convert_fusion.given_rows
  443.0 53.4 %key_sums.1 = (f32[256,1536]{1,0:T(8,128)}, f32[256,768]{1,0:T(8,128)}) custom-call(bf16[8,256,1536]{2,1,0:T(8,128)(2,1)} %pad_maximum_fusion.1.given, bf16[4,256,768]{2,1,0:T(8,128)(2,1)} %bitcast_convert_fusion.given_rows), custom_call_target="tpu_custom_call" | custom-call | bytes 12582912 | tf_op jit(solution)/shard_map/key_sums/pallas_call | solution.py:315
  500.8 2.3 copy.180
  505.1 3.1 fusion.114
  532.0 2.8 pad_maximum_fusion.2.given
  534.9 77.9 %totals.1 = (bf16[192,3072]{1,0:T(8,128)(2,1)}, f32[24,768]{1,0:T(8,128)}) custom-call(bf16[4,192,3072]{2,1,0:T(8,128)(2,1)} %pad_maximum_fusion.2.given, f32[24,768]{1,0:T(8,128)} %pad.10.given_small), custom_call_target="tpu_custom_call" | custom-call | bytes 18874368 | tf_op jit(solution)/shard_map/totals/pallas_call | solution.py:315
  614.8 2.5 slice.306
  620.6 2.5 fusion.100
  624.2 20.8 %copy.187 = f32[8,512,3,768]{3,1,2,0:T(8,128)} copy(bf16[8,512,3,768]{3,1,0,2:T(8,128)(2,1)} %all-reduce.5.cloned.1.call-done) | data formatting | bytes 56623104
  (344 shorter events, 97.8 us)
Async XLA Ops:
  7.2 174.0 %copy-start = (f32[768,12]{0,1:T(8,128)S(1)}, f32[768,12]{0,1:T(8,128)}, u32[]{:S(2)}) copy-start(f32[768,12]{0,1:T(8,128)} %param.22) | copy-start | bytes 110596
  7.2 35.6 %copy-start.29 = (bf16[1,256,768]{2,1,0:T(8,128)(2,1)S(1)}, bf16[1,256,768]{2,1,0:T(8,128)(2,1)}, u32[]{:S(2)}) copy-start(bf16[1,256,768]{2,1,0:T(8,128)(2,1)} %param.13) | copy-start | bytes 1179652
  7.2 213.5 %all-gather.2.cloned.1.call-start = ((), (), s32[]{:S(2)}) async-start(), calls=%async_computation | async-start | bytes 1966080 | tf_op jit(solution)/shard_map/all_gather | solution.py:812
  12.6 94.5 %copy-start.62 = (f32[256]{0:T(256)}, f32[256]{0:T(256)S(1)}, u32[]{:S(2)}) copy-start(f32[256]{0:T(256)S(1)} %get-tuple-element.134) | copy-start | bytes 3076
  13.3 93.8 %copy-start.58 = (f32[768]{0:T(1024)}, f32[768]{0:T(1024)S(1)}, u32[]{:S(2)}) copy-start(f32[768]{0:T(1024)S(1)} %convert_element_type.232) | copy-start | bytes 9220
  47.2 61.9 %copy-start.52 = (f32[256,32]{0,1:T(8,128)}, f32[256,32]{0,1:T(8,128)S(1)}, u32[]{:S(2)}) copy-start(f32[256,32]{0,1:T(8,128)S(1)} %get-tuple-element.132) | copy-start | bytes 98308
  94.9 529.3 %all-reduce.5.cloned.1.call-start = ((), (), s32[]{:S(2)}) async-start(), calls=%async_computation.1 | async-start | bytes 37748736 | tf_op jit(solution)/shard_map/psum | solution.py:929
  132.3 5.3 copy-start.97
  132.3 5.3 copy-start.66
  148.8 4.9 copy-start.22
  153.7 18.4 %copy-start.93 = (f32[2,256]{1,0:T(2,128)}, f32[2,256]{1,0:T(2,128)S(1)}, u32[]{:S(2)}) copy-start(f32[2,256]{1,0:T(2,128)S(1)} %get-tuple-element.147) | copy-start | bytes 6148
  175.7 5.9 copy-start.64
  175.7 5.9 copy-start.74
  175.7 6.1 copy-start.67
  175.7 6.2 copy-start.73
  175.7 6.3 copy-start.77
  175.7 6.2 copy-start.78
  175.8 41.9 %copy-start.37 = (bf16[1,256,768]{2,1,0:T(8,128)(2,1)S(1)}, bf16[1,256,768]{2,1,0:T(8,128)(2,1)}, u32[]{:S(2)}) copy-start(bf16[1,256,768]{2,1,0:T(8,128)(2,1)} %param.17) | copy-start | bytes 1179652
  175.8 41.9 %copy-start.83 = (bf16[2,768]{1,0:T(2,128)(2,1)S(1)}, bf16[2,768]{1,0:T(2,128)(2,1)}, u32[]{:S(2)}) copy-start(bf16[2,768]{1,0:T(2,128)(2,1)} %param.24) | copy-start | bytes 9220
  215.0 5.7 copy-start.49
  218.9 9.8 %copy-start.71 = (f32[256,2]{0,1:T(2,128)}, f32[256,2]{0,1:T(2,128)S(1)}, u32[]{:S(2)}) copy-start(f32[256,2]{0,1:T(2,128)S(1)} %get-tuple-element.105) | copy-start | bytes 6148
  238.6 16.3 %slice-start.2 = ((s8[18874368]{0:T(1024)(128)(4,1)}), s8[4194304]{0:T(1024)(128)(4,1)S(1)}, s32[]{:S(2)}) async-start(s8[18874368]{0:T(1024)(128)(4,1)} %bitcast.628), calls=%async_computation.4 | async-start | bytes 8388608
  238.6 16.3 %slice-start.3 = ((s8[18874368]{0:T(1024)(128)(4,1)}), s8[4194304]{0:T(1024)(128)(4,1)S(1)}, s32[]{:S(2)}) async-start(s8[18874368]{0:T(1024)(128)(4,1)} %bitcast.628), calls=%async_computation.5 | async-start | bytes 8388608
  245.3 9.6 %slice-start.4 = ((s8[18874368]{0:T(1024)(128)(4,1)}), s8[4194304]{0:T(1024)(128)(4,1)S(1)}, s32[]{:S(2)}) async-start(s8[18874368]{0:T(1024)(128)(4,1)} %bitcast.628), calls=%async_computation.6 | async-start | bytes 8388608
  245.3 9.6 %slice-start.5 = ((s8[18874368]{0:T(1024)(128)(4,1)}), s8[4194304]{0:T(1024)(128)(4,1)S(1)}, s32[]{:S(2)}) async-start(s8[18874368]{0:T(1024)(128)(4,1)} %bitcast.628), calls=%async_computation.7 | async-start | bytes 8388608
  245.3 9.6 %slice-start.6 = ((s8[18874368]{0:T(1024)(128)(4,1)}), s8[2097152]{0:T(1024)(128)(4,1)S(1)}, s32[]{:S(2)}) async-start(s8[18874368]{0:T(1024)(128)(4,1)} %bitcast.628), calls=%async_computation.8 | async-start | bytes 4194304
  258.3 4.9 copy-start.2
  296.5 5.5 copy-start.50
  313.3 32.8 %copy-start.76 = (f32[256,2]{0,1:T(2,128)S(1)}, f32[256,2]{0,1:T(2,128)}, u32[]{:S(2)}) copy-start(f32[256,2]{0,1:T(2,128)} %get-tuple-element.104) | copy-start | bytes 6148
  313.3 32.8 %copy-start.82 = (f32[256]{0:T(256)S(1)}, f32[256]{0:T(256)}, u32[]{:S(2)}) copy-start(f32[256]{0:T(256)} %get-tuple-element.110) | copy-start | bytes 3076
  313.3 33.6 %copy-start.8 = (f32[1,256,768]{2,1,0:T(8,128)S(1)}, f32[1,256,768]{2,1,0:T(8,128)}, u32[]{:S(2)}) copy-start(f32[1,256,768]{2,1,0:T(8,128)} %copy-done.7) | copy-start | bytes 2359300
  313.3 33.6 %copy-start.38 = (bf16[1,256,768]{2,1,0:T(8,128)(2,1)S(1)}, bf16[1,256,768]{2,1,0:T(8,128)(2,1)}, u32[]{:S(2)}) copy-start(bf16[1,256,768]{2,1,0:T(8,128)(2,1)} %param.17) | copy-start | bytes 1179652
  313.3 33.6 %copy-start.69 = (f32[256]{0:T(256)S(1)}, f32[256]{0:T(256)}, u32[]{:S(2)}) copy-start(f32[256]{0:T(256)} %copy-done.68) | copy-start | bytes 3076
  313.3 33.6 %copy-start.70 = (f32[256]{0:T(256)S(1)}, f32[256]{0:T(256)}, u32[]{:S(2)}) copy-start(f32[256]{0:T(256)} %fusion.206) | copy-start | bytes 3076
  313.3 35.9 %copy-start.81 = (f32[256]{0:T(256)S(1)}, f32[256]{0:T(256)}, u32[]{:S(2)}) copy-start(f32[256]{0:T(256)} %get-tuple-element.135) | copy-start | bytes 3076
  313.3 37.1 %copy-start.39 = (bf16[4,192,768]{2,1,0:T(8,128)(2,1)S(1)}, bf16[4,192,768]{2,1,0:T(8,128)(2,1)}, u32[]{:S(2)}) copy-start(bf16[4,192,768]{2,1,0:T(8,128)(2,1)} %get-tuple-element.29) | copy-start | bytes 3538948
  384.8 5.4 copy-start.43
  384.8 5.5 copy-start.47
  410.9 10.5 %copy-start.9 = (bf16[2,256,2048]{2,1,0:T(8,128)(2,1)}, bf16[2,256,2048]{2,1,0:T(8,128)(2,1)S(1)}, u32[]{:S(2)}) copy-start(bf16[2,256,2048]{2,1,0:T(8,128)(2,1)S(1)} %multiply_convert_fusion.2) | copy-start | bytes 6291460
  414.7 6.2 copy-start.13
  428.9 11.9 %slice-start = ((s8[6291456]{0:T(1024)(128)(4,1)}), s8[2097152]{0:T(1024)(128)(4,1)S(1)}, s32[]{:S(2)}) async-start(s8[6291456]{0:T(1024)(128)(4,1)} %bitcast.625), calls=%async_computation.2 | async-start | bytes 4194304
  434.2 6.5 %slice-start.1 = ((s8[6291456]{0:T(1024)(128)(4,1)}), s8[4194304]{0:T(1024)(128)(4,1)S(1)}, s32[]{:S(2)}) async-start(s8[6291456]{0:T(1024)(128)(4,1)} %bitcast.625), calls=%async_computation.3 | async-start | bytes 8388608
  434.2 6.5 %copy-start.51 = (bf16[4,256,512]{1,2,0:T(8,128)(2,1)S(1)}, bf16[4,256,512]{1,2,0:T(8,128)(2,1)}, u32[]{:S(2)}) copy-start(bf16[4,256,512]{1,2,0:T(8,128)(2,1)} %copy.165) | copy-start | bytes 3145732
  443.0 57.4 %copy-start.65 = (f32[1,256,12]{1,0,2:T(1,128)S(1)}, f32[1,256,12]{1,0,2:T(1,128)}, u32[]{:S(2)}) copy-start(f32[1,256,12]{1,0,2:T(1,128)} %param.14) | copy-start | bytes 36868
  443.0 60.1 %copy-start.12 = (bf16[2,256,2048]{2,1,0:T(8,128)(2,1)S(1)}, bf16[2,256,2048]{2,1,0:T(8,128)(2,1)}, u32[]{:S(2)}) copy-start(bf16[2,256,2048]{2,1,0:T(8,128)(2,1)} %copy-done.11) | copy-start | bytes 6291460
  503.1 5.1 copy-start.16
  503.2 7.1 %copy-start.14 = (bf16[2,256,2048]{2,1,0:T(8,128)(2,1)S(1)}, bf16[2,256,2048]{2,1,0:T(8,128)(2,1)}, u32[]{:S(2)}) copy-start(bf16[2,256,2048]{2,1,0:T(8,128)(2,1)} %copy-done.13) | copy-start | bytes 6291460
  503.2 7.1 %copy-start.23 = (bf16[2048,768]{0,1:T(8,128)(2,1)S(1)}, bf16[2048,768]{0,1:T(8,128)(2,1)}, u32[]{:S(2)}) copy-start(bf16[2048,768]{0,1:T(8,128)(2,1)} %copy.160) | copy-start | bytes 9437188
  505.1 5.9 copy-start.10
  512.6 12.6 %copy-start.6 = (bf16[4,192,1536]{2,1,0:T(8,128)(2,1)S(1)}, bf16[4,192,1536]{2,1,0:T(8,128)(2,1)}, u32[]{:S(2)}) copy-start(bf16[4,192,1536]{2,1,0:T(8,128)(2,1)} %weights.1) | copy-start | bytes 7077892
  520.0 7.0 %copy-start.59 = (f32[768]{0:T(1024)S(1)}, f32[768]{0:T(1024)}, u32[]{:S(2)}) copy-start(f32[768]{0:T(1024)} %copy-done.58) | copy-start | bytes 9220
  520.0 7.0 %copy-start.63 = (f32[256]{0:T(256)S(1)}, f32[256]{0:T(256)}, u32[]{:S(2)}) copy-start(f32[256]{0:T(256)} %copy-done.62) | copy-start | bytes 3076
  521.9 5.1 copy-start.30
  523.2 5.1 copy-start.79
  534.8 82.4 %copy-start.75 = (f32[12,12]{1,0:T(8,128)S(1)}, f32[12,12]{1,0:T(8,128)}, u32[]{:S(2)}) copy-start(f32[12,12]{1,0:T(8,128)} %param.23) | copy-start | bytes 1732
  534.8 85.7 %copy-start.28 = (bf16[1,256,768]{2,1,0:T(8,128)(2,1)S(1)}, bf16[1,256,768]{2,1,0:T(8,128)(2,1)}, u32[]{:S(2)}) copy-start(bf16[1,256,768]{2,1,0:T(8,128)(2,1)} %copy-done.26) | copy-start | bytes 1179652
  534.8 85.7 %copy-start.72 = (f32[256,2]{0,1:T(2,128)S(1)}, f32[256,2]{0,1:T(2,128)}, u32[]{:S(2)}) copy-start(f32[256,2]{0,1:T(2,128)} %copy-done.71) | copy-start | bytes 6148
  534.8 85.7 %copy-start.84 = (bf16[2,768]{1,0:T(2,128)(2,1)S(1)}, bf16[2,768]{1,0:T(2,128)(2,1)}, u32[]{:S(2)}) copy-start(bf16[2,768]{1,0:T(2,128)(2,1)} %param.24) | copy-start | bytes 9220
  612.7 5.3 copy-start.61
  612.8 10.3 %copy-start.25 = (f32[1,256,768]{2,1,0:T(8,128)S(1)}, f32[1,256,768]{2,1,0:T(8,128)}, u32[]{:S(2)}) copy-start(f32[1,256,768]{2,1,0:T(8,128)} %copy-done.24) | copy-start | bytes 2359300
  612.8 10.3 %copy-start.31 = (bf16[1,256,768]{2,1,0:T(8,128)(2,1)S(1)}, bf16[1,256,768]{2,1,0:T(8,128)(2,1)}, u32[]{:S(2)}) copy-start(bf16[1,256,768]{2,1,0:T(8,128)(2,1)} %param.13) | copy-start | bytes 1179652
  612.8 10.3 %copy-start.35 = (f32[256,768]{1,0:T(8,128)S(1)}, f32[256,768]{1,0:T(8,128)}, u32[]{:S(2)}) copy-start(f32[256,768]{1,0:T(8,128)} %copy-done.34) | copy-start | bytes 2359300
  612.8 10.3 %copy-start.80 = (f32[256]{0:T(256)S(1)}, f32[256]{0:T(256)}, u32[]{:S(2)}) copy-start(f32[256]{0:T(256)} %get-tuple-element.133) | copy-start | bytes 3076
  624.2 20.8 %copy-start.1 = (f32[768,12]{0,1:T(8,128)S(1)}, f32[768,12]{0,1:T(8,128)}, u32[]{:S(2)}) copy-start(f32[768,12]{0,1:T(8,128)} %param.22) | copy-start | bytes 110596
  (45 other events, 136.1 us)
Sparse Core Ops, SparseCore 0:
  95.0 35.2 all-gather.1
  313.4 275.2 all-reduce.4

commit v3 on v2

--- a/solution.py
+++ b/solution.py
@@ -489,32 +489,35 @@
 
 
 def reduce_keys(parts, row_parts, count, ctx_count):
-    _, rows, width = parts.shape
+    _, _, rows, width = parts.shape
     chips = ctx_count // 2
-    half = rows // 2
-    lands = (6, half, width) if chips == 4 else (chips - 1, rows, width)
+    lands = (6, 1, rows, width) if chips == 4 else (chips - 1, 2, rows, width)
 
     def kernel(given, given_rows, total, rows_total, met, paired, passing, landing,
                row_passing, row_landing, send, recv):
         copies = Copies(send, recv)
         _, core, _, _, sibling = own_place(ctx_count)
-        spans = (pl.ds(0, rows), pl.ds(0, half), pl.ds(half, half))
+        spans = (pl.ds(0, 2), pl.ds(0, 1), pl.ds(1, 1))
         meet(ring_peers("fsdp", count) + plane_peers(ctx_count))
         exchanged = []
         for q in range(chips):
-            copy = copies.make(given.at[2 * q + 1 - core], met.at[q], {"ctx": sibling})
-            copy.start()
-            exchanged.append(copy)
+            for kind in range(2):
+                copy = copies.make(
+                    given.at[kind, 2 * q + 1 - core], met.at[q, kind], {"ctx": sibling}
+                )
+                copy.start()
+                exchanged.append((q, kind, copy))
 
         def finish(part, value):
-            total[spans[part], :] = value
+            total[spans[part]] = value
 
         def planes():
             yield
-            for q, copy in enumerate(exchanged):
+            for q, kind, copy in exchanged:
                 copy.wait_recv()
-                paired[q] = (
-                    given[2 * q + core].astype(jnp.float32) + met[q].astype(jnp.float32)
+                paired[q, kind] = (
+                    given[kind, 2 * q + core].astype(jnp.float32)
+                    + met[q, kind].astype(jnp.float32)
                 ).astype(paired.dtype)
             yield from plane_reduce(
                 copies, lambda q, part: paired.at[q, spans[part]],
@@ -527,23 +530,23 @@
                 copies, lambda d: given_rows.at[d], row_passing, row_landing, count, rows_total
             ),
         )
-        for copy in exchanged:
+        for _, _, copy in exchanged:
             copy.wait_send()
 
     _, row_count, row_width = row_parts.shape
     return remote_call(
         kernel, "key_sums",
-        [struct((rows, width), jnp.float32), struct((row_count, row_width), jnp.float32)],
+        [struct((2, rows, width), jnp.float32), struct((row_count, row_width), jnp.float32)],
         [parts, row_parts], [pltpu.VMEM] * 2, [pltpu.VMEM] * 2,
         [
-            pltpu.VMEM((chips, rows, width), parts.dtype),
-            pltpu.VMEM((chips, rows, width), parts.dtype),
-            pltpu.VMEM((2, half, width), parts.dtype),
+            pltpu.VMEM((chips, 2, rows, width), parts.dtype),
+            pltpu.VMEM((chips, 2, rows, width), parts.dtype),
+            pltpu.VMEM((2, 1, rows, width), parts.dtype),
             pltpu.VMEM(lands, parts.dtype),
             pltpu.VMEM((2, count - 1, row_count, row_width), parts.dtype),
             pltpu.VMEM((2, count - 1, row_count, row_width), parts.dtype),
         ],
-        2 * chips + 8 + 2 * count, ctx_count * rows * width * 4,
+        3 * chips + 8 + 2 * count, ctx_count * rows * width * 8,
     )
 
 
@@ -683,6 +686,250 @@
     )
 
 
+def local_call(kernel, name, grid, results, operands, in_specs, out_specs, scratch, flops, cost):
+    return pl.pallas_call(
+        kernel,
+        grid=grid,
+        out_shape=results,
+        in_specs=in_specs,
+        out_specs=out_specs,
+        scratch_shapes=scratch,
+        compiler_params=pltpu.CompilerParams(vmem_limit_bytes=VMEM_LIMIT),
+        cost_estimate=pl.CostEstimate(flops=flops, bytes_accessed=cost, transcendentals=0),
+        name=name,
+    )(*operands)
+
+
+def whole_block(shape):
+    return pl.BlockSpec(shape, lambda *_: (0,) * len(shape))
+
+
+def product(left, right, left_dim=1, right_dim=0):
+    return lax.dot_general(
+        left, right, (((left_dim,), (right_dim,)), ((), ())), preferred_element_type=jnp.float32
+    )
+
+
+def expert_layers(routed_rows, block_rows, notes, weights):
+    peers, piece_len, width = routed_rows.shape
+    experts, _, units, _ = weights.shape
+    capacity = piece_len // 4
+    count = peers * capacity
+
+    def kernel(routed, block, note, w, grads, out_parts, grad_parts, dots, out_sum, grad_sum):
+        expert = pl.program_id(0)
+        low = jnp.bfloat16
+
+        @pl.when(expert == 0)
+        def _():
+            out_sum[...] = jnp.zeros_like(out_sum)
+            grad_sum[...] = jnp.zeros_like(grad_sum)
+            dots[...] = jnp.zeros_like(dots)
+
+        slots = (
+            lax.broadcasted_iota(jnp.int32, (capacity, piece_len), 0) + expert * capacity
+        ).astype(jnp.float32)
+        hots, firsts, seconds, gates, taken, blocks = [], [], [], [], [], []
+        for g in range(peers):
+            first = note[g, 0:1, :] == slots
+            second = note[g, 1:2, :] == slots
+            gates.append(
+                jnp.sum(
+                    jnp.where(first, note[g, 2:3, :], 0.0)
+                    + jnp.where(second, note[g, 3:4, :], 0.0),
+                    axis=1,
+                    keepdims=True,
+                )
+            )
+            first, second = jnp.where(first, 1.0, 0.0), jnp.where(second, 1.0, 0.0)
+            hot = (first + second).astype(low)
+            taken.append(product(hot, routed[g]).astype(low))
+            blocks.append(product(hot, block[g]))
+            hots.append(hot)
+            firsts.append(first)
+            seconds.append(second)
+        rows = jnp.concatenate(taken, axis=0)
+        block_part = jnp.concatenate(blocks, axis=0)
+        gate = jnp.concatenate(gates, axis=0)
+        grad_out = (gate * block_part).astype(low)
+        w_gate, w_up, w_down = w[0, 0], w[0, 1], w[0, 2]
+        gate_proj = product(rows, w_gate, 1, 1)
+        up_proj = product(rows, w_up, 1, 1)
+        grad_hidden = product(grad_out, w_down, 1, 1)
+        sigmoid = 1.0 / (1.0 + jnp.exp(-gate_proj))
+        silu = gate_proj * sigmoid
+        hidden = (silu * up_proj).astype(low)
+        grad_gate_proj = (
+            grad_hidden * up_proj * sigmoid * (1.0 + gate_proj * (1.0 - sigmoid))
+        ).astype(low)
+        grad_up_proj = (grad_hidden * silu).astype(low)
+        grads[0, 0] = product(grad_gate_proj, rows, 0, 0).astype(low)
+        grads[0, 1] = product(grad_up_proj, rows, 0, 0).astype(low)
+        grads[0, 2] = product(hidden, grad_out, 0, 0).astype(low)
+        expert_out = product(hidden, w_down)
+        grad_in = (product(grad_gate_proj, w_gate) + product(grad_up_proj, w_up)).astype(low)
+        row_dots = jnp.sum(block_part * expert_out, axis=1, keepdims=True)
+        gated = (gate * expert_out).astype(low)
+        for g in range(peers):
+            span = slice(g * capacity, (g + 1) * capacity)
+            out_sum[g] += product(hots[g], gated[span], 0, 0)
+            grad_sum[g] += product(hots[g], grad_in[span], 0, 0)
+            dots[g, 0:1, :] += jnp.sum(firsts[g] * row_dots[span], axis=0, keepdims=True)
+            dots[g, 1:2, :] += jnp.sum(seconds[g] * row_dots[span], axis=0, keepdims=True)
+
+        @pl.when(expert == experts - 1)
+        def _():
+            out_parts[...] = out_sum[...].astype(low)
+            grad_parts[...] = grad_sum[...].astype(low)
+
+    rows_shape = (peers, piece_len, width)
+    low = jnp.bfloat16
+    expert_block = pl.BlockSpec((1, 3, units, width), lambda e: (e, 0, 0, 0))
+    return local_call(
+        kernel, "experts", (experts,),
+        [struct(weights.shape, low), struct(rows_shape, low), struct(rows_shape, low),
+         struct(notes.shape, jnp.float32)],
+        [routed_rows, block_rows, notes, weights],
+        [whole_block(rows_shape), whole_block(rows_shape), whole_block(notes.shape), expert_block],
+        [expert_block, whole_block(rows_shape), whole_block(rows_shape), whole_block(notes.shape)],
+        [pltpu.VMEM(rows_shape, jnp.float32), pltpu.VMEM(rows_shape, jnp.float32)],
+        18 * experts * count * units * width, 4 * weights.size,
+    )
+
+
+def score_bias(length, first_row, rows, keys):
+    key_place = lax.broadcasted_iota(jnp.int32, (keys, rows), 0)
+    query_place = first_row + lax.broadcasted_iota(jnp.int32, (keys, rows), 1)
+    return jnp.where(key_place <= jnp.minimum(query_place, length - 1), 0.0, MASKED)
+
+
+def head_masks(shape):
+    lane = lax.broadcasted_iota(jnp.int32, shape, 1)
+    return [lane < HEAD_DIM, lane >= HEAD_DIM]
+
+
+def attention_forward(places, queries, pairs):
+    rows, width = queries.shape
+    keys = pairs.shape[0]
+    tile = 2 * HEAD_DIM
+    tiles = width // tile
+
+    def kernel(place, query, key, value, mixed, sums, bias):
+        step = pl.program_id(0)
+
+        @pl.when(step == 0)
+        def _():
+            bias[...] = score_bias(place[0], place[1], rows, keys)
+
+        own_masks = head_masks((rows, tile))
+        scaled = query[...] * HEAD_DIM**-0.5
+        outs = []
+        for head in range(2):
+            chosen = jnp.where(own_masks[head], scaled, 0)
+            scores = product(key[...], chosen, 1, 1) + bias[...]
+            top = jnp.max(scores, axis=0, keepdims=True)
+            weights = jnp.exp(scores - top)
+            total = jnp.sum(weights, axis=0, keepdims=True)
+            probabilities = (weights * (1.0 / total)).astype(jnp.bfloat16)
+            outs.append(product(probabilities, value[...], 0, 0))
+            sums[0, head : head + 1, :] = top + jnp.log(total)
+        mixed[...] = jnp.where(own_masks[0], outs[0], outs[1]).astype(mixed.dtype)
+
+    return pl.pallas_call(
+        kernel,
+        grid_spec=pltpu.PrefetchScalarGridSpec(
+            num_scalar_prefetch=1,
+            grid=(tiles,),
+            in_specs=[
+                pl.BlockSpec((rows, tile), lambda i, _: (0, i)),
+                pl.BlockSpec((keys, tile), lambda i, _: (0, i)),
+                pl.BlockSpec((keys, tile), lambda i, _: (0, i + tiles)),
+            ],
+            out_specs=[
+                pl.BlockSpec((rows, tile), lambda i, _: (0, i)),
+                pl.BlockSpec((1, 8, rows), lambda i, _: (i, 0, 0)),
+            ],
+            scratch_shapes=[pltpu.VMEM((keys, rows), jnp.float32)],
+        ),
+        out_shape=[struct((rows, width), jnp.bfloat16), struct((tiles, 8, rows), jnp.float32)],
+        compiler_params=pltpu.CompilerParams(vmem_limit_bytes=VMEM_LIMIT),
+        cost_estimate=pl.CostEstimate(
+            flops=4 * rows * keys * width, bytes_accessed=pairs.size * 2, transcendentals=0
+        ),
+        name="attention",
+    )(places, queries, pairs, pairs)
+
+
+def attention_backward(places, queries, pairs, sums, mixed, grad_mixed):
+    rows, width = queries.shape
+    keys = pairs.shape[0]
+    tile = 2 * HEAD_DIM
+    tiles = width // tile
+    scaling = HEAD_DIM**-0.5
+
+    def kernel(place, query, key, value, total, out, grad_out, grad_query, grad_pair, bias):
+        step = pl.program_id(0)
+
+        @pl.when(step == 0)
+        def _():
+            bias[...] = score_bias(place[0], place[1], rows, keys)
+
+        own_masks = head_masks((rows, tile))
+        scaled = query[...] * scaling
+        inner = out[...].astype(jnp.float32) * grad_out[...].astype(jnp.float32)
+        grads, key_sum, value_sum = [], None, None
+        for head in range(2):
+            chosen = jnp.where(own_masks[head], scaled, 0)
+            upstream = jnp.where(own_masks[head], grad_out[...], 0)
+            ones = jnp.where(own_masks[head][:8], 1.0, 0.0)
+            inner_row = lax.dot_general(
+                ones, inner, (((1,), (1,)), ((), ())),
+                precision=HIGHEST, preferred_element_type=jnp.float32,
+            )[0:1]
+            scores = product(key[...], chosen, 1, 1) + bias[...]
+            probabilities = jnp.exp(scores - total[0, head : head + 1, :])
+            grad_probs = product(value[...], upstream, 1, 1)
+            grad_scores = (probabilities * (grad_probs - inner_row)).astype(jnp.bfloat16)
+            key_part = product(grad_scores, chosen)
+            value_part = product(probabilities.astype(jnp.bfloat16), upstream)
+            key_sum = key_part if key_sum is None else key_sum + key_part
+            value_sum = value_part if value_sum is None else value_sum + value_part
+            grads.append(product(grad_scores, key[...], 0, 0) * scaling)
+        grad_query[...] = jnp.where(own_masks[0], grads[0], grads[1])
+        grad_pair[0] = key_sum.astype(grad_pair.dtype)
+        grad_pair[1] = value_sum.astype(grad_pair.dtype)
+
+    own_block = pl.BlockSpec((rows, tile), lambda i, _: (0, i))
+    key_block = pl.BlockSpec((keys, tile), lambda i, _: (0, i))
+    low = jnp.bfloat16
+    return pl.pallas_call(
+        kernel,
+        grid_spec=pltpu.PrefetchScalarGridSpec(
+            num_scalar_prefetch=1,
+            grid=(tiles,),
+            in_specs=[
+                own_block,
+                key_block,
+                pl.BlockSpec((keys, tile), lambda i, _: (0, i + tiles)),
+                pl.BlockSpec((1, 8, rows), lambda i, _: (i, 0, 0)),
+                own_block,
+                own_block,
+            ],
+            out_specs=[own_block, pl.BlockSpec((2, keys, tile), lambda i, _: (0, 0, i))],
+            scratch_shapes=[pltpu.VMEM((keys, rows), jnp.float32)],
+        ),
+        out_shape=[
+            struct((rows, width), jnp.float32),
+            struct((2, keys, width), low),
+        ],
+        compiler_params=pltpu.CompilerParams(vmem_limit_bytes=VMEM_LIMIT),
+        cost_estimate=pl.CostEstimate(
+            flops=10 * rows * keys * width, bytes_accessed=pairs.size * 4, transcendentals=0
+        ),
+        name="attention_back",
+    )(places, queries, pairs, pairs, sums, mixed, grad_mixed)
+
+
 def normalize_rows(values, gain_row):
     scaling = lax.rsqrt(jnp.mean(values * values, axis=-1, keepdims=True) + EPSILON)
     return (values * scaling * gain_row, scaling)
@@ -717,46 +964,6 @@
         ],
         axis=-1,
     )
-
-
-def masked_scores(queries, key_rows, allowed):
-    scaling = queries.shape[-1] ** (-0.5)
-    scores = (
-        jnp.einsum("qhd,khd->hqk", queries, key_rows, preferred_element_type=jnp.float32) * scaling
-    )
-    return jnp.where(allowed[None], scores, MASKED)
-
-
-def attend_forward(queries, key_rows, values, allowed):
-    scores = masked_scores(queries, key_rows, allowed)
-    row_max = jnp.max(scores, axis=-1, keepdims=True)
-    weights = jnp.exp(scores - row_max)
-    row_total = jnp.sum(weights, axis=-1, keepdims=True)
-    probabilities = (weights / row_total).astype(jnp.bfloat16)
-    attended = jnp.einsum("hqk,khd->qhd", probabilities, values, preferred_element_type=jnp.float32)
-    return (attended, row_max, row_total)
-
-
-def attend_backward(queries, key_rows, values, allowed, row_max, row_total, grad_out):
-    scaling = queries.shape[-1] ** (-0.5)
-    scores = masked_scores(queries, key_rows, allowed)
-    probabilities = jnp.exp(scores - row_max) / row_total
-    probs_low = probabilities.astype(jnp.bfloat16)
-    grad_probs = jnp.einsum("qhd,khd->hqk", grad_out, values, preferred_element_type=jnp.float32)
-    inner_sum = jnp.sum(probabilities * grad_probs, axis=-1, keepdims=True)
-    grad_scores = (probabilities * (grad_probs - inner_sum)).astype(jnp.bfloat16)
-    grad_queries = (
-        jnp.einsum("hqk,khd->qhd", grad_scores, key_rows, preferred_element_type=jnp.float32)
-        * scaling
-    )
-    grad_keys = (
-        jnp.einsum("hqk,qhd->khd", grad_scores, queries, preferred_element_type=jnp.float32)
-        * scaling
-    )
-    grad_values = jnp.einsum(
-        "hqk,qhd->khd", probs_low, grad_out, preferred_element_type=jnp.float32
-    )
-    return (grad_queries, grad_keys, grad_values)
 
 
 def per_device(
@@ -817,32 +1024,10 @@
         cosine_table,
         sine_table,
     ).astype(jnp.bfloat16)
-    key_all = all_pairs[:, :model_width].reshape(groups, slot_len, head_count, HEAD_DIM)
-    value_all = all_pairs[:, model_width:].reshape(groups, slot_len, head_count, HEAD_DIM)
-    maxima_list = []
-    totals_list = []
-    group_index = 0
-    allowed = (key_positions[None, :] <= positions[:, None]) & (
-        key_positions[None, :] < lengths[group_index]
-    )
-    mask_list = [allowed]
-    head_parts = []
-    for part_index in range(part_count):
-        first_head = part_index * part_heads
-        last_head = first_head + part_heads
-        attended, row_max, row_total = attend_forward(
-            queries[group_index, :, first_head:last_head],
-            key_all[group_index, :, first_head:last_head],
-            value_all[group_index, :, first_head:last_head],
-            allowed,
-        )
-        head_parts.append(attended)
-        maxima_list.append(row_max)
-        totals_list.append(row_total)
-    attended_list = [jnp.concatenate(head_parts, axis=1)]
-    mixed_low = (
-        jnp.stack(attended_list).reshape(groups, piece_len, model_width).astype(jnp.bfloat16)
-    )
+    places = jnp.stack([lengths[0], lax.axis_index("ctx") * piece_len]).astype(jnp.int32)
+    query_rows = queries.reshape(piece_len, model_width)
+    mixed_rows, score_sums = attention_forward(places, query_rows, all_pairs)
+    mixed_low = mixed_rows[None]
     attention = jnp.einsum("gpd,de->gpe", mixed_low, full_out, preferred_element_type=jnp.float32)
     residual_sum = inputs + attention
     normed_two, scale_two = normalize_rows(residual_sum, gain_two)
@@ -866,67 +1051,10 @@
     )
     notes = jnp.concatenate([slot_of[0].T, gate_weights[0].T, jnp.zeros((4, piece_len))], axis=0)
     routed_rows, all_notes = gather_rows(routed_low[0], notes, fsdp_count)
-    peers = fsdp_count
-    all_slot_of = all_notes[:, :2].swapaxes(1, 2)
-    slot_hot = all_slot_of[..., None] == jnp.arange(slot_count, dtype=jnp.float32)
-    all_gate = jnp.sum(
-        jnp.where(slot_hot, all_notes[:, 2:4].swapaxes(1, 2)[..., None], 0.0), axis=(1, 2)
-    )
-    all_hot = (
-        jnp.sum(slot_hot.astype(jnp.float32), axis=2)
-        .astype(jnp.bfloat16)
-        .reshape(peers, piece_len, experts, capacity)
-    )
-    gate_rows = all_gate.reshape(peers, experts, capacity).swapaxes(0, 1)[..., None]
-    row_pairs = jnp.concatenate([routed_rows, cotangent_rows], axis=-1)
-    buffers = jnp.einsum(
-        "gpec,gpd->egcd", all_hot, row_pairs, preferred_element_type=jnp.float32
-    ).astype(jnp.bfloat16)
-    expert_in = buffers[..., :model_width].reshape(experts, peers * capacity, model_width)
-    block_rows = buffers[..., model_width:].astype(jnp.float32)
-    grad_out = (
-        (gate_rows * block_rows)
-        .astype(jnp.bfloat16)
-        .reshape(experts, peers * capacity, model_width)
-    )
-    w_gate, w_up, w_down = w_expert[:, :, 0], w_expert[:, :, 1], w_expert[:, :, 2]
-
-    def apply(spec, left, right):
-        return jnp.einsum(spec, left, right, preferred_element_type=jnp.float32)
-
-    gate_proj = apply("ecd,efd->ecf", expert_in, w_gate)
-    up_proj = apply("ecd,efd->ecf", expert_in, w_up)
-    sigmoid_gate = jax.nn.sigmoid(gate_proj)
-    silu_gate = gate_proj * sigmoid_gate
-    hidden = (silu_gate * up_proj).astype(jnp.bfloat16)
-    expert_out = apply("ecf,efd->ecd", hidden, w_down).reshape(buffers.shape[:3] + (model_width,))
-    grad_hidden = apply("ecd,efd->ecf", grad_out, w_down)
-    grad_gate_proj = (
-        grad_hidden * up_proj * sigmoid_gate * (1.0 + gate_proj * (1.0 - sigmoid_gate))
-    ).astype(jnp.bfloat16)
-    grad_up_proj = (grad_hidden * silu_gate).astype(jnp.bfloat16)
-    grad_in = (
-        apply("ecf,efd->ecd", grad_gate_proj, w_gate) + apply("ecf,efd->ecd", grad_up_proj, w_up)
-    ).reshape(expert_out.shape)
-    slot_dot = jnp.sum(block_rows * expert_out, axis=-1).swapaxes(0, 1).reshape(peers, slot_count)
-    route_dot = jnp.sum(jnp.where(slot_hot, slot_dot[:, None, None, :], 0.0), axis=-1)
-    dot_notes = jnp.concatenate(
-        [route_dot.swapaxes(1, 2), jnp.zeros((peers, 6, piece_len), jnp.float32)], axis=1
-    )
-    grad_parts = apply("gpec,egcd->gpd", all_hot, grad_in.astype(jnp.bfloat16)).astype(jnp.bfloat16)
-    out_parts = apply(
-        "gpec,egcd->gpd", all_hot, (gate_rows * expert_out).astype(jnp.bfloat16)
-    ).astype(jnp.bfloat16)
-    grad_weights = jnp.stack(
-        [
-            apply("ecf,ecd->efd", grad_gate_proj, expert_in).astype(jnp.bfloat16),
-            apply("ecf,ecd->efd", grad_up_proj, expert_in).astype(jnp.bfloat16),
-            apply("ecf,ecd->efd", hidden, grad_out).astype(jnp.bfloat16),
-        ],
-        axis=2,
-    )
-    grad_weights, grad_parts = lax.optimization_barrier((grad_weights, grad_parts))
-    expert_sum = lax.psum(grad_weights, "ctx").astype(jnp.float32)
+    grad_weights, out_parts, grad_parts, dot_notes = expert_layers(
+        routed_rows, cotangent_rows, all_notes, w_expert.swapaxes(1, 2)
+    )
+    expert_sum = lax.psum(grad_weights, "ctx").astype(jnp.float32).swapaxes(1, 2)
     ffn_grad, dot_sums = reduce_rows(grad_parts, dot_notes, fsdp_count)
     ffn_grad = ffn_grad[None]
     copy_hot = route_hot[..., experts + 1]
@@ -964,45 +1092,17 @@
     grad_wout = jnp.einsum(
         "gpd,gpe->de", mixed_low, grad_attention, preferred_element_type=jnp.float32
     )
-    grad_mixed = (
-        jnp.einsum("gpe,de->gpd", grad_attention, full_out, preferred_element_type=jnp.float32)
-        .astype(jnp.bfloat16)
-        .reshape(split_shape)
-    )
-    group_index = 0
-    query_parts = []
-    key_parts = []
-    value_parts = []
-    for part_index in range(part_count):
-        first_head = part_index * part_heads
-        last_head = first_head + part_heads
-        grad_query, grad_key, grad_value = attend_backward(
-            queries[group_index, :, first_head:last_head],
-            key_all[group_index, :, first_head:last_head],
-            value_all[group_index, :, first_head:last_head],
-            mask_list[group_index],
-            maxima_list[part_count * group_index + part_index],
-            totals_list[part_count * group_index + part_index],
-            grad_mixed[group_index, :, first_head:last_head],
-        )
-        query_parts.append(grad_query)
-        key_parts.append(grad_key)
-        value_parts.append(grad_value)
-    query_grads = [jnp.concatenate(query_parts, axis=1)]
-    key_grads_list = [jnp.concatenate(key_parts, axis=1)]
-    value_grads_list = [jnp.concatenate(value_parts, axis=1)]
-    pair_grads = jnp.concatenate(
-        [
-            key_grads_list[0].reshape(ctx_count, piece_len, model_width),
-            value_grads_list[0].reshape(ctx_count, piece_len, model_width),
-        ],
-        axis=-1,
+    grad_mixed = jnp.einsum(
+        "gpe,de->gpd", grad_attention, full_out, preferred_element_type=jnp.float32
     ).astype(jnp.bfloat16)
+    query_grad, pair_grads = attention_backward(
+        places, query_rows, all_pairs, score_sums, mixed_rows, grad_mixed[0]
+    )
+    pair_grads = pair_grads.reshape(2, ctx_count, piece_len, model_width)
     pair_grad, ffn_sum = reduce_keys(pair_grads, out_parts, fsdp_count, ctx_count)
     output = (live_rows * (residual_sum + special_sum + ffn_sum[None])).astype(jnp.bfloat16)
-    key_grad = pair_grad[None, :, :model_width]
-    value_grad = pair_grad[None, :, model_width:]
-    query_back = rotate(jnp.stack(query_grads), cosine_table, -sine_table).reshape(
+    key_grad, value_grad = pair_grad[:1], pair_grad[1:]
+    query_back = rotate(query_grad.reshape(split_shape), cosine_table, -sine_table).reshape(
         groups, piece_len, model_width
     )
     key_back = rotate(key_grad.reshape(split_shape), cosine_table, -sine_table).reshape(

time: 657 us -> 508 us (0.77)
  matrix products: 193 us -> 18.7 us
  Pallas kernels: 271 us -> 362 us
  local copies, waits for them, and re-layouts: 103 us -> 29.1 us
  waiting for transfers between devices: 0.04 us -> 49.2 us
  other arithmetic: 68.2 us -> 33 us
    dot_general x41 -> x0, matrix products: 132 us -> none  [the longest x11 55.4 us: apply(): return jnp.einsum(spec, left, right, preferred_element_type=jnp.float32)]
    pallas_call x0 -> x3, Pallas kernels: none -> 83.6 us  [the longest x1 36.1 us: local_call(): pl.pallas_call(kernel, grid=grid, out_shape=results, in_specs=in_specs, o...]
    psum x1, waiting for transfers between devices: 0.01 us -> 49.2 us  [per_device(): lax.psum(grad_weights, 'ctx').astype(jnp.float32).swapaxes(1, 2)]
    unnamed x218 -> x63, local copies, waits for them, and re-layouts: 43 us -> 4.03 us
    sub x6 -> x0, matrix products: 31.3 us -> none  [attend_forward(): weights = jnp.exp(scores - row_max)]
    convert_element_type x8 -> x1, other arithmetic: 23 us -> 0.01 us  [rope_tables(): angles = positions.astype(jnp.float32)[:, None] * frequency[None, :]]
    transpose x0 -> x1, other arithmetic: none -> 20.8 us  [per_device(): lax.psum(grad_weights, 'ctx').astype(jnp.float32).swapaxes(1, 2)]
    slice x9 -> x4, local copies, waits for them, and re-layouts: 19.8 us -> 3.71 us  [the longest x3 3.55 us: per_device(): key_grad, value_grad = (pair_grad[:1], pair_grad[1:])]
  transfers between devices with their start and end apart: 2 -> 2, of which waited for: 0 -> 1; matrix products, arithmetic and copies ran while one was open for 36% -> 9% of each run, Pallas kernels for 30% -> 49%
where the time goes in v3:
time: 508 us; the launch traced here: 507 us
  Pallas kernels  362 us (71%)
  waiting for transfers between devices  49.2 us (10%)
  other arithmetic  33 us (6%)
  local copies, waits for them, and re-layouts  29.1 us (6%)
  matrix products  18.7 us (4%)
  between operations  15.3 us (3%)
    pallas_call x6, Pallas kernels, remote_call(): pl.pallas_call(kernel, out_shape=results, in_specs=[pl.BlockSpec(memory_s...  278 us
    psum x1, waiting for transfers between devices, per_device(): lax.psum(grad_weights, 'ctx').astype(jnp.float32).swapaxes(1, 2)  49.2 us
    pallas_call x1, Pallas kernels, local_call(): pl.pallas_call(kernel, grid=grid, out_shape=results, in_specs=in_specs, o...  36.1 us
    pallas_call x1, Pallas kernels, attention_forward(): pl.pallas_call(kernel, grid_spec=pltpu.PrefetchScalarGridSpec(num_scalar_...  25.4 us
    pallas_call x1, Pallas kernels, attention_backward(): pl.pallas_call(kernel, grid_spec=pltpu.PrefetchScalarGridSpec(num_scalar_...  22 us
    transpose x1, other arithmetic, per_device(): lax.psum(grad_weights, 'ctx').astype(jnp.float32).swapaxes(1, 2)  20.8 us
  transfers between devices with their start and end apart: 2, of which 1 were waited for; matrix products, arithmetic and copies ran while one was open for 9% of the time, Pallas kernels for 49%

profile of v3, /device:TPU:0, one launch (start us, length us, event | category | flops | bytes accessed | tf_op | source)
XLA Modules:
  0.0 507.0 jit_solution(12753272567408517021)
XLA Ops:
  7.3 1.8 slice.90.refs_1_
  9.0 1.9 slice.85.source
  11.1 29.5 %weights.1 = bf16[4,192,1536]{2,1,0:T(8,128)(2,1)} custom-call(bf16[192,1536]{1,0:T(8,128)(2,1)} %slice.85.source), custom_call_target="tpu_custom_call" | custom-call | bytes 4718592 | tf_op jit(solution)/shard_map/weights/pallas_call | solution.py:315
  40.7 2.5 convolution_bitcast_fusion
  44.0 0.3 copy.58
  44.8 0.5 copy-done.12
  45.3 0.8 broadcast_multiply_fusion
  46.1 0.9 pad_maximum_fusion.1.refs_0_
  47.1 45.5 %keys.1 = (bf16[8,256,1536]{2,1,0:T(8,128)(2,1)}, bf16[4,192,768]{2,1,0:T(8,128)(2,1)}, bf16[4,192,768]{2,1,0:T(8,128)(2,1)}) custom-call(bf16[256,1536]{1,0:T(8,128)(2,1)} %pad_maximum_fusion.1.refs_0_, bf16[192,768]{1,0:T(8,128)(2,1)} %slice.90.refs_1_, bf16[192,768]{1,0:T(8,128)(2,1)} %refs_2_.1), custom_call_target="tpu_custom_call" | custom-call | bytes 12582912 | tf_op jit(solution)/shard_map/keys/pallas_call | solution.py:315
  93.0 1.1 reduce-window.6
  94.9 1.5 copy.60
  96.3 1.9 convolution_bitcast_fusion.3
  98.4 0.9 copy.61.query
  99.4 0.6 pad_add_fusion.place
  100.0 25.4 %attention.1 = (bf16[256,768]{1,0:T(8,128)(2,1)}, f32[6,8,256]{2,1,0:T(8,128)}) custom-call(s32[2]{0:T(128)} %pad_add_fusion.place, bf16[256,768]{1,0:T(8,128)(2,1)} %copy.61.query, bf16[2048,1536]{1,0:T(8,128)(2,1)} %bitcast.166, bf16[2048,1536]{1,0:T(8,128)(2,1)} %bitcast.167), custom_call_target="tpu_custom_call" | custom-call | flops 1610612736 | bytes 6291456 | tf_op jit(solution)/shard_map/attention/pallas_call | solution.py:838
  125.4 1.6 multiply_reduce_fusion.2
  127.0 0.3 fusion.11
  127.3 0.5 fusion.55
  128.1 0.7 maximum_maximum_fusion.own_notes
  128.8 32.1 %rows.1 = (bf16[4,256,768]{2,1,0:T(8,128)(2,1)}, f32[4,8,256]{2,1,0:T(8,128)}) custom-call(bf16[256,768]{1,0:T(8,128)(2,1)} %bitcast.173, f32[8,256]{1,0:T(8,128)} %maximum_maximum_fusion.own_notes), custom_call_target="tpu_custom_call" | custom-call | bytes 3145728 | tf_op jit(solution)/shard_map/rows/pallas_call | solution.py:315
  160.9 36.1 %experts.1 = (bf16[8,3,512,768]{3,2,1,0:T(8,128)(2,1)}, bf16[4,256,768]{2,1,0:T(8,128)(2,1)}, bf16[4,256,768]{2,1,0:T(8,128)(2,1)}, f32[4,8,256]{2,1,0:T(8,128)}) custom-call(bf16[4,256,768]{2,1,0:T(8,128)(2,1)} %get-tuple-element.38.routed, bf16[4,256,768]{2,1,0:T(8,128)(2,1)} %all-gather.2.cloned.1.call-done.block, f32[4,8,256]{2,1,0:T(8,128)} %get-tuple-element.40.note, ...), custom_call_target="tpu_custom_call" | custom-call | flops 14495514624 | bytes 37748736 | tf_op jit(solution)/shard_map/experts/pallas_call | solution.py:690
  197.1 1.0 copy-done.17
  198.0 0.9 copy.73
  199.0 0.5 fusion.25
  199.7 0.6 fusion.23
  200.2 33.9 %row_sums.1 = (f32[256,768]{1,0:T(8,128)}, f32[8,256]{1,0:T(8,128)}) custom-call(bf16[4,256,768]{2,1,0:T(8,128)(2,1)} %get-tuple-element.41.given, f32[4,8,256]{2,1,0:T(8,128)} %get-tuple-element.42.given_notes), custom_call_target="tpu_custom_call" | custom-call | bytes 3145728 | tf_op jit(solution)/shard_map/row_sums/pallas_call | solution.py:315
  234.1 0.7 multiply_reduce_fusion.6
  234.9 2.2 multiply_reduce_fusion
  237.2 0.3 subtract_add_fusion
  237.5 0.9 copy-done.3
  238.4 1.3 convolution_convert_fusion.2.grad_out
  239.6 22.0 %attention_back.1 = (f32[256,768]{1,0:T(8,128)}, bf16[2,2048,768]{2,1,0:T(8,128)(2,1)}) custom-call(s32[2]{0:T(128)} %pad_add_fusion.place, bf16[256,768]{1,0:T(8,128)(2,1)} %copy.61.query, bf16[2048,1536]{1,0:T(8,128)(2,1)} %bitcast.168, bf16[2048,1536]{1,0:T(8,128)(2,1)} %bitcast.169, f32[6,8,256]{2,1,0:T(8,128)} %get-tuple-element.37.total, ...), custom_call_target="tpu_custom_call" | custom-call | flops 4026531840 | bytes 12582912 | tf_op jit(solution)/shard_map/attention_back/pallas_call | solution.py:905
  261.7 52.6 %key_sums.1 = (f32[2,256,768]{2,1,0:T(8,128)}, f32[256,768]{1,0:T(8,128)}) custom-call(bf16[2,8,256,768]{3,2,1,0:T(8,128)(2,1)} %bitcast.174, bf16[4,256,768]{2,1,0:T(8,128)(2,1)} %get-tuple-element.46.given_rows), custom_call_target="tpu_custom_call" | custom-call | bytes 12582912 | tf_op jit(solution)/shard_map/key_sums/pallas_call | solution.py:315
  314.3 2.0 slice.161
  316.3 1.3 slice.101
  318.0 0.3 copy.68
  318.8 0.9 copy.69
  319.7 0.9 copy.72
  320.6 0.8 maximum_convert_fusion
  321.4 2.1 copy.71
  323.5 2.1 fusion.62
  325.6 0.8 convolution_add_fusion
  326.6 0.5 fusion.20
  327.1 0.4 copy-done.10
  327.5 0.4 copy-done.6
  327.9 0.3 fusion.53
  328.2 0.6 pad.9.given_small
  328.9 0.9 copy.70
  329.8 1.3 slice_bitcast_fusion.2
  331.1 0.5 convolution_convert_fusion.1
  331.6 1.1 convolution_convert_fusion
  332.7 2.9 pad_maximum_fusion.given
  335.6 84.3 %totals.1 = (bf16[192,3072]{1,0:T(8,128)(2,1)}, f32[24,768]{1,0:T(8,128)}) custom-call(bf16[4,192,3072]{2,1,0:T(8,128)(2,1)} %pad_maximum_fusion.given, f32[24,768]{1,0:T(8,128)} %pad.9.given_small), custom_call_target="tpu_custom_call" | custom-call | bytes 18874368 | tf_op jit(solution)/shard_map/totals/pallas_call | solution.py:315
  419.9 1.9 slice.127
  421.8 1.3 slice.126
  423.3 0.6 copy.75
  423.9 0.6 slice.111
  424.5 0.7 reshape_squeeze.3
  425.2 0.6 slice_reduce_fusion.1
  425.8 0.6 slice_bitcast_fusion
  426.5 2.5 fusion.6
  429.0 1.1 fusion.17
  430.1 49.2 %all-reduce.4.cloned.1.call-done = bf16[8,512,3,768]{3,1,2,0:T(8,128)(2,1)} async-done(((bf16[8,512,3,768]{3,1,2,0:T(8,128)(2,1)}), bf16[8,512,3,768]{3,1,2,0:T(8,128)(2,1)}) %all-reduce.4.cloned.1.call-update) | async-done | bytes 18874384 | tf_op jit(solution)/shard_map/psum | solution.py:1057
  479.3 20.8 %transpose.77 = f32[8,512,3,768]{3,1,2,0:T(8,128)} convert(bf16[8,512,3,768]{3,1,2,0:T(8,128)(2,1)} %all-reduce.4.cloned.1.call-done) | non-fusion elementwise | flops 9437184 | bytes 56623104 | tf_op jit(solution)/shard_map/transpose | solution.py:1057
  (117 shorter events, 4.0 us)
Async XLA Ops:
  7.2 120.2 %copy-start = (f32[768,12]{0,1:T(8,128)S(1)}, f32[768,12]{0,1:T(8,128)}, u32[]{:S(2)}) copy-start(f32[768,12]{0,1:T(8,128)} %param.22) | copy-start | bytes 110596
  7.2 3.8 copy-start.7
  7.2 3.9 copy-start.29
  7.2 153.7 %all-gather.2.cloned.1.call-start = ((), (), s32[]{:S(2)}) async-start(), calls=%async_computation | async-start | bytes 1966080 | tf_op jit(solution)/shard_map/all_gather | solution.py:1019
  44.3 1.0 copy-start.12
  46.1 46.5 %copy-start.30 = (bf16[768]{0:T(1024)(128)(2,1)S(1)}, bf16[768]{0:T(1024)(128)(2,1)}, u32[]{:S(2)}) copy-start(bf16[768]{0:T(1024)(128)(2,1)} %param.21) | copy-start | bytes 4612
  46.1 46.5 %copy-start.26 = (s32[1,256,2]{1,2,0:T(2,128)S(1)}, s32[1,256,2]{1,2,0:T(2,128)}, u32[]{:S(2)}) copy-start(s32[1,256,2]{1,2,0:T(2,128)} %param.15) | copy-start | bytes 6148
  92.6 2.3 copy-start.15
  92.6 386.7 %all-reduce.4.cloned.1.call-start = ((), (), s32[]{:S(2)}) async-start(), calls=%async_computation.1 | async-start | bytes 37748736 | tf_op jit(solution)/shard_map/psum | solution.py:1057
  100.0 25.4 %copy-start.13 = (bf16[4,192,768]{2,1,0:T(8,128)(2,1)S(1)}, bf16[4,192,768]{2,1,0:T(8,128)(2,1)}, u32[]{:S(2)}) copy-start(bf16[4,192,768]{2,1,0:T(8,128)(2,1)} %get-tuple-element.36) | copy-start | bytes 3538948
  127.0 0.8 copy-start.25
  127.0 0.8 copy-start.27
  127.3 1.5 copy-start.5
  197.0 1.0 copy-start.17
  197.0 1.9 copy-start.28
  237.4 0.9 copy-start.3
  316.3 1.9 copy-start.20
  321.4 4.2 copy-start.2
  323.5 2.1 copy-start.18
  323.5 2.1 copy-start.19
  325.6 1.0 copy-start.8
  326.6 0.9 copy-start.10
  326.6 1.3 copy-start.6
  326.6 4.5 copy-start.4
  326.6 4.5 copy-start.16
  329.8 1.8 copy-start.21
  329.8 1.8 copy-start.22
  329.8 1.8 copy-start.23
  419.9 1.9 copy-start.14
  421.8 2.1 copy-start.24
  423.1 5.8 %copy-start.9 = (bf16[1,256,768]{2,1,0:T(8,128)(2,1)S(1)}, bf16[1,256,768]{2,1,0:T(8,128)(2,1)}, u32[]{:S(2)}) copy-start(bf16[1,256,768]{2,1,0:T(8,128)(2,1)} %param.13) | copy-start | bytes 1179652
  423.1 5.8 %copy-start.11 = (f32[256,768]{1,0:T(8,128)S(1)}, f32[256,768]{1,0:T(8,128)}, u32[]{:S(2)}) copy-start(f32[256,768]{1,0:T(8,128)} %copy-done.10) | copy-start | bytes 2359300
  479.3 20.8 %copy-start.1 = (f32[768,12]{0,1:T(8,128)S(1)}, f32[768,12]{0,1:T(8,128)}, u32[]{:S(2)}) copy-start(f32[768,12]{0,1:T(8,128)} %param.22) | copy-start | bytes 110596
Sparse Core Ops, SparseCore 0:
  92.7 35.2 all-gather.1
  197.2 282.0 all-reduce.3

commit v4 on v3

--- a/solution.py
+++ b/solution.py
@@ -453,19 +453,25 @@
     )
 
 
-def reduce_rows(parts, notes, count):
+def reduce_rows(parts, notes, shared, count, ctx_count):
     _, rows, width = parts.shape
 
-    def kernel(given, given_notes, total, notes_total, passing, landing, noted, send, recv):
+    def kernel(given, given_notes, own, total, notes_total, all_shared,
+               passing, landing, noted, send, recv):
         copies = Copies(send, recv)
-        rank = lax.axis_index("fsdp")
-        meet(ring_peers("fsdp", count))
-        pushes = []
+        rank, place = lax.axis_index("fsdp"), lax.axis_index("ctx")
+        meet(ring_peers("fsdp", count) + ring_peers("ctx", ctx_count))
+        pushes, spread = [], []
         for step in range(1, count):
             peer = lax.rem(rank + step, count)
             copy = copies.make(given_notes.at[peer], noted.at[step - 1], {"fsdp": peer})
             copy.start()
             pushes.append(copy)
+        for step in range(1, ctx_count):
+            copy = copies.make(own, all_shared.at[place], {"ctx": lax.rem(place + step, ctx_count)})
+            copy.start()
+            spread.append(copy)
+        all_shared[place] = own[...]
         together(
             line_reduce(copies, lambda d: given.at[d], passing, landing, count, total)
         )
@@ -474,17 +480,23 @@
             copy.wait()
             sums = sums + noted[step]
         notes_total[...] = sums
+        for copy in spread:
+            copy.wait()
 
     return remote_call(
         kernel, "row_sums",
-        [struct((rows, width), jnp.float32), struct(notes.shape[1:], notes.dtype)],
-        [parts, notes], [pltpu.VMEM] * 2, [pltpu.VMEM] * 2,
+        [
+            struct((rows, width), jnp.float32),
+            struct(notes.shape[1:], notes.dtype),
+            struct((ctx_count,) + shared.shape, shared.dtype),
+        ],
+        [parts, notes, shared], [pltpu.VMEM] * 3, [pltpu.VMEM] * 3,
         [
             pltpu.VMEM((2, count - 1, rows, width), parts.dtype),
             pltpu.VMEM((2, count - 1, rows, width), parts.dtype),
             pltpu.VMEM((count - 1,) + notes.shape[1:], notes.dtype),
         ],
-        4 * count, count * rows * width * 4,
+        4 * count + ctx_count, count * rows * width * 4,
     )
 
 
@@ -550,7 +562,7 @@
     )
 
 
-def reduce_weights(parts, small, count, ctx_count):
+def reduce_weights(parts, small, half_grads, row_parts, count, ctx_count):
     _, rows, width = parts.shape
     chips = ctx_count // 2
     half, share = rows // 2, width // chips
@@ -558,7 +570,10 @@
     first = max(count // 2, 1)
     lands = (6, first, half, share) if chips == 4 else (chips - 1, count, half, share)
 
-    def kernel(given, given_small, total, small_total, met, paired, passing, landing, merged,
+    own = half_grads.shape[0]
+
+    def kernel(given, given_small, half_ref, given_rows, total, small_total, grads_ref, rows_total,
+               row_passing, row_landing, met, paired, passing, landing, merged,
                line_passing, line_landing, line_total, own_total, small_met, small_sum,
                small_plane, small_plane_sum, small_line, send, recv):
         copies = Copies(send, recv)
@@ -581,6 +596,11 @@
         exchanged = []
         for d in range(count):
             copy = copies.make(given.at[d, theirs], met.at[d], {"ctx": sibling})
+            copy.start()
+            exchanged.append(copy)
+
+        for i in range(own):
+            copy = copies.make(half_ref.at[i], grads_ref.at[i], {"ctx": sibling})
             copy.start()
             exchanged.append(copy)
 
@@ -617,7 +637,7 @@
             merged[spans[part]] = value.astype(merged.dtype)
 
         def large_stream():
-            for d, copy in enumerate(exchanged):
+            for d, copy in enumerate(exchanged[:count]):
                 copy.wait_recv()
                 for q in range(chips):
                     paired[q, d] = (
@@ -656,17 +676,34 @@
             for copy in forwarded:
                 copy.wait()
 
-        together(small_stream(), large_stream())
+        together(
+            line_reduce(
+                copies, lambda d: given_rows.at[d], row_passing, row_landing, count, rows_total
+            ),
+            small_stream(),
+            large_stream(),
+        )
         for copy in exchanged:
             copy.wait_send()
+        for copy in exchanged[count:]:
+            copy.wait_recv()
 
     kind = parts.dtype
     f32 = jnp.float32
     return remote_call(
         kernel, "totals",
-        [struct((rows, width), kind), struct(small.shape, f32)],
-        [parts, small], [pltpu.VMEM] * 2, [pltpu.VMEM] * 2,
         [
+            struct((rows, width), kind),
+            struct(small.shape, f32),
+            struct(half_grads.shape, kind),
+            struct(row_parts.shape[1:], f32),
+        ],
+        [parts, small, half_grads, row_parts],
+        [pltpu.VMEM, pltpu.VMEM, pl.ANY, pltpu.VMEM],
+        [pltpu.VMEM, pltpu.VMEM, pl.ANY, pltpu.VMEM],
+        [
+            pltpu.VMEM((2, count - 1) + row_parts.shape[1:], kind),
+            pltpu.VMEM((2, count - 1) + row_parts.shape[1:], kind),
             pltpu.VMEM((count, half, width), kind),
             pltpu.VMEM((chips, count, half, share), kind),
             pltpu.VMEM((2, first, half, share), kind),
@@ -682,7 +719,7 @@
             pltpu.VMEM(small.shape, f32),
             pltpu.VMEM((count - 1,) + small.shape, f32),
         ],
-        count + 8 + 3 * count + 4 * chips, parts.size * 8,
+        count + 8 + 5 * count + 4 * chips + own, parts.size * 8,
     )
 
 
@@ -716,7 +753,7 @@
     capacity = piece_len // 4
     count = peers * capacity
 
-    def kernel(routed, block, note, w, grads, out_parts, grad_parts, dots, out_sum, grad_sum):
+    def kernel(routed, block, note, w, out_parts, grad_parts, dots, out_sum, grad_sum):
         expert = pl.program_id(0)
         low = jnp.bfloat16
 
@@ -763,9 +800,6 @@
             grad_hidden * up_proj * sigmoid * (1.0 + gate_proj * (1.0 - sigmoid))
         ).astype(low)
         grad_up_proj = (grad_hidden * silu).astype(low)
-        grads[0, 0] = product(grad_gate_proj, rows, 0, 0).astype(low)
-        grads[0, 1] = product(grad_up_proj, rows, 0, 0).astype(low)
-        grads[0, 2] = product(hidden, grad_out, 0, 0).astype(low)
         expert_out = product(hidden, w_down)
         grad_in = (product(grad_gate_proj, w_gate) + product(grad_up_proj, w_up)).astype(low)
         row_dots = jnp.sum(block_part * expert_out, axis=1, keepdims=True)
@@ -787,14 +821,166 @@
     expert_block = pl.BlockSpec((1, 3, units, width), lambda e: (e, 0, 0, 0))
     return local_call(
         kernel, "experts", (experts,),
-        [struct(weights.shape, low), struct(rows_shape, low), struct(rows_shape, low),
+        [struct(rows_shape, low), struct(rows_shape, low),
          struct(notes.shape, jnp.float32)],
         [routed_rows, block_rows, notes, weights],
         [whole_block(rows_shape), whole_block(rows_shape), whole_block(notes.shape), expert_block],
-        [expert_block, whole_block(rows_shape), whole_block(rows_shape), whole_block(notes.shape)],
+        [whole_block(rows_shape), whole_block(rows_shape), whole_block(notes.shape)],
         [pltpu.VMEM(rows_shape, jnp.float32), pltpu.VMEM(rows_shape, jnp.float32)],
-        18 * experts * count * units * width, 4 * weights.size,
-    )
+        12 * experts * count * units * width, 2 * weights.size,
+    )
+
+
+def expert_gradients(first, counts, routed_rows, block_rows, notes, weights):
+    pieces, piece_len, width = routed_rows.shape
+    experts, _, units, _ = weights.shape
+    capacity = piece_len // 4
+    own = experts // 2
+    tile = 256
+    room = pieces * capacity + tile
+    batch = max(d for d in range(1, own + 1) if own % d == 0 and (d == 1 or d * room * width * 4 <= 30 << 20))
+    low = jnp.bfloat16
+
+    def kernel(start, count, routed, block, note, w, grads, final, rows, grad_rows, ends):
+        turn, step = pl.program_id(0), pl.program_id(1)
+        expert = start[0] + turn * batch
+
+        @pl.when(step == 0)
+        def _():
+            for j in range(batch):
+                ends[j] = 0
+
+        piece = jnp.minimum(step, pieces - 1)
+        numbers = [count[piece * experts + expert + j] for j in range(batch)]
+
+        @pl.when((step < pieces) & (sum(numbers) > 0))
+        def _():
+            slots = (
+                lax.broadcasted_iota(jnp.int32, (batch * capacity, piece_len), 0)
+                + expert * capacity
+            ).astype(jnp.float32)
+            first = note[0, 0:1, :] == slots
+            second = note[0, 1:2, :] == slots
+            gate = jnp.sum(
+                jnp.where(first, note[0, 2:3, :], 0.0) + jnp.where(second, note[0, 3:4, :], 0.0),
+                axis=1,
+                keepdims=True,
+            )
+            hot = (jnp.where(first, 1.0, 0.0) + jnp.where(second, 1.0, 0.0)).astype(low)
+            taken = product(hot, routed[0]).astype(low)
+            grad_out = (gate * product(hot, block[0])).astype(low)
+            for j in range(batch):
+                place = pl.ds(pl.multiple_of(ends[j], 16), capacity)
+                span = slice(j * capacity, (j + 1) * capacity)
+                rows[j, place, :] = taken[span]
+                grad_rows[j, place, :] = grad_out[span]
+                ends[j] += (numbers[j] + 15) // 16 * 16
+
+        @pl.when(step >= pieces)
+        def _():
+            j = jnp.maximum(step - pieces, 0)
+            end = pl.multiple_of(ends[j], 16)
+            rest = pl.ds(end, tile)
+            rows[j, rest, :] = jnp.zeros((tile, width), low)
+            grad_rows[j, rest, :] = jnp.zeros((tile, width), low)
+            final[...] = jnp.zeros_like(final)
+
+            def one_tile(index, _):
+                place = pl.ds(pl.multiple_of(index * tile, tile), tile)
+                x = rows[j, place, :]
+                grad_out = grad_rows[j, place, :]
+                gate_proj = product(x, w[0, 0], 1, 1)
+                up_proj = product(x, w[0, 1], 1, 1)
+                grad_hidden = product(grad_out, w[0, 2], 1, 1)
+                sigmoid = 1.0 / (1.0 + jnp.exp(-gate_proj))
+                silu = gate_proj * sigmoid
+                hidden = (silu * up_proj).astype(low)
+                grad_gate_proj = (
+                    grad_hidden * up_proj * sigmoid * (1.0 + gate_proj * (1.0 - sigmoid))
+                ).astype(low)
+                grad_up_proj = (grad_hidden * silu).astype(low)
+                final[0, 0] += product(grad_gate_proj, x, 0, 0)
+                final[0, 1] += product(grad_up_proj, x, 0, 0)
+                final[0, 2] += product(hidden, grad_out, 0, 0)
+                return 0
+
+            lax.fori_loop(0, (end + tile - 1) // tile, one_tile, 0)
+            grads[...] = final[...].astype(low)
+
+    def piece_block(shape):
+        return pl.BlockSpec(
+            (1,) + shape[1:], lambda turn, step, *_: (jnp.minimum(step, pieces - 1), 0, 0)
+        )
+
+    def local(turn, step):
+        return turn * batch + jnp.maximum(step - pieces, 0)
+
+    return pl.pallas_call(
+        kernel,
+        grid_spec=pltpu.PrefetchScalarGridSpec(
+            num_scalar_prefetch=2,
+            grid=(own // batch, pieces + batch),
+            in_specs=[
+                piece_block(routed_rows.shape),
+                piece_block(block_rows.shape),
+                piece_block(notes.shape),
+                pl.BlockSpec(
+                    (1, 3, units, width),
+                    lambda turn, step, start, _: (start[0] + local(turn, step), 0, 0, 0),
+                ),
+            ],
+            out_specs=[
+                pl.BlockSpec(
+                    (1, 3, units, width), lambda turn, step, *_: (local(turn, step), 0, 0, 0)
+                ),
+                pl.BlockSpec(
+                    (1, 3, units, width),
+                    lambda turn, step, start, _: (start[0] + local(turn, step), 0, 0, 0),
+                ),
+            ],
+            scratch_shapes=[
+                pltpu.VMEM((batch, room, width), low),
+                pltpu.VMEM((batch, room, width), low),
+                pltpu.SMEM((batch,), jnp.int32),
+            ],
+        ),
+        out_shape=[
+            struct((own, 3, units, width), low),
+            struct((experts, 3, units, width), jnp.float32),
+        ],
+        compiler_params=pltpu.CompilerParams(vmem_limit_bytes=VMEM_LIMIT),
+        cost_estimate=pl.CostEstimate(
+            flops=12 * own * pieces * capacity * units * width // 2,
+            bytes_accessed=routed_rows.size * 4 + weights.size * 2,
+            transcendentals=0,
+        ),
+        name="expert_gradients",
+    )(first, counts, routed_rows, block_rows, notes, weights)
+
+
+def other_gradients(first, received, final):
+    own, _, units, width = received.shape
+    block = (1, 1, units, width)
+
+    def kernel(start, given, _, result):
+        result[...] = given[...].astype(jnp.float32)
+
+    return pl.pallas_call(
+        kernel,
+        grid_spec=pltpu.PrefetchScalarGridSpec(
+            num_scalar_prefetch=1,
+            grid=(own, 3),
+            in_specs=[
+                pl.BlockSpec(block, lambda i, k, _: (i, k, 0, 0)),
+                pl.BlockSpec(memory_space=pl.ANY),
+            ],
+            out_specs=pl.BlockSpec(block, lambda i, k, start: (start[0] + i, k, 0, 0)),
+        ),
+        out_shape=struct(final.shape, jnp.float32),
+        input_output_aliases={2: 0},
+        compiler_params=pltpu.CompilerParams(vmem_limit_bytes=VMEM_LIMIT),
+        name="other_gradients",
+    )(first, received, final)
 
 
 def score_bias(length, first_row, rows, keys):
@@ -863,6 +1049,7 @@
 def attention_backward(places, queries, pairs, sums, mixed, grad_mixed):
     rows, width = queries.shape
     keys = pairs.shape[0]
+    pieces = keys // rows
     tile = 2 * HEAD_DIM
     tiles = width // tile
     scaling = HEAD_DIM**-0.5
@@ -896,8 +1083,8 @@
             value_sum = value_part if value_sum is None else value_sum + value_part
             grads.append(product(grad_scores, key[...], 0, 0) * scaling)
         grad_query[...] = jnp.where(own_masks[0], grads[0], grads[1])
-        grad_pair[0] = key_sum.astype(grad_pair.dtype)
-        grad_pair[1] = value_sum.astype(grad_pair.dtype)
+        grad_pair[:, 0] = key_sum.astype(grad_pair.dtype).reshape(pieces, rows, tile)
+        grad_pair[:, 1] = value_sum.astype(grad_pair.dtype).reshape(pieces, rows, tile)
 
     own_block = pl.BlockSpec((rows, tile), lambda i, _: (0, i))
     key_block = pl.BlockSpec((keys, tile), lambda i, _: (0, i))
@@ -915,12 +1102,15 @@
                 own_block,
                 own_block,
             ],
-            out_specs=[own_block, pl.BlockSpec((2, keys, tile), lambda i, _: (0, 0, i))],
+            out_specs=[
+                own_block,
+                pl.BlockSpec((pieces, 2, rows, tile), lambda i, _: (0, 0, 0, i)),
+            ],
             scratch_shapes=[pltpu.VMEM((keys, rows), jnp.float32)],
         ),
         out_shape=[
             struct((rows, width), jnp.float32),
-            struct((2, keys, width), low),
+            struct((pieces, 2, rows, width), low),
         ],
         compiler_params=pltpu.CompilerParams(vmem_limit_bytes=VMEM_LIMIT),
         cost_estimate=pl.CostEstimate(
@@ -1008,15 +1198,15 @@
         .reshape(piece_len, model_width)
     )
     value_local = projected[0, :, model_width:].astype(jnp.bfloat16)
+    cotangent_low = live_rows.astype(jnp.bfloat16) * cotangent
+    own_pairs = jnp.concatenate([key_local, value_local], axis=-1)
+    cotangent_low, own_pairs = lax.optimization_barrier((cotangent_low, own_pairs))
+    cotangent_rows = lax.all_gather(cotangent_low, "fsdp", axis=0, tiled=True)
     all_pairs, (full_query, full_out) = gather_keys(
-        jnp.concatenate([key_local, value_local], axis=-1),
-        [w_qkv[:, :model_width], w_out],
-        fsdp_count,
-        ctx_count,
-    )
-    cotangent_low = live_rows.astype(jnp.bfloat16) * cotangent
-    cotangent_own, all_pairs = lax.optimization_barrier((cotangent_low, all_pairs))
-    cotangent_rows = lax.all_gather(cotangent_own, "fsdp", axis=0, tiled=True)
+        own_pairs, [w_qkv[:, :model_width], w_out], fsdp_count, ctx_count
+    )
+    cotangent_rows, all_pairs = lax.optimization_barrier((cotangent_rows, all_pairs))
+    slot_block = lax.all_gather(cotangent_rows, "ctx", axis=0, tiled=True)
     queries = rotate(
         jnp.einsum(
             "gpd,de->gpe", normed_one_low, full_query, preferred_element_type=jnp.float32
@@ -1049,13 +1239,30 @@
     slot_of = jnp.where(is_ffn > 0.5, expert_of * capacity + order_in, -1.0).reshape(
         groups, piece_len, 2
     )
-    notes = jnp.concatenate([slot_of[0].T, gate_weights[0].T, jnp.zeros((4, piece_len))], axis=0)
+    live_counts = jnp.sum(
+        assign_hot * jnp.repeat(live_rows[..., 0], 2, axis=1)[..., None], axis=(0, 1)
+    )
+    notes = jnp.concatenate(
+        [
+            slot_of[0].T,
+            gate_weights[0].T,
+            jnp.pad(live_counts[None], ((0, 3), (0, piece_len - experts))),
+        ],
+        axis=0,
+    )
     routed_rows, all_notes = gather_rows(routed_low[0], notes, fsdp_count)
-    grad_weights, out_parts, grad_parts, dot_notes = expert_layers(
-        routed_rows, cotangent_rows, all_notes, w_expert.swapaxes(1, 2)
-    )
-    expert_sum = lax.psum(grad_weights, "ctx").astype(jnp.float32).swapaxes(1, 2)
-    ffn_grad, dot_sums = reduce_rows(grad_parts, dot_notes, fsdp_count)
+    expert_weights = w_expert.swapaxes(1, 2)
+    out_parts, grad_parts, dot_notes = expert_layers(
+        routed_rows, cotangent_rows, all_notes, expert_weights
+    )
+    slot_block, routed_rows, out_parts = lax.optimization_barrier(
+        (slot_block, routed_rows, out_parts)
+    )
+    slot_routed = lax.all_gather(routed_rows, "ctx", axis=0, tiled=True)
+    ffn_grad, dot_sums, slot_notes = reduce_rows(
+        grad_parts, dot_notes, all_notes, fsdp_count, ctx_count
+    )
+    slot_notes = slot_notes.reshape((ctx_count * fsdp_count,) + notes.shape)
     ffn_grad = ffn_grad[None]
     copy_hot = route_hot[..., experts + 1]
     const_hot = route_hot[..., experts + 2 :]
@@ -1098,9 +1305,16 @@
     query_grad, pair_grads = attention_backward(
         places, query_rows, all_pairs, score_sums, mixed_rows, grad_mixed[0]
     )
-    pair_grads = pair_grads.reshape(2, ctx_count, piece_len, model_width)
-    pair_grad, ffn_sum = reduce_keys(pair_grads, out_parts, fsdp_count, ctx_count)
-    output = (live_rows * (residual_sum + special_sum + ffn_sum[None])).astype(jnp.bfloat16)
+    counts = slot_notes[:, 4, :experts].astype(jnp.int32).reshape(-1)
+    counts, slot_routed, pair_grads = lax.optimization_barrier((counts, slot_routed, pair_grads))
+    first_expert = lax.rem(lax.axis_index("ctx"), 2) * (experts // 2)
+    half_grads, expert_half = expert_gradients(
+        first_expert.astype(jnp.int32)[None], counts, slot_routed, slot_block, slot_notes, expert_weights
+    )
+    pair_grad = lax.psum_scatter(
+        pair_grads.reshape(1, -1, model_width), "ctx", scatter_dimension=1, tiled=True
+    )
+    pair_grad = pair_grad.astype(jnp.float32).reshape(2, piece_len, model_width)
     key_grad, value_grad = pair_grad[:1], pair_grad[1:]
     query_back = rotate(query_grad.reshape(split_shape), cosine_table, -sine_table).reshape(
         groups, piece_len, model_width
@@ -1138,7 +1352,12 @@
         [grad_router.T, grad_const, grad_gain_one[None], grad_gain_two[None], mixing_row], axis=0
     )
     small = jnp.pad(small, ((0, -small.shape[0] % 8), (0, 0)))
-    weight_sum, small_sum = reduce_weights(weight_parts, small, fsdp_count, ctx_count)
+    weight_sum, small_sum, expert_grads, ffn_sum = reduce_weights(
+        weight_parts, small, half_grads, out_parts, fsdp_count, ctx_count
+    )
+    other_first = (experts // 2 - first_expert).astype(jnp.int32)[None]
+    expert_sum = other_gradients(other_first, expert_grads, expert_half).swapaxes(1, 2)
+    output = (live_rows * (residual_sum + special_sum + ffn_sum[None])).astype(jnp.bfloat16)
     weight_sum = weight_sum.astype(jnp.float32)
     wqkv_sum, wout_sum = weight_sum[:, : 3 * model_width], weight_sum[:, 3 * model_width :]
     router_sum, const_sum = small_sum[:few].T, small_sum[few : few + 2]

time: 508 us -> 453 us (0.89)
  waiting for transfers between devices: 49.2 us -> 5.33 us
  other arithmetic: 33 us -> 14 us
    pallas_call x0 -> x2, Pallas kernels: none -> 78.6 us  [the longest x1 65.9 us: expert_gradients(): pl.pallas_call(kernel, grid_spec=pltpu.PrefetchScalarGridSpec(num_scalar_...]
    pallas_call x6 -> x5, Pallas kernels: 278 us -> 208 us  [remote_call(): pl.pallas_call(kernel, out_shape=results, in_specs=[pl.BlockSpec(memory_s...]
    psum x1 -> x0, waiting for transfers between devices: 49.2 us -> none  [per_device(): lax.psum(grad_weights, 'ctx').astype(jnp.float32).swapaxes(1, 2)]
    transpose x1 -> x0, other arithmetic: 20.8 us -> none  [per_device(): lax.psum(grad_weights, 'ctx').astype(jnp.float32).swapaxes(1, 2)]
    pallas_call x1, Pallas kernels: 36.1 us -> 28.7 us  [local_call(): pl.pallas_call(kernel, grid=grid, out_shape=results, in_specs=in_specs, o...]
    all_gather x1 -> x3, waiting for transfers between devices: 0.02 us -> 5.26 us  [the longest x1 5.22 us: per_device(): slot_routed = lax.all_gather(routed_rows, 'ctx', axis=0, tiled=True)]
  transfers between devices with their start and end apart: 2 -> 4, of which waited for: 1 -> 1; matrix products, arithmetic and copies ran while one was open for 9% -> 6% of each run, Pallas kernels for 49% -> 58%
where the time goes in v4:
time: 453 us; the launch traced here: 451 us
  Pallas kernels  363 us (80%)
  local copies, waits for them, and re-layouts  31 us (7%)
  matrix products  22.3 us (5%)
  between operations  15 us (3%)
  other arithmetic  14 us (3%)
  waiting for transfers between devices  5.33 us (1%)
    pallas_call x5, Pallas kernels, remote_call(): pl.pallas_call(kernel, out_shape=results, in_specs=[pl.BlockSpec(memory_s...  208 us
    pallas_call x1, Pallas kernels, expert_gradients(): pl.pallas_call(kernel, grid_spec=pltpu.PrefetchScalarGridSpec(num_scalar_...  65.9 us
    pallas_call x1, Pallas kernels, local_call(): pl.pallas_call(kernel, grid=grid, out_shape=results, in_specs=in_specs, o...  28.7 us
    pallas_call x1, Pallas kernels, attention_forward(): pl.pallas_call(kernel, grid_spec=pltpu.PrefetchScalarGridSpec(num_scalar_...  25.4 us
    pallas_call x1, Pallas kernels, attention_backward(): pl.pallas_call(kernel, grid_spec=pltpu.PrefetchScalarGridSpec(num_scalar_...  22.2 us
    pallas_call x1, Pallas kernels, other_gradients(): pl.pallas_call(kernel, grid_spec=pltpu.PrefetchScalarGridSpec(num_scalar_...  12.6 us
  transfers between devices with their start and end apart: 4, of which 1 were waited for; matrix products, arithmetic and copies ran while one was open for 6% of the time, Pallas kernels for 58%

profile of v4, /device:TPU:0, one launch (start us, length us, event | category | flops | bytes accessed | tf_op | source)
XLA Modules:
  0.0 450.7 jit_solution(13881224213364382178)
XLA Ops:
  7.2 1.9 slice.90.source
  9.2 29.5 %weights.1 = bf16[4,192,1536]{2,1,0:T(8,128)(2,1)} custom-call(bf16[192,1536]{1,0:T(8,128)(2,1)} %slice.90.source), custom_call_target="tpu_custom_call" | custom-call | bytes 4718592 | tf_op jit(solution)/shard_map/weights/pallas_call | solution.py:315
  38.8 2.5 convolution_bitcast_fusion
  42.2 0.3 copy.58
  43.0 0.5 copy-done.5
  43.4 0.8 broadcast_multiply_fusion
  44.3 0.9 pad_maximum_fusion.1.refs_0_
  45.3 1.7 slice.95.refs_1_
  47.0 50.1 %keys.1 = (bf16[8,256,1536]{2,1,0:T(8,128)(2,1)}, bf16[4,192,768]{2,1,0:T(8,128)(2,1)}, bf16[4,192,768]{2,1,0:T(8,128)(2,1)}) custom-call(bf16[256,1536]{1,0:T(8,128)(2,1)} %pad_maximum_fusion.1.refs_0_, bf16[192,768]{1,0:T(8,128)(2,1)} %slice.95.refs_1_, bf16[192,768]{1,0:T(8,128)(2,1)} %refs_2_.1), custom_call_target="tpu_custom_call" | custom-call | bytes 12582912 | tf_op jit(solution)/shard_map/keys/pallas_call | solution.py:315
  97.2 1.2 copy-done.10
  98.4 1.4 copy.60
  99.8 1.8 convolution_bitcast_fusion.3
  101.8 0.9 copy.61.query
  103.2 1.1 reduce-window.6
  105.1 0.6 pad_add_fusion.place
  105.7 25.4 %attention.1 = (bf16[256,768]{1,0:T(8,128)(2,1)}, f32[6,8,256]{2,1,0:T(8,128)}) custom-call(s32[2]{0:T(128)} %pad_add_fusion.place, bf16[256,768]{1,0:T(8,128)(2,1)} %copy.61.query, bf16[2048,1536]{1,0:T(8,128)(2,1)} %bitcast.173, bf16[2048,1536]{1,0:T(8,128)(2,1)} %bitcast.174), custom_call_target="tpu_custom_call" | custom-call | flops 1610612736 | bytes 6291456 | tf_op jit(solution)/shard_map/attention/pallas_call | solution.py:1024
  131.1 1.6 multiply_reduce_fusion.2
  132.7 0.3 fusion.11
  133.0 0.4 fusion.56
  133.8 0.6 select_maximum_fusion.own_notes
  134.4 33.2 %rows.1 = (bf16[4,256,768]{2,1,0:T(8,128)(2,1)}, f32[4,8,256]{2,1,0:T(8,128)}) custom-call(bf16[256,768]{1,0:T(8,128)(2,1)} %bitcast.177, f32[8,256]{1,0:T(8,128)} %select_maximum_fusion.own_notes), custom_call_target="tpu_custom_call" | custom-call | bytes 3145728 | tf_op jit(solution)/shard_map/rows/pallas_call | solution.py:315
  167.6 28.7 %experts.1 = (bf16[4,256,768]{2,1,0:T(8,128)(2,1)}, bf16[4,256,768]{2,1,0:T(8,128)(2,1)}, f32[4,8,256]{2,1,0:T(8,128)}) custom-call(bf16[4,256,768]{2,1,0:T(8,128)(2,1)} %get-tuple-element.60.routed, bf16[4,256,768]{2,1,0:T(8,128)(2,1)} %all-gather.4.cloned.1.call-done.block, f32[4,8,256]{2,1,0:T(8,128)} %get-tuple-element.52.note.own, ...), custom_call_target="tpu_custom_call" | custom-call | flops 9663676416 | bytes 18874368 | tf_op jit(solution)/shard_map/experts/pallas_call | solution.py:727
  196.4 0.6 copy-done.22
  196.9 0.5 fusion.25
  197.5 35.0 %row_sums.1 = (f32[256,768]{1,0:T(8,128)}, f32[8,256]{1,0:T(8,128)}, f32[8,4,8,256]{3,2,1,0:T(8,128)}) custom-call(bf16[4,256,768]{2,1,0:T(8,128)(2,1)} %get-tuple-element.53.given, f32[4,8,256]{2,1,0:T(8,128)} %get-tuple-element.54.given_notes, f32[4,8,256]{2,1,0:T(8,128)} %get-tuple-element.52.note.own), custom_call_target="tpu_custom_call" | custom-call | bytes 3145728 | tf_op jit(solution)/shard_map/row_sums/pallas_call | solution.py:315
  232.5 1.0 fusion.38
  233.5 0.7 convert_element_type.138.count
  234.2 0.7 multiply_reduce_fusion.7
  235.0 2.2 multiply_reduce_fusion
  237.3 0.3 subtract_add_fusion
  237.5 1.0 copy-done.8
  238.5 1.3 convolution_convert_fusion.2.grad_out
  239.8 22.2 %attention_back.1 = (f32[256,768]{1,0:T(8,128)}, bf16[8,2,256,768]{3,2,1,0:T(8,128)(2,1)}) custom-call(s32[2]{0:T(128)} %pad_add_fusion.place, bf16[256,768]{1,0:T(8,128)(2,1)} %copy.61.query, bf16[2048,1536]{1,0:T(8,128)(2,1)} %bitcast.175, bf16[2048,1536]{1,0:T(8,128)(2,1)} %bitcast.176, f32[6,8,256]{2,1,0:T(8,128)} %get-tuple-element.49.total, ...), custom_call_target="tpu_custom_call" | custom-call | flops 4026531840 | bytes 12582912 | tf_op jit(solution)/shard_map/attention_back/pallas_call | solution.py:1092
  261.9 5.2 %all-gather.8.cloned.1.call-done.routed = bf16[32,256,768]{2,1,0:T(8,128)(2,1)} async-done(((bf16[4,256,768]{2,1,0:T(8,128)(2,1)}), bf16[32,256,768]{2,1,0:T(8,128)(2,1)}) %all-gather.8.cloned.1.call-update) | async-done | bytes 12582928 | tf_op jit(solution)/shard_map/all_gather | solution.py:1261
  267.2 1.0 copy-done.12
  268.2 0.9 copy.72
  269.1 2.3 copy.68
  271.9 0.6 copy.75
  272.5 0.6 fusion.23
  273.1 0.3 fusion.54
  273.4 1.5 convolution_convert_fusion.1
  274.9 65.9 %expert_gradients.1 = (bf16[4,3,512,768]{3,2,1,0:T(8,128)(2,1)}, f32[8,3,512,768]{3,2,1,0:T(8,128)}) custom-call(s32[1]{0:T(128)} %bitcast.56.start, s32[256]{0:T(256)} %convert_element_type.138.count, bf16[32,256,768]{2,1,0:T(8,128)(2,1)} %all-gather.8.cloned.1.call-done.routed, bf16[32,256,768]{2,1,0:T(8,128)(2,1)} %all-gather.6.cloned.1.call-done.block, ...), custom_call_target="tpu_custom_call" | custom-call | flops 19327352832 | bytes 44040192 | tf_op jit(solution)/shard_map/expert_gradients/pallas_call | solution.py:918
  340.8 1.9 slice.131
  342.8 2.3 copy.69
  345.1 2.3 multiply_subtract_fusion.1
  347.4 0.9 copy.70
  348.3 2.7 fusion.63
  351.0 0.9 copy.73
  352.0 2.9 fusion.20
  355.0 1.2 fusion.19
  356.2 0.9 copy.62
  357.1 0.9 copy.71
  358.1 0.6 pad.14.given_small
  358.7 2.2 convolution_convert_fusion
  360.9 2.9 pad_maximum_fusion.given
  363.8 60.2 %totals.1 = (bf16[192,3072]{1,0:T(8,128)(2,1)}, f32[24,768]{1,0:T(8,128)}, bf16[4,3,512,768]{3,2,1,0:T(8,128)(2,1)}, f32[256,768]{1,0:T(8,128)}) custom-call(bf16[4,192,3072]{2,1,0:T(8,128)(2,1)} %pad_maximum_fusion.given, f32[24,768]{1,0:T(8,128)} %pad.14.given_small, bf16[4,3,512,768]{3,2,1,0:T(8,128)(2,1)} %get-tuple-element.66.half_ref, ...), custom_call_target="tpu_custom_call" | custom-call | bytes 18874368 | tf_op jit(solution)/shard_map/totals/pallas_call | solution.py:315
  424.1 2.6 slice.135
  426.7 0.9 slice.136
  427.6 0.6 slice_reduce_fusion.1
  428.2 0.6 slice_bitcast_fusion
  428.8 0.6 slice.117
  429.4 1.4 fusion.6
  430.8 0.7 reshape_squeeze.3
  431.5 12.6 %other_gradients.1 = f32[8,3,512,768]{3,2,1,0:T(8,128)} custom-call(s32[1]{0:T(128)} %bitcast.62.start, bf16[4,3,512,768]{3,2,1,0:T(8,128)(2,1)} %get-tuple-element.71.given, f32[8,3,512,768]{3,2,1,0:T(8,128)} %get-tuple-element.72._), custom_call_target="tpu_custom_call", output_to_operand_aliasing={{}: (2, {})} | custom-call | tf_op jit(solution)/shard_map/other_gradients/pallas_call | solution.py:968
  (111 shorter events, 3.5 us)
Async XLA Ops:
  7.2 125.9 %copy-start = (f32[768,12]{0,1:T(8,128)S(1)}, f32[768,12]{0,1:T(8,128)}, u32[]{:S(2)}) copy-start(f32[768,12]{0,1:T(8,128)} %param.22) | copy-start | bytes 110596
  7.2 89.9 %all-gather.4.cloned.1.call-start = ((), (), s32[]{:S(2)}) async-start(), calls=%async_computation.1 | async-start | bytes 1966080 | tf_op jit(solution)/shard_map/all_gather | solution.py:1204
  9.2 29.5 %copy-start.23 = (bf16[768]{0:T(1024)(128)(2,1)S(1)}, bf16[768]{0:T(1024)(128)(2,1)}, u32[]{:S(2)}) copy-start(bf16[768]{0:T(1024)(128)(2,1)} %param.20) | copy-start | bytes 4612
  9.2 29.5 %copy-start.4 = (bf16[1,256,768]{2,1,0:T(8,128)(2,1)S(1)}, bf16[1,256,768]{2,1,0:T(8,128)(2,1)}, u32[]{:S(2)}) copy-start(bf16[1,256,768]{2,1,0:T(8,128)(2,1)} %param.13) | copy-start | bytes 1179652
  42.4 1.0 copy-start.5
  45.2 151.0 %all-gather.6.cloned.1.call-start = ((), (), s32[]{:S(2)}) async-start(), calls=%async_computation.2 | async-start | bytes 14155776 | tf_op jit(solution)/shard_map/all_gather | solution.py:1209
  97.1 1.3 copy-start.10
  97.2 170.0 %all-gather.8.cloned.1.call-start = ((), (), s32[]{:S(2)}) async-start(), calls=%async_computation.3 | async-start | bytes 14155776 | tf_op jit(solution)/shard_map/all_gather | solution.py:1261
  101.7 1.1 copy-start.24
  101.7 1.1 copy-start.20
  105.7 25.4 %copy-start.7 = (bf16[4,192,768]{2,1,0:T(8,128)(2,1)S(1)}, bf16[4,192,768]{2,1,0:T(8,128)(2,1)}, u32[]{:S(2)}) copy-start(bf16[4,192,768]{2,1,0:T(8,128)(2,1)} %get-tuple-element.48) | copy-start | bytes 3538948
  132.7 0.8 copy-start.19
  132.7 0.8 copy-start.21
  133.0 1.4 copy-start.2
  196.3 0.7 copy-start.22
  196.3 144.5 %reduce-scatter.2.cloned.1.call-start = ((), (), s32[]{:S(2)}) async-start(), calls=%async_computation.4 | async-start | bytes 7077888 | tf_op jit(solution)/shard_map/reduce_scatter | solution.py:1314
  237.2 1.3 copy-start.8
  267.2 1.0 copy-start.12
  267.2 5.9 %copy-start.3 = (bf16[1,256,768]{2,1,0:T(8,128)(2,1)S(1)}, bf16[1,256,768]{2,1,0:T(8,128)(2,1)}, u32[]{:S(2)}) copy-start(bf16[1,256,768]{2,1,0:T(8,128)(2,1)} %copy-done.2) | copy-start | bytes 1179652
  269.1 4.3 copy-start.13
  348.3 2.7 copy-start.15
  351.0 1.0 slice-start
  356.2 2.5 copy-start.11
  356.2 2.6 copy-start.16
  357.1 1.6 copy-start.17
  358.7 2.2 copy-start.6
  424.0 2.7 copy-start.9
  424.1 3.5 copy-start.18
  424.1 5.4 %copy-start.14 = (f32[256,768]{1,0:T(8,128)S(1)}, f32[256,768]{1,0:T(8,128)}, u32[]{:S(2)}) copy-start(f32[256,768]{1,0:T(8,128)} %get-tuple-element.68) | copy-start | bytes 2359300
  431.5 12.6 %copy-start.1 = (f32[768,12]{0,1:T(8,128)S(1)}, f32[768,12]{0,1:T(8,128)}, u32[]{:S(2)}) copy-start(f32[768,12]{0,1:T(8,128)} %param.22) | copy-start | bytes 110596
Sparse Core Ops, SparseCore 0:
  45.4 46.8 all-gather.3
  97.3 70.4 all-gather.5
  196.4 70.6 all-gather.7
  270.4 61.7 reduce-scatter.1

commit v5 on v4

--- a/solution.py
+++ b/solution.py
@@ -360,21 +360,84 @@
 
 def gather_weights(weight, count, ctx_count):
     rows, width = weight.shape
-
-    def kernel(source, target, local, send, recv):
+    chips = ctx_count // 2
+    parts = chips if chips == 4 and width % (128 * chips) == 0 else 1
+    half, share = rows // 2, width // parts
+
+    def kernel(source, target, send, recv):
         copies = Copies(send, recv)
         rank = lax.axis_index("fsdp")
-        meet(line_peers(count) + plane_peers(ctx_count)[:1])
-        keep = pltpu.make_async_copy(source, target.at[rank], local)
-        keep.start()
-        block = SharedBlock(copies, source, target, count, ctx_count)
-        together(block.stream)
-        block.wait()
-        keep.wait()
+        place, core, chip, _, sibling = own_place(ctx_count)
+        span = pl.ds(pl.multiple_of(core * half, math.gcd(half, 256)), half)
+        meet(
+            (ring_peers("fsdp", count) if parts > 1 else line_peers(count))
+            + plane_peers(ctx_count)[:1]
+            + (ring_peers("ctx", ctx_count, 2) if parts > 1 else [])
+        )
+
+        def held(origin, part):
+            return target.at[origin, span, pl.ds(pl.multiple_of(part * share, 128), share)]
+
+        mine = chip if parts > 1 else 0
+        received, forwarded = [], []
+
+        def hand(allowed, ref):
+            copy = copies.make(ref, ref, {"ctx": sibling})
+
+            @pl.when(allowed)
+            def _():
+                copy.start()
+
+            forwarded.append((allowed, copy))
+
+        def arrived(allowed, origin, ref):
+            for step in range(1, parts):
+                copy = copies.make(ref, ref, {"ctx": lax.rem(place + 2 * step, ctx_count)})
+
+                @pl.when(allowed)
+                def _():
+                    copy.start()
+
+                received.append((allowed, origin, lax.rem(chip + chips - step, chips), copy))
+            hand(allowed, ref)
+
+        if parts > 1:
+            pushes = []
+            for step in range(1, count):
+                copy = copies.make(
+                    source.at[span, pl.ds(pl.multiple_of(mine * share, 128), share)],
+                    held(rank, mine),
+                    {"fsdp": lax.rem(rank + step, count)},
+                )
+                copy.start()
+                pushes.append(copy)
+            target[rank] = source[...]
+            for step, copy in enumerate(pushes, 1):
+                copy.wait()
+                origin = lax.rem(rank + count - step, count)
+                arrived(rank >= 0, origin, held(origin, mine))
+        else:
+            target[rank] = source[...]
+            together(
+                line_gather(copies, held(rank, mine), lambda i: held(i, mine), count, arrived)
+            )
+        for allowed, origin, part, copy in received:
+
+            @pl.when(allowed)
+            def _():
+                copy.wait()
+
+            hand(allowed, held(origin, part))
+        for allowed, copy in forwarded:
+
+            @pl.when(allowed)
+            def _():
+                copy.wait()
 
     (full,) = remote_call(
         kernel, "weights", [struct((count, rows, width), weight.dtype)], [weight],
-        [pl.ANY], [pl.ANY], [pltpu.SemaphoreType.DMA], 4 * count, count * rows * width * 4,
+        [pltpu.VMEM], [pltpu.VMEM], [], 2 * count + 4 * count * (2 * parts - 1),
+        count * rows * width * 4,
     )
     return full.reshape(count * rows, width)
 
@@ -417,7 +480,7 @@
     results += [struct((count,) + w.shape, w.dtype) for w in weights]
     gathered, *full = remote_call(
         kernel, "keys", results, [block, *weights],
-        [pl.ANY] * (1 + len(weights)), [pl.ANY] * (1 + len(weights)),
+        [pltpu.VMEM] * (1 + len(weights)), [pl.ANY] * (1 + len(weights)),
         [pltpu.SemaphoreType.DMA((1 + len(weights),))],
         16 + 2 * ctx_count + 4 * count * len(weights),
         ctx_count * rows * width * 4,
@@ -448,7 +511,7 @@
     return remote_call(
         kernel, "rows",
         [struct((count,) + block.shape, block.dtype), struct((count,) + notes.shape, notes.dtype)],
-        [block, notes], [pl.ANY] * 2, [pl.ANY] * 2, [pltpu.SemaphoreType.DMA((2,))],
+        [block, notes], [pltpu.VMEM] * 2, [pl.ANY] * 2, [pltpu.SemaphoreType.DMA((2,))],
         4 * count, count * block.size * 4,
     )
 
@@ -731,7 +794,7 @@
         in_specs=in_specs,
         out_specs=out_specs,
         scratch_shapes=scratch,
-        compiler_params=pltpu.CompilerParams(vmem_limit_bytes=VMEM_LIMIT),
+        compiler_params=pltpu.CompilerParams(vmem_limit_bytes=60 * 1024 * 1024),
         cost_estimate=pl.CostEstimate(flops=flops, bytes_accessed=cost, transcendentals=0),
         name=name,
     )(*operands)
@@ -840,6 +903,8 @@
     room = pieces * capacity + tile
     batch = max(d for d in range(1, own + 1) if own % d == 0 and (d == 1 or d * room * width * 4 <= 30 << 20))
     low = jnp.bfloat16
+    group = 4
+    steps = pieces // group
 
     def kernel(start, count, routed, block, note, w, grads, final, rows, grad_rows, ends):
         turn, step = pl.program_id(0), pl.program_id(1)
@@ -850,42 +915,41 @@
             for j in range(batch):
                 ends[j] = 0
 
-        piece = jnp.minimum(step, pieces - 1)
-        numbers = [count[piece * experts + expert + j] for j in range(batch)]
-
-        @pl.when((step < pieces) & (sum(numbers) > 0))
+        for part in range(group):
+            piece = jnp.minimum(step * group + part, pieces - 1)
+            numbers = [count[piece * experts + expert + j] for j in range(batch)]
+
+            @pl.when((step < steps) & (sum(numbers) > 0))
+            def _():
+                slots = (
+                    lax.broadcasted_iota(jnp.int32, (batch * capacity, piece_len), 0)
+                    + expert * capacity
+                ).astype(jnp.float32)
+                first = note[part, 0:1, :] == slots
+                second = note[part, 1:2, :] == slots
+                gate = jnp.sum(
+                    jnp.where(first, note[part, 2:3, :], jnp.where(second, note[part, 3:4, :], 0.0)),
+                    axis=1,
+                    keepdims=True,
+                )
+                hot = jnp.where(first | second, 1.0, 0.0).astype(low)
+                taken = product(hot, routed[part]).astype(low)
+                grad_out = (gate * product(hot, block[part])).astype(low)
+                for j in range(batch):
+                    place = pl.ds(pl.multiple_of(ends[j], 16), capacity)
+                    span = slice(j * capacity, (j + 1) * capacity)
+                    rows[j, place, :] = taken[span]
+                    grad_rows[j, place, :] = grad_out[span]
+                    ends[j] += (numbers[j] + 15) // 16 * 16
+
+        @pl.when(step >= steps)
         def _():
-            slots = (
-                lax.broadcasted_iota(jnp.int32, (batch * capacity, piece_len), 0)
-                + expert * capacity
-            ).astype(jnp.float32)
-            first = note[0, 0:1, :] == slots
-            second = note[0, 1:2, :] == slots
-            gate = jnp.sum(
-                jnp.where(first, note[0, 2:3, :], 0.0) + jnp.where(second, note[0, 3:4, :], 0.0),
-                axis=1,
-                keepdims=True,
-            )
-            hot = (jnp.where(first, 1.0, 0.0) + jnp.where(second, 1.0, 0.0)).astype(low)
-            taken = product(hot, routed[0]).astype(low)
-            grad_out = (gate * product(hot, block[0])).astype(low)
-            for j in range(batch):
-                place = pl.ds(pl.multiple_of(ends[j], 16), capacity)
-                span = slice(j * capacity, (j + 1) * capacity)
-                rows[j, place, :] = taken[span]
-                grad_rows[j, place, :] = grad_out[span]
-                ends[j] += (numbers[j] + 15) // 16 * 16
-
-        @pl.when(step >= pieces)
-        def _():
-            j = jnp.maximum(step - pieces, 0)
+            j = jnp.maximum(step - steps, 0)
             end = pl.multiple_of(ends[j], 16)
             rest = pl.ds(end, tile)
             rows[j, rest, :] = jnp.zeros((tile, width), low)
             grad_rows[j, rest, :] = jnp.zeros((tile, width), low)
-            final[...] = jnp.zeros_like(final)
-
-            def one_tile(index, _):
+            def terms(index):
                 place = pl.ds(pl.multiple_of(index * tile, tile), tile)
                 x = rows[j, place, :]
                 grad_out = grad_rows[j, place, :]
@@ -899,27 +963,36 @@
                     grad_hidden * up_proj * sigmoid * (1.0 + gate_proj * (1.0 - sigmoid))
                 ).astype(low)
                 grad_up_proj = (grad_hidden * silu).astype(low)
-                final[0, 0] += product(grad_gate_proj, x, 0, 0)
-                final[0, 1] += product(grad_up_proj, x, 0, 0)
-                final[0, 2] += product(hidden, grad_out, 0, 0)
+                return (
+                    product(grad_gate_proj, x, 0, 0),
+                    product(grad_up_proj, x, 0, 0),
+                    product(hidden, grad_out, 0, 0),
+                )
+
+            for k, term in enumerate(terms(0)):
+                final[0, k] = term
+
+            def one_tile(index, _):
+                for k, term in enumerate(terms(index)):
+                    final[0, k] += term
                 return 0
 
-            lax.fori_loop(0, (end + tile - 1) // tile, one_tile, 0)
+            lax.fori_loop(1, (end + tile - 1) // tile, one_tile, 0)
             grads[...] = final[...].astype(low)
 
     def piece_block(shape):
         return pl.BlockSpec(
-            (1,) + shape[1:], lambda turn, step, *_: (jnp.minimum(step, pieces - 1), 0, 0)
+            (group,) + shape[1:], lambda turn, step, *_: (jnp.minimum(step, steps - 1), 0, 0)
         )
 
     def local(turn, step):
-        return turn * batch + jnp.maximum(step - pieces, 0)
+        return turn * batch + jnp.maximum(step - steps, 0)
 
     return pl.pallas_call(
         kernel,
         grid_spec=pltpu.PrefetchScalarGridSpec(
             num_scalar_prefetch=2,
-            grid=(own // batch, pieces + batch),
+            grid=(own // batch, steps + batch),
             in_specs=[
                 piece_block(routed_rows.shape),
                 piece_block(block_rows.shape),
@@ -948,7 +1021,7 @@
             struct((own, 3, units, width), low),
             struct((experts, 3, units, width), jnp.float32),
         ],
-        compiler_params=pltpu.CompilerParams(vmem_limit_bytes=VMEM_LIMIT),
+        compiler_params=pltpu.CompilerParams(vmem_limit_bytes=60 * 1024 * 1024),
         cost_estimate=pl.CostEstimate(
             flops=12 * own * pieces * capacity * units * width // 2,
             bytes_accessed=routed_rows.size * 4 + weights.size * 2,
@@ -978,7 +1051,7 @@
         ),
         out_shape=struct(final.shape, jnp.float32),
         input_output_aliases={2: 0},
-        compiler_params=pltpu.CompilerParams(vmem_limit_bytes=VMEM_LIMIT),
+        compiler_params=pltpu.CompilerParams(vmem_limit_bytes=60 * 1024 * 1024),
         name="other_gradients",
     )(first, received, final)
 
@@ -994,19 +1067,105 @@
     return [lane < HEAD_DIM, lane >= HEAD_DIM]
 
 
-def attention_forward(places, queries, pairs):
-    rows, width = queries.shape
+def turn_halves(values, cosines, sines):
+    lane = lax.broadcasted_iota(jnp.int32, values.shape, 1)
+    half = HEAD_DIM // 2
+    swapped = jnp.where(
+        lax.rem(lane, HEAD_DIM) < half,
+        pltpu.roll(values, 2 * HEAD_DIM - half, 1),
+        pltpu.roll(values, half, 1),
+    )
+    return values * cosines + swapped * sines
+
+
+def project_keys(tokens, gain, weights, turns):
+    rows, width = tokens.shape
+    tile = 2 * HEAD_DIM
+
+    def kernel(token, gain_row, weight, turn, normed, pairs):
+        x = token[...].astype(jnp.float32)
+        scaling = lax.rsqrt(jnp.mean(x * x, axis=1, keepdims=True) + EPSILON)
+        normed[...] = (x * scaling * gain_row[...]).astype(jnp.bfloat16)
+        for i in range(2 * width // tile):
+            span = slice(i * tile, (i + 1) * tile)
+            values = product(normed[...], weight[:, span])
+            if i < width // tile:
+                values = turn_halves(values, turn[0], turn[1])
+            pairs[:, span] = values.astype(jnp.bfloat16)
+
+    return pl.pallas_call(
+        kernel,
+        out_shape=[struct((rows, width), jnp.bfloat16), struct((rows, 2 * width), jnp.bfloat16)],
+        compiler_params=pltpu.CompilerParams(vmem_limit_bytes=VMEM_LIMIT),
+        name="project_keys",
+    )(tokens, gain, weights, turns)
+
+
+def projection_gradients(
+    pair_grad, query_grad, normed, tokens, gain, turns, full_query, full_kv, mixed, grad_attention,
+    grad_residual,
+):
+    rows, width = tokens.shape
+    tile = 2 * HEAD_DIM
+    low = jnp.bfloat16
+
+    def kernel(pair, query, normed_ref, token, gain_row, turn, w_query, w_kv, mix, attention,
+               residual, weight_grad, token_grad, gain_grad, projected):
+        for i in range(width // tile):
+            span = slice(i * tile, (i + 1) * tile)
+            projected[:, span] = turn_halves(query[:, span], turn[0], -turn[1]).astype(low)
+            keys = pair[0:rows, span].astype(jnp.float32)
+            projected[:, width + i * tile : width + (i + 1) * tile] = turn_halves(
+                keys, turn[0], -turn[1]
+            ).astype(low)
+        projected[:, 2 * width :] = pair[rows:, :]
+        for i in range(3):
+            span = slice(i * width, (i + 1) * width)
+            weight_grad[:, span] = product(normed_ref[...], projected[:, span], 0, 0).astype(low)
+        weight_grad[:, 3 * width :] = product(mix[...], attention[...], 0, 0).astype(low)
+        grad_normed = product(projected[:, :width], w_query[...], 1, 1) + product(
+            projected[:, width:], w_kv[...], 1, 1
+        )
+        x = token[...].astype(jnp.float32)
+        scaling = lax.rsqrt(jnp.mean(x * x, axis=1, keepdims=True) + EPSILON)
+        scaled = x * scaling
+        gain_grad[...] = jnp.broadcast_to(
+            jnp.sum(grad_normed * scaled, axis=0, keepdims=True), gain_grad.shape
+        )
+        grad_hat = grad_normed * gain_row[...]
+        inner = jnp.mean(grad_hat * x, axis=1, keepdims=True)
+        token_grad[...] = residual[...] + scaling * grad_hat - scaled * (scaling * scaling * inner)
+
+    return pl.pallas_call(
+        kernel,
+        out_shape=[
+            struct((width, 4 * width), low),
+            struct((rows, width), jnp.float32),
+            struct((8, width), jnp.float32),
+        ],
+        scratch_shapes=[pltpu.VMEM((rows, 3 * width), low)],
+        compiler_params=pltpu.CompilerParams(vmem_limit_bytes=VMEM_LIMIT),
+        name="projection_gradients",
+    )(pair_grad, query_grad, normed, tokens, gain, turns, full_query, full_kv, mixed,
+      grad_attention, grad_residual)
+
+
+def attention_forward(places, normed, w_query, turns, pairs):
+    rows, width = normed.shape
     keys = pairs.shape[0]
     tile = 2 * HEAD_DIM
     tiles = width // tile
 
-    def kernel(place, query, key, value, mixed, sums, bias):
+    def kernel(place, normed_ref, weight, turn, key, value, mixed, query, sums, bias):
         step = pl.program_id(0)
 
         @pl.when(step == 0)
         def _():
             bias[...] = score_bias(place[0], place[1], rows, keys)
 
+        query[...] = turn_halves(
+            product(normed_ref[...], weight[...]), turn[0], turn[1]
+        ).astype(query.dtype)
         own_masks = head_masks((rows, tile))
         scaled = query[...] * HEAD_DIM**-0.5
         outs = []
@@ -1027,23 +1186,30 @@
             num_scalar_prefetch=1,
             grid=(tiles,),
             in_specs=[
-                pl.BlockSpec((rows, tile), lambda i, _: (0, i)),
+                whole_block((rows, width)),
+                pl.BlockSpec((width, tile), lambda i, _: (0, i)),
+                whole_block(turns.shape),
                 pl.BlockSpec((keys, tile), lambda i, _: (0, i)),
                 pl.BlockSpec((keys, tile), lambda i, _: (0, i + tiles)),
             ],
             out_specs=[
                 pl.BlockSpec((rows, tile), lambda i, _: (0, i)),
+                pl.BlockSpec((rows, tile), lambda i, _: (0, i)),
                 pl.BlockSpec((1, 8, rows), lambda i, _: (i, 0, 0)),
             ],
             scratch_shapes=[pltpu.VMEM((keys, rows), jnp.float32)],
         ),
-        out_shape=[struct((rows, width), jnp.bfloat16), struct((tiles, 8, rows), jnp.float32)],
-        compiler_params=pltpu.CompilerParams(vmem_limit_bytes=VMEM_LIMIT),
+        out_shape=[
+            struct((rows, width), jnp.bfloat16),
+            struct((rows, width), jnp.bfloat16),
+            struct((tiles, 8, rows), jnp.float32),
+        ],
+        compiler_params=pltpu.CompilerParams(vmem_limit_bytes=60 * 1024 * 1024),
         cost_estimate=pl.CostEstimate(
             flops=4 * rows * keys * width, bytes_accessed=pairs.size * 2, transcendentals=0
         ),
         name="attention",
-    )(places, queries, pairs, pairs)
+    )(places, normed, w_query, turns, pairs, pairs)
 
 
 def attention_backward(places, queries, pairs, sums, mixed, grad_mixed):
@@ -1112,7 +1278,7 @@
             struct((rows, width), jnp.float32),
             struct((pieces, 2, rows, width), low),
         ],
-        compiler_params=pltpu.CompilerParams(vmem_limit_bytes=VMEM_LIMIT),
+        compiler_params=pltpu.CompilerParams(vmem_limit_bytes=60 * 1024 * 1024),
         cost_estimate=pl.CostEstimate(
             flops=10 * rows * keys * width, bytes_accessed=pairs.size * 4, transcendentals=0
         ),
@@ -1134,26 +1300,12 @@
     return (grad_values, grad_gain)
 
 
-def rope_tables(positions, head_size):
+def rope_angles(positions, head_size):
     half_dim = head_size // 2
     frequency = jnp.exp(
         jnp.arange(half_dim, dtype=jnp.float32) * (-2.0 * math.log(10000.0) / head_size)
     )
-    angles = positions.astype(jnp.float32)[:, None] * frequency[None, :]
-    return (jnp.cos(angles)[:, None, :], jnp.sin(angles)[:, None, :])
-
-
-def rotate(values, cosine_table, sine_table):
-    half_dim = values.shape[-1] // 2
-    first_half = values[..., :half_dim]
-    second_half = values[..., half_dim:]
-    return jnp.concatenate(
-        [
-            first_half * cosine_table - second_half * sine_table,
-            second_half * cosine_table + first_half * sine_table,
-        ],
-        axis=-1,
-    )
+    return positions.astype(jnp.float32)[:, None] * frequency[None, :]
 
 
 def per_device(
@@ -1172,51 +1324,33 @@
     w_expert,
 ):
     groups, piece_len, model_width = tokens.shape
-    head_count = model_width // HEAD_DIM
-    part_heads = 2
-    part_count = head_count // part_heads
-    slot_len = piece_len * lax.axis_size("ctx")
     positions = lax.axis_index("ctx") * piece_len + jnp.arange(piece_len, dtype=jnp.int32)
-    key_positions = jnp.arange(slot_len, dtype=jnp.int32)
     live_rows = (positions[None, :] < lengths[:, None]).astype(jnp.float32)[..., None]
     experts = w_expert.shape[0]
     capacity = piece_len // 4
     slot_count = experts * capacity
-    split_shape = (groups, piece_len, head_count, HEAD_DIM)
     fsdp_count, ctx_count = lax.axis_size("fsdp"), lax.axis_size("ctx")
     full_kv = gather_weights(w_qkv[:, model_width:], fsdp_count, ctx_count)
     inputs = tokens.astype(jnp.float32)
     gain_one = gain_attn.astype(jnp.float32)
     gain_two = gain_moe.astype(jnp.float32)
-    normed_one, scale_one = normalize_rows(inputs, gain_one)
-    normed_one_low = normed_one.astype(jnp.bfloat16)
-    projected = jnp.einsum("gpd,de->gpe", normed_one_low, full_kv, preferred_element_type=jnp.float32)
-    cosine_table, sine_table = rope_tables(positions, HEAD_DIM)
-    key_local = (
-        rotate(projected[..., :model_width].reshape(split_shape), cosine_table, sine_table)
-        .astype(jnp.bfloat16)
-        .reshape(piece_len, model_width)
-    )
-    value_local = projected[0, :, model_width:].astype(jnp.bfloat16)
+    angles = rope_angles(positions, HEAD_DIM)
+    cosines, sines = jnp.cos(angles), jnp.sin(angles)
+    turns = jnp.stack(
+        [jnp.tile(cosines, (1, 4)), jnp.concatenate([-sines, sines, -sines, sines], axis=1)]
+    )
+    normed_one_low, own_pairs = project_keys(tokens[0], gain_one[None], full_kv, turns)
     cotangent_low = live_rows.astype(jnp.bfloat16) * cotangent
-    own_pairs = jnp.concatenate([key_local, value_local], axis=-1)
-    cotangent_low, own_pairs = lax.optimization_barrier((cotangent_low, own_pairs))
-    cotangent_rows = lax.all_gather(cotangent_low, "fsdp", axis=0, tiled=True)
     all_pairs, (full_query, full_out) = gather_keys(
         own_pairs, [w_qkv[:, :model_width], w_out], fsdp_count, ctx_count
     )
+    cotangent_rows = lax.all_gather(cotangent_low, "fsdp", axis=0, tiled=True)
     cotangent_rows, all_pairs = lax.optimization_barrier((cotangent_rows, all_pairs))
     slot_block = lax.all_gather(cotangent_rows, "ctx", axis=0, tiled=True)
-    queries = rotate(
-        jnp.einsum(
-            "gpd,de->gpe", normed_one_low, full_query, preferred_element_type=jnp.float32
-        ).reshape(split_shape),
-        cosine_table,
-        sine_table,
-    ).astype(jnp.bfloat16)
     places = jnp.stack([lengths[0], lax.axis_index("ctx") * piece_len]).astype(jnp.int32)
-    query_rows = queries.reshape(piece_len, model_width)
-    mixed_rows, score_sums = attention_forward(places, query_rows, all_pairs)
+    mixed_rows, query_rows, score_sums = attention_forward(
+        places, normed_one_low, full_query, turns, all_pairs
+    )
     mixed_low = mixed_rows[None]
     attention = jnp.einsum("gpd,de->gpe", mixed_low, full_out, preferred_element_type=jnp.float32)
     residual_sum = inputs + attention
@@ -1252,13 +1386,11 @@
     )
     routed_rows, all_notes = gather_rows(routed_low[0], notes, fsdp_count)
     expert_weights = w_expert.swapaxes(1, 2)
+    slot_block, routed_rows = lax.optimization_barrier((slot_block, routed_rows))
+    slot_routed = lax.all_gather(routed_rows, "ctx", axis=0, tiled=True)
     out_parts, grad_parts, dot_notes = expert_layers(
         routed_rows, cotangent_rows, all_notes, expert_weights
     )
-    slot_block, routed_rows, out_parts = lax.optimization_barrier(
-        (slot_block, routed_rows, out_parts)
-    )
-    slot_routed = lax.all_gather(routed_rows, "ctx", axis=0, tiled=True)
     ffn_grad, dot_sums, slot_notes = reduce_rows(
         grad_parts, dot_notes, all_notes, fsdp_count, ctx_count
     )
@@ -1296,9 +1428,6 @@
     grad_norm_two, grad_gain_two = normalize_back(residual_sum, scale_two, gain_two, grad_routed)
     grad_residual = grad_block + grad_norm_two
     grad_attention = grad_residual.astype(jnp.bfloat16)
-    grad_wout = jnp.einsum(
-        "gpd,gpe->de", mixed_low, grad_attention, preferred_element_type=jnp.float32
-    )
     grad_mixed = jnp.einsum(
         "gpe,de->gpd", grad_attention, full_out, preferred_element_type=jnp.float32
     ).astype(jnp.bfloat16)
@@ -1314,42 +1443,25 @@
     pair_grad = lax.psum_scatter(
         pair_grads.reshape(1, -1, model_width), "ctx", scatter_dimension=1, tiled=True
     )
-    pair_grad = pair_grad.astype(jnp.float32).reshape(2, piece_len, model_width)
-    key_grad, value_grad = pair_grad[:1], pair_grad[1:]
-    query_back = rotate(query_grad.reshape(split_shape), cosine_table, -sine_table).reshape(
-        groups, piece_len, model_width
-    )
-    key_back = rotate(key_grad.reshape(split_shape), cosine_table, -sine_table).reshape(
-        groups, piece_len, model_width
-    )
-    grad_projected = jnp.concatenate([query_back, key_back, value_grad], axis=-1).astype(
-        jnp.bfloat16
-    )
-    grad_wqkv = jnp.einsum(
-        "gpd,gpe->de", normed_one_low, grad_projected, preferred_element_type=jnp.float32
-    )
-    grad_normed_one = jnp.einsum(
-        "gpe,de->gpd",
-        grad_projected[..., :model_width],
+    weight_parts, grad_inputs, grad_gain_one = projection_gradients(
+        pair_grad[0],
+        query_grad,
+        normed_one_low,
+        tokens[0],
+        gain_one[None],
+        turns,
         full_query,
-        preferred_element_type=jnp.float32,
-    ) + jnp.einsum(
-        "gpe,de->gpd",
-        grad_projected[..., model_width:],
         full_kv,
-        preferred_element_type=jnp.float32,
-    )
-    grad_norm_one, grad_gain_one = normalize_back(inputs, scale_one, gain_one, grad_normed_one)
-    grad_inputs = grad_residual + grad_norm_one
-    weight_parts = (
-        jnp.concatenate([grad_wqkv, grad_wout], axis=-1)
-        .astype(jnp.bfloat16)
-        .reshape(fsdp_count, -1, 4 * model_width)
-    )
+        mixed_rows,
+        grad_attention[0],
+        grad_residual[0],
+    )
+    grad_inputs = grad_inputs[None]
+    weight_parts = weight_parts.reshape(fsdp_count, -1, 4 * model_width)
     few = experts + 4
     mixing_row = jnp.pad(grad_mixing.reshape(1, -1), ((0, 0), (0, model_width - few * few)))
     small = jnp.concatenate(
-        [grad_router.T, grad_const, grad_gain_one[None], grad_gain_two[None], mixing_row], axis=0
+        [grad_router.T, grad_const, grad_gain_one[:1], grad_gain_two[None], mixing_row], axis=0
     )
     small = jnp.pad(small, ((0, -small.shape[0] % 8), (0, 0)))
     weight_sum, small_sum, expert_grads, ffn_sum = reduce_weights(

time: 453 us -> 406 us (0.90)
  local copies, waits for them, and re-layouts: 31 us -> 12.1 us
  matrix products: 22.3 us -> 8.8 us
  Pallas kernels: 363 us -> 352 us
    pallas_call x5, Pallas kernels: 208 us -> 192 us  [remote_call(): pl.pallas_call(kernel, out_shape=results, in_specs=[pl.BlockSpec(memory_s...]
    dot_general x6 -> x0, matrix products: 13.7 us -> none  [the longest x1 2.94 us: per_device(): jnp.einsum('gpe,de->gpd', grad_projected[..., model_width:], full_kv, pre...]
    pallas_call x0 -> x2, Pallas kernels: none -> 12.2 us  [the longest x1 8 us: projection_gradients(): pl.pallas_call(kernel, out_shape=[struct((width, 4 * width), low), struct...]
    all_gather x1, waiting for transfers between devices: 0.01 us -> 8.77 us  [per_device(): slot_block = lax.all_gather(cotangent_rows, 'ctx', axis=0, tiled=True)]
    all_gather x1, waiting for transfers between devices: 5.22 us -> 0.02 us  [per_device(): slot_routed = lax.all_gather(routed_rows, 'ctx', axis=0, tiled=True)]
  transfers between devices with their start and end apart: 4 -> 4, of which waited for: 1 -> 1; matrix products, arithmetic and copies ran while one was open for 6% -> 5% of each run, Pallas kernels for 58% -> 67%
where the time goes in v5:
time: 406 us; the launch traced here: 407 us
  Pallas kernels  352 us (87%)
  between operations  14.9 us (4%)
  local copies, waits for them, and re-layouts  12.1 us (3%)
  other arithmetic  9.48 us (2%)
  waiting for transfers between devices  8.88 us (2%)
  matrix products  8.8 us (2%)
    pallas_call x5, Pallas kernels, remote_call(): pl.pallas_call(kernel, out_shape=results, in_specs=[pl.BlockSpec(memory_s...  192 us
    pallas_call x1, Pallas kernels, expert_gradients(): pl.pallas_call(kernel, grid_spec=pltpu.PrefetchScalarGridSpec(num_scalar_...  62.6 us
    pallas_call x1, Pallas kernels, local_call(): pl.pallas_call(kernel, grid=grid, out_shape=results, in_specs=in_specs, o...  28.7 us
    pallas_call x1, Pallas kernels, attention_backward(): pl.pallas_call(kernel, grid_spec=pltpu.PrefetchScalarGridSpec(num_scalar_...  22.1 us
    pallas_call x1, Pallas kernels, attention_forward(): pl.pallas_call(kernel, grid_spec=pltpu.PrefetchScalarGridSpec(num_scalar_...  22 us
    pallas_call x1, Pallas kernels, other_gradients(): pl.pallas_call(kernel, grid_spec=pltpu.PrefetchScalarGridSpec(num_scalar_...  12.6 us
    all_gather x1, waiting for transfers between devices, per_device(): slot_block = lax.all_gather(cotangent_rows, 'ctx', axis=0, tiled=True)  8.77 us
  transfers between devices with their start and end apart: 4, of which 1 were waited for; matrix products, arithmetic and copies ran while one was open for 5% of the time, Pallas kernels for 67%

profile of v5, /device:TPU:0, one launch (start us, length us, event | category | flops | bytes accessed | tf_op | source)
XLA Modules:
  0.0 406.8 jit_solution(17282061101773207512)
XLA Ops:
  8.0 1.8 broadcast_multiply_fusion
  9.9 0.0 all-gather.6.cloned.1.call-start
  9.9 0.9 slice.51.source
  10.8 0.7 slice.52.refs_1_
  11.5 0.6 reshape.476.gain_row
  12.1 25.6 %weights.1 = bf16[4,192,1536]{2,1,0:T(8,128)(2,1)} custom-call(bf16[192,1536]{1,0:T(8,128)(2,1)} %slice.51.source), custom_call_target="tpu_custom_call" | custom-call | bytes 4718592 | tf_op jit(solution)/shard_map/weights/pallas_call | solution.py:315
  37.7 0.5 multiply_cosine_fusion
  38.3 0.1 copy.44
  38.4 0.1 copy.45
  38.5 0.2 maximum_bitcast_fusion
  38.6 0.7 pad_maximum_fusion.turn
  39.4 4.2 %project_keys.1 = (bf16[256,768]{1,0:T(8,128)(2,1)}, bf16[256,1536]{1,0:T(8,128)(2,1)}) custom-call(bf16[256,768]{1,0:T(8,128)(2,1)} %bitcast.140, f32[1,768]{1,0:T(1,128)} %reshape.476.gain_row, bf16[768,1536]{1,0:T(8,128)(2,1)} %bitcast.131, f32[2,256,128]{2,1,0:T(8,128)} %pad_maximum_fusion.turn), custom_call_target="tpu_custom_call" | custom-call | tf_op jit(solution)/shard_map/project_keys/pallas_call | solution.py:1096
  43.5 35.8 %keys.1 = (bf16[8,256,1536]{2,1,0:T(8,128)(2,1)}, bf16[4,192,768]{2,1,0:T(8,128)(2,1)}, bf16[4,192,768]{2,1,0:T(8,128)(2,1)}) custom-call(bf16[256,1536]{1,0:T(8,128)(2,1)} %get-tuple-element.46.refs_0_, bf16[192,768]{1,0:T(8,128)(2,1)} %slice.52.refs_1_, bf16[192,768]{1,0:T(8,128)(2,1)} %refs_2_.1), custom_call_target="tpu_custom_call" | custom-call | bytes 12582912 | tf_op jit(solution)/shard_map/keys/pallas_call | solution.py:315
  79.4 0.0 all-gather.8.cloned.1.call-start
  79.5 0.1 multiply_reduce_fusion.4
  79.6 0.2 copy.46
  79.8 0.1 copy.47
  79.9 1.1 reduce-window.6
  81.0 0.1 copy.48
  81.2 0.2 slice_reduce_fusion
  81.4 0.2 fusion.15
  81.6 0.1 reduce_sum.148
  81.7 0.1 copy.49
  81.8 0.6 pad_add_fusion.place
  82.4 22.0 %attention.1 = (bf16[256,768]{1,0:T(8,128)(2,1)}, bf16[256,768]{1,0:T(8,128)(2,1)}, f32[6,8,256]{2,1,0:T(8,128)}) custom-call(s32[2]{0:T(128)} %pad_add_fusion.place, bf16[256,768]{1,0:T(8,128)(2,1)} %get-tuple-element.45.normed_ref, bf16[768,768]{1,0:T(8,128)(2,1)} %bitcast.138, f32[2,256,128]{2,1,0:T(8,128)} %pad_maximum_fusion.turn, ...), custom_call_target="tpu_custom_call" | custom-call | flops 1610612736 | bytes 6291456 | tf_op jit(solution)/shard_map/attention/pallas_call | solution.py:1183
  104.5 1.6 multiply_reduce_fusion.2
  106.1 0.3 fusion.8
  106.5 0.5 fusion.33
  106.9 0.2 convolution_add_fusion
  107.2 0.6 select_maximum_fusion.own_notes
  107.8 34.2 %rows.1 = (bf16[4,256,768]{2,1,0:T(8,128)(2,1)}, f32[4,8,256]{2,1,0:T(8,128)}) custom-call(bf16[256,768]{1,0:T(8,128)(2,1)} %bitcast.133, f32[8,256]{1,0:T(8,128)} %select_maximum_fusion.own_notes), custom_call_target="tpu_custom_call" | custom-call | bytes 3145728 | tf_op jit(solution)/shard_map/rows/pallas_call | solution.py:315
  142.0 8.8 %all-gather.6.cloned.1.call-done.block = bf16[32,256,768]{2,1,0:T(8,128)(2,1)} async-done(((bf16[4,256,768]{2,1,0:T(8,128)(2,1)}), bf16[32,256,768]{2,1,0:T(8,128)(2,1)}) %all-gather.6.cloned.1.call-update) | async-done | bytes 12582928 | tf_op jit(solution)/shard_map/all_gather | solution.py:1349
  150.8 0.2 reduce-scatter.2.cloned.1.call-start
  151.1 0.5 fusion.11
  151.6 0.1 fusion.28
  151.7 28.7 %experts.1 = (bf16[4,256,768]{2,1,0:T(8,128)(2,1)}, bf16[4,256,768]{2,1,0:T(8,128)(2,1)}, f32[4,8,256]{2,1,0:T(8,128)}) custom-call(bf16[4,256,768]{2,1,0:T(8,128)(2,1)} %get-tuple-element.54.routed, bf16[4,256,768]{2,1,0:T(8,128)(2,1)} %all-gather.4.cloned.1.call-done.block, f32[4,8,256]{2,1,0:T(8,128)} %get-tuple-element.55.note.own, ...), custom_call_target="tpu_custom_call" | custom-call | flops 9663676416 | bytes 18874368 | tf_op jit(solution)/shard_map/experts/pallas_call | solution.py:790
  180.4 36.0 %row_sums.1 = (f32[256,768]{1,0:T(8,128)}, f32[8,256]{1,0:T(8,128)}, f32[8,4,8,256]{3,2,1,0:T(8,128)}) custom-call(bf16[4,256,768]{2,1,0:T(8,128)(2,1)} %get-tuple-element.56.given, f32[4,8,256]{2,1,0:T(8,128)} %get-tuple-element.57.given_notes, f32[4,8,256]{2,1,0:T(8,128)} %get-tuple-element.55.note.own), custom_call_target="tpu_custom_call" | custom-call | bytes 3145728 | tf_op jit(solution)/shard_map/row_sums/pallas_call | solution.py:315
  216.5 1.0 fusion.18
  217.4 0.7 convert_element_type.92.count
  218.1 0.7 multiply_reduce_fusion.7
  218.9 2.3 multiply_reduce_fusion
  221.2 1.2 convert_bitcast_fusion
  222.3 1.2 convolution_convert_fusion.grad_out
  223.6 22.1 %attention_back.1 = (f32[256,768]{1,0:T(8,128)}, bf16[8,2,256,768]{3,2,1,0:T(8,128)(2,1)}) custom-call(s32[2]{0:T(128)} %pad_add_fusion.place, bf16[256,768]{1,0:T(8,128)(2,1)} %get-tuple-element.59.query, bf16[2048,1536]{1,0:T(8,128)(2,1)} %bitcast.129, bf16[2048,1536]{1,0:T(8,128)(2,1)} %bitcast.130, f32[6,8,256]{2,1,0:T(8,128)} %get-tuple-element.60.total, ...), custom_call_target="tpu_custom_call" | custom-call | flops 4026531840 | bytes 12582912 | tf_op jit(solution)/shard_map/attention_back/pallas_call | solution.py:1258
  245.7 0.6 fusion.9
  246.3 0.1 convolution_bitcast_fusion.4
  246.4 0.1 copy.50
  246.5 0.1 reshape.475
  246.7 0.1 convolution_bitcast_fusion.3
  246.8 0.6 copy.51
  247.4 0.3 fusion.31
  247.7 62.6 %expert_gradients.1 = (bf16[4,3,512,768]{3,2,1,0:T(8,128)(2,1)}, f32[8,3,512,768]{3,2,1,0:T(8,128)}) custom-call(s32[1]{0:T(128)} %bitcast.38.start, s32[256]{0:T(256)} %convert_element_type.92.count, bf16[32,256,768]{2,1,0:T(8,128)(2,1)} %all-gather.8.cloned.1.call-done.routed, bf16[32,256,768]{2,1,0:T(8,128)(2,1)} %all-gather.6.cloned.1.call-done.block, ...), custom_call_target="tpu_custom_call" | custom-call | flops 19327352832 | bytes 44040192 | tf_op jit(solution)/shard_map/expert_gradients/pallas_call | solution.py:991
  310.3 8.0 %projection_gradients.1 = (bf16[768,3072]{1,0:T(8,128)(2,1)}, f32[256,768]{1,0:T(8,128)}, f32[8,768]{1,0:T(8,128)}) custom-call(bf16[512,768]{1,0:T(8,128)(2,1)} %bitcast.146, f32[256,768]{1,0:T(8,128)} %get-tuple-element.65.query, bf16[256,768]{1,0:T(8,128)(2,1)} %get-tuple-element.45.normed_ref, bf16[256,768]{1,0:T(8,128)(2,1)} %bitcast.141, ...), custom_call_target="tpu_custom_call" | custom-call | tf_op jit(solution)/shard_map/projection_gradients/pallas_call | solution.py:1139
  318.3 0.7 slice.60
  319.1 0.6 pad.14.given_small
  319.7 60.5 %totals.1 = (bf16[192,3072]{1,0:T(8,128)(2,1)}, f32[24,768]{1,0:T(8,128)}, bf16[4,3,512,768]{3,2,1,0:T(8,128)(2,1)}, f32[256,768]{1,0:T(8,128)}) custom-call(bf16[4,192,3072]{2,1,0:T(8,128)(2,1)} %bitcast.135, f32[24,768]{1,0:T(8,128)} %pad.14.given_small, bf16[4,3,512,768]{3,2,1,0:T(8,128)(2,1)} %get-tuple-element.71.half_ref, ...), custom_call_target="tpu_custom_call" | custom-call | bytes 18874368 | tf_op jit(solution)/shard_map/totals/pallas_call | solution.py:315
  380.2 2.6 slice.73
  382.9 0.9 slice.74
  383.7 0.6 slice_reduce_fusion.1
  384.3 0.6 slice_bitcast_fusion
  385.0 0.6 slice.67
  385.6 1.4 fusion.7
  387.0 0.7 reshape_squeeze.3
  387.6 12.6 %other_gradients.1 = f32[8,3,512,768]{3,2,1,0:T(8,128)} custom-call(s32[1]{0:T(128)} %bitcast.43.start, bf16[4,3,512,768]{3,2,1,0:T(8,128)(2,1)} %get-tuple-element.77.given, f32[8,3,512,768]{3,2,1,0:T(8,128)} %get-tuple-element.78._), custom_call_target="tpu_custom_call", output_to_operand_aliasing={{}: (2, {})} | custom-call | tf_op jit(solution)/shard_map/other_gradients/pallas_call | solution.py:1041
  (69 shorter events, 0.6 us)
Async XLA Ops:
  7.2 99.3 %copy-start = (f32[768,12]{0,1:T(8,128)S(1)}, f32[768,12]{0,1:T(8,128)}, u32[]{:S(2)}) copy-start(f32[768,12]{0,1:T(8,128)} %param.22) | copy-start | bytes 110596
  7.2 2.7 copy-start.9
  7.2 4.3 %copy-start.17 = (bf16[768]{0:T(1024)(128)(2,1)S(1)}, bf16[768]{0:T(1024)(128)(2,1)}, u32[]{:S(2)}) copy-start(bf16[768]{0:T(1024)(128)(2,1)} %param.20) | copy-start | bytes 4612
  7.2 72.1 %all-gather.4.cloned.1.call-start = ((), (), s32[]{:S(2)}) async-start(), calls=%async_computation.1 | async-start | bytes 1966080 | tf_op jit(solution)/shard_map/all_gather | solution.py:1347
  9.9 140.9 %all-gather.6.cloned.1.call-start = ((), (), s32[]{:S(2)}) async-start(), calls=%async_computation.2 | async-start | bytes 14155776 | tf_op jit(solution)/shard_map/all_gather | solution.py:1349
  43.5 35.9 %copy-start.16 = (bf16[768]{0:T(1024)(128)(2,1)S(1)}, bf16[768]{0:T(1024)(128)(2,1)}, u32[]{:S(2)}) copy-start(bf16[768]{0:T(1024)(128)(2,1)} %param.21) | copy-start | bytes 4612
  43.5 35.9 %copy-start.13 = (s32[1,256,2]{1,2,0:T(2,128)S(1)}, s32[1,256,2]{1,2,0:T(2,128)}, u32[]{:S(2)}) copy-start(s32[1,256,2]{1,2,0:T(2,128)} %param.15) | copy-start | bytes 6148
  79.4 166.3 %all-gather.8.cloned.1.call-start = ((), (), s32[]{:S(2)}) async-start(), calls=%async_computation.3 | async-start | bytes 14155776 | tf_op jit(solution)/shard_map/all_gather | solution.py:1390
  82.4 22.0 %copy-start.5 = (bf16[4,192,768]{2,1,0:T(8,128)(2,1)S(1)}, bf16[4,192,768]{2,1,0:T(8,128)(2,1)}, u32[]{:S(2)}) copy-start(bf16[4,192,768]{2,1,0:T(8,128)(2,1)} %get-tuple-element.51) | copy-start | bytes 3538948
  82.4 22.1 %copy-start.7 = (bf16[1,256,768]{2,1,0:T(8,128)(2,1)S(1)}, bf16[1,256,768]{2,1,0:T(8,128)(2,1)}, u32[]{:S(2)}) copy-start(bf16[1,256,768]{2,1,0:T(8,128)(2,1)} %param.13) | copy-start | bytes 1179652
  104.4 1.7 copy-start.4
  106.1 0.9 copy-start.12
  106.1 0.8 copy-start.14
  106.4 1.4 copy-start.2
  106.4 44.6 %copy-start.15 = (bf16[2,768]{1,0:T(2,128)(2,1)S(1)}, bf16[2,768]{1,0:T(2,128)(2,1)}, u32[]{:S(2)}) copy-start(bf16[2,768]{1,0:T(2,128)(2,1)} %param.24) | copy-start | bytes 9220
  150.8 159.5 %reduce-scatter.2.cloned.1.call-start = ((), (), s32[]{:S(2)}) async-start(), calls=%async_computation.4 | async-start | bytes 7077888 | tf_op jit(solution)/shard_map/reduce_scatter | solution.py:1443
  222.3 23.3 %copy-start.8 = (bf16[256,768]{1,0:T(8,128)(2,1)}, bf16[256,768]{1,0:T(8,128)(2,1)S(1)}, u32[]{:S(2)}) copy-start(bf16[256,768]{1,0:T(8,128)(2,1)S(1)} %get-tuple-element.132.attention) | copy-start | bytes 1179652
  245.7 1.8 copy-start.3
  380.2 2.7 copy-start.6
  380.2 3.5 copy-start.11
  380.2 5.4 %copy-start.10 = (f32[256,768]{1,0:T(8,128)S(1)}, f32[256,768]{1,0:T(8,128)}, u32[]{:S(2)}) copy-start(f32[256,768]{1,0:T(8,128)} %get-tuple-element.73) | copy-start | bytes 2359300
  387.6 12.6 %copy-start.1 = (f32[768,12]{0,1:T(8,128)S(1)}, f32[768,12]{0,1:T(8,128)}, u32[]{:S(2)}) copy-start(f32[768,12]{0,1:T(8,128)} %param.22) | copy-start | bytes 110596
Sparse Core Ops, SparseCore 0:
  10.2 42.6 all-gather.3
  79.5 71.2 all-gather.5
  152.7 73.0 all-gather.7
  245.8 60.2 reduce-scatter.1

commit v6 on v5

--- a/solution.py
+++ b/solution.py
@@ -183,6 +183,24 @@
         @pl.when(allowed)
         def _():
             copy.wait_send()
+
+
+def push_reduce(copies, part, landing, count, total):
+    rank = lax.axis_index("fsdp")
+    sent = []
+    for step in range(1, count):
+        peer = lax.rem(rank + step, count)
+        copy = copies.make(part(peer), landing.at[step - 1], {"fsdp": peer})
+        copy.start()
+        sent.append(copy)
+    yield
+    value = part(rank)[...].astype(jnp.float32)
+    for step, copy in enumerate(sent):
+        copy.wait_recv()
+        value = value + landing[step].astype(jnp.float32)
+    total[...] = value
+    for copy in sent:
+        copy.wait_send()
 
 
 def push_gather(copies, own, slot, axis, count, stride=1):
@@ -311,7 +329,7 @@
 
 
 def remote_call(kernel, name, results, operands, in_spaces, out_spaces, scratch, copies, cost):
-    ids = ("weights", "keys", "rows", "row_sums", "key_sums", "totals")
+    ids = ("weights", "keys", "rows", "row_sums", "pair_sums", "totals")
     return pl.pallas_call(
         kernel,
         out_shape=results,
@@ -358,8 +376,8 @@
                 copy.wait()
 
 
-def gather_weights(weight, count, ctx_count):
-    rows, width = weight.shape
+def gather_weights(weight, skip, count, ctx_count):
+    rows, width = weight.shape[0], weight.shape[1] - skip
     chips = ctx_count // 2
     parts = chips if chips == 4 and width % (128 * chips) == 0 else 1
     half, share = rows // 2, width // parts
@@ -405,21 +423,21 @@
             pushes = []
             for step in range(1, count):
                 copy = copies.make(
-                    source.at[span, pl.ds(pl.multiple_of(mine * share, 128), share)],
+                    source.at[span, pl.ds(pl.multiple_of(skip + mine * share, 128), share)],
                     held(rank, mine),
                     {"fsdp": lax.rem(rank + step, count)},
                 )
                 copy.start()
                 pushes.append(copy)
-            target[rank] = source[...]
+            target[rank] = source[:, skip:]
             for step, copy in enumerate(pushes, 1):
                 copy.wait()
                 origin = lax.rem(rank + count - step, count)
                 arrived(rank >= 0, origin, held(origin, mine))
         else:
-            target[rank] = source[...]
+            target[rank] = source[:, skip:]
             together(
-                line_gather(copies, held(rank, mine), lambda i: held(i, mine), count, arrived)
+                line_gather(copies, source.at[span, pl.ds(skip, width)], lambda i: held(i, mine), count, arrived)
             )
         for allowed, origin, part, copy in received:
 
@@ -442,12 +460,13 @@
     return full.reshape(count * rows, width)
 
 
-def gather_keys(block, weights, count, ctx_count):
+def gather_keys(block, weights, wide, count, ctx_count):
     rows, width = block.shape
     half = rows // 2
 
     def kernel(*refs):
         own, *sources = refs[: 1 + len(weights)]
+        sources = [source.at[:, pl.ds(0, wide)] for source in sources]
         gathered, *targets = refs[1 + len(weights) : 2 + 2 * len(weights)]
         local, send, recv = refs[2 + 2 * len(weights) :]
         copies = Copies(send, recv)
@@ -477,7 +496,7 @@
             copy.wait()
 
     results = [struct((ctx_count, rows, width), block.dtype)]
-    results += [struct((count,) + w.shape, w.dtype) for w in weights]
+    results += [struct((count, w.shape[0], wide), w.dtype) for w in weights]
     gathered, *full = remote_call(
         kernel, "keys", results, [block, *weights],
         [pltpu.VMEM] * (1 + len(weights)), [pl.ANY] * (1 + len(weights)),
@@ -563,81 +582,49 @@
     )
 
 
-def reduce_keys(parts, row_parts, count, ctx_count):
-    _, _, rows, width = parts.shape
+def pair_sums(parts, ctx_count):
     chips = ctx_count // 2
-    lands = (6, 1, rows, width) if chips == 4 else (chips - 1, 2, rows, width)
-
-    def kernel(given, given_rows, total, rows_total, met, paired, passing, landing,
-               row_passing, row_landing, send, recv):
+
+    def kernel(given, total, met, send, recv):
         copies = Copies(send, recv)
         _, core, _, _, sibling = own_place(ctx_count)
-        spans = (pl.ds(0, 2), pl.ds(0, 1), pl.ds(1, 1))
-        meet(ring_peers("fsdp", count) + plane_peers(ctx_count))
+        meet(plane_peers(ctx_count)[:1])
         exchanged = []
         for q in range(chips):
-            for kind in range(2):
-                copy = copies.make(
-                    given.at[kind, 2 * q + 1 - core], met.at[q, kind], {"ctx": sibling}
-                )
-                copy.start()
-                exchanged.append((q, kind, copy))
-
-        def finish(part, value):
-            total[spans[part]] = value
-
-        def planes():
-            yield
-            for q, kind, copy in exchanged:
-                copy.wait_recv()
-                paired[q, kind] = (
-                    given[kind, 2 * q + core].astype(jnp.float32)
-                    + met[q, kind].astype(jnp.float32)
-                ).astype(paired.dtype)
-            yield from plane_reduce(
-                copies, lambda q, part: paired.at[q, spans[part]],
-                passing, landing, ctx_count, finish,
-            )
-
-        together(
-            planes(),
-            line_reduce(
-                copies, lambda d: given_rows.at[d], row_passing, row_landing, count, rows_total
-            ),
-        )
-        for _, _, copy in exchanged:
+            copy = copies.make(given.at[2 * q + 1 - core], met.at[q], {"ctx": sibling})
+            copy.start()
+            exchanged.append(copy)
+        for q, copy in enumerate(exchanged):
+            copy.wait_recv()
+            total[q] = (
+                given[2 * q + core].astype(jnp.float32) + met[q].astype(jnp.float32)
+            ).astype(total.dtype)
+        for copy in exchanged:
             copy.wait_send()
 
-    _, row_count, row_width = row_parts.shape
-    return remote_call(
-        kernel, "key_sums",
-        [struct((2, rows, width), jnp.float32), struct((row_count, row_width), jnp.float32)],
-        [parts, row_parts], [pltpu.VMEM] * 2, [pltpu.VMEM] * 2,
-        [
-            pltpu.VMEM((chips, 2, rows, width), parts.dtype),
-            pltpu.VMEM((chips, 2, rows, width), parts.dtype),
-            pltpu.VMEM((2, 1, rows, width), parts.dtype),
-            pltpu.VMEM(lands, parts.dtype),
-            pltpu.VMEM((2, count - 1, row_count, row_width), parts.dtype),
-            pltpu.VMEM((2, count - 1, row_count, row_width), parts.dtype),
-        ],
-        3 * chips + 8 + 2 * count, ctx_count * rows * width * 8,
-    )
+    shape = (chips,) + parts.shape[1:]
+    (sums,) = remote_call(
+        kernel, "pair_sums", [struct(shape, parts.dtype)], [parts], [pltpu.VMEM], [pltpu.VMEM],
+        [pltpu.VMEM(shape, parts.dtype)], chips, parts.size * 4,
+    )
+    return sums
 
 
 def reduce_weights(parts, small, half_grads, row_parts, count, ctx_count):
     _, rows, width = parts.shape
     chips = ctx_count // 2
     half, share = rows // 2, width // chips
+    chunks = 2 if share % 256 == 0 else 1
+    piece = share // chunks
     row_unit = math.gcd(half, 256)
     first = max(count // 2, 1)
-    lands = (6, first, half, share) if chips == 4 else (chips - 1, count, half, share)
+    lands = (6, first, half, piece) if chips == 4 else (chips - 1, count, half, piece)
 
     own = half_grads.shape[0]
 
     def kernel(given, given_small, half_ref, given_rows, total, small_total, grads_ref, rows_total,
                row_passing, row_landing, met, paired, passing, landing, merged,
-               line_passing, line_landing, line_total, own_total, small_met, small_sum,
+               line_landing, line_total, own_total, small_met, small_sum,
                small_plane, small_plane_sum, small_line, send, recv):
         copies = Copies(send, recv)
         rank = lax.axis_index("fsdp")
@@ -646,8 +633,8 @@
         mine = pl.ds(pl.multiple_of(core * half, row_unit), half)
         theirs = pl.ds(pl.multiple_of((1 - core) * half, row_unit), half)
 
-        def columns(q):
-            return pl.ds(pl.multiple_of(q * share, 128), share)
+        def columns(q, c):
+            return pl.ds(pl.multiple_of(q * share + c * piece, 128), piece)
 
         meet(
             ring_peers("fsdp", count)
@@ -696,44 +683,48 @@
                 copy.wait()
             small_total[...] = small_plane_sum[...] + jnp.sum(small_line[...], axis=0)
 
-        def finish(part, value):
-            merged[spans[part]] = value.astype(merged.dtype)
-
-        def large_stream():
+        def large_stream(c):
+            def finish(part, value):
+                merged[c, spans[part]] = value.astype(merged.dtype)
+
             for d, copy in enumerate(exchanged[:count]):
-                copy.wait_recv()
+                if c == 0:
+                    copy.wait_recv()
                 for q in range(chips):
-                    paired[q, d] = (
-                        given[d, mine, q * share : (q + 1) * share].astype(jnp.float32)
-                        + met[d, :, q * share : (q + 1) * share].astype(jnp.float32)
+                    span = slice(q * share + c * piece, q * share + (c + 1) * piece)
+                    paired[c, q, d] = (
+                        given[d, mine, span].astype(jnp.float32)
+                        + met[d, :, span].astype(jnp.float32)
                     ).astype(paired.dtype)
             yield from plane_reduce(
-                copies, lambda q, part: paired.at[q, spans[part]],
-                passing, landing, ctx_count, finish,
+                copies, lambda q, part: paired.at[c, q, spans[part]],
+                passing.at[c], landing.at[c], ctx_count, finish,
             )
-            yield from line_reduce(
-                copies, lambda d: merged.at[d], line_passing, line_landing, count, line_total
+            yield from push_reduce(
+                copies, lambda d: merged.at[c, d], line_landing.at[c], count, line_total.at[c]
             )
-            own_total[...] = line_total[...].astype(own_total.dtype)
+            own_total[c] = line_total[c].astype(own_total.dtype)
             sent = []
             forwarded = []
-            copy = copies.make(own_total, total.at[mine, columns(chip)], {"ctx": sibling})
+            target = total.at[mine, columns(chip, c)]
+            copy = copies.make(own_total.at[c], target, {"ctx": sibling})
             copy.start()
             forwarded.append(copy)
             for step in range(1, chips):
                 copy = copies.make(
-                    own_total, total.at[mine, columns(chip)],
-                    {"ctx": lax.rem(place + 2 * step, ctx_count)},
+                    own_total.at[c], target, {"ctx": lax.rem(place + 2 * step, ctx_count)}
                 )
                 copy.start()
                 sent.append(copy)
-            total[mine, columns(chip)] = own_total[...]
+            total[mine, columns(chip, c)] = own_total[c]
+            yield
             for step, copy in enumerate(sent, 1):
                 copy.wait_recv()
-                held = total.at[mine, columns(lax.rem(chip + chips - step, chips))]
+                held = total.at[mine, columns(lax.rem(chip + chips - step, chips), c)]
                 copy = copies.make(held, held, {"ctx": sibling})
                 copy.start()
                 forwarded.append(copy)
+            yield
             for copy in sent:
                 copy.wait_send()
             for copy in forwarded:
@@ -744,7 +735,7 @@
                 copies, lambda d: given_rows.at[d], row_passing, row_landing, count, rows_total
             ),
             small_stream(),
-            large_stream(),
+            *[large_stream(c) for c in range(chunks)],
         )
         for copy in exchanged:
             copy.wait_send()
@@ -768,21 +759,20 @@
             pltpu.VMEM((2, count - 1) + row_parts.shape[1:], kind),
             pltpu.VMEM((2, count - 1) + row_parts.shape[1:], kind),
             pltpu.VMEM((count, half, width), kind),
-            pltpu.VMEM((chips, count, half, share), kind),
-            pltpu.VMEM((2, first, half, share), kind),
-            pltpu.VMEM(lands, kind),
-            pltpu.VMEM((count, half, share), kind),
-            pltpu.VMEM((2, count - 1, half, share), kind),
-            pltpu.VMEM((2, count - 1, half, share), kind),
-            pltpu.VMEM((half, share), f32),
-            pltpu.VMEM((half, share), kind),
+            pltpu.VMEM((chunks, chips, count, half, piece), kind),
+            pltpu.VMEM((chunks, 2, first, half, piece), kind),
+            pltpu.VMEM((chunks,) + lands, kind),
+            pltpu.VMEM((chunks, count, half, piece), kind),
+            pltpu.VMEM((chunks, count - 1, half, piece), kind),
+            pltpu.VMEM((chunks, half, piece), f32),
+            pltpu.VMEM((chunks, half, piece), kind),
             pltpu.VMEM(small.shape, f32),
             pltpu.VMEM(small.shape, f32),
             pltpu.VMEM((chips - 1,) + small.shape, f32),
             pltpu.VMEM(small.shape, f32),
             pltpu.VMEM((count - 1,) + small.shape, f32),
         ],
-        count + 8 + 5 * count + 4 * chips + own, parts.size * 8,
+        8 + 8 * count + 6 * chips + own + chunks * (8 + 2 * count + 3 * chips), parts.size * 8,
     )
 
 
@@ -816,40 +806,44 @@
     capacity = piece_len // 4
     count = peers * capacity
 
-    def kernel(routed, block, note, w, out_parts, grad_parts, dots, out_sum, grad_sum):
+    slots = experts * capacity
+
+    def kernel(routed, block, note, w, out_parts, grad_parts, dots, hots, taken, blocks, outs, ins):
         expert = pl.program_id(0)
         low = jnp.bfloat16
 
+        def chosen(g, first_slot, number):
+            places = (
+                lax.broadcasted_iota(jnp.int32, (number, piece_len), 0) + first_slot
+            ).astype(jnp.float32)
+            return note[g, 0:1, :] == places, note[g, 1:2, :] == places
+
         @pl.when(expert == 0)
         def _():
-            out_sum[...] = jnp.zeros_like(out_sum)
-            grad_sum[...] = jnp.zeros_like(grad_sum)
             dots[...] = jnp.zeros_like(dots)
-
-        slots = (
-            lax.broadcasted_iota(jnp.int32, (capacity, piece_len), 0) + expert * capacity
-        ).astype(jnp.float32)
-        hots, firsts, seconds, gates, taken, blocks = [], [], [], [], [], []
+            for g in range(peers):
+                first, second = chosen(g, 0, slots)
+                hots[g] = jnp.where(first | second, 1.0, 0.0).astype(low)
+                taken[g] = product(hots[g], routed[g]).astype(low)
+                blocks[g] = product(hots[g], block[g]).astype(low)
+
+        span = pl.ds(pl.multiple_of(expert * capacity, 16), capacity)
+        firsts, seconds, gates = [], [], []
         for g in range(peers):
-            first = note[g, 0:1, :] == slots
-            second = note[g, 1:2, :] == slots
+            first, second = chosen(g, expert * capacity, capacity)
             gates.append(
                 jnp.sum(
-                    jnp.where(first, note[g, 2:3, :], 0.0)
-                    + jnp.where(second, note[g, 3:4, :], 0.0),
+                    jnp.where(first, note[g, 2:3, :], jnp.where(second, note[g, 3:4, :], 0.0)),
                     axis=1,
                     keepdims=True,
                 )
             )
-            first, second = jnp.where(first, 1.0, 0.0), jnp.where(second, 1.0, 0.0)
-            hot = (first + second).astype(low)
-            taken.append(product(hot, routed[g]).astype(low))
-            blocks.append(product(hot, block[g]))
-            hots.append(hot)
             firsts.append(first)
             seconds.append(second)
-        rows = jnp.concatenate(taken, axis=0)
-        block_part = jnp.concatenate(blocks, axis=0)
+        rows = jnp.concatenate([taken[g, span, :] for g in range(peers)], axis=0)
+        block_part = jnp.concatenate(
+            [blocks[g, span, :] for g in range(peers)], axis=0
+        ).astype(jnp.float32)
         gate = jnp.concatenate(gates, axis=0)
         grad_out = (gate * block_part).astype(low)
         w_gate, w_up, w_down = w[0, 0], w[0, 1], w[0, 2]
@@ -868,16 +862,19 @@
         row_dots = jnp.sum(block_part * expert_out, axis=1, keepdims=True)
         gated = (gate * expert_out).astype(low)
         for g in range(peers):
-            span = slice(g * capacity, (g + 1) * capacity)
-            out_sum[g] += product(hots[g], gated[span], 0, 0)
-            grad_sum[g] += product(hots[g], grad_in[span], 0, 0)
-            dots[g, 0:1, :] += jnp.sum(firsts[g] * row_dots[span], axis=0, keepdims=True)
-            dots[g, 1:2, :] += jnp.sum(seconds[g] * row_dots[span], axis=0, keepdims=True)
+            part = slice(g * capacity, (g + 1) * capacity)
+            outs[g, span, :] = gated[part]
+            ins[g, span, :] = grad_in[part]
+            for k, hit in enumerate((firsts[g], seconds[g])):
+                dots[g, k : k + 1, :] += jnp.sum(
+                    jnp.where(hit, row_dots[part], 0.0), axis=0, keepdims=True
+                )
 
         @pl.when(expert == experts - 1)
         def _():
-            out_parts[...] = out_sum[...].astype(low)
-            grad_parts[...] = grad_sum[...].astype(low)
+            for g in range(peers):
+                out_parts[g] = product(hots[g], outs[g], 0, 0).astype(low)
+                grad_parts[g] = product(hots[g], ins[g], 0, 0).astype(low)
 
     rows_shape = (peers, piece_len, width)
     low = jnp.bfloat16
@@ -889,7 +886,8 @@
         [routed_rows, block_rows, notes, weights],
         [whole_block(rows_shape), whole_block(rows_shape), whole_block(notes.shape), expert_block],
         [whole_block(rows_shape), whole_block(rows_shape), whole_block(notes.shape)],
-        [pltpu.VMEM(rows_shape, jnp.float32), pltpu.VMEM(rows_shape, jnp.float32)],
+        [pltpu.VMEM((peers, slots, piece_len), low)]
+        + [pltpu.VMEM((peers, slots, width), low)] * 4,
         12 * experts * count * units * width, 2 * weights.size,
     )
 
@@ -1031,29 +1029,56 @@
     )(first, counts, routed_rows, block_rows, notes, weights)
 
 
-def other_gradients(first, received, final):
+def last_results(first, received, final, weight_sums, small, base, live, ffn_sum, few):
     own, _, units, width = received.shape
-    block = (1, 1, units, width)
-
-    def kernel(start, given, _, result):
+    rows = weight_sums.shape[0]
+    block = (1, 3, units, width)
+    shapes = [(rows, 3 * width), (rows, width), base.shape, (few, width), (2, width)]
+    shapes += [(width,), (width,), (1, width)]
+
+    def kernel(start, given, _, sums, few_sums, base_ref, live_ref, ffn, result, qkv, out, output,
+               router, const, gain_one, gain_two, mixing):
         result[...] = given[...].astype(jnp.float32)
+
+        @pl.when(pl.program_id(0) == 0)
+        def _():
+            qkv[...] = sums[:, : 3 * width].astype(jnp.float32)
+            out[...] = sums[:, 3 * width :].astype(jnp.float32)
+            output[...] = (base_ref[...] + live_ref[...] * ffn[...]).astype(output.dtype)
+            router[...] = few_sums[0:few, :]
+            const[...] = few_sums[few : few + 2, :]
+            gain_one[...] = few_sums[few + 2, :]
+            gain_two[...] = few_sums[few + 3, :]
+            mixing[...] = few_sums[few + 4 : few + 5, :]
 
     return pl.pallas_call(
         kernel,
         grid_spec=pltpu.PrefetchScalarGridSpec(
             num_scalar_prefetch=1,
-            grid=(own, 3),
+            grid=(own,),
             in_specs=[
-                pl.BlockSpec(block, lambda i, k, _: (i, k, 0, 0)),
+                pl.BlockSpec(block, lambda i, _: (i, 0, 0, 0)),
                 pl.BlockSpec(memory_space=pl.ANY),
+                whole_block(weight_sums.shape),
+                whole_block(small.shape),
+                whole_block(base.shape),
+                whole_block(live.shape),
+                whole_block(ffn_sum.shape),
             ],
-            out_specs=pl.BlockSpec(block, lambda i, k, start: (start[0] + i, k, 0, 0)),
+            out_specs=[pl.BlockSpec(block, lambda i, start: (start[0] + i, 0, 0, 0))]
+            + [whole_block(shape) for shape in shapes],
         ),
-        out_shape=struct(final.shape, jnp.float32),
+        out_shape=[
+            struct(final.shape, jnp.float32),
+            struct(shapes[0], jnp.float32),
+            struct(shapes[1], jnp.float32),
+            struct(shapes[2], jnp.bfloat16),
+        ]
+        + [struct(shape, jnp.float32) for shape in shapes[3:]],
         input_output_aliases={2: 0},
-        compiler_params=pltpu.CompilerParams(vmem_limit_bytes=60 * 1024 * 1024),
-        name="other_gradients",
-    )(first, received, final)
+        compiler_params=pltpu.CompilerParams(vmem_limit_bytes=VMEM_LIMIT),
+        name="last_results",
+    )(first, received, final, weight_sums, small, base, live, ffn_sum)
 
 
 def score_bias(length, first_row, rows, keys):
@@ -1102,23 +1127,30 @@
 
 
 def projection_gradients(
-    pair_grad, query_grad, normed, tokens, gain, turns, full_query, full_kv, mixed, grad_attention,
+    pair_grads, query_grad, normed, tokens, gain, turns, full_query, full_kv, mixed, grad_attention,
     grad_residual,
 ):
     rows, width = tokens.shape
     tile = 2 * HEAD_DIM
     low = jnp.bfloat16
 
-    def kernel(pair, query, normed_ref, token, gain_row, turn, w_query, w_kv, mix, attention,
-               residual, weight_grad, token_grad, gain_grad, projected):
+    def kernel(*refs):
+        pairs = refs[: len(pair_grads)]
+        (query, normed_ref, token, gain_row, turn, w_query, w_kv, mix, attention, residual, weight_grad,
+         token_grad, gain_grad, projected) = refs[len(pair_grads) :]
+
+        def summed(kind, span):
+            return sum(pair[kind, :, span].astype(jnp.float32) for pair in pairs)
+
         for i in range(width // tile):
             span = slice(i * tile, (i + 1) * tile)
             projected[:, span] = turn_halves(query[:, span], turn[0], -turn[1]).astype(low)
-            keys = pair[0:rows, span].astype(jnp.float32)
             projected[:, width + i * tile : width + (i + 1) * tile] = turn_halves(
-                keys, turn[0], -turn[1]
+                summed(0, span), turn[0], -turn[1]
             ).astype(low)
-        projected[:, 2 * width :] = pair[rows:, :]
+            projected[:, 2 * width + i * tile : 2 * width + (i + 1) * tile] = summed(
+                1, span
+            ).astype(low)
         for i in range(3):
             span = slice(i * width, (i + 1) * width)
             weight_grad[:, span] = product(normed_ref[...], projected[:, span], 0, 0).astype(low)
@@ -1146,7 +1178,7 @@
         scratch_shapes=[pltpu.VMEM((rows, 3 * width), low)],
         compiler_params=pltpu.CompilerParams(vmem_limit_bytes=VMEM_LIMIT),
         name="projection_gradients",
-    )(pair_grad, query_grad, normed, tokens, gain, turns, full_query, full_kv, mixed,
+    )(*pair_grads, query_grad, normed, tokens, gain, turns, full_query, full_kv, mixed,
       grad_attention, grad_residual)
 
 
@@ -1212,7 +1244,7 @@
     )(places, normed, w_query, turns, pairs, pairs)
 
 
-def attention_backward(places, queries, pairs, sums, mixed, grad_mixed):
+def attention_backward(places, queries, pairs, sums, mixed, grad_mixed, start, stop):
     rows, width = queries.shape
     keys = pairs.shape[0]
     pieces = keys // rows
@@ -1252,35 +1284,36 @@
         grad_pair[:, 0] = key_sum.astype(grad_pair.dtype).reshape(pieces, rows, tile)
         grad_pair[:, 1] = value_sum.astype(grad_pair.dtype).reshape(pieces, rows, tile)
 
-    own_block = pl.BlockSpec((rows, tile), lambda i, _: (0, i))
-    key_block = pl.BlockSpec((keys, tile), lambda i, _: (0, i))
+    own_block = pl.BlockSpec((rows, tile), lambda i, _: (0, i + start))
+    key_block = pl.BlockSpec((keys, tile), lambda i, _: (0, i + start))
+    number = stop - start
     low = jnp.bfloat16
     return pl.pallas_call(
         kernel,
         grid_spec=pltpu.PrefetchScalarGridSpec(
             num_scalar_prefetch=1,
-            grid=(tiles,),
+            grid=(number,),
             in_specs=[
                 own_block,
                 key_block,
-                pl.BlockSpec((keys, tile), lambda i, _: (0, i + tiles)),
-                pl.BlockSpec((1, 8, rows), lambda i, _: (i, 0, 0)),
+                pl.BlockSpec((keys, tile), lambda i, _: (0, i + start + tiles)),
+                pl.BlockSpec((1, 8, rows), lambda i, _: (i + start, 0, 0)),
                 own_block,
                 own_block,
             ],
             out_specs=[
-                own_block,
+                pl.BlockSpec((rows, tile), lambda i, _: (0, i)),
                 pl.BlockSpec((pieces, 2, rows, tile), lambda i, _: (0, 0, 0, i)),
             ],
             scratch_shapes=[pltpu.VMEM((keys, rows), jnp.float32)],
         ),
         out_shape=[
-            struct((rows, width), jnp.float32),
-            struct((pieces, 2, rows, width), low),
+            struct((rows, number * tile), jnp.float32),
+            struct((pieces, 2, rows, number * tile), low),
         ],
         compiler_params=pltpu.CompilerParams(vmem_limit_bytes=60 * 1024 * 1024),
         cost_estimate=pl.CostEstimate(
-            flops=10 * rows * keys * width, bytes_accessed=pairs.size * 4, transcendentals=0
+            flops=10 * rows * keys * number * tile, bytes_accessed=pairs.size * 2, transcendentals=0
         ),
         name="attention_back",
     )(places, queries, pairs, pairs, sums, mixed, grad_mixed)
@@ -1330,7 +1363,7 @@
     capacity = piece_len // 4
     slot_count = experts * capacity
     fsdp_count, ctx_count = lax.axis_size("fsdp"), lax.axis_size("ctx")
-    full_kv = gather_weights(w_qkv[:, model_width:], fsdp_count, ctx_count)
+    full_kv = gather_weights(w_qkv, model_width, fsdp_count, ctx_count)
     inputs = tokens.astype(jnp.float32)
     gain_one = gain_attn.astype(jnp.float32)
     gain_two = gain_moe.astype(jnp.float32)
@@ -1342,7 +1375,7 @@
     normed_one_low, own_pairs = project_keys(tokens[0], gain_one[None], full_kv, turns)
     cotangent_low = live_rows.astype(jnp.bfloat16) * cotangent
     all_pairs, (full_query, full_out) = gather_keys(
-        own_pairs, [w_qkv[:, :model_width], w_out], fsdp_count, ctx_count
+        own_pairs, [w_qkv, w_out], model_width, fsdp_count, ctx_count
     )
     cotangent_rows = lax.all_gather(cotangent_low, "fsdp", axis=0, tiled=True)
     cotangent_rows, all_pairs = lax.optimization_barrier((cotangent_rows, all_pairs))
@@ -1386,11 +1419,13 @@
     )
     routed_rows, all_notes = gather_rows(routed_low[0], notes, fsdp_count)
     expert_weights = w_expert.swapaxes(1, 2)
-    slot_block, routed_rows = lax.optimization_barrier((slot_block, routed_rows))
-    slot_routed = lax.all_gather(routed_rows, "ctx", axis=0, tiled=True)
     out_parts, grad_parts, dot_notes = expert_layers(
         routed_rows, cotangent_rows, all_notes, expert_weights
     )
+    slot_block, routed_rows, grad_parts = lax.optimization_barrier(
+        (slot_block, routed_rows, grad_parts)
+    )
+    slot_routed = lax.all_gather(routed_rows, "ctx", axis=0, tiled=True)
     ffn_grad, dot_sums, slot_notes = reduce_rows(
         grad_parts, dot_notes, all_notes, fsdp_count, ctx_count
     )
@@ -1431,20 +1466,27 @@
     grad_mixed = jnp.einsum(
         "gpe,de->gpd", grad_attention, full_out, preferred_element_type=jnp.float32
     ).astype(jnp.bfloat16)
+    counts = slot_notes[:, 4, :experts].astype(jnp.int32).reshape(-1)
+    first_expert = lax.rem(lax.axis_index("ctx"), 2) * (experts // 2)
+    tiles = model_width // (2 * HEAD_DIM)
     query_grad, pair_grads = attention_backward(
-        places, query_rows, all_pairs, score_sums, mixed_rows, grad_mixed[0]
-    )
-    counts = slot_notes[:, 4, :experts].astype(jnp.int32).reshape(-1)
-    counts, slot_routed, pair_grads = lax.optimization_barrier((counts, slot_routed, pair_grads))
-    first_expert = lax.rem(lax.axis_index("ctx"), 2) * (experts // 2)
+        places, query_rows, all_pairs, score_sums, mixed_rows, grad_mixed[0], 0, tiles
+    )
+    chip_grads = pair_sums(pair_grads, ctx_count)
+    counts, chip_grads = lax.optimization_barrier((counts, chip_grads))
+    chips = ctx_count // 2
+    chip = lax.axis_index("ctx") // 2
+    arrived = [lax.dynamic_index_in_dim(chip_grads, chip, 0, keepdims=False)]
+    for step in range(1, chips):
+        block = lax.dynamic_index_in_dim(chip_grads, lax.rem(chip + step, chips), 0, keepdims=False)
+        ring = [(i, (i + 2 * step) % ctx_count) for i in range(ctx_count)]
+        arrived.append(lax.ppermute(block, "ctx", ring))
     half_grads, expert_half = expert_gradients(
         first_expert.astype(jnp.int32)[None], counts, slot_routed, slot_block, slot_notes, expert_weights
     )
-    pair_grad = lax.psum_scatter(
-        pair_grads.reshape(1, -1, model_width), "ctx", scatter_dimension=1, tiled=True
-    )
+    half_grads, query_grad = lax.optimization_barrier((half_grads, query_grad))
     weight_parts, grad_inputs, grad_gain_one = projection_gradients(
-        pair_grad[0],
+        arrived,
         query_grad,
         normed_one_low,
         tokens[0],
@@ -1468,13 +1510,13 @@
         weight_parts, small, half_grads, out_parts, fsdp_count, ctx_count
     )
     other_first = (experts // 2 - first_expert).astype(jnp.int32)[None]
-    expert_sum = other_gradients(other_first, expert_grads, expert_half).swapaxes(1, 2)
-    output = (live_rows * (residual_sum + special_sum + ffn_sum[None])).astype(jnp.bfloat16)
-    weight_sum = weight_sum.astype(jnp.float32)
-    wqkv_sum, wout_sum = weight_sum[:, : 3 * model_width], weight_sum[:, 3 * model_width :]
-    router_sum, const_sum = small_sum[:few].T, small_sum[few : few + 2]
-    gain_one_sum, gain_two_sum = small_sum[few + 2], small_sum[few + 3]
-    mixing_sum = small_sum[few + 4, : few * few].reshape(few, few)
+    expert_sum, wqkv_sum, wout_sum, output, router_sum, const_sum, *rest = last_results(
+        other_first, expert_grads, expert_half, weight_sum, small_sum,
+        (live_rows * (residual_sum + special_sum))[0], live_rows[0], ffn_sum, few,
+    )
+    expert_sum, output, router_sum = expert_sum.swapaxes(1, 2), output[None], router_sum.T
+    gain_one_sum, gain_two_sum, mixing_row = rest
+    mixing_sum = mixing_row[0, : few * few].reshape(few, few)
     return (
         output,
         grad_inputs,

time: 406 us -> 400 us (0.985); the launches traced: 407 us -> 395 us
  waiting for transfers between devices: 8.88 us -> 0.1 us
  Pallas kernels: 352 us -> 346 us
    pallas_call x5 -> x6, Pallas kernels: 192 us -> 207 us  [remote_call(): pl.pallas_call(kernel, out_shape=results, in_specs=[pl.BlockSpec(memory_s...]
    pallas_call x1, Pallas kernels: 62.6 us -> 49.1 us  [expert_gradients(): pl.pallas_call(kernel, grid_spec=pltpu.PrefetchScalarGridSpec(num_scalar_...]
    all_gather x1, waiting for transfers between devices: 8.77 us -> 0.02 us  [per_device(): slot_block = lax.all_gather(cotangent_rows, 'ctx', axis=0, tiled=True)]
    pallas_call x1, Pallas kernels: 28.7 us -> 20.9 us  [local_call(): pl.pallas_call(kernel, grid=grid, out_shape=results, in_specs=in_specs, o...]
    slice x8 -> x2, local copies, waits for them, and re-layouts: 6.46 us -> 0.86 us  [the longest x1 0.7 us: per_device(): mixing_sum = mixing_row[0, :few * few].reshape(few, few)]
  transfers between devices with their start and end apart: 4 -> 6, of which waited for: 1 -> 0; matrix products, arithmetic and copies ran while one was open for 5% -> 6% of each run, Pallas kernels for 67% -> 66%
where the time goes in v6:
time: 400 us; the launch traced here: 395 us
  Pallas kernels  346 us (86%)
  between operations  14.9 us (4%)
  local copies, waits for them, and re-layouts  11.5 us (3%)
  other arithmetic  10.2 us (3%)
  matrix products  8.9 us (2%)
    pallas_call x6, Pallas kernels, remote_call(): pl.pallas_call(kernel, out_shape=results, in_specs=[pl.BlockSpec(memory_s...  207 us
    pallas_call x1, Pallas kernels, expert_gradients(): pl.pallas_call(kernel, grid_spec=pltpu.PrefetchScalarGridSpec(num_scalar_...  49.1 us
    pallas_call x1, Pallas kernels, attention_forward(): pl.pallas_call(kernel, grid_spec=pltpu.PrefetchScalarGridSpec(num_scalar_...  22 us
    pallas_call x1, Pallas kernels, attention_backward(): pl.pallas_call(kernel, grid_spec=pltpu.PrefetchScalarGridSpec(num_scalar_...  22 us
    pallas_call x1, Pallas kernels, local_call(): pl.pallas_call(kernel, grid=grid, out_shape=results, in_specs=in_specs, o...  20.9 us
    pallas_call x1, Pallas kernels, last_results(): pl.pallas_call(kernel, grid_spec=pltpu.PrefetchScalarGridSpec(num_scalar_...  12.5 us
    pallas_call x1, Pallas kernels, projection_gradients(): pl.pallas_call(kernel, out_shape=[struct((width, 4 * width), low), struct...  8.81 us
  transfers between devices with their start and end apart: 6, of which 0 were waited for; matrix products, arithmetic and copies ran while one was open for 6% of the time, Pallas kernels for 66%

profile of v6, /device:TPU:0, one launch (start us, length us, event | category | flops | bytes accessed | tf_op | source)
XLA Modules:
  0.0 394.8 jit_solution(7882703760523001356)
XLA Ops:
  7.9 1.8 broadcast_multiply_fusion
  9.8 0.0 all-gather.6.cloned.1.call-start
  9.8 1.3 reshape.480.gain_row.refs_7_
  11.1 0.5 multiply_cosine_fusion
  11.7 0.1 copy.44
  11.7 0.1 copy.45
  11.8 25.7 %weights.1 = bf16[4,192,1536]{2,1,0:T(8,128)(2,1)} custom-call(bf16[192,2304]{1,0:T(8,128)(2,1)} %refs_1_.1), custom_call_target="tpu_custom_call" | custom-call | bytes 4718592 | tf_op jit(solution)/shard_map/weights/pallas_call | solution.py:333
  37.5 0.2 maximum_bitcast_fusion
  37.7 0.7 pad_maximum_fusion.turn.refs_8_
  38.4 4.2 %project_keys.1 = (bf16[256,768]{1,0:T(8,128)(2,1)}, bf16[256,1536]{1,0:T(8,128)(2,1)}) custom-call(bf16[256,768]{1,0:T(8,128)(2,1)} %bitcast.144, f32[1,768]{1,0:T(1,128)} %reshape.480.gain_row.refs_7_, bf16[768,1536]{1,0:T(8,128)(2,1)} %bitcast.136, f32[2,256,128]{2,1,0:T(8,128)} %pad_maximum_fusion.turn.refs_8_), custom_call_target="tpu_custom_call" | custom-call | tf_op jit(solution)/shard_map/project_keys/pallas_call | solution.py:1121
  42.6 35.8 %keys.1 = (bf16[8,256,1536]{2,1,0:T(8,128)(2,1)}, bf16[4,192,768]{2,1,0:T(8,128)(2,1)}, bf16[4,192,768]{2,1,0:T(8,128)(2,1)}) custom-call(bf16[256,1536]{1,0:T(8,128)(2,1)} %get-tuple-element.56.refs_0_, bf16[192,2304]{1,0:T(8,128)(2,1)} %refs_1_.1, bf16[192,768]{1,0:T(8,128)(2,1)} %refs_2_.1), custom_call_target="tpu_custom_call" | custom-call | bytes 12582912 | tf_op jit(solution)/shard_map/keys/pallas_call | solution.py:333
  78.5 0.0 all-gather.8.cloned.1.call-start
  78.6 0.1 multiply_reduce_fusion.4
  78.7 0.2 copy.46
  78.9 0.1 copy.47
  79.0 1.1 reduce-window.6
  80.1 0.2 slice_reduce_fusion
  80.3 0.1 copy.48
  80.5 0.2 fusion.14
  80.6 0.1 reduce_sum.143
  80.8 0.1 copy.49
  80.9 0.7 pad_add_fusion.place
  81.6 22.0 %attention.1 = (bf16[256,768]{1,0:T(8,128)(2,1)}, bf16[256,768]{1,0:T(8,128)(2,1)}, f32[6,8,256]{2,1,0:T(8,128)}) custom-call(s32[2]{0:T(128)} %pad_add_fusion.place, bf16[256,768]{1,0:T(8,128)(2,1)} %get-tuple-element.59.normed_ref.refs_5_, bf16[768,768]{1,0:T(8,128)(2,1)} %bitcast.140, f32[2,256,128]{2,1,0:T(8,128)} %pad_maximum_fusion.turn.refs_8_, ...), custom_call_target="tpu_custom_call" | custom-call | flops 1610612736 | bytes 6291456 | tf_op jit(solution)/shard_map/attention/pallas_call | solution.py:1215
  103.6 1.6 multiply_reduce_fusion.2
  105.3 0.3 fusion.7
  105.6 0.5 fusion.33
  106.1 0.2 convolution_add_fusion
  106.4 0.6 select_maximum_fusion.own_notes
  107.0 34.4 %rows.1 = (bf16[4,256,768]{2,1,0:T(8,128)(2,1)}, f32[4,8,256]{2,1,0:T(8,128)}) custom-call(bf16[256,768]{1,0:T(8,128)(2,1)} %bitcast.138, f32[8,256]{1,0:T(8,128)} %select_maximum_fusion.own_notes), custom_call_target="tpu_custom_call" | custom-call | bytes 3145728 | tf_op jit(solution)/shard_map/rows/pallas_call | solution.py:333
  141.4 20.9 %experts.1 = (bf16[4,256,768]{2,1,0:T(8,128)(2,1)}, bf16[4,256,768]{2,1,0:T(8,128)(2,1)}, f32[4,8,256]{2,1,0:T(8,128)}) custom-call(bf16[4,256,768]{2,1,0:T(8,128)(2,1)} %get-tuple-element.77.routed, bf16[4,256,768]{2,1,0:T(8,128)(2,1)} %all-gather.4.cloned.1.call-done.block, f32[4,8,256]{2,1,0:T(8,128)} %get-tuple-element.65.note.own, ...), custom_call_target="tpu_custom_call" | custom-call | flops 9663676416 | bytes 18874368 | tf_op jit(solution)/shard_map/experts/pallas_call | solution.py:780
  162.4 0.7 fusion.15.live_ref
  163.1 0.5 fusion.10
  163.6 0.1 fusion.28
  163.8 1.5 fusion.5.base_ref
  165.3 0.6 fusion.8
  165.9 35.1 %row_sums.1 = (f32[256,768]{1,0:T(8,128)}, f32[8,256]{1,0:T(8,128)}, f32[8,4,8,256]{3,2,1,0:T(8,128)}) custom-call(bf16[4,256,768]{2,1,0:T(8,128)(2,1)} %get-tuple-element.67.given, f32[4,8,256]{2,1,0:T(8,128)} %get-tuple-element.68.given_notes, f32[4,8,256]{2,1,0:T(8,128)} %get-tuple-element.65.note.own), custom_call_target="tpu_custom_call" | custom-call | bytes 3145728 | tf_op jit(solution)/shard_map/row_sums/pallas_call | solution.py:333
  201.0 0.7 multiply_reduce_fusion.7
  201.7 2.3 multiply_reduce_fusion
  204.0 1.2 convert_bitcast_fusion
  205.2 1.2 convolution_convert_fusion.grad_out
  206.5 22.0 %attention_back.1 = (f32[256,768]{1,0:T(8,128)}, bf16[8,2,256,768]{3,2,1,0:T(8,128)(2,1)}) custom-call(s32[2]{0:T(128)} %pad_add_fusion.place, bf16[256,768]{1,0:T(8,128)(2,1)} %get-tuple-element.70.query, bf16[2048,1536]{1,0:T(8,128)(2,1)} %bitcast.134, bf16[2048,1536]{1,0:T(8,128)(2,1)} %bitcast.135, f32[6,8,256]{2,1,0:T(8,128)} %get-tuple-element.71.total, ...), custom_call_target="tpu_custom_call" | custom-call | flops 4026531840 | bytes 6291456 | tf_op jit(solution)/shard_map/attention_back/pallas_call | solution.py:1291
  228.4 11.3 %pair_sums.1 = bf16[4,2,256,768]{3,2,1,0:T(8,128)(2,1)} custom-call(bf16[8,2,256,768]{3,2,1,0:T(8,128)(2,1)} %get-tuple-element.74.given), custom_call_target="tpu_custom_call" | custom-call | bytes 12582912 | tf_op jit(solution)/shard_map/pair_sums/pallas_call | solution.py:333
  239.7 0.1 convolution_bitcast_fusion.3
  239.9 0.6 copy.52
  240.5 0.1 convolution_bitcast_fusion.4
  240.6 0.1 copy.50
  240.7 0.1 reshape.479
  240.8 1.0 fusion.18
  241.8 0.7 convert_element_type.94.count
  242.5 3.5 dynamic-slice_bitcast_fusion
  246.0 1.5 collective-permute-start.2
  247.5 1.3 collective-permute-start
  248.8 0.3 fusion.31
  249.1 49.1 %expert_gradients.1 = (bf16[4,3,512,768]{3,2,1,0:T(8,128)(2,1)}, f32[8,3,512,768]{3,2,1,0:T(8,128)}) custom-call(s32[1]{0:T(128)} %bitcast.37.start, s32[256]{0:T(256)} %convert_element_type.94.count, bf16[32,256,768]{2,1,0:T(8,128)(2,1)} %all-gather.8.cloned.1.call-done.routed, bf16[32,256,768]{2,1,0:T(8,128)(2,1)} %all-gather.6.cloned.1.call-done.block, ...), custom_call_target="tpu_custom_call" | custom-call | flops 19327352832 | bytes 44040192 | tf_op jit(solution)/shard_map/expert_gradients/pallas_call | solution.py:989
  298.2 0.8 copy-done.8
  299.0 0.3 copy-done.9
  299.3 0.3 copy-done.10
  299.6 8.8 %projection_gradients.1 = (bf16[768,3072]{1,0:T(8,128)(2,1)}, f32[256,768]{1,0:T(8,128)}, f32[8,768]{1,0:T(8,128)}) custom-call(bf16[2,256,768]{2,1,0:T(8,128)(2,1)} %get-tuple-element.161.refs_0_, bf16[2,256,768]{2,1,0:T(8,128)(2,1)} %copy-done.10, bf16[2,256,768]{2,1,0:T(8,128)(2,1)} %copy-done.9, bf16[2,256,768]{2,1,0:T(8,128)(2,1)} %copy-done.8, ...), custom_call_target="tpu_custom_call" | custom-call | tf_op jit(solution)/shard_map/projection_gradients/pallas_call | solution.py:1171
  308.4 0.7 slice.34
  309.2 0.6 pad.14.given_small
  309.8 64.5 %totals.1 = (bf16[192,3072]{1,0:T(8,128)(2,1)}, f32[24,768]{1,0:T(8,128)}, bf16[4,3,512,768]{3,2,1,0:T(8,128)(2,1)}, f32[256,768]{1,0:T(8,128)}) custom-call(bf16[4,192,3072]{2,1,0:T(8,128)(2,1)} %bitcast.139, f32[24,768]{1,0:T(8,128)} %pad.14.given_small, bf16[4,3,512,768]{3,2,1,0:T(8,128)(2,1)} %get-tuple-element.84.half_ref, ...), custom_call_target="tpu_custom_call" | custom-call | bytes 18874368 | tf_op jit(solution)/shard_map/totals/pallas_call | solution.py:333
  374.4 12.5 %last_results.1 = (f32[8,3,512,768]{3,2,1,0:T(8,128)}, f32[192,2304]{1,0:T(8,128)}, f32[192,768]{1,0:T(8,128)}, bf16[256,768]{1,0:T(8,128)(2,1)}, f32[12,768]{1,...) custom-call(s32[1]{0:T(128)} %bitcast.start, ...), custom_call_target="tpu_custom_call", output_to_operand_aliasing={{0}: (2, {})} | custom-call | tf_op jit(solution)/shard_map/last_results/pallas_call | solution.py:1054
  386.9 0.7 slice_reduce_fusion.1
  387.6 0.7 reshape_squeeze.3
  (64 shorter events, 0.6 us)
Async XLA Ops:
  7.2 98.4 %copy-start = (f32[768,12]{0,1:T(8,128)S(1)}, f32[768,12]{0,1:T(8,128)}, u32[]{:S(2)}) copy-start(f32[768,12]{0,1:T(8,128)} %param.22) | copy-start | bytes 110596
  7.2 71.2 %all-gather.4.cloned.1.call-start = ((), (), s32[]{:S(2)}) async-start(), calls=%async_computation | async-start | bytes 1966080 | tf_op jit(solution)/shard_map/all_gather | solution.py:1380
  9.8 152.6 %all-gather.6.cloned.1.call-start = ((), (), s32[]{:S(2)}) async-start(), calls=%async_computation.1 | async-start | bytes 14155776 | tf_op jit(solution)/shard_map/all_gather | solution.py:1382
  42.6 35.9 %copy-start.15 = (bf16[768]{0:T(1024)(128)(2,1)S(1)}, bf16[768]{0:T(1024)(128)(2,1)}, u32[]{:S(2)}) copy-start(bf16[768]{0:T(1024)(128)(2,1)} %param.21) | copy-start | bytes 4612
  42.6 35.9 %copy-start.12 = (s32[1,256,2]{1,2,0:T(2,128)S(1)}, s32[1,256,2]{1,2,0:T(2,128)}, u32[]{:S(2)}) copy-start(s32[1,256,2]{1,2,0:T(2,128)} %param.15) | copy-start | bytes 6148
  78.5 170.6 %all-gather.8.cloned.1.call-start = ((), (), s32[]{:S(2)}) async-start(), calls=%async_computation.2 | async-start | bytes 14155776 | tf_op jit(solution)/shard_map/all_gather | solution.py:1428
  81.6 22.1 %copy-start.5 = (bf16[4,192,768]{2,1,0:T(8,128)(2,1)S(1)}, bf16[4,192,768]{2,1,0:T(8,128)(2,1)}, u32[]{:S(2)}) copy-start(bf16[4,192,768]{2,1,0:T(8,128)(2,1)} %get-tuple-element.63) | copy-start | bytes 3538948
  81.6 22.1 %copy-start.6 = (bf16[1,256,768]{2,1,0:T(8,128)(2,1)S(1)}, bf16[1,256,768]{2,1,0:T(8,128)(2,1)}, u32[]{:S(2)}) copy-start(bf16[1,256,768]{2,1,0:T(8,128)(2,1)} %param.13) | copy-start | bytes 1179652
  103.6 1.7 copy-start.4
  103.6 2.4 copy-start.11
  103.6 2.4 copy-start.13
  105.6 1.4 copy-start.2
  162.3 0.8 copy-start.14
  162.3 1.5 copy-start.3
  205.2 23.2 %copy-start.7 = (bf16[256,768]{1,0:T(8,128)(2,1)}, bf16[256,768]{1,0:T(8,128)(2,1)S(1)}, u32[]{:S(2)}) copy-start(bf16[256,768]{1,0:T(8,128)(2,1)S(1)} %get-tuple-element.152.refs_12_) | copy-start | bytes 1179652
  246.0 52.2 %collective-permute-start.2 = (bf16[2,256,768]{2,1,0:T(8,128)(2,1)}, bf16[2,256,768]{2,1,0:T(8,128)(2,1)S(1)}, u32[]{:S(2)}, u32[]{:S(2)}) collective-permute-start(bf16[2,256,768]{2,1,0:T(8,128)(2,1)} %get-tuple-element.158), channel_id=1, source_target_pairs={{0,24},{4,28},{8,0},{12,4},{16,8},{20,12},{24,16},{28,20},{1,25},{... | collective-permute-start | bytes 2359304 | tf_op jit(solution)/shard_map/ppermute | solution.py:1483
  247.5 50.7 %collective-permute-start.1 = (bf16[2,256,768]{2,1,0:T(8,128)(2,1)}, bf16[2,256,768]{2,1,0:T(8,128)(2,1)S(1)}, u32[]{:S(2)}, u32[]{:S(2)}) collective-permute-start(bf16[2,256,768]{2,1,0:T(8,128)(2,1)} %get-tuple-element.159), channel_id=1, source_target_pairs={{0,16},{4,20},{8,24},{12,28},{16,0},{20,4},{24,8},{28,12},{1,17},{... | collective-permute-start | bytes 2359304 | tf_op jit(solution)/shard_map/ppermute | solution.py:1483
  247.5 50.7 %collective-permute-start = (bf16[2,256,768]{2,1,0:T(8,128)(2,1)}, bf16[2,256,768]{2,1,0:T(8,128)(2,1)S(1)}, u32[]{:S(2)}, u32[]{:S(2)}) collective-permute-start(bf16[2,256,768]{2,1,0:T(8,128)(2,1)} %get-tuple-element.160), channel_id=1, source_target_pairs={{0,8},{4,12},{8,16},{12,20},{16,24},{20,28},{24,0},{28,4},{1,9},{5... | collective-permute-start | bytes 2359304 | tf_op jit(solution)/shard_map/ppermute | solution.py:1483
  298.2 0.9 copy-start.8
  298.2 1.1 copy-start.9
  298.2 1.4 copy-start.10
  374.4 13.9 %copy-start.1 = (f32[768,12]{0,1:T(8,128)S(1)}, f32[768,12]{0,1:T(8,128)}, u32[]{:S(2)}) copy-start(f32[768,12]{0,1:T(8,128)} %param.22) | copy-start | bytes 110596
Sparse Core Ops, SparseCore 0:
  10.2 42.9 all-gather.3
  78.6 71.4 all-gather.5
  162.5 72.5 all-gather.7

commit v7 on v6

--- a/solution.py
+++ b/solution.py
@@ -582,50 +582,95 @@
     )
 
 
-def pair_sums(parts, ctx_count):
+def pair_sums(parts, early, ctx_count):
     chips = ctx_count // 2
-
-    def kernel(given, total, met, send, recv):
+    shape, kind = parts.shape[1:], parts.dtype
+    _, rows, width = shape
+    number = 0 if early is None else early.shape[1]
+    if number:
+        half, share = early.shape[2] // 2, width // 2
+        low_half = half // 2
+    else:
+        low_half = 0
+
+    def kernel(*refs):
+        given, refs = refs[0], refs[1:]
+        if number:
+            given_early, refs = refs[0], refs[1:]
+        totals, refs = refs[:chips], refs[chips:]
+        met, *met_early, send, recv = refs
         copies = Copies(send, recv)
-        _, core, _, _, sibling = own_place(ctx_count)
+        _, core, chip, _, sibling = own_place(ctx_count)
         meet(plane_peers(ctx_count)[:1])
         exchanged = []
-        for q in range(chips):
+        for k in range(chips):
+            q = lax.rem(chip + k, chips)
             copy = copies.make(given.at[2 * q + 1 - core], met.at[q], {"ctx": sibling})
             copy.start()
             exchanged.append(copy)
-        for q, copy in enumerate(exchanged):
+        if number:
+            mine = pl.ds(pl.multiple_of(core * half, 16), half)
+            theirs = pl.ds(pl.multiple_of((1 - core) * half, 16), half)
+            for which in range(2):
+                for d in range(number):
+                    copy = copies.make(
+                        given_early.at[which, d, theirs], met_early[0].at[which, d], {"ctx": sibling}
+                    )
+                    copy.start()
+                    exchanged.append(copy)
+        for k in range(chips):
+            q = lax.rem(chip + k, chips)
+            exchanged[k].wait_recv()
+            for which in range(2):
+                totals[k][which * rows : (which + 1) * rows, :] = (
+                    given[2 * q + core, which].astype(jnp.float32)
+                    + met[q, which].astype(jnp.float32)
+                ).astype(kind)
+        for copy in exchanged[chips:]:
             copy.wait_recv()
-            total[q] = (
-                given[2 * q + core].astype(jnp.float32) + met[q].astype(jnp.float32)
-            ).astype(total.dtype)
+        if number:
+            for k in range(chips):
+                q = lax.rem(chip + k, chips)
+                which = q // 2
+                columns = pl.ds(pl.multiple_of(lax.rem(q, 2) * share, 128), share)
+                for d in range(number):
+                    value = (
+                        given_early[which, d, mine, columns].astype(jnp.float32)
+                        + met_early[0][which, d, :, columns].astype(jnp.float32)
+                    ).astype(kind)
+                    place = 2 * rows + d * low_half
+                    totals[k][place : place + low_half, :share] = value[:low_half]
+                    totals[k][place : place + low_half, share:] = value[low_half:]
         for copy in exchanged:
             copy.wait_send()
 
-    shape = (chips,) + parts.shape[1:]
-    (sums,) = remote_call(
-        kernel, "pair_sums", [struct(shape, parts.dtype)], [parts], [pltpu.VMEM], [pltpu.VMEM],
-        [pltpu.VMEM(shape, parts.dtype)], chips, parts.size * 4,
-    )
-    return sums
-
-
-def reduce_weights(parts, small, half_grads, row_parts, count, ctx_count):
+    results = [struct((2 * rows + number * low_half, width), kind)] * chips
+    operands, scratch = [parts], [pltpu.VMEM((chips,) + shape, kind)]
+    if number:
+        operands = operands + [early]
+        scratch = scratch + [pltpu.VMEM((2, number, half, width), kind)]
+    return remote_call(
+        kernel, "pair_sums", results, operands, [pltpu.VMEM] * len(operands),
+        [pltpu.VMEM] * len(results), scratch, chips + 2 * number, parts.size * 4,
+    )
+
+
+def reduce_weights(parts, early, small, half_grads, row_parts, count, ctx_count):
     _, rows, width = parts.shape
     chips = ctx_count // 2
     half, share = rows // 2, width // chips
-    chunks = 2 if share % 256 == 0 else 1
-    piece = share // chunks
+    chunks = 2 if early else 1
     row_unit = math.gcd(half, 256)
     first = max(count // 2, 1)
-    lands = (6, first, half, piece) if chips == 4 else (chips - 1, count, half, piece)
+    lands = (6, first, half, share) if chips == 4 else (chips - 1, count, half, share)
 
     own = half_grads.shape[0]
 
-    def kernel(given, given_small, half_ref, given_rows, total, small_total, grads_ref, rows_total,
-               row_passing, row_landing, met, paired, passing, landing, merged,
-               line_landing, line_total, own_total, small_met, small_sum,
-               small_plane, small_plane_sum, small_line, send, recv):
+    def kernel(*refs):
+        early_refs, refs = refs[: len(early)], refs[len(early) :]
+        (given, given_small, half_ref, given_rows, total, small_total, grads_ref, rows_total,
+         row_passing, row_landing, met, paired, passing, landing, merged, line_landing, line_total,
+         own_total, small_met, small_sum, small_plane, small_plane_sum, small_line, send, recv) = refs
         copies = Copies(send, recv)
         rank = lax.axis_index("fsdp")
         place, core, chip, _, sibling = own_place(ctx_count)
@@ -633,8 +678,8 @@
         mine = pl.ds(pl.multiple_of(core * half, row_unit), half)
         theirs = pl.ds(pl.multiple_of((1 - core) * half, row_unit), half)
 
-        def columns(q, c):
-            return pl.ds(pl.multiple_of(q * share + c * piece, 128), piece)
+        def columns(q):
+            return pl.ds(pl.multiple_of(q * share, 128), share)
 
         meet(
             ring_peers("fsdp", count)
@@ -687,26 +732,28 @@
             def finish(part, value):
                 merged[c, spans[part]] = value.astype(merged.dtype)
 
-            for d, copy in enumerate(exchanged[:count]):
-                if c == 0:
+            if c > 0:
+                merged[c] = early_refs[0][...]
+            else:
+                for d, copy in enumerate(exchanged[:count]):
                     copy.wait_recv()
-                for q in range(chips):
-                    span = slice(q * share + c * piece, q * share + (c + 1) * piece)
-                    paired[c, q, d] = (
-                        given[d, mine, span].astype(jnp.float32)
-                        + met[d, :, span].astype(jnp.float32)
-                    ).astype(paired.dtype)
-            yield from plane_reduce(
-                copies, lambda q, part: paired.at[c, q, spans[part]],
-                passing.at[c], landing.at[c], ctx_count, finish,
-            )
+                    for q in range(chips):
+                        span = slice(q * share, (q + 1) * share)
+                        paired[q, d] = (
+                            given[d, mine, span].astype(jnp.float32)
+                            + met[d, :, span].astype(jnp.float32)
+                        ).astype(paired.dtype)
+                yield from plane_reduce(
+                    copies, lambda q, part: paired.at[q, spans[part]],
+                    passing, landing, ctx_count, finish,
+                )
             yield from push_reduce(
                 copies, lambda d: merged.at[c, d], line_landing.at[c], count, line_total.at[c]
             )
             own_total[c] = line_total[c].astype(own_total.dtype)
             sent = []
             forwarded = []
-            target = total.at[mine, columns(chip, c)]
+            target = total.at[c, mine, columns(chip)]
             copy = copies.make(own_total.at[c], target, {"ctx": sibling})
             copy.start()
             forwarded.append(copy)
@@ -716,11 +763,11 @@
                 )
                 copy.start()
                 sent.append(copy)
-            total[mine, columns(chip, c)] = own_total[c]
+            total[c, mine, columns(chip)] = own_total[c]
             yield
             for step, copy in enumerate(sent, 1):
                 copy.wait_recv()
-                held = total.at[mine, columns(lax.rem(chip + chips - step, chips), c)]
+                held = total.at[c, mine, columns(lax.rem(chip + chips - step, chips))]
                 copy = copies.make(held, held, {"ctx": sibling})
                 copy.start()
                 forwarded.append(copy)
@@ -735,7 +782,7 @@
                 copies, lambda d: given_rows.at[d], row_passing, row_landing, count, rows_total
             ),
             small_stream(),
-            *[large_stream(c) for c in range(chunks)],
+            *[large_stream(c) for c in reversed(range(chunks))],
         )
         for copy in exchanged:
             copy.wait_send()
@@ -747,25 +794,25 @@
     return remote_call(
         kernel, "totals",
         [
-            struct((rows, width), kind),
+            struct((chunks, rows, width), kind),
             struct(small.shape, f32),
             struct(half_grads.shape, kind),
             struct(row_parts.shape[1:], f32),
         ],
-        [parts, small, half_grads, row_parts],
-        [pltpu.VMEM, pltpu.VMEM, pl.ANY, pltpu.VMEM],
+        [*early, parts, small, half_grads, row_parts],
+        [pltpu.VMEM] * len(early) + [pltpu.VMEM, pltpu.VMEM, pl.ANY, pltpu.VMEM],
         [pltpu.VMEM, pltpu.VMEM, pl.ANY, pltpu.VMEM],
         [
             pltpu.VMEM((2, count - 1) + row_parts.shape[1:], kind),
             pltpu.VMEM((2, count - 1) + row_parts.shape[1:], kind),
             pltpu.VMEM((count, half, width), kind),
-            pltpu.VMEM((chunks, chips, count, half, piece), kind),
-            pltpu.VMEM((chunks, 2, first, half, piece), kind),
-            pltpu.VMEM((chunks,) + lands, kind),
-            pltpu.VMEM((chunks, count, half, piece), kind),
-            pltpu.VMEM((chunks, count - 1, half, piece), kind),
-            pltpu.VMEM((chunks, half, piece), f32),
-            pltpu.VMEM((chunks, half, piece), kind),
+            pltpu.VMEM((chips, count, half, share), kind),
+            pltpu.VMEM((2, first, half, share), kind),
+            pltpu.VMEM(lands, kind),
+            pltpu.VMEM((chunks, count, half, share), kind),
+            pltpu.VMEM((chunks, count - 1, half, share), kind),
+            pltpu.VMEM((chunks, half, share), f32),
+            pltpu.VMEM((chunks, half, share), kind),
             pltpu.VMEM(small.shape, f32),
             pltpu.VMEM(small.shape, f32),
             pltpu.VMEM((chips - 1,) + small.shape, f32),
@@ -1031,7 +1078,7 @@
 
 def last_results(first, received, final, weight_sums, small, base, live, ffn_sum, few):
     own, _, units, width = received.shape
-    rows = weight_sums.shape[0]
+    rows = weight_sums.shape[1]
     block = (1, 3, units, width)
     shapes = [(rows, 3 * width), (rows, width), base.shape, (few, width), (2, width)]
     shapes += [(width,), (width,), (1, width)]
@@ -1042,8 +1089,12 @@
 
         @pl.when(pl.program_id(0) == 0)
         def _():
-            qkv[...] = sums[:, : 3 * width].astype(jnp.float32)
-            out[...] = sums[:, 3 * width :].astype(jnp.float32)
+            both = sums.shape[0] == 2
+            first_part = sums[1] if both else sums[0, :, : 2 * width]
+            second_part = sums[0] if both else sums[0, :, 2 * width :]
+            qkv[:, :width] = first_part[:, :width].astype(jnp.float32)
+            qkv[:, width:] = second_part.astype(jnp.float32)
+            out[...] = first_part[:, width:].astype(jnp.float32)
             output[...] = (base_ref[...] + live_ref[...] * ffn[...]).astype(output.dtype)
             router[...] = few_sums[0:few, :]
             const[...] = few_sums[few : few + 2, :]
@@ -1127,36 +1178,37 @@
 
 
 def projection_gradients(
-    pair_grads, query_grad, normed, tokens, gain, turns, full_query, full_kv, mixed, grad_attention,
-    grad_residual,
+    pair_grads, query_rows, normed, tokens, gain, turns, full_query, full_kv, grad_residual, number
 ):
     rows, width = tokens.shape
+    below = (pair_grads[0].shape[0] - 2 * rows) // max(number, 1)
     tile = 2 * HEAD_DIM
     low = jnp.bfloat16
 
     def kernel(*refs):
         pairs = refs[: len(pair_grads)]
-        (query, normed_ref, token, gain_row, turn, w_query, w_kv, mix, attention, residual, weight_grad,
-         token_grad, gain_grad, projected) = refs[len(pair_grads) :]
+        (query, normed_ref, token, gain_row, turn, w_query, w_kv, residual, weight_grad, token_grad,
+         gain_grad, *early, projected) = refs[len(pair_grads) :]
 
         def summed(kind, span):
-            return sum(pair[kind, :, span].astype(jnp.float32) for pair in pairs)
+            place = slice(kind * rows, (kind + 1) * rows)
+            return sum(pair[place, span].astype(jnp.float32) for pair in pairs)
+
+        for d in range(number):
+            place = slice(2 * rows + d * below, 2 * rows + (d + 1) * below)
+            value = sum(pair[place, :].astype(jnp.float32) for pair in pairs).astype(low)
+            early[0][d, :below] = value[:, : width // 2]
+            early[0][d, below:] = value[:, width // 2 :]
 
         for i in range(width // tile):
             span = slice(i * tile, (i + 1) * tile)
-            projected[:, span] = turn_halves(query[:, span], turn[0], -turn[1]).astype(low)
-            projected[:, width + i * tile : width + (i + 1) * tile] = turn_halves(
-                summed(0, span), turn[0], -turn[1]
-            ).astype(low)
-            projected[:, 2 * width + i * tile : 2 * width + (i + 1) * tile] = summed(
-                1, span
-            ).astype(low)
-        for i in range(3):
+            projected[:, span] = turn_halves(summed(0, span), turn[0], -turn[1]).astype(low)
+            projected[:, width + i * tile : width + (i + 1) * tile] = summed(1, span).astype(low)
+        for i in range(2):
             span = slice(i * width, (i + 1) * width)
             weight_grad[:, span] = product(normed_ref[...], projected[:, span], 0, 0).astype(low)
-        weight_grad[:, 3 * width :] = product(mix[...], attention[...], 0, 0).astype(low)
-        grad_normed = product(projected[:, :width], w_query[...], 1, 1) + product(
-            projected[:, width:], w_kv[...], 1, 1
+        grad_normed = product(query[...], w_query[...], 1, 1) + product(
+            projected[...], w_kv[...], 1, 1
         )
         x = token[...].astype(jnp.float32)
         scaling = lax.rsqrt(jnp.mean(x * x, axis=1, keepdims=True) + EPSILON)
@@ -1171,20 +1223,21 @@
     return pl.pallas_call(
         kernel,
         out_shape=[
-            struct((width, 4 * width), low),
+            struct((width, 2 * width), low),
             struct((rows, width), jnp.float32),
             struct((8, width), jnp.float32),
-        ],
-        scratch_shapes=[pltpu.VMEM((rows, 3 * width), low)],
+        ]
+        + ([struct((number, 2 * below, width // 2), low)] if number else []),
+        scratch_shapes=[pltpu.VMEM((rows, 2 * width), low)],
         compiler_params=pltpu.CompilerParams(vmem_limit_bytes=VMEM_LIMIT),
         name="projection_gradients",
-    )(*pair_grads, query_grad, normed, tokens, gain, turns, full_query, full_kv, mixed,
-      grad_attention, grad_residual)
+    )(*pair_grads, query_rows, normed, tokens, gain, turns, full_query, full_kv, grad_residual)
 
 
 def attention_forward(places, normed, w_query, turns, pairs):
     rows, width = normed.shape
     keys = pairs.shape[0]
+    chunk = min(keys, 1024)
     tile = 2 * HEAD_DIM
     tiles = width // tile
 
@@ -1203,14 +1256,25 @@
         outs = []
         for head in range(2):
             chosen = jnp.where(own_masks[head], scaled, 0)
-            scores = product(key[...], chosen, 1, 1) + bias[...]
-            top = jnp.max(scores, axis=0, keepdims=True)
-            weights = jnp.exp(scores - top)
-            total = jnp.sum(weights, axis=0, keepdims=True)
-            probabilities = (weights * (1.0 / total)).astype(jnp.bfloat16)
-            outs.append(product(probabilities, value[...], 0, 0))
+            parts = [
+                product(key[place : place + chunk, :], chosen, 1, 1) + bias[place : place + chunk, :]
+                for place in range(0, keys, chunk)
+            ]
+            top = parts[0]
+            for part in parts[1:]:
+                top = jnp.maximum(top, part)
+            top = jnp.max(top, axis=0, keepdims=True)
+            turned, total = 0.0, 0.0
+            for i, part in enumerate(parts):
+                weights = jnp.exp(part - top)
+                total = total + jnp.sum(weights, axis=0, keepdims=True)
+                turned = turned + product(
+                    value[i * chunk : (i + 1) * chunk, :], weights.astype(jnp.bfloat16), 0, 0
+                )
+            span = slice(head * HEAD_DIM, (head + 1) * HEAD_DIM)
+            outs.append(turned[span] * (1.0 / total))
             sums[0, head : head + 1, :] = top + jnp.log(total)
-        mixed[...] = jnp.where(own_masks[0], outs[0], outs[1]).astype(mixed.dtype)
+        mixed[...] = jnp.transpose(jnp.concatenate(outs, axis=0)).astype(mixed.dtype)
 
     return pl.pallas_call(
         kernel,
@@ -1244,7 +1308,9 @@
     )(places, normed, w_query, turns, pairs, pairs)
 
 
-def attention_backward(places, queries, pairs, sums, mixed, grad_mixed, start, stop):
+def attention_backward(
+    places, queries, pairs, sums, mixed, grad_mixed, normed, turns, grad_attention
+):
     rows, width = queries.shape
     keys = pairs.shape[0]
     pieces = keys // rows
@@ -1252,7 +1318,8 @@
     tiles = width // tile
     scaling = HEAD_DIM**-0.5
 
-    def kernel(place, query, key, value, total, out, grad_out, grad_query, grad_pair, bias):
+    def kernel(place, query, key, value, total, out, grad_out, normed_ref, turn, all_out, attention,
+               grad_query, grad_pair, weight_grad, bias):
         step = pl.program_id(0)
 
         @pl.when(step == 0)
@@ -1279,44 +1346,54 @@
             value_part = product(probabilities.astype(jnp.bfloat16), upstream)
             key_sum = key_part if key_sum is None else key_sum + key_part
             value_sum = value_part if value_sum is None else value_sum + value_part
-            grads.append(product(grad_scores, key[...], 0, 0) * scaling)
-        grad_query[...] = jnp.where(own_masks[0], grads[0], grads[1])
+            span = slice(head * HEAD_DIM, (head + 1) * HEAD_DIM)
+            grads.append(product(key[...], grad_scores, 0, 0)[span] * scaling)
+        grad_query[...] = turn_halves(
+            jnp.transpose(jnp.concatenate(grads, axis=0)), turn[0], -turn[1]
+        ).astype(grad_query.dtype)
+        weight_grad[0] = product(normed_ref[...], grad_query[...], 0, 0).astype(weight_grad.dtype)
+        weight_grad[1] = product(all_out[...], attention[...], 0, 0).astype(weight_grad.dtype)
         grad_pair[:, 0] = key_sum.astype(grad_pair.dtype).reshape(pieces, rows, tile)
         grad_pair[:, 1] = value_sum.astype(grad_pair.dtype).reshape(pieces, rows, tile)
 
-    own_block = pl.BlockSpec((rows, tile), lambda i, _: (0, i + start))
-    key_block = pl.BlockSpec((keys, tile), lambda i, _: (0, i + start))
-    number = stop - start
+    own_block = pl.BlockSpec((rows, tile), lambda i, _: (0, i))
+    key_block = pl.BlockSpec((keys, tile), lambda i, _: (0, i))
     low = jnp.bfloat16
     return pl.pallas_call(
         kernel,
         grid_spec=pltpu.PrefetchScalarGridSpec(
             num_scalar_prefetch=1,
-            grid=(number,),
+            grid=(tiles,),
             in_specs=[
                 own_block,
                 key_block,
-                pl.BlockSpec((keys, tile), lambda i, _: (0, i + start + tiles)),
-                pl.BlockSpec((1, 8, rows), lambda i, _: (i + start, 0, 0)),
+                pl.BlockSpec((keys, tile), lambda i, _: (0, i + tiles)),
+                pl.BlockSpec((1, 8, rows), lambda i, _: (i, 0, 0)),
                 own_block,
+                own_block,
+                whole_block((rows, width)),
+                whole_block(turns.shape),
+                whole_block((rows, width)),
                 own_block,
             ],
             out_specs=[
-                pl.BlockSpec((rows, tile), lambda i, _: (0, i)),
+                own_block,
                 pl.BlockSpec((pieces, 2, rows, tile), lambda i, _: (0, 0, 0, i)),
+                pl.BlockSpec((2, width, tile), lambda i, _: (0, 0, i)),
             ],
             scratch_shapes=[pltpu.VMEM((keys, rows), jnp.float32)],
         ),
         out_shape=[
-            struct((rows, number * tile), jnp.float32),
-            struct((pieces, 2, rows, number * tile), low),
+            struct((rows, width), low),
+            struct((pieces, 2, rows, width), low),
+            struct((2, width, width), low),
         ],
         compiler_params=pltpu.CompilerParams(vmem_limit_bytes=60 * 1024 * 1024),
         cost_estimate=pl.CostEstimate(
-            flops=10 * rows * keys * number * tile, bytes_accessed=pairs.size * 2, transcendentals=0
+            flops=10 * rows * keys * width, bytes_accessed=pairs.size * 2, transcendentals=0
         ),
         name="attention_back",
-    )(places, queries, pairs, pairs, sums, mixed, grad_mixed)
+    )(places, queries, pairs, pairs, sums, mixed, grad_mixed, normed, turns, mixed, grad_attention)
 
 
 def normalize_rows(values, gain_row):
@@ -1468,38 +1545,40 @@
     ).astype(jnp.bfloat16)
     counts = slot_notes[:, 4, :experts].astype(jnp.int32).reshape(-1)
     first_expert = lax.rem(lax.axis_index("ctx"), 2) * (experts // 2)
-    tiles = model_width // (2 * HEAD_DIM)
-    query_grad, pair_grads = attention_backward(
-        places, query_rows, all_pairs, score_sums, mixed_rows, grad_mixed[0], 0, tiles
-    )
-    chip_grads = pair_sums(pair_grads, ctx_count)
-    counts, chip_grads = lax.optimization_barrier((counts, chip_grads))
+    query_back, pair_grads, early_parts = attention_backward(
+        places, query_rows, all_pairs, score_sums, mixed_rows, grad_mixed[0], normed_one_low, turns,
+        grad_attention[0],
+    )
+    early_parts = early_parts.reshape(2, fsdp_count, -1, model_width)
     chips = ctx_count // 2
-    chip = lax.axis_index("ctx") // 2
-    arrived = [lax.dynamic_index_in_dim(chip_grads, chip, 0, keepdims=False)]
-    for step in range(1, chips):
-        block = lax.dynamic_index_in_dim(chip_grads, lax.rem(chip + step, chips), 0, keepdims=False)
+    split = chips == 4
+    chip_grads = pair_sums(pair_grads, early_parts if split else None, ctx_count)
+    counts, *chip_grads = lax.optimization_barrier((counts, *chip_grads))
+
+    arrived = list(chip_grads[:1])
+    for step, block in enumerate(chip_grads[1:], 1):
         ring = [(i, (i + 2 * step) % ctx_count) for i in range(ctx_count)]
         arrived.append(lax.ppermute(block, "ctx", ring))
     half_grads, expert_half = expert_gradients(
         first_expert.astype(jnp.int32)[None], counts, slot_routed, slot_block, slot_notes, expert_weights
     )
-    half_grads, query_grad = lax.optimization_barrier((half_grads, query_grad))
-    weight_parts, grad_inputs, grad_gain_one = projection_gradients(
+    half_grads, query_back = lax.optimization_barrier((half_grads, query_back))
+    weight_parts, grad_inputs, grad_gain_one, *early_sums = projection_gradients(
         arrived,
-        query_grad,
+        query_back,
         normed_one_low,
         tokens[0],
         gain_one[None],
         turns,
         full_query,
         full_kv,
-        mixed_rows,
-        grad_attention[0],
         grad_residual[0],
+        fsdp_count if split else 0,
     )
     grad_inputs = grad_inputs[None]
-    weight_parts = weight_parts.reshape(fsdp_count, -1, 4 * model_width)
+    weight_parts = weight_parts.reshape(fsdp_count, -1, 2 * model_width)
+    if not split:
+        weight_parts = jnp.concatenate([early_parts[0], early_parts[1], weight_parts], axis=-1)
     few = experts + 4
     mixing_row = jnp.pad(grad_mixing.reshape(1, -1), ((0, 0), (0, model_width - few * few)))
     small = jnp.concatenate(
@@ -1507,7 +1586,7 @@
     )
     small = jnp.pad(small, ((0, -small.shape[0] % 8), (0, 0)))
     weight_sum, small_sum, expert_grads, ffn_sum = reduce_weights(
-        weight_parts, small, half_grads, out_parts, fsdp_count, ctx_count
+        weight_parts, early_sums, small, half_grads, out_parts, fsdp_count, ctx_count
     )
     other_first = (experts // 2 - first_expert).astype(jnp.int32)[None]
     expert_sum, wqkv_sum, wout_sum, output, router_sum, const_sum, *rest = last_results(

time: 400 us -> 391 us (0.978)
  Pallas kernels: 346 us -> 340 us
    pallas_call x6, Pallas kernels: 207 us -> 200 us  [remote_call(): pl.pallas_call(kernel, out_shape=results, in_specs=[pl.BlockSpec(memory_s...]
    pallas_call x1, Pallas kernels: 22 us -> 17.8 us  [attention_forward(): pl.pallas_call(kernel, grid_spec=pltpu.PrefetchScalarGridSpec(num_scalar_...]
  transfers between devices with their start and end apart: 6 -> 6, of which waited for: 0 -> 0; matrix products, arithmetic and copies ran while one was open for 6% -> 6% of each run, Pallas kernels for 66% -> 68%
where the time goes in v7:
time: 391 us; the launch traced here: 388 us
  Pallas kernels  340 us (87%)
  between operations  14.9 us (4%)
  other arithmetic  11.3 us (3%)
  matrix products  9.62 us (2%)
  local copies, waits for them, and re-layouts  7.87 us (2%)
  starting transfers between devices  4.23 us (1%)
    pallas_call x6, Pallas kernels, remote_call(): pl.pallas_call(kernel, out_shape=results, in_specs=[pl.BlockSpec(memory_s...  200 us
    pallas_call x1, Pallas kernels, expert_gradients(): pl.pallas_call(kernel, grid_spec=pltpu.PrefetchScalarGridSpec(num_scalar_...  52.2 us
    pallas_call x1, Pallas kernels, attention_backward(): pl.pallas_call(kernel, grid_spec=pltpu.PrefetchScalarGridSpec(num_scalar_...  25.4 us
    pallas_call x1, Pallas kernels, local_call(): pl.pallas_call(kernel, grid=grid, out_shape=results, in_specs=in_specs, o...  21.1 us
    pallas_call x1, Pallas kernels, attention_forward(): pl.pallas_call(kernel, grid_spec=pltpu.PrefetchScalarGridSpec(num_scalar_...  17.8 us
    pallas_call x1, Pallas kernels, last_results(): pl.pallas_call(kernel, grid_spec=pltpu.PrefetchScalarGridSpec(num_scalar_...  12.5 us
  transfers between devices with their start and end apart: 6, of which 0 were waited for; matrix products, arithmetic and copies ran while one was open for 6% of the time, Pallas kernels for 68%

profile of v7, /device:TPU:0, one launch (start us, length us, event | category | flops | bytes accessed | tf_op | source)
XLA Modules:
  0.0 388.5 jit_solution(6486866776456013097)
XLA Ops:
  7.2 0.0 all-gather.4.cloned.1.call-start
  7.9 1.8 broadcast_multiply_fusion
  9.8 0.0 all-gather.6.cloned.1.call-start
  9.8 1.3 reshape.484.gain_row.refs_7_
  11.1 0.5 multiply_cosine_fusion
  11.7 0.1 copy.44
  11.7 0.1 copy.45
  11.8 25.7 %weights.1 = bf16[4,192,1536]{2,1,0:T(8,128)(2,1)} custom-call(bf16[192,2304]{1,0:T(8,128)(2,1)} %refs_1_.1), custom_call_target="tpu_custom_call" | custom-call | bytes 4718592 | tf_op jit(solution)/shard_map/weights/pallas_call | solution.py:333
  37.5 0.2 maximum_bitcast_fusion
  37.7 0.7 pad_maximum_fusion.turn.refs_8_
  38.4 4.2 %project_keys.1 = (bf16[256,768]{1,0:T(8,128)(2,1)}, bf16[256,1536]{1,0:T(8,128)(2,1)}) custom-call(bf16[256,768]{1,0:T(8,128)(2,1)} %bitcast.136, f32[1,768]{1,0:T(1,128)} %reshape.484.gain_row.refs_7_, bf16[768,1536]{1,0:T(8,128)(2,1)} %bitcast.129, f32[2,256,128]{2,1,0:T(8,128)} %pad_maximum_fusion.turn.refs_8_), custom_call_target="tpu_custom_call" | custom-call | tf_op jit(solution)/shard_map/project_keys/pallas_call | solution.py:1172
  42.6 35.8 %keys.1 = (bf16[8,256,1536]{2,1,0:T(8,128)(2,1)}, bf16[4,192,768]{2,1,0:T(8,128)(2,1)}, bf16[4,192,768]{2,1,0:T(8,128)(2,1)}) custom-call(bf16[256,1536]{1,0:T(8,128)(2,1)} %get-tuple-element.65.refs_0_, bf16[192,2304]{1,0:T(8,128)(2,1)} %refs_1_.1, bf16[192,768]{1,0:T(8,128)(2,1)} %refs_2_.1), custom_call_target="tpu_custom_call" | custom-call | bytes 12582912 | tf_op jit(solution)/shard_map/keys/pallas_call | solution.py:333
  78.4 0.0 all-gather.8.cloned.1.call-start
  78.6 0.1 multiply_reduce_fusion.4
  78.7 0.2 copy.46
  78.9 0.1 copy.47
  79.0 1.1 reduce-window.6
  80.1 0.2 slice_reduce_fusion
  80.3 0.1 copy.48
  80.5 0.2 fusion.14
  80.6 0.1 reduce_sum.143
  80.8 0.1 copy.49
  80.9 0.6 pad_add_fusion.place
  81.5 17.8 %attention.1 = (bf16[256,768]{1,0:T(8,128)(2,1)}, bf16[256,768]{1,0:T(8,128)(2,1)}, f32[6,8,256]{2,1,0:T(8,128)}) custom-call(s32[2]{0:T(128)} %pad_add_fusion.place, bf16[256,768]{1,0:T(8,128)(2,1)} %get-tuple-element.68.normed_ref.refs_5_, bf16[768,768]{1,0:T(8,128)(2,1)} %bitcast.132, f32[2,256,128]{2,1,0:T(8,128)} %pad_maximum_fusion.turn.refs_8_, ...), custom_call_target="tpu_custom_call" | custom-call | flops 1610612736 | bytes 6291456 | tf_op jit(solution)/shard_map/attention/pallas_call | solution.py:1279
  99.3 1.6 multiply_reduce_fusion.2
  101.0 0.3 fusion.7
  101.3 0.4 fusion.33
  101.8 0.2 convolution_add_fusion
  102.1 0.6 select_maximum_fusion.own_notes
  102.7 34.3 %rows.1 = (bf16[4,256,768]{2,1,0:T(8,128)(2,1)}, f32[4,8,256]{2,1,0:T(8,128)}) custom-call(bf16[256,768]{1,0:T(8,128)(2,1)} %bitcast.131, f32[8,256]{1,0:T(8,128)} %select_maximum_fusion.own_notes), custom_call_target="tpu_custom_call" | custom-call | bytes 3145728 | tf_op jit(solution)/shard_map/rows/pallas_call | solution.py:333
  137.0 21.1 %experts.1 = (bf16[4,256,768]{2,1,0:T(8,128)(2,1)}, bf16[4,256,768]{2,1,0:T(8,128)(2,1)}, f32[4,8,256]{2,1,0:T(8,128)}) custom-call(bf16[4,256,768]{2,1,0:T(8,128)(2,1)} %get-tuple-element.94.routed, bf16[4,256,768]{2,1,0:T(8,128)(2,1)} %all-gather.4.cloned.1.call-done.block, f32[4,8,256]{2,1,0:T(8,128)} %get-tuple-element.74.note.own, ...), custom_call_target="tpu_custom_call" | custom-call | flops 9663676416 | bytes 18874368 | tf_op jit(solution)/shard_map/experts/pallas_call | solution.py:827
  158.2 0.7 fusion.15.live_ref
  158.8 0.5 fusion.10
  159.4 0.1 fusion.28
  159.5 1.5 fusion.5.base_ref
  161.0 0.6 fusion.8
  161.6 35.4 %row_sums.1 = (f32[256,768]{1,0:T(8,128)}, f32[8,256]{1,0:T(8,128)}, f32[8,4,8,256]{3,2,1,0:T(8,128)}) custom-call(bf16[4,256,768]{2,1,0:T(8,128)(2,1)} %get-tuple-element.76.given, f32[4,8,256]{2,1,0:T(8,128)} %get-tuple-element.77.given_notes, f32[4,8,256]{2,1,0:T(8,128)} %get-tuple-element.74.note.own), custom_call_target="tpu_custom_call" | custom-call | bytes 3145728 | tf_op jit(solution)/shard_map/row_sums/pallas_call | solution.py:333
  197.0 0.7 multiply_reduce_fusion.7
  197.8 3.0 multiply_reduce_fusion
  200.8 0.1 convolution_bitcast_fusion.3
  200.9 0.6 copy.52
  201.6 0.1 convolution_bitcast_fusion.4
  201.7 0.1 copy.50
  201.8 0.1 reshape.483
  201.9 1.0 fusion.18
  202.9 0.7 convert_element_type.94.count
  203.5 2.3 convert_bitcast_fusion
  205.9 1.3 convolution_convert_fusion.grad_out
  207.1 25.4 %attention_back.1 = (bf16[256,768]{1,0:T(8,128)(2,1)}, bf16[8,2,256,768]{3,2,1,0:T(8,128)(2,1)}, bf16[2,768,768]{2,1,0:T(8,128)(2,1)}) custom-call(s32[2]{0:T(128)} %pad_add_fusion.place, bf16[256,768]{1,0:T(8,128)(2,1)} %get-tuple-element.79.query, bf16[2048,1536]{1,0:T(8,128)(2,1)} %bitcast.126, bf16[2048,1536]{1,0:T(8,128)(2,1)} %bitcast.127, ...), custom_call_target="tpu_custom_call" | custom-call | flops 4026531840 | bytes 6291456 | tf_op jit(solution)/shard_map/attention_back/pallas_call | solution.py:1362
  232.5 13.4 %pair_sums.1 = (bf16[704,768]{1,0:T(8,128)(2,1)}, bf16[704,768]{1,0:T(8,128)(2,1)}, bf16[704,768]{1,0:T(8,128)(2,1)}, bf16[704,768]{1,0:T(8,128)(2,1)}) custom-call(bf16[8,2,256,768]{3,2,1,0:T(8,128)(2,1)} %get-tuple-element.83.refs_0_, bf16[2,4,192,768]{3,2,1,0:T(8,128)(2,1)} %bitcast.142), custom_call_target="tpu_custom_call" | custom-call | bytes 12582912 | tf_op jit(solution)/shard_map/pair_sums/pallas_call | solution.py:333
  246.0 0.1 collective-permute-start
  246.0 1.2 collective-permute-start.1
  247.3 2.8 collective-permute-start.2
  250.1 0.3 fusion.31
  250.4 52.2 %expert_gradients.1 = (bf16[4,3,512,768]{3,2,1,0:T(8,128)(2,1)}, f32[8,3,512,768]{3,2,1,0:T(8,128)}) custom-call(s32[1]{0:T(128)} %bitcast.34.start, s32[256]{0:T(256)} %convert_element_type.94.count, bf16[32,256,768]{2,1,0:T(8,128)(2,1)} %all-gather.8.cloned.1.call-done.routed, bf16[32,256,768]{2,1,0:T(8,128)(2,1)} %all-gather.6.cloned.1.call-done.block, ...), custom_call_target="tpu_custom_call" | custom-call | flops 19327352832 | bytes 44040192 | tf_op jit(solution)/shard_map/expert_gradients/pallas_call | solution.py:1036
  302.6 1.0 copy-done.8
  303.6 0.3 copy-done.9
  303.9 7.4 %projection_gradients.1 = (bf16[768,1536]{1,0:T(8,128)(2,1)}, f32[256,768]{1,0:T(8,128)}, f32[8,768]{1,0:T(8,128)}, bf16[4,96,384]{2,1,0:T(8,128)(2,1)}) custom-call(bf16[704,768]{1,0:T(8,128)(2,1)} %get-tuple-element.89.refs_0_, bf16[704,768]{1,0:T(8,128)(2,1)} %copy-done.8, bf16[704,768]{1,0:T(8,128)(2,1)} %copy-done.9, ...), custom_call_target="tpu_custom_call" | custom-call | tf_op jit(solution)/shard_map/projection_gradients/pallas_call | solution.py:1223
  311.3 0.7 slice.34
  312.1 0.6 pad.14.refs_2_
  312.7 55.3 %totals.1 = (bf16[2,192,1536]{2,1,0:T(8,128)(2,1)}, f32[24,768]{1,0:T(8,128)}, bf16[4,3,512,768]{3,2,1,0:T(8,128)(2,1)}, f32[256,768]{1,0:T(8,128)}) custom-call(bf16[4,96,384]{2,1,0:T(8,128)(2,1)} %get-tuple-element.99.refs_0_, bf16[4,192,1536]{2,1,0:T(8,128)(2,1)} %bitcast.141, f32[24,768]{1,0:T(8,128)} %pad.14.refs_2_, ...), custom_call_target="tpu_custom_call" | custom-call | bytes 9437184 | tf_op jit(solution)/shard_map/totals/pallas_call | solution.py:333
  368.1 12.5 %last_results.1 = (f32[8,3,512,768]{3,2,1,0:T(8,128)}, f32[192,2304]{1,0:T(8,128)}, f32[192,768]{1,0:T(8,128)}, bf16[256,768]{1,0:T(8,128)(2,1)}, f32[12,768]{1,...) custom-call(s32[1]{0:T(128)} %bitcast.start, ...), custom_call_target="tpu_custom_call", output_to_operand_aliasing={{0}: (2, {})} | custom-call | tf_op jit(solution)/shard_map/last_results/pallas_call | solution.py:1105
  380.6 0.7 slice_reduce_fusion.1
  381.3 0.7 reshape_squeeze.3
  (61 shorter events, 0.5 us)
Async XLA Ops:
  7.2 94.2 %copy-start = (f32[768,12]{0,1:T(8,128)S(1)}, f32[768,12]{0,1:T(8,128)}, u32[]{:S(2)}) copy-start(f32[768,12]{0,1:T(8,128)} %param.22) | copy-start | bytes 110596
  7.2 71.2 %all-gather.4.cloned.1.call-start = ((), (), s32[]{:S(2)}) async-start(), calls=%async_computation | async-start | bytes 1966080 | tf_op jit(solution)/shard_map/all_gather | solution.py:1457
  9.8 148.4 %all-gather.6.cloned.1.call-start = ((), (), s32[]{:S(2)}) async-start(), calls=%async_computation.1 | async-start | bytes 14155776 | tf_op jit(solution)/shard_map/all_gather | solution.py:1459
  42.6 35.9 %copy-start.14 = (bf16[768]{0:T(1024)(128)(2,1)S(1)}, bf16[768]{0:T(1024)(128)(2,1)}, u32[]{:S(2)}) copy-start(bf16[768]{0:T(1024)(128)(2,1)} %param.21) | copy-start | bytes 4612
  42.6 35.9 %copy-start.11 = (s32[1,256,2]{1,2,0:T(2,128)S(1)}, s32[1,256,2]{1,2,0:T(2,128)}, u32[]{:S(2)}) copy-start(s32[1,256,2]{1,2,0:T(2,128)} %param.15) | copy-start | bytes 6148
  78.4 171.9 %all-gather.8.cloned.1.call-start = ((), (), s32[]{:S(2)}) async-start(), calls=%async_computation.2 | async-start | bytes 14155776 | tf_op jit(solution)/shard_map/all_gather | solution.py:1505
  81.5 17.9 %copy-start.5 = (bf16[4,192,768]{2,1,0:T(8,128)(2,1)S(1)}, bf16[4,192,768]{2,1,0:T(8,128)(2,1)}, u32[]{:S(2)}) copy-start(bf16[4,192,768]{2,1,0:T(8,128)(2,1)} %get-tuple-element.72) | copy-start | bytes 3538948
  81.5 17.9 %copy-start.6 = (bf16[1,256,768]{2,1,0:T(8,128)(2,1)S(1)}, bf16[1,256,768]{2,1,0:T(8,128)(2,1)}, u32[]{:S(2)}) copy-start(bf16[1,256,768]{2,1,0:T(8,128)(2,1)} %param.13) | copy-start | bytes 1179652
  99.3 1.7 copy-start.4
  101.0 0.8 copy-start.10
  101.0 0.8 copy-start.12
  101.3 1.4 copy-start.2
  158.1 0.7 copy-start.13
  158.1 1.4 copy-start.3
  205.9 1.3 copy-start.7
  246.0 56.6 %collective-permute-start = (bf16[704,768]{1,0:T(8,128)(2,1)}, bf16[704,768]{1,0:T(8,128)(2,1)S(1)}, u32[]{:S(2)}, u32[]{:S(2)}) collective-permute-start(bf16[704,768]{1,0:T(8,128)(2,1)} %get-tuple-element.90), channel_id=1, source_target_pairs={{0,8},{4,12},{8,16},{12,20},{16,24},{20,28},{24,0},{28,4},{1,9},{5... | collective-permute-start | bytes 3244040 | tf_op jit(solution)/shard_map/ppermute | solution.py:1561
  246.0 56.5 %collective-permute-start.1 = (bf16[704,768]{1,0:T(8,128)(2,1)}, bf16[704,768]{1,0:T(8,128)(2,1)S(1)}, u32[]{:S(2)}, u32[]{:S(2)}) collective-permute-start(bf16[704,768]{1,0:T(8,128)(2,1)} %get-tuple-element.91), channel_id=1, source_target_pairs={{0,16},{4,20},{8,24},{12,28},{16,0},{20,4},{24,8},{28,12},{1,17},{... | collective-permute-start | bytes 3244040 | tf_op jit(solution)/shard_map/ppermute | solution.py:1561
  247.3 55.4 %collective-permute-start.2 = (bf16[704,768]{1,0:T(8,128)(2,1)}, bf16[704,768]{1,0:T(8,128)(2,1)}, u32[]{:S(2)}, u32[]{:S(2)}) collective-permute-start(bf16[704,768]{1,0:T(8,128)(2,1)} %get-tuple-element.92), channel_id=1, source_target_pairs={{0,24},{4,28},{8,0},{12,4},{16,8},{20,12},{24,16},{28,20},{1,25},{... | collective-permute-start | bytes 3244040 | tf_op jit(solution)/shard_map/ppermute | solution.py:1561
  302.6 1.0 copy-start.8
  302.6 1.3 copy-start.9
  368.0 13.9 %copy-start.1 = (f32[768,12]{0,1:T(8,128)S(1)}, f32[768,12]{0,1:T(8,128)}, u32[]{:S(2)}) copy-start(f32[768,12]{0,1:T(8,128)} %param.22) | copy-start | bytes 110596
Sparse Core Ops, SparseCore 0:
  10.2 42.9 all-gather.3
  78.6 71.4 all-gather.5
  158.3 71.3 all-gather.7

commit v8 on v7

--- a/solution.py
+++ b/solution.py
@@ -512,6 +512,8 @@
 def gather_rows(block, notes, count):
     def kernel(own, own_notes, gathered, all_notes, local, send, recv):
         copies = Copies(send, recv)
+        half = own.shape[0] // 2
+        parts = (pl.ds(0, half), pl.ds(half, half))
         rank = lax.axis_index("fsdp")
         meet(ring_peers("fsdp", count))
         kept = [
@@ -522,7 +524,12 @@
             copy.start()
         together(
             push_gather(copies, own_notes, lambda step: all_notes.at[rank], "fsdp", count),
-            line_gather(copies, own, lambda i: gathered.at[i], count),
+            *[
+                line_gather(
+                    copies, own.at[part], lambda i, part=part: gathered.at[i, part], count
+                )
+                for part in parts
+            ],
         )
         for copy in kept:
             copy.wait()
@@ -531,12 +538,13 @@
         kernel, "rows",
         [struct((count,) + block.shape, block.dtype), struct((count,) + notes.shape, notes.dtype)],
         [block, notes], [pltpu.VMEM] * 2, [pl.ANY] * 2, [pltpu.SemaphoreType.DMA((2,))],
-        4 * count, count * block.size * 4,
+        6 * count, count * block.size * 4,
     )
 
 
 def reduce_rows(parts, notes, shared, count, ctx_count):
     _, rows, width = parts.shape
+    half = rows // 2
 
     def kernel(given, given_notes, own, total, notes_total, all_shared,
                passing, landing, noted, send, recv):
@@ -555,7 +563,17 @@
             spread.append(copy)
         all_shared[place] = own[...]
         together(
-            line_reduce(copies, lambda d: given.at[d], passing, landing, count, total)
+            *[
+                line_reduce(
+                    copies,
+                    lambda d, part=part: given.at[d, part],
+                    passing.at[i],
+                    landing.at[i],
+                    count,
+                    total.at[part],
+                )
+                for i, part in enumerate((pl.ds(0, half), pl.ds(half, half)))
+            ]
         )
         sums = given_notes[rank]
         for step, copy in enumerate(pushes):
@@ -574,11 +592,11 @@
         ],
         [parts, notes, shared], [pltpu.VMEM] * 3, [pltpu.VMEM] * 3,
         [
-            pltpu.VMEM((2, count - 1, rows, width), parts.dtype),
-            pltpu.VMEM((2, count - 1, rows, width), parts.dtype),
+            pltpu.VMEM((2, 2, count - 1, half, width), parts.dtype),
+            pltpu.VMEM((2, 2, count - 1, half, width), parts.dtype),
             pltpu.VMEM((count - 1,) + notes.shape[1:], notes.dtype),
         ],
-        4 * count + ctx_count, count * rows * width * 4,
+        6 * count + ctx_count, count * rows * width * 4,
     )
 
 

time: 391 us -> 381 us (0.974)
  Pallas kernels: 340 us -> 325 us
    pallas_call x1, Pallas kernels: 52.2 us -> 43 us  [expert_gradients(): pl.pallas_call(kernel, grid_spec=pltpu.PrefetchScalarGridSpec(num_scalar_...]
    pallas_call x6, Pallas kernels: 200 us -> 194 us  [remote_call(): pl.pallas_call(kernel, out_shape=results, in_specs=[pl.BlockSpec(memory_s...]
  transfers between devices with their start and end apart: 6 -> 6, of which waited for: 0 -> 2; matrix products, arithmetic and copies ran while one was open for 6% -> 6% of each run, Pallas kernels for 68% -> 66%
where the time goes in v8:
time: 381 us; the launch traced here: 375 us
  Pallas kernels  325 us (85%)
  between operations  14.9 us (4%)
  other arithmetic  11.3 us (3%)
  matrix products  9.61 us (3%)
  local copies, waits for them, and re-layouts  7.5 us (2%)
  starting transfers between devices  4.47 us (1%)
    pallas_call x6, Pallas kernels, remote_call(): pl.pallas_call(kernel, out_shape=results, in_specs=[pl.BlockSpec(memory_s...  194 us
    pallas_call x1, Pallas kernels, expert_gradients(): pl.pallas_call(kernel, grid_spec=pltpu.PrefetchScalarGridSpec(num_scalar_...  43 us
    pallas_call x1, Pallas kernels, attention_backward(): pl.pallas_call(kernel, grid_spec=pltpu.PrefetchScalarGridSpec(num_scalar_...  25.4 us
    pallas_call x1, Pallas kernels, local_call(): pl.pallas_call(kernel, grid=grid, out_shape=results, in_specs=in_specs, o...  21 us
    pallas_call x1, Pallas kernels, attention_forward(): pl.pallas_call(kernel, grid_spec=pltpu.PrefetchScalarGridSpec(num_scalar_...  17.8 us
    pallas_call x1, Pallas kernels, last_results(): pl.pallas_call(kernel, grid_spec=pltpu.PrefetchScalarGridSpec(num_scalar_...  12.5 us
  transfers between devices with their start and end apart: 6, of which 2 were waited for; matrix products, arithmetic and copies ran while one was open for 6% of the time, Pallas kernels for 66%

profile of v8, /device:TPU:0, one launch (start us, length us, event | category | flops | bytes accessed | tf_op | source)
XLA Modules:
  0.0 375.3 jit_solution(10849965272840999008)
XLA Ops:
  7.9 1.8 broadcast_multiply_fusion
  9.8 0.0 all-gather.6.cloned.1.call-start
  9.8 1.3 reshape.484.gain_row.refs_7_
  11.1 0.5 multiply_cosine_fusion
  11.7 0.1 copy.44
  11.7 0.1 copy.45
  11.8 25.7 %weights.1 = bf16[4,192,1536]{2,1,0:T(8,128)(2,1)} custom-call(bf16[192,2304]{1,0:T(8,128)(2,1)} %refs_1_.1), custom_call_target="tpu_custom_call" | custom-call | bytes 4718592 | tf_op jit(solution)/shard_map/weights/pallas_call | solution.py:333
  37.5 0.2 maximum_bitcast_fusion
  37.7 0.7 pad_maximum_fusion.turn.refs_8_
  38.4 4.2 %project_keys.1 = (bf16[256,768]{1,0:T(8,128)(2,1)}, bf16[256,1536]{1,0:T(8,128)(2,1)}) custom-call(bf16[256,768]{1,0:T(8,128)(2,1)} %bitcast.136, f32[1,768]{1,0:T(1,128)} %reshape.484.gain_row.refs_7_, bf16[768,1536]{1,0:T(8,128)(2,1)} %bitcast.129, f32[2,256,128]{2,1,0:T(8,128)} %pad_maximum_fusion.turn.refs_8_), custom_call_target="tpu_custom_call" | custom-call | tf_op jit(solution)/shard_map/project_keys/pallas_call | solution.py:1190
  42.6 35.8 %keys.1 = (bf16[8,256,1536]{2,1,0:T(8,128)(2,1)}, bf16[4,192,768]{2,1,0:T(8,128)(2,1)}, bf16[4,192,768]{2,1,0:T(8,128)(2,1)}) custom-call(bf16[256,1536]{1,0:T(8,128)(2,1)} %get-tuple-element.65.refs_0_, bf16[192,2304]{1,0:T(8,128)(2,1)} %refs_1_.1, bf16[192,768]{1,0:T(8,128)(2,1)} %refs_2_.1), custom_call_target="tpu_custom_call" | custom-call | bytes 12582912 | tf_op jit(solution)/shard_map/keys/pallas_call | solution.py:333
  78.4 0.0 all-gather.8.cloned.1.call-start
  78.6 0.1 multiply_reduce_fusion.4
  78.7 0.2 copy.46
  78.9 0.1 copy.47
  79.0 1.1 reduce-window.6
  80.1 0.2 slice_reduce_fusion
  80.3 0.1 copy.48
  80.5 0.2 fusion.14
  80.6 0.1 reduce_sum.143
  80.8 0.1 copy.49
  80.9 0.6 pad_add_fusion.place
  81.5 17.8 %attention.1 = (bf16[256,768]{1,0:T(8,128)(2,1)}, bf16[256,768]{1,0:T(8,128)(2,1)}, f32[6,8,256]{2,1,0:T(8,128)}) custom-call(s32[2]{0:T(128)} %pad_add_fusion.place, bf16[256,768]{1,0:T(8,128)(2,1)} %get-tuple-element.68.normed_ref.refs_5_, bf16[768,768]{1,0:T(8,128)(2,1)} %bitcast.132, f32[2,256,128]{2,1,0:T(8,128)} %pad_maximum_fusion.turn.refs_8_, ...), custom_call_target="tpu_custom_call" | custom-call | flops 1610612736 | bytes 6291456 | tf_op jit(solution)/shard_map/attention/pallas_call | solution.py:1297
  99.3 1.6 multiply_reduce_fusion.2
  101.0 0.3 fusion.7
  101.3 0.4 fusion.33
  101.8 0.2 convolution_add_fusion
  102.1 0.6 select_maximum_fusion.own_notes
  102.7 31.5 %rows.1 = (bf16[4,256,768]{2,1,0:T(8,128)(2,1)}, f32[4,8,256]{2,1,0:T(8,128)}) custom-call(bf16[256,768]{1,0:T(8,128)(2,1)} %bitcast.131, f32[8,256]{1,0:T(8,128)} %select_maximum_fusion.own_notes), custom_call_target="tpu_custom_call" | custom-call | bytes 3145728 | tf_op jit(solution)/shard_map/rows/pallas_call | solution.py:333
  134.2 21.0 %experts.1 = (bf16[4,256,768]{2,1,0:T(8,128)(2,1)}, bf16[4,256,768]{2,1,0:T(8,128)(2,1)}, f32[4,8,256]{2,1,0:T(8,128)}) custom-call(bf16[4,256,768]{2,1,0:T(8,128)(2,1)} %get-tuple-element.94.routed, bf16[4,256,768]{2,1,0:T(8,128)(2,1)} %all-gather.4.cloned.1.call-done.block, f32[4,8,256]{2,1,0:T(8,128)} %get-tuple-element.74.note.own, ...), custom_call_target="tpu_custom_call" | custom-call | flops 9663676416 | bytes 18874368 | tf_op jit(solution)/shard_map/experts/pallas_call | solution.py:845
  155.3 0.7 fusion.15.live_ref
  155.9 0.5 fusion.10
  156.5 0.1 fusion.28
  156.6 1.5 fusion.5.base_ref
  158.1 0.6 fusion.8
  158.7 30.9 %row_sums.1 = (f32[256,768]{1,0:T(8,128)}, f32[8,256]{1,0:T(8,128)}, f32[8,4,8,256]{3,2,1,0:T(8,128)}) custom-call(bf16[4,256,768]{2,1,0:T(8,128)(2,1)} %get-tuple-element.76.given, f32[4,8,256]{2,1,0:T(8,128)} %get-tuple-element.77.given_notes, f32[4,8,256]{2,1,0:T(8,128)} %get-tuple-element.74.note.own), custom_call_target="tpu_custom_call" | custom-call | bytes 3145728 | tf_op jit(solution)/shard_map/row_sums/pallas_call | solution.py:333
  189.6 0.7 multiply_reduce_fusion.7
  190.4 3.0 multiply_reduce_fusion
  193.5 0.1 convolution_bitcast_fusion.3
  193.6 0.6 copy.52
  194.2 0.1 convolution_bitcast_fusion.4
  194.4 0.1 copy.50
  194.5 0.1 reshape.483
  194.6 1.0 fusion.18
  195.5 0.7 convert_element_type.94.count
  196.2 2.3 convert_bitcast_fusion
  198.5 1.3 convolution_convert_fusion.grad_out
  199.8 25.4 %attention_back.1 = (bf16[256,768]{1,0:T(8,128)(2,1)}, bf16[8,2,256,768]{3,2,1,0:T(8,128)(2,1)}, bf16[2,768,768]{2,1,0:T(8,128)(2,1)}) custom-call(s32[2]{0:T(128)} %pad_add_fusion.place, bf16[256,768]{1,0:T(8,128)(2,1)} %get-tuple-element.79.query, bf16[2048,1536]{1,0:T(8,128)(2,1)} %bitcast.126, bf16[2048,1536]{1,0:T(8,128)(2,1)} %bitcast.127, ...), custom_call_target="tpu_custom_call" | custom-call | flops 4026531840 | bytes 6291456 | tf_op jit(solution)/shard_map/attention_back/pallas_call | solution.py:1380
  225.2 13.4 %pair_sums.1 = (bf16[704,768]{1,0:T(8,128)(2,1)}, bf16[704,768]{1,0:T(8,128)(2,1)}, bf16[704,768]{1,0:T(8,128)(2,1)}, bf16[704,768]{1,0:T(8,128)(2,1)}) custom-call(bf16[8,2,256,768]{3,2,1,0:T(8,128)(2,1)} %get-tuple-element.83.refs_0_, bf16[2,4,192,768]{3,2,1,0:T(8,128)(2,1)} %bitcast.142), custom_call_target="tpu_custom_call" | custom-call | bytes 12582912 | tf_op jit(solution)/shard_map/pair_sums/pallas_call | solution.py:333
  238.6 1.3 collective-permute-start
  239.9 0.9 collective-permute-start.1
  240.9 2.1 collective-permute-start.2
  243.0 0.3 fusion.31
  243.3 43.0 %expert_gradients.1 = (bf16[4,3,512,768]{3,2,1,0:T(8,128)(2,1)}, f32[8,3,512,768]{3,2,1,0:T(8,128)}) custom-call(s32[1]{0:T(128)} %bitcast.34.start, s32[256]{0:T(256)} %convert_element_type.94.count, bf16[32,256,768]{2,1,0:T(8,128)(2,1)} %all-gather.8.cloned.1.call-done.routed, bf16[32,256,768]{2,1,0:T(8,128)(2,1)} %all-gather.6.cloned.1.call-done.block, ...), custom_call_target="tpu_custom_call" | custom-call | flops 19327352832 | bytes 44040192 | tf_op jit(solution)/shard_map/expert_gradients/pallas_call | solution.py:1054
  286.3 2.5 collective-permute-done.1.refs_2_
  288.7 0.1 collective-permute-done.2.refs_3_
  288.8 0.9 copy-done.9
  289.7 7.4 %projection_gradients.1 = (bf16[768,1536]{1,0:T(8,128)(2,1)}, f32[256,768]{1,0:T(8,128)}, f32[8,768]{1,0:T(8,128)}, bf16[4,96,384]{2,1,0:T(8,128)(2,1)}) custom-call(bf16[704,768]{1,0:T(8,128)(2,1)} %get-tuple-element.89.refs_0_, bf16[704,768]{1,0:T(8,128)(2,1)} %copy-done.8, bf16[704,768]{1,0:T(8,128)(2,1)} %copy-done.9, ...), custom_call_target="tpu_custom_call" | custom-call | tf_op jit(solution)/shard_map/projection_gradients/pallas_call | solution.py:1241
  297.1 0.7 slice.34
  297.9 0.6 pad.14.refs_2_
  298.5 56.3 %totals.1 = (bf16[2,192,1536]{2,1,0:T(8,128)(2,1)}, f32[24,768]{1,0:T(8,128)}, bf16[4,3,512,768]{3,2,1,0:T(8,128)(2,1)}, f32[256,768]{1,0:T(8,128)}) custom-call(bf16[4,96,384]{2,1,0:T(8,128)(2,1)} %get-tuple-element.99.refs_0_, bf16[4,192,1536]{2,1,0:T(8,128)(2,1)} %bitcast.141, f32[24,768]{1,0:T(8,128)} %pad.14.refs_2_, ...), custom_call_target="tpu_custom_call" | custom-call | bytes 9437184 | tf_op jit(solution)/shard_map/totals/pallas_call | solution.py:333
  354.9 12.5 %last_results.1 = (f32[8,3,512,768]{3,2,1,0:T(8,128)}, f32[192,2304]{1,0:T(8,128)}, f32[192,768]{1,0:T(8,128)}, bf16[256,768]{1,0:T(8,128)(2,1)}, f32[12,768]{1,...) custom-call(s32[1]{0:T(128)} %bitcast.start, ...), custom_call_target="tpu_custom_call", output_to_operand_aliasing={{0}: (2, {})} | custom-call | tf_op jit(solution)/shard_map/last_results/pallas_call | solution.py:1123
  367.4 0.7 slice_reduce_fusion.1
  368.1 0.7 reshape_squeeze.3
  (61 shorter events, 0.6 us)
Async XLA Ops:
  7.2 94.2 %copy-start = (f32[768,12]{0,1:T(8,128)S(1)}, f32[768,12]{0,1:T(8,128)}, u32[]{:S(2)}) copy-start(f32[768,12]{0,1:T(8,128)} %param.22) | copy-start | bytes 110596
  7.2 71.2 %all-gather.4.cloned.1.call-start = ((), (), s32[]{:S(2)}) async-start(), calls=%async_computation | async-start | bytes 1966080 | tf_op jit(solution)/shard_map/all_gather | solution.py:1475
  9.8 145.4 %all-gather.6.cloned.1.call-start = ((), (), s32[]{:S(2)}) async-start(), calls=%async_computation.1 | async-start | bytes 14155776 | tf_op jit(solution)/shard_map/all_gather | solution.py:1477
  42.6 35.9 %copy-start.14 = (bf16[768]{0:T(1024)(128)(2,1)S(1)}, bf16[768]{0:T(1024)(128)(2,1)}, u32[]{:S(2)}) copy-start(bf16[768]{0:T(1024)(128)(2,1)} %param.21) | copy-start | bytes 4612
  42.6 35.9 %copy-start.11 = (s32[1,256,2]{1,2,0:T(2,128)S(1)}, s32[1,256,2]{1,2,0:T(2,128)}, u32[]{:S(2)}) copy-start(s32[1,256,2]{1,2,0:T(2,128)} %param.15) | copy-start | bytes 6148
  78.4 164.8 %all-gather.8.cloned.1.call-start = ((), (), s32[]{:S(2)}) async-start(), calls=%async_computation.2 | async-start | bytes 14155776 | tf_op jit(solution)/shard_map/all_gather | solution.py:1523
  81.5 17.9 %copy-start.5 = (bf16[4,192,768]{2,1,0:T(8,128)(2,1)S(1)}, bf16[4,192,768]{2,1,0:T(8,128)(2,1)}, u32[]{:S(2)}) copy-start(bf16[4,192,768]{2,1,0:T(8,128)(2,1)} %get-tuple-element.72) | copy-start | bytes 3538948
  81.5 17.9 %copy-start.6 = (bf16[1,256,768]{2,1,0:T(8,128)(2,1)S(1)}, bf16[1,256,768]{2,1,0:T(8,128)(2,1)}, u32[]{:S(2)}) copy-start(bf16[1,256,768]{2,1,0:T(8,128)(2,1)} %param.13) | copy-start | bytes 1179652
  99.3 1.7 copy-start.4
  101.0 0.8 copy-start.10
  101.0 0.8 copy-start.12
  101.3 1.4 copy-start.2
  155.2 0.7 copy-start.13
  155.2 1.4 copy-start.3
  198.5 1.3 copy-start.7
  238.6 47.6 %collective-permute-start = (bf16[704,768]{1,0:T(8,128)(2,1)}, bf16[704,768]{1,0:T(8,128)(2,1)S(1)}, u32[]{:S(2)}, u32[]{:S(2)}) collective-permute-start(bf16[704,768]{1,0:T(8,128)(2,1)} %get-tuple-element.90), channel_id=1, source_target_pairs={{0,8},{4,12},{8,16},{12,20},{16,24},{20,28},{24,0},{28,4},{1,9},{5... | collective-permute-start | bytes 3244040 | tf_op jit(solution)/shard_map/ppermute | solution.py:1579
  239.9 48.8 %collective-permute-start.1 = (bf16[704,768]{1,0:T(8,128)(2,1)}, bf16[704,768]{1,0:T(8,128)(2,1)S(1)}, u32[]{:S(2)}, u32[]{:S(2)}) collective-permute-start(bf16[704,768]{1,0:T(8,128)(2,1)} %get-tuple-element.91), channel_id=1, source_target_pairs={{0,16},{4,20},{8,24},{12,28},{16,0},{20,4},{24,8},{28,12},{1,17},{... | collective-permute-start | bytes 3244040 | tf_op jit(solution)/shard_map/ppermute | solution.py:1579
  240.9 48.0 %collective-permute-start.2 = (bf16[704,768]{1,0:T(8,128)(2,1)}, bf16[704,768]{1,0:T(8,128)(2,1)}, u32[]{:S(2)}, u32[]{:S(2)}) collective-permute-start(bf16[704,768]{1,0:T(8,128)(2,1)} %get-tuple-element.92), channel_id=1, source_target_pairs={{0,24},{4,28},{8,0},{12,4},{16,8},{20,12},{24,16},{28,20},{1,25},{... | collective-permute-start | bytes 3244040 | tf_op jit(solution)/shard_map/ppermute | solution.py:1579
  286.3 2.5 copy-start.8
  288.7 1.0 copy-start.9
  354.9 13.9 %copy-start.1 = (f32[768,12]{0,1:T(8,128)S(1)}, f32[768,12]{0,1:T(8,128)}, u32[]{:S(2)}) copy-start(f32[768,12]{0,1:T(8,128)} %param.22) | copy-start | bytes 110596
Sparse Core Ops, SparseCore 0:
  10.2 42.9 all-gather.3
  78.6 71.4 all-gather.5
  155.4 70.6 all-gather.7
